TPU v7x, 32 devices: a whole 2x2x4 slice. The times are simulated.
32 devices in a mesh: seq: 4 (over y, x), chan: 8 (over z, core).
Axes of the slice: x: 2, y: 2, z: 4, core: 2. Of those that a mesh axis runs over, the one named last changes fastest.
Arguments:
- tokens: bfloat16 [14336, 2048], P('seq', 'chan'), may hold values from -6 to 6
- w_query: bfloat16 [2048, 256], replicated, may hold values from -0.125 to 0.125
- w_key: bfloat16 [2048, 256], replicated, may hold values from -0.125 to 0.125
- w_value: bfloat16 [2048, 2048], P(None, 'chan'), may hold values from -0.125 to 0.125
- w_out: bfloat16 [2048, 2048], replicated, may hold values from -0.125 to 0.125
- gain: float32 [2048], replicated, may hold values from 0.1 to 1.9
Outputs:
- mixed: bfloat16 [14336, 2048], P('seq', 'chan')
All inputs are finite; a program needn't handle non-finite values.
Results may differ from a plain program's by a relative error of at most 0.019.
Values may be sent and summed in bfloat16 or wider, within the bound.
No kernel may reach another device: no remote copies, remote signals or barrier semaphores. Data moves between devices by JAX's collectives and lax.ppermute only.
A program may use at most 128 MiB of HBM per device.

v0:
```python
import functools

import jax
import jax.numpy as jnp
import numpy as np
from jax import lax
from jax.experimental import pallas as pl
from jax.experimental.pallas import tpu as pltpu
from jax.sharding import PartitionSpec as P

HEADS = 16
FEAT = 16
HEAD_DIM = 128
PACKED = 160
LANES = 128
HELD = LANES // FEAT
MIB = 1024 * 1024

F32 = jnp.float32
BF16 = jnp.bfloat16
NN = (((1,), (0,)), ((), ()))
NT = (((1,), (1,)), ((), ()))


def dot(a, b, dims=NN):
    return lax.dot_general(a, b, dims, preferred_element_type=F32)


def feature_tables():
    first = np.zeros((FEAT, PACKED), np.float32)
    second = np.zeros((FEAT, PACKED), np.float32)
    first_bias = np.zeros((PACKED,), np.float32)
    second_bias = np.zeros((PACKED,), np.float32)
    scale = np.zeros((PACKED,), np.float32)
    first_bias[0] = second_bias[0] = scale[0] = 1.0
    place = 1
    for i in range(FEAT):
        first[i, place] = 1.0
        second_bias[place] = 1.0
        scale[place] = 1.0 / 4.0
        place += 1
    for i in range(FEAT):
        for j in range(i, FEAT):
            first[i, place] = 1.0
            second[j, place] = 1.0
            scale[place] = 1.0 / 32.0 if i == j else 1.0 / 16.0
            place += 1
    return first, second, first_bias, second_bias, scale


def placed(table):
    out = np.zeros((HELD, LANES, PACKED), np.float32)
    for place in range(HELD):
        out[place, place * FEAT : (place + 1) * FEAT] = table
    return out


def project_kernel(
    per_group, x_ref, wq_ref, wk_ref, wv_ref, ta_ref, tb_ref, bias_ref, q_ref, k_ref, v_ref, s_ref, row_ref
):
    step = pl.program_id(0)
    groups, _, width = x_ref.shape

    @pl.when(step == 0)
    def _():
        for c in range(groups):
            row_ref[:, c * width : (c + 1) * width] = x_ref[c]
        q_ref[...] = dot(row_ref[...], wq_ref[...]).astype(BF16)
        k_ref[...] = dot(row_ref[...], wk_ref[...]).astype(BF16)

    wv = wv_ref[...].reshape(row_ref.shape[1], wv_ref.shape[-1])
    value = dot(row_ref[...], wv).astype(BF16)
    v_ref[...] = value
    for i in range(per_group):
        head = step * per_group + i
        lanes = pl.multiple_of((head // HELD) * LANES, LANES)
        key = k_ref[:, pl.ds(lanes, LANES)]
        place = lax.rem(head, HELD)
        left = dot(ta_ref[place], key, NT) + bias_ref[:, 0:1]
        right = dot(tb_ref[place], key, NT) + bias_ref[:, 1:2]
        phi = (left * right).astype(BF16)
        s_ref[i] = dot(phi, value[:, i * HEAD_DIM : (i + 1) * HEAD_DIM]).astype(BF16)


def local_kernel(per_group, q_ref, k_ref, v_ref, ta_ref, tb_ref, bias_ref, num_ref, phi_ref):
    step = pl.program_id(0)
    rows = q_ref.shape[0]
    half = rows // 2
    for i in range(per_group):
        head = step * per_group + i
        lanes = pl.multiple_of((head // HELD) * LANES, LANES)
        place = lax.rem(head, HELD)
        query = q_ref[:, pl.ds(lanes, LANES)]
        key = k_ref[:, pl.ds(lanes, LANES)]
        left = dot(query, ta_ref[place]) + bias_ref[0:1]
        right = dot(query, tb_ref[place]) + bias_ref[1:2]
        phi_ref[i] = (left * right).astype(BF16)
        lane = lax.broadcasted_iota(jnp.int32, (rows, LANES), 1)
        mine = jnp.where(lane // FEAT == place, query * jnp.asarray(0.25, BF16), jnp.zeros_like(query))
        columns = slice(i * HEAD_DIM, (i + 1) * HEAD_DIM)
        for low in (0, half):
            seen = low + half
            s = dot(mine[low:seen], key[:seen], NT)
            weight = 1.0 + s + 0.5 * s * s
            t_at = lax.broadcasted_iota(jnp.int32, (half, seen), 0) + low
            j_at = lax.broadcasted_iota(jnp.int32, (half, seen), 1)
            weight = jnp.where(t_at >= j_at, weight, 0.0).astype(BF16)
            num_ref[low:seen, columns] = dot(weight, v_ref[:seen, columns])


def prefix_kernel(slab_ref, line_ref, totals_ref, out_ref):
    run = jnp.zeros(line_ref.shape[1:], F32)
    for s in range(totals_ref.shape[0]):
        keep = jnp.where(s < slab_ref[0], 1.0, 0.0)
        run = run + totals_ref[s].astype(F32) * keep
    for c in range(line_ref.shape[0]):
        out_ref[c] = run.astype(BF16)
        run = run + line_ref[c].astype(F32)


def output_kernel(head_steps, out_steps, num_ref, phi_ref, state_ref, gain_ref, w_ref, out_ref, hidden_ref):
    step = pl.program_id(0)
    per_step = HEADS // head_steps

    @pl.when(step < head_steps)
    def _():
        for i in range(per_step):
            columns = slice(i * HEAD_DIM, (i + 1) * HEAD_DIM)
            num = num_ref[:, columns] + dot(phi_ref[i], state_ref[i])
            mean_square = jnp.mean(num * num, axis=1, keepdims=True)
            hidden = num * lax.rsqrt(mean_square + 1e-05) * gain_ref[:, columns]
            at = pl.multiple_of((step * per_step + i) * HEAD_DIM, HEAD_DIM)
            hidden_ref[:, pl.ds(at, HEAD_DIM)] = hidden.astype(BF16)

    @pl.when(step >= head_steps)
    def _():
        width = out_ref.shape[2]
        for c in range(out_ref.shape[0]):
            part = dot(hidden_ref[...], w_ref[:, c * width : (c + 1) * width])
            out_ref[c] = part.astype(BF16)


def whole(shape):
    return pl.BlockSpec(shape, lambda i: (0,) * len(shape))


def params(mib):
    return pltpu.CompilerParams(vmem_limit_bytes=mib * MIB)


def per_device(tokens, w_query, w_key, w_value, w_out, gain):
    groups = lax.axis_size("chan")
    slabs = lax.axis_size("seq")
    my_slab = lax.axis_index("seq")
    width = tokens.shape[1]
    rows = tokens.shape[0] // groups
    model = w_value.shape[0]
    value_width = w_value.shape[1]
    part = model // slabs
    per_group = HEADS // groups
    narrow = w_query.shape[1]

    first, second, first_bias, second_bias, scale = feature_tables()
    key_a = jnp.asarray(placed(first).transpose(0, 2, 1), BF16)
    key_b = jnp.asarray(placed(second).transpose(0, 2, 1), BF16)
    key_bias = jnp.asarray(np.stack([first_bias, second_bias], axis=1))
    query_a = jnp.asarray(placed(first * scale), BF16)
    query_b = jnp.asarray(placed(second), BF16)
    query_bias = jnp.asarray(np.stack([first_bias * scale, second_bias]))

    value_part = lax.dynamic_slice_in_dim(w_value, my_slab * part, part, 0)
    value_all = lax.all_gather(value_part, "chan", axis=0, tiled=False)
    value_all = lax.all_gather(value_all, "seq", axis=0, tiled=False)

    x = lax.all_to_all(
        tokens.reshape(groups, rows, width), "chan", split_axis=0, concat_axis=0, tiled=True
    )
    query, key, value, own = pl.pallas_call(
        functools.partial(project_kernel, per_group),
        grid=(groups,),
        in_specs=[
            whole((groups, rows, width)),
            whole((model, narrow)),
            whole((model, narrow)),
            pl.BlockSpec((slabs, 1, part, value_width), lambda i: (0, i, 0, 0)),
            whole((HELD, PACKED, LANES)),
            whole((HELD, PACKED, LANES)),
            whole((PACKED, 2)),
        ],
        out_specs=[
            whole((rows, narrow)),
            whole((rows, narrow)),
            pl.BlockSpec((rows, value_width), lambda i: (0, i)),
            pl.BlockSpec((per_group, PACKED, HEAD_DIM), lambda i: (i, 0, 0)),
        ],
        out_shape=[
            jax.ShapeDtypeStruct((rows, narrow), BF16),
            jax.ShapeDtypeStruct((rows, narrow), BF16),
            jax.ShapeDtypeStruct((rows, model), BF16),
            jax.ShapeDtypeStruct((HEADS, PACKED, HEAD_DIM), BF16),
        ],
        scratch_shapes=[pltpu.VMEM((rows, model), BF16)],
        compiler_params=params(32),
        cost_estimate=pl.CostEstimate(
            flops=2 * rows * model * (model + 2 * narrow), bytes_accessed=14 * MIB, transcendentals=0
        ),
    )(x, w_query, w_key, value_all, key_a, key_b, key_bias)

    line = lax.all_to_all(
        own.reshape(groups, per_group, PACKED, HEAD_DIM), "chan", split_axis=0, concat_axis=0, tiled=True
    )
    total = jnp.sum(line.astype(F32), axis=0).astype(BF16)
    totals = lax.all_gather(total, "seq", axis=0, tiled=False)
    vmem = pl.BlockSpec(memory_space=pltpu.VMEM)
    prefix = pl.pallas_call(
        prefix_kernel,
        in_specs=[pl.BlockSpec(memory_space=pltpu.SMEM), vmem, vmem],
        out_specs=vmem,
        out_shape=jax.ShapeDtypeStruct(line.shape, BF16),
    )(my_slab.reshape(1), line, totals)
    prefix = lax.all_to_all(prefix, "chan", split_axis=0, concat_axis=0, tiled=True)
    prefix = prefix.reshape(HEADS, PACKED, HEAD_DIM)

    local, phi = pl.pallas_call(
        functools.partial(local_kernel, per_group),
        grid=(groups,),
        in_specs=[
            whole((rows, narrow)),
            whole((rows, narrow)),
            pl.BlockSpec((rows, value_width), lambda i: (0, i)),
            whole((HELD, LANES, PACKED)),
            whole((HELD, LANES, PACKED)),
            whole((2, PACKED)),
        ],
        out_specs=[
            pl.BlockSpec((rows, value_width), lambda i: (0, i)),
            pl.BlockSpec((per_group, rows, PACKED), lambda i: (i, 0, 0)),
        ],
        out_shape=[
            jax.ShapeDtypeStruct((rows, model), F32),
            jax.ShapeDtypeStruct((HEADS, rows, PACKED), BF16),
        ],
        compiler_params=params(32),
        cost_estimate=pl.CostEstimate(
            flops=HEADS * rows * rows * 600, bytes_accessed=8 * MIB, transcendentals=0
        ),
    )(query, key, value, query_a, query_b, query_bias)

    head_steps = 4
    out_steps = 4
    per_step = HEADS // head_steps
    per_out = groups // out_steps
    out = pl.pallas_call(
        functools.partial(output_kernel, head_steps, out_steps),
        grid=(head_steps + out_steps,),
        in_specs=[
            pl.BlockSpec((rows, per_step * HEAD_DIM), lambda i: (0, jnp.minimum(i, head_steps - 1))),
            pl.BlockSpec((per_step, rows, PACKED), lambda i: (jnp.minimum(i, head_steps - 1), 0, 0)),
            pl.BlockSpec((per_step, PACKED, HEAD_DIM), lambda i: (jnp.minimum(i, head_steps - 1), 0, 0)),
            pl.BlockSpec((1, per_step * HEAD_DIM), lambda i: (0, jnp.minimum(i, head_steps - 1))),
            pl.BlockSpec((model, per_out * width), lambda i: (0, jnp.maximum(i - head_steps, 0))),
        ],
        out_specs=pl.BlockSpec((per_out, rows, width), lambda i: (jnp.maximum(i - head_steps, 0), 0, 0)),
        out_shape=jax.ShapeDtypeStruct((groups, rows, width), BF16),
        scratch_shapes=[pltpu.VMEM((rows, model), BF16)],
        compiler_params=params(32),
        cost_estimate=pl.CostEstimate(
            flops=2 * rows * model * model, bytes_accessed=16 * MIB, transcendentals=0
        ),
    )(local, phi, prefix, gain.reshape(1, HEADS * HEAD_DIM), w_out)
    out = lax.all_to_all(out, "chan", split_axis=0, concat_axis=0, tiled=True)
    return out.reshape(groups * rows, width)


def solution(mesh):
    return jax.shard_map(
        per_device,
        mesh=mesh,
        in_specs=(P("seq", "chan"), P(), P(), P(None, "chan"), P(), P()),
        out_specs=P("seq", "chan"),
        check_vma=False,
    )
```

profile of v0, /device:TPU:0, one launch (start us, length us, event | category | flops | bytes accessed | tf_op | source)
XLA Modules:
  0.0 277.6 jit_solution(5577744927896481122)
XLA Ops:
  6.5 1.2 copy-done
  7.8 0.7 constant_dynamic-slice_fusion
  8.5 0.0 all-gather.6.cloned.1.call-update
  8.5 0.0 all-gather.8.cloned.1.call-start
  8.6 32.2 %all-gather.6.cloned.1.call-done = bf16[4096,256]{1,0:T(8,128)(2,1)} async-done(((bf16[512,256]{1,0:T(8,128)(2,1)}), bf16[4096,256]{1,0:T(8,128)(2,1)}) %all-gather.6.cloned.1.call-update) | async-done | bytes 2097168 | tf_op jit(solution)/shard_map/all_gather | solution.py:172
  40.8 0.0 all-gather.8.cloned.1.call-update
  40.8 47.1 %all_to_all.20.x_ref = bf16[8,448,256]{2,1,0:T(8,128)(2,1)S(1)} all-to-all(bf16[8,448,256]{2,1,0:T(8,128)(2,1)} %bitcast.15), channel_id=1, replica_groups=mesh['seq'=4,'chan'=8] {'chan'}, dimensions={0} | all-to-all | bytes 3670016 | tf_op jit(solution)/shard_map/all_to_all | solution.py:175
  87.9 41.8 %all-gather.8.cloned.1.call-done = bf16[32,512,256]{2,1,0:T(8,128)(2,1)} async-done(((bf16[8,512,256]{2,1,0:T(8,128)(2,1)}), bf16[32,512,256]{2,1,0:T(8,128)(2,1)}) %all-gather.8.cloned.1.call-update) | async-done | bytes 8388624 | tf_op jit(solution)/shard_map/all_gather | solution.py:173
  129.8 3.4 %copy-done.7 = bf16[32,512,256]{2,1,0:T(8,128)(2,1)S(1)} copy-done((bf16[32,512,256]{2,1,0:T(8,128)(2,1)S(1)}, bf16[32,512,256]{2,1,0:T(8,128)(2,1)}, u32[]{:S(2)}) %copy-start.7) | copy-done | bytes 8388632
  133.2 1.2 copy-done.8
  134.4 1.2 copy-done.9
  135.6 0.9 copy-done.14
  136.5 12.9 %shard_map.118 = (bf16[448,256]{1,0:T(8,128)(2,1)S(1)}, bf16[448,256]{1,0:T(8,128)(2,1)S(1)}, bf16[448,2048]{1,0:T(8,128)(2,1)S(1)}, bf16[16,160,128]{2,1,0:T(8,128)(2,1)S(1)}) custom-call(bf16[8,448,256]{2,1,0:T(8,128)(2,1)S(1)} %all_to_all.20.x_ref, bf16[2048,256]{1,0:T(8,128)(2,1)S(1)} %copy-done.8, bf16[2048,256]{1,0:T(8,128)(2,1)S(1)} %copy-done.9, ...), custom_call_target="tpu_custom_call" | custom-call | flops 4697620480 | bytes 14680064 | tf_op jit(solution)/shard_map/pallas_call | solution.py:178
  149.4 1.2 copy-done.16
  150.6 0.7 copy-done.18
  151.3 0.7 copy-done.20
  152.0 22.6 %all_to_all.21.line_ref = bf16[8,2,160,128]{3,2,1,0:T(8,128)(2,1)S(1)} all-to-all(bf16[8,2,160,128]{3,2,1,0:T(8,128)(2,1)S(1)} %bitcast.10), channel_id=1, replica_groups=mesh['seq'=4,'chan'=8] {'chan'}, dimensions={0} | all-to-all | bytes 1310720 | tf_op jit(solution)/shard_map/all_to_all | solution.py:209
  174.5 0.1 reduce_sum.12
  174.7 10.0 %all-gather.2 = bf16[8,160,128]{2,1,0:T(8,128)(2,1)} all-gather(bf16[2,160,128]{2,1,0:T(8,128)(2,1)S(1)} %reduce_sum.12), channel_id=4, replica_groups=mesh['seq'=4,'chan'=8] {'seq'}, dimensions={0}, use_global_device_ids=true | all-gather | bytes 409600 | tf_op jit(solution)/shard_map/all_gather | solution.py:213
  184.7 2.2 shard_map.120
  186.9 3.5 %all-to-all-start.2 = ((bf16[8,2,160,128]{3,2,1,0:T(8,128)(2,1)}), bf16[8,2,160,128]{3,2,1,0:T(8,128)(2,1)S(1)}, u32[]{:S(2)}, u32[]{:S(2)}) async-start(bf16[8,2,160,128]{3,2,1,0:T(8,128)(2,1)} %shard_map.120), calls=%async_computation.2 | async-start | bytes 1310720 | tf_op jit(solution)/shard_map/all_to_all | solution.py:221
  190.5 1.5 copy-done.17
  192.0 8.6 %shard_map.119 = (f32[448,2048]{1,0:T(8,128)S(1)}, bf16[16,448,160]{2,1,0:T(8,128)(2,1)S(1)}) custom-call(bf16[448,256]{1,0:T(8,128)(2,1)S(1)} %copy-done.19, bf16[448,256]{1,0:T(8,128)(2,1)S(1)} %copy-done.21, bf16[448,2048]{1,0:T(8,128)(2,1)S(1)} %copy-done.17, bf16[8,128,160]{2,1,0:T(8,128)(2,1)S(1)} %copy-done.11, bf16[8,128,160]{2,1,0:T(8,128)(2,1)S(1)} %copy-done.10, ...), custom_call_target="tpu_custom_call" | custom-call | flops 1926758400 | bytes 8388608 | tf_op jit(solution)/shard_map/pallas_call | solution.py:224
  200.6 1.8 copy-done.2
  202.4 1.8 copy-done.4
  204.2 4.3 %all-to-all-done.2 = bf16[8,2,160,128]{3,2,1,0:T(8,128)(2,1)S(1)} async-done(((bf16[8,2,160,128]{3,2,1,0:T(8,128)(2,1)}), bf16[8,2,160,128]{3,2,1,0:T(8,128)(2,1)S(1)}, u32[]{:S(2)}, u32[]{:S(2)}) %all-to-all-start.2) | async-done | bytes 655392 | tf_op jit(solution)/shard_map/all_to_all | solution.py:221
  208.5 3.4 %copy-done.1 = bf16[2048,2048]{1,0:T(8,128)(2,1)S(1)} copy-done((bf16[2048,2048]{1,0:T(8,128)(2,1)S(1)}, bf16[2048,2048]{1,0:T(8,128)(2,1)}, u32[]{:S(2)}) %copy-start.1) | copy-done | bytes 8388632
  211.9 2.0 copy-done.3
  214.0 2.0 copy-done.5
  216.0 7.7 %shard_map.121 = bf16[8,448,256]{2,1,0:T(8,128)(2,1)S(1)} custom-call(f32[448,2048]{1,0:T(8,128)S(1)} %copy-done.3, bf16[16,448,160]{2,1,0:T(8,128)(2,1)S(1)} %copy-done.5, bf16[16,160,128]{2,1,0:T(8,128)(2,1)S(1)} %bitcast.9, f32[1,2048]{1,0:T(1,128)S(1)} %bitcast.11, bf16[2048,2048]{1,0:T(8,128)(2,1)S(1)} %copy-done.1), custom_call_target="tpu_custom_call" | custom-call | flops 3758096384 | bytes 16777216 | tf_op jit(solution)/shard_map/pallas_call | solution.py:253
  223.7 45.9 %all_to_all.22 = bf16[8,448,256]{2,1,0:T(8,128)(2,1)S(1)} all-to-all(bf16[8,448,256]{2,1,0:T(8,128)(2,1)S(1)} %shard_map.121), channel_id=1, replica_groups=mesh['seq'=4,'chan'=8] {'chan'}, dimensions={0} | all-to-all | bytes 3670016 | tf_op jit(solution)/shard_map/all_to_all | solution.py:271
  269.6 1.2 copy.14
  (33 shorter events, 0.1 us)
Async XLA Ops:
  6.5 1.2 copy-start
  6.5 34.3 %all-gather.6.cloned.1.call-start = ((), (), s32[]{:S(2)}) async-start(), calls=%async_computation.4 | async-start | bytes 2359296 | tf_op jit(solution)/shard_map/all_gather | solution.py:172
  8.5 121.3 %all-gather.8.cloned.1.call-start = ((), (), s32[]{:S(2)}) async-start(), calls=%async_computation.5 | async-start | bytes 10485760 | tf_op jit(solution)/shard_map/all_gather | solution.py:173
  40.8 89.0 %copy-start.12 = (bf16[8,160,128]{2,1,0:T(8,128)(2,1)S(1)}, bf16[8,160,128]{2,1,0:T(8,128)(2,1)}, u32[]{:S(2)}) copy-start(bf16[8,160,128]{2,1,0:T(8,128)(2,1)} %constant.27.clone.tb_ref) | copy-start | bytes 983044
  40.8 88.9 %copy-start.13 = (bf16[8,160,128]{2,1,0:T(8,128)(2,1)S(1)}, bf16[8,160,128]{2,1,0:T(8,128)(2,1)}, u32[]{:S(2)}) copy-start(bf16[8,160,128]{2,1,0:T(8,128)(2,1)} %constant.26.clone.ta_ref) | copy-start | bytes 983044
  129.8 3.4 %copy-start.7 = (bf16[32,512,256]{2,1,0:T(8,128)(2,1)S(1)}, bf16[32,512,256]{2,1,0:T(8,128)(2,1)}, u32[]{:S(2)}) copy-start(bf16[32,512,256]{2,1,0:T(8,128)(2,1)} %all-gather.8.cloned.1.call-done) | copy-start | bytes 25165828
  133.2 1.2 copy-start.8
  134.4 1.2 copy-start.9
  135.6 0.9 copy-start.14
  149.4 1.2 copy-start.16
  150.6 0.7 copy-start.18
  151.3 0.7 copy-start.20
  174.5 10.1 %copy-start.22 = (bf16[8,2,160,128]{3,2,1,0:T(8,128)(2,1)}, bf16[8,2,160,128]{3,2,1,0:T(8,128)(2,1)S(1)}, u32[]{:S(2)}) copy-start(bf16[8,2,160,128]{3,2,1,0:T(8,128)(2,1)S(1)} %all_to_all.21.line_ref) | copy-start | bytes 1966084
  174.6 15.8 %copy-start.10 = (bf16[8,128,160]{2,1,0:T(8,128)(2,1)S(1)}, bf16[8,128,160]{2,1,0:T(8,128)(2,1)}, u32[]{:S(2)}) copy-start(bf16[8,128,160]{2,1,0:T(8,128)(2,1)} %constant.30.clone.tb_ref) | copy-start | bytes 983044
  174.6 15.8 %copy-start.11 = (bf16[8,128,160]{2,1,0:T(8,128)(2,1)S(1)}, bf16[8,128,160]{2,1,0:T(8,128)(2,1)}, u32[]{:S(2)}) copy-start(bf16[8,128,160]{2,1,0:T(8,128)(2,1)} %constant.29.clone.ta_ref) | copy-start | bytes 983044
  174.7 15.8 %copy-start.15 = (f32[2,160]{1,0:T(2,128)S(1)}, f32[2,160]{1,0:T(2,128)}, u32[]{:S(2)}) copy-start(f32[2,160]{1,0:T(2,128)} %constant.31.clone.bias_ref) | copy-start | bytes 3844
  174.7 15.8 %copy-start.19 = (bf16[448,256]{1,0:T(8,128)(2,1)S(1)}, bf16[448,256]{1,0:T(8,128)(2,1)}, u32[]{:S(2)}) copy-start(bf16[448,256]{1,0:T(8,128)(2,1)} %copy-done.18) | copy-start | bytes 688132
  174.7 15.8 %copy-start.21 = (bf16[448,256]{1,0:T(8,128)(2,1)S(1)}, bf16[448,256]{1,0:T(8,128)(2,1)}, u32[]{:S(2)}) copy-start(bf16[448,256]{1,0:T(8,128)(2,1)} %copy-done.20) | copy-start | bytes 688132
  186.9 21.6 %all-to-all-start.2 = ((bf16[8,2,160,128]{3,2,1,0:T(8,128)(2,1)}), bf16[8,2,160,128]{3,2,1,0:T(8,128)(2,1)S(1)}, u32[]{:S(2)}, u32[]{:S(2)}) async-start(bf16[8,2,160,128]{3,2,1,0:T(8,128)(2,1)} %shard_map.120), calls=%async_computation.2 | async-start | bytes 1310720 | tf_op jit(solution)/shard_map/all_to_all | solution.py:221
  190.5 1.5 copy-start.17
  192.0 16.5 %copy-start.6 = (f32[2048]{0:T(1024)S(1)}, f32[2048]{0:T(1024)}, u32[]{:S(2)}) copy-start(f32[2048]{0:T(1024)} %param.17) | copy-start | bytes 24580
  200.6 1.8 copy-start.2
  202.3 1.8 copy-start.4
  208.5 3.4 %copy-start.1 = (bf16[2048,2048]{1,0:T(8,128)(2,1)S(1)}, bf16[2048,2048]{1,0:T(8,128)(2,1)}, u32[]{:S(2)}) copy-start(bf16[2048,2048]{1,0:T(8,128)(2,1)} %w_ref.1) | copy-start | bytes 25165828
  211.9 2.0 copy-start.3
  213.9 2.0 copy-start.5
Sparse Core Ops, SparseCore 0:
  9.0 31.7 all-gather.5
  42.6 87.0 all-gather.7
where the time goes:
time: 278 us
  blocking collectives  126 us (45%)
  waiting for transfers between devices  78.5 us (28%)
  Pallas kernels  31.3 us (11%)
  local copies, waits for them, and re-layouts  25.1 us (9%)
  between operations  13.6 us (5%)
  starting transfers between devices  3.58 us (1%)
    all_to_all x1, blocking collectives, per_device(): lax.all_to_all(tokens.reshape(groups, rows, width), 'chan', split_axis=0,...  47.1 us
    all_to_all x1, blocking collectives, per_device(): out = lax.all_to_all(out, 'chan', split_axis=0, concat_axis=0, tiled=True)  45.9 us
    all_gather x1, waiting for transfers between devices, per_device(): value_all = lax.all_gather(value_all, 'seq', axis=0, tiled=False)  41.8 us
    all_gather x1, waiting for transfers between devices, per_device(): value_all = lax.all_gather(value_part, 'chan', axis=0, tiled=False)  32.2 us
    unnamed x47, local copies, waits for them, and re-layouts  24.4 us
    all_to_all x1, blocking collectives, per_device(): lax.all_to_all(own.reshape(groups, per_group, PACKED, HEAD_DIM), 'chan',...  22.6 us
    pallas_call x1, Pallas kernels, per_device(): pl.pallas_call(functools.partial(project_kernel, per_group), grid=(groups...  12.9 us
    all_gather x1, blocking collectives, per_device(): totals = lax.all_gather(total, 'seq', axis=0, tiled=False)  9.98 us
  transfers between devices with their start and end apart: 3, of which 3 were waited for; matrix products, arithmetic and copies ran while one was open for 0% of the time, Pallas kernels for 3%

commit v1 on v0

v1 whole, which is shorter than its diff:
```python
import jax
import jax.numpy as jnp
import numpy as np
from jax import lax
from jax.experimental import pallas as pl
from jax.experimental.pallas import tpu as pltpu
from jax.sharding import PartitionSpec as P

HEADS = 16
FEAT = 16
HEAD_DIM = 128
PACKED = 160
LANES = 128
HELD = LANES // FEAT
MIB = 1024 * 1024

F32 = jnp.float32
BF16 = jnp.bfloat16
NN = (((1,), (0,)), ((), ()))
NT = (((1,), (1,)), ((), ()))


def dot(a, b, dims=NN):
    return lax.dot_general(a, b, dims, preferred_element_type=F32)


def feature_tables():
    first = np.zeros((FEAT, PACKED), np.float32)
    second = np.zeros((FEAT, PACKED), np.float32)
    first_bias = np.zeros((PACKED,), np.float32)
    second_bias = np.zeros((PACKED,), np.float32)
    scale = np.zeros((PACKED,), np.float32)
    first_bias[0] = second_bias[0] = scale[0] = 1.0
    place = 1
    for i in range(FEAT):
        first[i, place] = 1.0
        second_bias[place] = 1.0
        scale[place] = 1.0 / 4.0
        place += 1
    for i in range(FEAT):
        for j in range(i, FEAT):
            first[i, place] = 1.0
            second[j, place] = 1.0
            scale[place] = 1.0 / 32.0 if i == j else 1.0 / 16.0
            place += 1
    return first, second, first_bias, second_bias, scale


def placed(table):
    out = np.zeros((HELD, LANES, PACKED), np.float32)
    for place in range(HELD):
        out[place, place * FEAT : (place + 1) * FEAT] = table
    return out


def project_kernel(
    core_ref,
    per_group,
    first_mine,
    second_mine,
    first_other,
    second_other,
    wq_ref,
    wk_ref,
    wv_ref,
    ta_ref,
    tb_ref,
    bias_ref,
    q_ref,
    k_ref,
    v_ref,
    early_ref,
    total_ref,
    row_ref,
):
    step = pl.program_id(0)
    core = core_ref[0]
    layers, rows, width = first_mine.shape

    @pl.when(step == 0)
    def _():
        for chunk, (mine, other) in enumerate(
            ((first_mine, first_other), (second_mine, second_other))
        ):
            at = slice(chunk * rows, (chunk + 1) * rows)
            for z in range(layers):
                here = pl.multiple_of((2 * z + core) * width, width)
                there = pl.multiple_of((2 * z + 1 - core) * width, width)
                row_ref[at, pl.ds(here, width)] = mine[z]
                row_ref[at, pl.ds(there, width)] = other[z]
            q_ref[chunk] = dot(row_ref[at, :], wq_ref[...]).astype(BF16)
            k_ref[chunk] = dot(row_ref[at, :], wk_ref[...]).astype(BF16)

    wv = wv_ref[...].reshape(row_ref.shape[1], wv_ref.shape[-1])
    for chunk in range(2):
        value = dot(row_ref[chunk * rows : (chunk + 1) * rows, :], wv).astype(BF16)
        v_ref[chunk] = value
        for i in range(per_group):
            head = (2 * step + core) * per_group + i
            lanes = pl.multiple_of((head // HELD) * LANES, LANES)
            key = k_ref[chunk, :, pl.ds(lanes, LANES)]
            place = lax.rem(head, HELD)
            left = dot(ta_ref[place], key, NT) + bias_ref[:, 0:1]
            right = dot(tb_ref[place], key, NT) + bias_ref[:, 1:2]
            phi = (left * right).astype(BF16)
            state = dot(phi, value[:, i * HEAD_DIM : (i + 1) * HEAD_DIM])
            if chunk == 0:
                early_ref[i] = state.astype(BF16)
                total_ref[i] = state
            else:
                total_ref[i] = total_ref[i] + state


def local_kernel(
    core_ref, per_group, q_ref, k_ref, v_ref, early_ref, ta_ref, tb_ref, bias_ref, num_ref, phi_ref
):
    chunk = pl.program_id(0)
    step = pl.program_id(1)
    rows = q_ref.shape[1]
    half = rows // 2
    for i in range(per_group):
        head = (2 * step + core_ref[0]) * per_group + i
        lanes = pl.multiple_of((head // HELD) * LANES, LANES)
        place = lax.rem(head, HELD)
        query = q_ref[0, :, pl.ds(lanes, LANES)]
        key = k_ref[0, :, pl.ds(lanes, LANES)]
        left = dot(query, ta_ref[place]) + bias_ref[0:1]
        right = dot(query, tb_ref[place]) + bias_ref[1:2]
        phi_ref[0, i] = (left * right).astype(BF16)
        lane = lax.broadcasted_iota(jnp.int32, (rows, LANES), 1)
        mine = jnp.where(lane // FEAT == place, query * jnp.asarray(0.25, BF16), jnp.zeros_like(query))
        columns = slice(i * HEAD_DIM, (i + 1) * HEAD_DIM)
        for low in (0, half):
            seen = low + half
            s = dot(mine[low:seen], key[:seen], NT)
            weight = 1.0 + s + 0.5 * s * s
            t_at = lax.broadcasted_iota(jnp.int32, (half, seen), 0) + low
            j_at = lax.broadcasted_iota(jnp.int32, (half, seen), 1)
            weight = jnp.where(t_at >= j_at, weight, 0.0).astype(BF16)
            num_ref[0, low:seen, columns] = dot(weight, v_ref[0, :seen, columns])

        @pl.when(chunk == 1)
        def _():
            num_ref[0, :, columns] += dot(phi_ref[0, i], early_ref[i])


def prefix_kernel(slab_ref, line_ref, totals_ref, out_ref):
    run = jnp.zeros(line_ref.shape[1:], F32)
    for s in range(totals_ref.shape[0]):
        keep = jnp.where(s < slab_ref[0], 1.0, 0.0)
        run = run + totals_ref[s].astype(F32) * keep
    for c in range(line_ref.shape[0]):
        out_ref[c] = run.astype(BF16)
        run = run + line_ref[c].astype(F32)


def hidden_kernel(chunk_ref, num_ref, phi_ref, state_ref, gain_ref, out_ref):
    for i in range(phi_ref.shape[1]):
        columns = slice(i * HEAD_DIM, (i + 1) * HEAD_DIM)
        num = num_ref[0, :, columns] + dot(phi_ref[0, i], state_ref[i])
        mean_square = jnp.mean(num * num, axis=1, keepdims=True)
        hidden = num * lax.rsqrt(mean_square + 1e-05) * gain_ref[:, columns]
        out_ref[:, columns] = hidden.astype(BF16)


def output_kernel(core_ref, layers, mine_ref, other_ref, w_ref, out_ref, hidden_ref):
    core = core_ref[0]

    @pl.when(pl.program_id(0) == 0)
    def _():
        block = mine_ref.shape[1] // layers
        for z in range(layers):
            columns = slice(z * block, (z + 1) * block)
            here = pl.multiple_of((2 * z + core) * block, block)
            there = pl.multiple_of((2 * z + 1 - core) * block, block)
            hidden_ref[:, pl.ds(here, block)] = mine_ref[:, columns]
            hidden_ref[:, pl.ds(there, block)] = other_ref[:, columns]

    width = out_ref.shape[2]
    for c in range(out_ref.shape[0]):
        part = dot(hidden_ref[...], w_ref[:, c * width : (c + 1) * width])
        out_ref[c] = part.astype(BF16)


def whole(shape):
    return pl.BlockSpec(shape, lambda *_: (0,) * len(shape))


def params(mib):
    return pltpu.CompilerParams(vmem_limit_bytes=mib * MIB)


def call(kernel, scalar, grid, in_specs, out_specs, out_shape, args, flops, scratch=(), mib=60):
    return pl.pallas_call(
        kernel,
        grid_spec=pltpu.PrefetchScalarGridSpec(
            num_scalar_prefetch=1,
            grid=grid,
            in_specs=in_specs,
            out_specs=out_specs,
            scratch_shapes=list(scratch),
        ),
        out_shape=out_shape,
        compiler_params=params(mib),
        cost_estimate=pl.CostEstimate(flops=flops, bytes_accessed=12 * MIB, transcendentals=0),
    )(scalar, *args)


def per_device(tokens, w_query, w_key, w_value, w_out, gain):
    slabs = lax.axis_size("seq")
    layers = lax.axis_size("z")
    groups = 2 * layers
    my_slab = lax.axis_index("seq")
    core = lax.axis_index("core").astype(jnp.int32)
    which = core.reshape(1)
    width = tokens.shape[1]
    rows = tokens.shape[0] // groups
    model, value_width = w_value.shape
    part = model // slabs
    per_group = HEADS // groups
    heads = HEADS // 2
    narrow = w_query.shape[1]
    swap = [(0, 1), (1, 0)]

    first, second, first_bias, second_bias, scale = feature_tables()
    key_a = jnp.asarray(placed(first).transpose(0, 2, 1), BF16)
    key_b = jnp.asarray(placed(second).transpose(0, 2, 1), BF16)
    key_bias = jnp.asarray(np.stack([first_bias, second_bias], axis=1))
    query_a = jnp.asarray(placed(first * scale), BF16)
    query_b = jnp.asarray(placed(second), BF16)
    query_bias = jnp.asarray(np.stack([first_bias * scale, second_bias]))
    gain_mine = lax.dynamic_index_in_dim(gain.reshape(layers, 2, value_width), core, 1, False)
    gain_mine = gain_mine.reshape(1, layers * value_width)

    value_part = lax.dynamic_slice_in_dim(w_value, my_slab * part, part, 0)
    value_all = lax.all_gather(value_part, "z", axis=0, tiled=False)
    value_all = lax.all_gather(value_all, "seq", axis=0, tiled=False)

    blocks = tokens.reshape(layers, 2, rows, width)
    mine = [
        lax.all_to_all(blocks[:, chunk], "z", split_axis=0, concat_axis=0, tiled=True)
        for chunk in range(2)
    ]
    other = [lax.ppermute(half, "core", swap) for half in mine]

    query, key, value, early, total = call(
        lambda core_ref, *refs: project_kernel(core_ref, per_group, *refs),
        which,
        (layers,),
        [whole((layers, rows, width))] * 4
        + [
            whole((model, narrow)),
            whole((model, narrow)),
            pl.BlockSpec((slabs, 1, part, value_width), lambda i, _: (0, i, 0, 0)),
            whole((HELD, PACKED, LANES)),
            whole((HELD, PACKED, LANES)),
            whole((PACKED, 2)),
        ],
        [
            whole((2, rows, narrow)),
            whole((2, rows, narrow)),
            pl.BlockSpec((2, rows, value_width), lambda i, _: (0, 0, i)),
            pl.BlockSpec((per_group, PACKED, HEAD_DIM), lambda i, _: (i, 0, 0)),
            pl.BlockSpec((per_group, PACKED, HEAD_DIM), lambda i, _: (i, 0, 0)),
        ],
        [
            jax.ShapeDtypeStruct((2, rows, narrow), BF16),
            jax.ShapeDtypeStruct((2, rows, narrow), BF16),
            jax.ShapeDtypeStruct((2, rows, layers * value_width), BF16),
            jax.ShapeDtypeStruct((heads, PACKED, HEAD_DIM), BF16),
            jax.ShapeDtypeStruct((heads, PACKED, HEAD_DIM), F32),
        ],
        (mine[0], mine[1], other[0], other[1], w_query, w_key, value_all, key_a, key_b, key_bias),
        4 * rows * model * (model // 2 + 2 * narrow),
        [pltpu.VMEM((2 * rows, model), BF16)],
    )

    own = total.astype(BF16).reshape(layers, per_group, PACKED, HEAD_DIM)
    line = lax.all_to_all(own, "z", split_axis=0, concat_axis=0, tiled=True)
    slab_total = jnp.sum(line.astype(F32), axis=0).astype(BF16)
    totals = lax.all_gather(slab_total, "seq", axis=0, tiled=False)
    vmem = pl.BlockSpec(memory_space=pltpu.VMEM)
    prefix = pl.pallas_call(
        prefix_kernel,
        in_specs=[pl.BlockSpec(memory_space=pltpu.SMEM), vmem, vmem],
        out_specs=vmem,
        out_shape=jax.ShapeDtypeStruct(line.shape, BF16),
    )(my_slab.reshape(1), line, totals)
    prefix = lax.all_to_all(prefix, "z", split_axis=0, concat_axis=0, tiled=True)
    prefix = prefix.reshape(heads, PACKED, HEAD_DIM)

    local, phi = call(
        lambda core_ref, *refs: local_kernel(core_ref, per_group, *refs),
        which,
        (2, layers),
        [
            pl.BlockSpec((1, rows, narrow), lambda c, i, _: (c, 0, 0)),
            pl.BlockSpec((1, rows, narrow), lambda c, i, _: (c, 0, 0)),
            pl.BlockSpec((1, rows, value_width), lambda c, i, _: (c, 0, i)),
            pl.BlockSpec((per_group, PACKED, HEAD_DIM), lambda c, i, _: (i, 0, 0)),
            whole((HELD, LANES, PACKED)),
            whole((HELD, LANES, PACKED)),
            whole((2, PACKED)),
        ],
        [
            pl.BlockSpec((1, rows, value_width), lambda c, i, _: (c, 0, i)),
            pl.BlockSpec((1, per_group, rows, PACKED), lambda c, i, _: (c, i, 0, 0)),
        ],
        [
            jax.ShapeDtypeStruct((2, rows, layers * value_width), F32),
            jax.ShapeDtypeStruct((2, heads, rows, PACKED), BF16),
        ],
        (query, key, value, early, query_a, query_b, query_bias),
        heads * rows * rows * 1200,
    )

    per_step = heads // 2

    def hidden(chunk):
        return call(
            hidden_kernel,
            chunk.reshape(1),
            (2,),
            [
                pl.BlockSpec((1, rows, per_step * HEAD_DIM), lambda i, c: (c[0], 0, i)),
                pl.BlockSpec((1, per_step, rows, PACKED), lambda i, c: (c[0], i, 0, 0)),
                pl.BlockSpec((per_step, PACKED, HEAD_DIM), lambda i, c: (i, 0, 0)),
                pl.BlockSpec((1, per_step * HEAD_DIM), lambda i, c: (0, i)),
            ],
            pl.BlockSpec((rows, per_step * HEAD_DIM), lambda i, c: (0, i)),
            jax.ShapeDtypeStruct((rows, heads * HEAD_DIM), BF16),
            (local, phi, prefix, gain_mine),
            rows * heads * HEAD_DIM * 600,
        )

    received = lax.ppermute(hidden(1 - core), "core", swap)
    kept = hidden(core)
    steps = 4
    per_out = groups // steps
    out = call(
        lambda core_ref, *refs: output_kernel(core_ref, layers, *refs),
        which,
        (steps,),
        [
            whole((rows, heads * HEAD_DIM)),
            whole((rows, heads * HEAD_DIM)),
            pl.BlockSpec((model, per_out * width), lambda i, _: (0, i)),
        ],
        pl.BlockSpec((per_out, rows, width), lambda i, _: (i, 0, 0)),
        jax.ShapeDtypeStruct((groups, rows, width), BF16),
        (kept, received, w_out),
        2 * rows * model * model,
        [pltpu.VMEM((rows, model), BF16)],
    )
    out = lax.all_to_all(out, ("z", "core"), split_axis=0, concat_axis=0, tiled=True)
    return out.reshape(groups * rows, width)


def solution(mesh):
    slabs, groups = mesh.shape["seq"], mesh.shape["chan"]
    split = jax.sharding.Mesh(mesh.devices.reshape(slabs, groups // 2, 2), ("seq", "z", "core"))
    chan = ("z", "core")
    return jax.shard_map(
        per_device,
        mesh=split,
        in_specs=(P("seq", chan), P(), P(), P(None, chan), P(), P()),
        out_specs=P("seq", chan),
        check_vma=False,
    )
```

time: 278 us -> 234 us (0.84)
  blocking collectives: 126 us -> 98.4 us
  waiting for transfers between devices: 78.5 us -> 55.5 us
  Pallas kernels: 31.3 us -> 50.9 us
  local copies, waits for them, and re-layouts: 25.1 us -> 6.55 us
  starting transfers between devices: 3.58 us -> 7.18 us
    all_gather x1, waiting for transfers between devices: 41.8 us -> 0.01 us  [per_device(): value_all = lax.all_gather(value_all, 'seq', axis=0, tiled=False)]
    all_to_all x3, blocking collectives: 116 us -> 88.1 us  [the longest x1 48.6 us: per_device(): lax.all_to_all(out, ('z', 'core'), split_axis=0, concat_axis=0, tiled=True)]
    unnamed x47 -> x17, local copies, waits for them, and re-layouts: 24.4 us -> 4.18 us
    pallas_call x3 -> x5, Pallas kernels: 29.1 us -> 49 us  [call(): pl.pallas_call(kernel, grid_spec=pltpu.PrefetchScalarGridSpec(num_scalar_...]
    all_to_all x1 -> x2, waiting for transfers between devices: 4.35 us -> 21.8 us  [the longest x1 21.8 us: per_device(): lax.all_to_all(blocks[:, chunk], 'z', split_axis=0, concat_axis=0, tiled=...]
    all_to_all x1 -> x2, starting transfers between devices: 3.54 us -> 7.06 us  [the longest x1 3.61 us: per_device(): lax.all_to_all(blocks[:, chunk], 'z', split_axis=0, concat_axis=0, tiled=...]
  transfers between devices with their start and end apart: 3 -> 7, of which waited for: 3 -> 3; matrix products, arithmetic and copies ran while one was open for 0% -> 1% of each run, Pallas kernels for 3% -> 8%
where the time goes in v1:
time: 234 us; the launch traced here: 233 us
  blocking collectives  98.4 us (42%)
  waiting for transfers between devices  55.5 us (24%)
  Pallas kernels  50.9 us (22%)
  between operations  13.5 us (6%)
  starting transfers between devices  7.18 us (3%)
  local copies, waits for them, and re-layouts  6.55 us (3%)
    pallas_call x5, Pallas kernels, call(): pl.pallas_call(kernel, grid_spec=pltpu.PrefetchScalarGridSpec(num_scalar_...  49 us
    all_to_all x1, blocking collectives, per_device(): lax.all_to_all(out, ('z', 'core'), split_axis=0, concat_axis=0, tiled=True)  48.6 us
    all_gather x1, waiting for transfers between devices, per_device(): value_all = lax.all_gather(value_part, 'z', axis=0, tiled=False)  31 us
    all_to_all x1, blocking collectives, per_device(): lax.all_to_all(blocks[:, chunk], 'z', split_axis=0, concat_axis=0, tiled=...  25.9 us
    all_to_all x1, waiting for transfers between devices, per_device(): lax.all_to_all(blocks[:, chunk], 'z', split_axis=0, concat_axis=0, tiled=...  21.8 us
    all_to_all x1, blocking collectives, per_device(): line = lax.all_to_all(own, 'z', split_axis=0, concat_axis=0, tiled=True)  13.6 us
    all_gather x1, blocking collectives, per_device(): totals = lax.all_gather(slab_total, 'seq', axis=0, tiled=False)  10.3 us
  transfers between devices with their start and end apart: 7, of which 3 were waited for; matrix products, arithmetic and copies ran while one was open for 1% of the time, Pallas kernels for 8%

profile of v1, /device:TPU:0, one launch (start us, length us, event | category | flops | bytes accessed | tf_op | source)
XLA Modules:
  0.0 233.2 jit_solution(10619692238801330707)
XLA Ops:
  6.5 1.2 copy-done
  7.8 0.7 constant_dynamic-slice_fusion.1
  8.5 0.0 all-gather.6.cloned.1.call-update
  8.5 0.0 all-gather.8.cloned.1.call-start
  8.6 31.0 %all-gather.6.cloned.1.call-done = bf16[2048,256]{1,0:T(8,128)(2,1)} async-done(((bf16[512,256]{1,0:T(8,128)(2,1)}), bf16[2048,256]{1,0:T(8,128)(2,1)}) %all-gather.6.cloned.1.call-update) | async-done | bytes 1048592 | tf_op jit(solution)/shard_map/all_gather | solution.py:236
  39.6 0.0 all-gather.8.cloned.1.call-update
  39.6 1.0 slice_bitcast_fusion
  40.7 25.9 %all_to_all.25.refs_0_ = bf16[4,448,256]{2,1,0:T(8,128)(2,1)S(1)} all-to-all(bf16[4,448,256]{2,1,0:T(8,128)(2,1)S(1)} %get-tuple-element.20), channel_id=1, replica_groups=mesh['seq'=4,'z'=4,'core'=2] {'z'}, dimensions={0} | all-to-all | bytes 1835008 | tf_op jit(solution)/shard_map/all_to_all | solution.py:241
  66.6 3.6 %all-to-all-start.1 = ((bf16[4,448,256]{2,1,0:T(8,128)(2,1)}), bf16[4,448,256]{2,1,0:T(8,128)(2,1)S(1)}, u32[]{:S(2)}, u32[]{:S(2)}) async-start(bf16[4,448,256]{2,1,0:T(8,128)(2,1)} %get-tuple-element.19), calls=%async_computation.1 | async-start | bytes 1835008 | tf_op jit(solution)/shard_map/all_to_all | solution.py:241
  70.2 0.1 collective-permute-start
  70.3 21.8 %all-to-all-done.1.refs_1_ = bf16[4,448,256]{2,1,0:T(8,128)(2,1)S(1)} async-done(((bf16[4,448,256]{2,1,0:T(8,128)(2,1)}), bf16[4,448,256]{2,1,0:T(8,128)(2,1)S(1)}, u32[]{:S(2)}, u32[]{:S(2)}) %all-to-all-start.1) | async-done | bytes 917536 | tf_op jit(solution)/shard_map/all_to_all | solution.py:241
  92.1 0.0 collective-permute-start.1
  92.1 0.0 collective-permute-done.refs_2_
  92.1 2.6 %collective-permute-done.1.refs_3_ = bf16[4,448,256]{2,1,0:T(8,128)(2,1)} collective-permute-done((bf16[4,448,256]{2,1,0:T(8,128)(2,1)S(1)}, bf16[4,448,256]{2,1,0:T(8,128)(2,1)}, u32[]{:S(2)}, u32[]{:S(2)}) %collective-permute-start.1) | collective-permute-done | bytes 917536 | tf_op jit(solution)/shard_map/ppermute | solution.py:244
  94.7 18.6 %shard_map.118 = (bf16[2,448,256]{2,1,0:T(8,128)(2,1)}, bf16[2,448,256]{2,1,0:T(8,128)(2,1)}, bf16[2,448,1024]{2,1,0:T(8,128)(2,1)}, bf16[8,160,128]{2,1,0:T(8,128)(2,1)}, f32[8,160,128]{2,1,0:T(8,128)}) custom-call(s32[1]{0:T(128)} %bitcast.core_ref.chunk_ref, bf16[4,448,256]{2,1,0:T(8,128)(2,1)} %copy-done.4, bf16[4,448,256]{2,1,0:T(8,128)(2,1)} %copy-done.5, ...), custom_call_target="tpu_custom_call" | custom-call | flops 5637144576 | bytes 12582912 | tf_op jit(solution)/shard_map/pallas_call | solution.py:194
  113.3 1.1 convert_element_type.2
  114.4 13.6 %all_to_all.26.line_ref = bf16[4,2,160,128]{3,2,1,0:T(8,128)(2,1)S(1)} all-to-all(bf16[4,2,160,128]{3,2,1,0:T(8,128)(2,1)S(1)} %bitcast.24), channel_id=1, replica_groups=mesh['seq'=4,'z'=4,'core'=2] {'z'}, dimensions={0} | all-to-all | bytes 655360 | tf_op jit(solution)/shard_map/all_to_all | solution.py:279
  128.1 10.3 %all-gather.2 = bf16[8,160,128]{2,1,0:T(8,128)(2,1)} all-gather(bf16[2,160,128]{2,1,0:T(8,128)(2,1)S(1)} %reduce_sum.12), channel_id=4, replica_groups=mesh['seq'=4,'z'=4,'core'=2] {'seq'}, dimensions={0}, use_global_device_ids=true | all-gather | bytes 409600 | tf_op jit(solution)/shard_map/all_gather | solution.py:281
  138.4 1.9 shard_map.120
  140.3 3.5 %all-to-all-start.3 = ((bf16[4,2,160,128]{3,2,1,0:T(8,128)(2,1)}), bf16[4,2,160,128]{3,2,1,0:T(8,128)(2,1)S(1)}, u32[]{:S(2)}, u32[]{:S(2)}) async-start(bf16[4,2,160,128]{3,2,1,0:T(8,128)(2,1)} %shard_map.120), calls=%async_computation.3 | async-start | bytes 655360 | tf_op jit(solution)/shard_map/all_to_all | solution.py:289
  143.8 0.6 constant_dynamic-slice_fusion
  144.4 15.3 %shard_map.119 = (f32[2,448,1024]{2,1,0:T(8,128)}, bf16[2,8,448,160]{3,2,1,0:T(8,128)(2,1)}) custom-call(s32[1]{0:T(128)} %bitcast.core_ref.chunk_ref, bf16[2,448,256]{2,1,0:T(8,128)(2,1)} %get-tuple-element.12.refs_0_, bf16[2,448,256]{2,1,0:T(8,128)(2,1)} %get-tuple-element.13.refs_1_, bf16[2,448,1024]{2,1,0:T(8,128)(2,1)} %get-tuple-element.14.refs_2_, ...), custom_call_target="tpu_custom_call" | custom-call | flops 1926758400 | bytes 12582912 | tf_op jit(solution)/shard_map/pallas_call | solution.py:194
  159.7 0.0 all-to-all-done.3
  159.7 0.7 copy-done.1
  160.4 3.3 %shard_map.122 = bf16[448,1024]{1,0:T(8,128)(2,1)} custom-call(s32[1]{0:T(128)} %bitcast.11.chunk_ref, f32[2,448,1024]{2,1,0:T(8,128)} %get-tuple-element.16.num_ref, bf16[2,8,448,160]{3,2,1,0:T(8,128)(2,1)} %get-tuple-element.17.phi_ref, bf16[8,160,128]{2,1,0:T(8,128)(2,1)} %bitcast.20, f32[1,1024]{1,0:T(1,128)} %bitcast.26), custom_call_target="tpu_custom_call" | custom-call | flops 275251200 | bytes 12582912 | tf_op jit(solution)/shard_map/pallas_call | solution.py:194
  163.8 0.0 collective-permute-start.2
  163.8 3.4 %shard_map.121.refs_0_ = bf16[448,1024]{1,0:T(8,128)(2,1)} custom-call(s32[1]{0:T(128)} %bitcast.core_ref.chunk_ref, f32[2,448,1024]{2,1,0:T(8,128)} %get-tuple-element.16.num_ref, bf16[2,8,448,160]{3,2,1,0:T(8,128)(2,1)} %get-tuple-element.17.phi_ref, bf16[8,160,128]{2,1,0:T(8,128)(2,1)} %bitcast.21, f32[1,1024]{1,0:T(1,128)} %bitcast.27), custom_call_target="tpu_custom_call" | custom-call | flops 275251200 | bytes 12582912 | tf_op jit(solution)/shard_map/pallas_call | solution.py:194
  167.2 0.0 collective-permute-done.2.refs_1_
  167.2 1.0 copy-done.7
  168.1 8.4 %shard_map.123 = bf16[8,448,256]{2,1,0:T(8,128)(2,1)} custom-call(s32[1]{0:T(128)} %bitcast.core_ref.chunk_ref, bf16[448,1024]{1,0:T(8,128)(2,1)} %shard_map.121.refs_0_, bf16[448,1024]{1,0:T(8,128)(2,1)} %copy-done.7, bf16[2048,2048]{1,0:T(8,128)(2,1)} %refs_2_.1), custom_call_target="tpu_custom_call" | custom-call | flops 3758096384 | bytes 12582912 | tf_op jit(solution)/shard_map/pallas_call | solution.py:194
  176.5 48.6 %all_to_all.27 = bf16[8,448,256]{2,1,0:T(8,128)(2,1)S(1)} all-to-all(bf16[8,448,256]{2,1,0:T(8,128)(2,1)} %shard_map.123), channel_id=1, replica_groups=mesh['seq'=4,'z'=4,'core'=2] {'z','core'}, dimensions={0} | all-to-all | bytes 3670016 | tf_op jit(solution)/shard_map/all_to_all | solution.py:355
  225.1 1.2 copy.20
  (17 shorter events, 0.1 us)
Async XLA Ops:
  6.5 1.2 copy-start
  6.5 33.1 %copy-start.3 = (bf16[3584,256]{1,0:T(8,128)(2,1)S(1)}, bf16[3584,256]{1,0:T(8,128)(2,1)}, u32[]{:S(2)}) copy-start(bf16[3584,256]{1,0:T(8,128)(2,1)} %param.12) | copy-start | bytes 5505028
  6.5 33.1 %all-gather.6.cloned.1.call-start = ((), (), s32[]{:S(2)}) async-start(), calls=%async_computation.5 | async-start | bytes 1310720 | tf_op jit(solution)/shard_map/all_gather | solution.py:236
  8.5 86.2 %all-gather.8.cloned.1.call-start = ((), (), s32[]{:S(2)}) async-start(), calls=%async_computation.6 | async-start | bytes 5242880 | tf_op jit(solution)/shard_map/all_gather | solution.py:237
  66.6 28.2 %copy-start.4 = (bf16[4,448,256]{2,1,0:T(8,128)(2,1)}, bf16[4,448,256]{2,1,0:T(8,128)(2,1)S(1)}, u32[]{:S(2)}) copy-start(bf16[4,448,256]{2,1,0:T(8,128)(2,1)S(1)} %all_to_all.25.refs_0_) | copy-start | bytes 2752516
  66.6 25.5 %all-to-all-start.1 = ((bf16[4,448,256]{2,1,0:T(8,128)(2,1)}), bf16[4,448,256]{2,1,0:T(8,128)(2,1)S(1)}, u32[]{:S(2)}, u32[]{:S(2)}) async-start(bf16[4,448,256]{2,1,0:T(8,128)(2,1)} %get-tuple-element.19), calls=%async_computation.1 | async-start | bytes 1835008 | tf_op jit(solution)/shard_map/all_to_all | solution.py:241
  70.2 21.9 %collective-permute-start = (bf16[4,448,256]{2,1,0:T(8,128)(2,1)S(1)}, bf16[4,448,256]{2,1,0:T(8,128)(2,1)}, u32[]{:S(2)}, u32[]{:S(2)}) collective-permute-start(bf16[4,448,256]{2,1,0:T(8,128)(2,1)S(1)} %all_to_all.25.refs_0_), channel_id=1, source_target_pairs={{0,1},{1,0},{2,3},{3,2},{4,5},{5,4},{6,7},{7,6},{8,9},{9,8},{10,11... | collective-permute-start | bytes 2752520 | tf_op jit(solution)/shard_map/ppermute | solution.py:244
  92.1 2.6 %copy-start.5 = (bf16[4,448,256]{2,1,0:T(8,128)(2,1)}, bf16[4,448,256]{2,1,0:T(8,128)(2,1)S(1)}, u32[]{:S(2)}) copy-start(bf16[4,448,256]{2,1,0:T(8,128)(2,1)S(1)} %all-to-all-done.1.refs_1_) | copy-start | bytes 2752516
  92.1 2.6 %collective-permute-start.1 = (bf16[4,448,256]{2,1,0:T(8,128)(2,1)S(1)}, bf16[4,448,256]{2,1,0:T(8,128)(2,1)}, u32[]{:S(2)}, u32[]{:S(2)}) collective-permute-start(bf16[4,448,256]{2,1,0:T(8,128)(2,1)S(1)} %all-to-all-done.1.refs_1_), channel_id=1, source_target_pairs={{0,1},{1,0},{2,3},{3,2},{4,5},{5,4},{6,7},{7,6},{8,9},{9,8},{10,11... | collective-permute-start | bytes 2752520 | tf_op jit(solution)/shard_map/ppermute | solution.py:244
  113.3 30.5 %copy-start.6 = (f32[2048]{0:T(1024)S(1)}, f32[2048]{0:T(1024)}, u32[]{:S(2)}) copy-start(f32[2048]{0:T(1024)} %param.17) | copy-start | bytes 24580
  128.0 10.4 %copy-start.2 = (bf16[4,2,160,128]{3,2,1,0:T(8,128)(2,1)}, bf16[4,2,160,128]{3,2,1,0:T(8,128)(2,1)S(1)}, u32[]{:S(2)}) copy-start(bf16[4,2,160,128]{3,2,1,0:T(8,128)(2,1)S(1)} %all_to_all.26.line_ref) | copy-start | bytes 983044
  140.3 19.4 %all-to-all-start.3 = ((bf16[4,2,160,128]{3,2,1,0:T(8,128)(2,1)}), bf16[4,2,160,128]{3,2,1,0:T(8,128)(2,1)S(1)}, u32[]{:S(2)}, u32[]{:S(2)}) async-start(bf16[4,2,160,128]{3,2,1,0:T(8,128)(2,1)} %shard_map.120), calls=%async_computation.3 | async-start | bytes 655360 | tf_op jit(solution)/shard_map/all_to_all | solution.py:289
  159.7 0.7 copy-start.1
  163.8 3.4 %collective-permute-start.2 = (bf16[448,1024]{1,0:T(8,128)(2,1)}, bf16[448,1024]{1,0:T(8,128)(2,1)S(1)}, u32[]{:S(2)}, u32[]{:S(2)}) collective-permute-start(bf16[448,1024]{1,0:T(8,128)(2,1)} %shard_map.122), channel_id=1, source_target_pairs={{0,1},{1,0},{2,3},{3,2},{4,5},{5,4},{6,7},{7,6},{8,9},{9,8},{10,11... | collective-permute-start | bytes 2752520 | tf_op jit(solution)/shard_map/ppermute | solution.py:336
  167.2 1.0 copy-start.7
Sparse Core Ops, SparseCore 0:
  8.9 30.6 all-gather.5
  41.4 52.1 all-gather.7

commit v2 on v1

--- a/solution.py
+++ b/solution.py
@@ -53,69 +53,87 @@
     return out
 
 
+def stacked(table, per_group):
+    every = placed(table).transpose(0, 2, 1)
+    own = [[p for p in range(HELD) if (p // per_group) % 2 == core] for core in range(2)]
+    return np.stack([every[places].reshape(-1, LANES) for places in own])
+
+
 def project_kernel(
-    core_ref,
+    at_ref,
     per_group,
-    first_mine,
-    second_mine,
-    first_other,
-    second_other,
+    counts,
+    mine_ref,
+    other_ref,
     wq_ref,
     wk_ref,
-    wv_ref,
-    ta_ref,
-    tb_ref,
+    table_ref,
     bias_ref,
-    q_ref,
-    k_ref,
-    v_ref,
-    early_ref,
-    total_ref,
-    row_ref,
+    *rest,
 ):
-    step = pl.program_id(0)
-    core = core_ref[0]
-    layers, rows, width = first_mine.shape
-
-    @pl.when(step == 0)
-    def _():
-        for chunk, (mine, other) in enumerate(
-            ((first_mine, first_other), (second_mine, second_other))
-        ):
-            at = slice(chunk * rows, (chunk + 1) * rows)
-            for z in range(layers):
-                here = pl.multiple_of((2 * z + core) * width, width)
-                there = pl.multiple_of((2 * z + 1 - core) * width, width)
-                row_ref[at, pl.ds(here, width)] = mine[z]
-                row_ref[at, pl.ds(there, width)] = other[z]
-            q_ref[chunk] = dot(row_ref[at, :], wq_ref[...]).astype(BF16)
-            k_ref[chunk] = dot(row_ref[at, :], wk_ref[...]).astype(BF16)
-
-    wv = wv_ref[...].reshape(row_ref.shape[1], wv_ref.shape[-1])
+    n_weights = sum(counts)
+    weights = rest[:n_weights]
+    q_ref, k_ref, v_ref, early_ref, total_ref, row_ref, w_ref, phi_ref, sems = rest[n_weights:]
+    core, layer, slab = at_ref[0], at_ref[1], at_ref[2]
+    layers, both, width = mine_ref.shape
+    rows = both // 2
+    copies = []
+    place = 0
+    for d, count in enumerate(counts):
+        for m in range(count):
+            source = weights[place]
+            part = source.shape[0]
+            start = 0 if count == 1 else pl.multiple_of((slab ^ m) * part, part)
+            copy = pltpu.make_async_copy(source, w_ref.at[d, pl.ds(start, part)], sems.at[place])
+            copy.start()
+            copies.append((d, copy))
+            place += 1
+
+    for z in range(layers):
+        here = pl.multiple_of((2 * z + core) * width, width)
+        there = pl.multiple_of((2 * z + 1 - core) * width, width)
+        row_ref[:, pl.ds(here, width)] = mine_ref[z]
+        row_ref[:, pl.ds(there, width)] = other_ref[z]
+    q = dot(row_ref[...], wq_ref[...]).astype(BF16)
+    k = dot(row_ref[...], wk_ref[...]).astype(BF16)
+    half = table_ref.shape[1] // 2
     for chunk in range(2):
-        value = dot(row_ref[chunk * rows : (chunk + 1) * rows, :], wv).astype(BF16)
-        v_ref[chunk] = value
-        for i in range(per_group):
-            head = (2 * step + core) * per_group + i
-            lanes = pl.multiple_of((head // HELD) * LANES, LANES)
-            key = k_ref[chunk, :, pl.ds(lanes, LANES)]
-            place = lax.rem(head, HELD)
-            left = dot(ta_ref[place], key, NT) + bias_ref[:, 0:1]
-            right = dot(tb_ref[place], key, NT) + bias_ref[:, 1:2]
-            phi = (left * right).astype(BF16)
-            state = dot(phi, value[:, i * HEAD_DIM : (i + 1) * HEAD_DIM])
-            if chunk == 0:
-                early_ref[i] = state.astype(BF16)
-                total_ref[i] = state
-            else:
-                total_ref[i] = total_ref[i] + state
+        at = slice(chunk * rows, (chunk + 1) * rows)
+        q_ref[chunk] = q[at]
+        k_ref[chunk] = k[at]
+        for lanes in range(0, k.shape[1], LANES):
+            product = dot(table_ref[0], k[at, lanes : lanes + LANES], NT)
+            left = product[:half] + bias_ref[:, 0:1]
+            right = product[half:] + bias_ref[:, 1:2]
+            to = (lanes // LANES) * half
+            phi_ref[chunk, to : to + half, :] = (left * right).astype(BF16)
+
+    block = v_ref.shape[2] // layers
+    for d in range(layers):
+        for slot, copy in copies:
+            if slot == d:
+                copy.wait()
+        z = lax.rem(layer + d, layers)
+        for chunk in range(2):
+            value = dot(row_ref[chunk * rows : (chunk + 1) * rows, :], w_ref[d]).astype(BF16)
+            v_ref[chunk, :, pl.ds(pl.multiple_of(z * block, block), block)] = value
+            for i in range(per_group):
+                head = z * per_group + i
+                phi = phi_ref[chunk, pl.ds(pl.multiple_of(head * PACKED, PACKED), PACKED), :]
+                state = dot(phi, value[:, i * HEAD_DIM : (i + 1) * HEAD_DIM])
+                if chunk == 0:
+                    early_ref[head] = state.astype(BF16)
+                    first = state if i == 0 else jnp.concatenate([first, state], axis=0)
+                else:
+                    total = first[i * PACKED : (i + 1) * PACKED] + state
+                    total_ref[head] = total.astype(BF16)
 
 
 def local_kernel(
-    core_ref, per_group, q_ref, k_ref, v_ref, early_ref, ta_ref, tb_ref, bias_ref, num_ref, phi_ref
+    core_ref, per_group, offset, q_ref, k_ref, v_ref, early_ref, ta_ref, tb_ref, bias_ref, num_ref, phi_ref
 ):
     chunk = pl.program_id(0)
-    step = pl.program_id(1)
+    step = pl.program_id(1) + offset
     rows = q_ref.shape[1]
     half = rows // 2
     for i in range(per_group):
@@ -154,10 +172,13 @@
         run = run + line_ref[c].astype(F32)
 
 
-def hidden_kernel(chunk_ref, num_ref, phi_ref, state_ref, gain_ref, out_ref):
-    for i in range(phi_ref.shape[1]):
+def hidden_kernel(chunk_ref, num_a, num_b, phi_a, phi_b, state_ref, gain_ref, out_ref):
+    held = phi_a.shape[1]
+    for i in range(2 * held):
         columns = slice(i * HEAD_DIM, (i + 1) * HEAD_DIM)
-        num = num_ref[0, :, columns] + dot(phi_ref[0, i], state_ref[i])
+        num_ref, phi_ref = (num_a, phi_a) if i < held else (num_b, phi_b)
+        at = (i % held) * HEAD_DIM
+        num = num_ref[0, :, at : at + HEAD_DIM] + dot(phi_ref[0, i % held], state_ref[i])
         mean_square = jnp.mean(num * num, axis=1, keepdims=True)
         hidden = num * lax.rsqrt(mean_square + 1e-05) * gain_ref[:, columns]
         out_ref[:, columns] = hidden.astype(BF16)
@@ -212,6 +233,7 @@
     groups = 2 * layers
     my_slab = lax.axis_index("seq")
     core = lax.axis_index("core").astype(jnp.int32)
+    layer = lax.axis_index("z").astype(jnp.int32)
     which = core.reshape(1)
     width = tokens.shape[1]
     rows = tokens.shape[0] // groups
@@ -223,60 +245,107 @@
     swap = [(0, 1), (1, 0)]
 
     first, second, first_bias, second_bias, scale = feature_tables()
-    key_a = jnp.asarray(placed(first).transpose(0, 2, 1), BF16)
-    key_b = jnp.asarray(placed(second).transpose(0, 2, 1), BF16)
-    key_bias = jnp.asarray(np.stack([first_bias, second_bias], axis=1))
+    sides = [stacked(first, per_group), stacked(second, per_group)]
+    key_table = jnp.asarray(np.concatenate(sides, axis=1), BF16)
+    repeat = HELD // 2
+    key_bias = jnp.asarray(np.stack([np.tile(first_bias, repeat), np.tile(second_bias, repeat)], axis=1))
     query_a = jnp.asarray(placed(first * scale), BF16)
     query_b = jnp.asarray(placed(second), BF16)
     query_bias = jnp.asarray(np.stack([first_bias * scale, second_bias]))
     gain_mine = lax.dynamic_index_in_dim(gain.reshape(layers, 2, value_width), core, 1, False)
     gain_mine = gain_mine.reshape(1, layers * value_width)
 
+    mine = lax.all_to_all(
+        tokens.reshape(layers, 2 * rows, width), "z", split_axis=0, concat_axis=0, tiled=True
+    )
+    other = lax.ppermute(mine, "core", swap)
+
     value_part = lax.dynamic_slice_in_dim(w_value, my_slab * part, part, 0)
-    value_all = lax.all_gather(value_part, "z", axis=0, tiled=False)
-    value_all = lax.all_gather(value_all, "seq", axis=0, tiled=False)
-
-    blocks = tokens.reshape(layers, 2, rows, width)
-    mine = [
-        lax.all_to_all(blocks[:, chunk], "z", split_axis=0, concat_axis=0, tiled=True)
-        for chunk in range(2)
-    ]
-    other = [lax.ppermute(half, "core", swap) for half in mine]
-
+    up, down = {0: value_part}, {0: value_part}
+    for k in range(1, layers):
+        up[k] = lax.ppermute(up[k - 1], "z", [(z, z + 1) for z in range(k - 1, layers - 1)])
+        down[k] = lax.ppermute(down[k - 1], "z", [(z, z - 1) for z in range(1, layers - k + 1)])
+    weights, counts = [w_value], [1]
+    for d in range(1, layers):
+        slot = jnp.where(layer + d < layers, down[d], up[layers - d])
+        if slabs == 4:
+            weights.append(slot)
+            for m in range(1, slabs):
+                weights.append(lax.ppermute(slot, "seq", [(s, s ^ m) for s in range(slabs)]))
+            counts.append(slabs)
+        else:
+            weights.append(lax.all_gather(slot, "seq", axis=0, tiled=True))
+            counts.append(1)
+
+    anywhere = pl.BlockSpec(memory_space=pl.ANY)
     query, key, value, early, total = call(
-        lambda core_ref, *refs: project_kernel(core_ref, per_group, *refs),
-        which,
-        (layers,),
-        [whole((layers, rows, width))] * 4
-        + [
+        lambda at_ref, *refs: project_kernel(at_ref, per_group, counts, *refs),
+        jnp.stack([core, layer, my_slab.astype(jnp.int32)]),
+        (1,),
+        [
+            whole((layers, 2 * rows, width)),
+            whole((layers, 2 * rows, width)),
             whole((model, narrow)),
             whole((model, narrow)),
-            pl.BlockSpec((slabs, 1, part, value_width), lambda i, _: (0, i, 0, 0)),
-            whole((HELD, PACKED, LANES)),
-            whole((HELD, PACKED, LANES)),
-            whole((PACKED, 2)),
-        ],
+            pl.BlockSpec((1,) + key_table.shape[1:], lambda i, at: (at[0], 0, 0)),
+            whole(key_bias.shape),
+        ]
+        + [anywhere] * len(weights),
         [
             whole((2, rows, narrow)),
             whole((2, rows, narrow)),
-            pl.BlockSpec((2, rows, value_width), lambda i, _: (0, 0, i)),
-            pl.BlockSpec((per_group, PACKED, HEAD_DIM), lambda i, _: (i, 0, 0)),
-            pl.BlockSpec((per_group, PACKED, HEAD_DIM), lambda i, _: (i, 0, 0)),
+            whole((2, rows, layers * value_width)),
+            whole((heads, PACKED, HEAD_DIM)),
+            whole((heads, PACKED, HEAD_DIM)),
         ],
         [
             jax.ShapeDtypeStruct((2, rows, narrow), BF16),
             jax.ShapeDtypeStruct((2, rows, narrow), BF16),
             jax.ShapeDtypeStruct((2, rows, layers * value_width), BF16),
             jax.ShapeDtypeStruct((heads, PACKED, HEAD_DIM), BF16),
-            jax.ShapeDtypeStruct((heads, PACKED, HEAD_DIM), F32),
+            jax.ShapeDtypeStruct((heads, PACKED, HEAD_DIM), BF16),
         ],
-        (mine[0], mine[1], other[0], other[1], w_query, w_key, value_all, key_a, key_b, key_bias),
+        (mine, other, w_query, w_key, key_table, key_bias, *weights),
         4 * rows * model * (model // 2 + 2 * narrow),
-        [pltpu.VMEM((2 * rows, model), BF16)],
+        [
+            pltpu.VMEM((2 * rows, model), BF16),
+            pltpu.VMEM((layers, model, value_width), BF16),
+            pltpu.VMEM((2, heads * PACKED, rows), BF16),
+            pltpu.SemaphoreType.DMA((len(weights),)),
+        ],
     )
 
-    own = total.astype(BF16).reshape(layers, per_group, PACKED, HEAD_DIM)
+    def local(part_of_heads):
+        offset = part_of_heads * (layers // 2)
+        return call(
+            lambda core_ref, *refs: local_kernel(core_ref, per_group, offset, *refs),
+            which,
+            (2, layers // 2),
+            [
+                pl.BlockSpec((1, rows, narrow), lambda c, i, _: (c, 0, 0)),
+                pl.BlockSpec((1, rows, narrow), lambda c, i, _: (c, 0, 0)),
+                pl.BlockSpec((1, rows, value_width), lambda c, i, _: (c, 0, i + offset)),
+                pl.BlockSpec((per_group, PACKED, HEAD_DIM), lambda c, i, _: (i + offset, 0, 0)),
+                whole((HELD, LANES, PACKED)),
+                whole((HELD, LANES, PACKED)),
+                whole((2, PACKED)),
+            ],
+            [
+                pl.BlockSpec((1, rows, value_width), lambda c, i, _: (c, 0, i)),
+                pl.BlockSpec((1, per_group, rows, PACKED), lambda c, i, _: (c, i, 0, 0)),
+            ],
+            [
+                jax.ShapeDtypeStruct((2, rows, layers * value_width // 2), F32),
+                jax.ShapeDtypeStruct((2, heads // 2, rows, PACKED), BF16),
+            ],
+            (query, key, value, early, query_a, query_b, query_bias),
+            heads * rows * rows * 600,
+        )
+
+    own = total.reshape(layers, per_group, PACKED, HEAD_DIM)
     line = lax.all_to_all(own, "z", split_axis=0, concat_axis=0, tiled=True)
+    num_a, phi_a = local(0)
+    line, num_a, phi_a = lax.optimization_barrier((line, num_a, phi_a))
     slab_total = jnp.sum(line.astype(F32), axis=0).astype(BF16)
     totals = lax.all_gather(slab_total, "seq", axis=0, tiled=False)
     vmem = pl.BlockSpec(memory_space=pltpu.VMEM)
@@ -288,48 +357,27 @@
     )(my_slab.reshape(1), line, totals)
     prefix = lax.all_to_all(prefix, "z", split_axis=0, concat_axis=0, tiled=True)
     prefix = prefix.reshape(heads, PACKED, HEAD_DIM)
-
-    local, phi = call(
-        lambda core_ref, *refs: local_kernel(core_ref, per_group, *refs),
-        which,
-        (2, layers),
-        [
-            pl.BlockSpec((1, rows, narrow), lambda c, i, _: (c, 0, 0)),
-            pl.BlockSpec((1, rows, narrow), lambda c, i, _: (c, 0, 0)),
-            pl.BlockSpec((1, rows, value_width), lambda c, i, _: (c, 0, i)),
-            pl.BlockSpec((per_group, PACKED, HEAD_DIM), lambda c, i, _: (i, 0, 0)),
-            whole((HELD, LANES, PACKED)),
-            whole((HELD, LANES, PACKED)),
-            whole((2, PACKED)),
-        ],
-        [
-            pl.BlockSpec((1, rows, value_width), lambda c, i, _: (c, 0, i)),
-            pl.BlockSpec((1, per_group, rows, PACKED), lambda c, i, _: (c, i, 0, 0)),
-        ],
-        [
-            jax.ShapeDtypeStruct((2, rows, layers * value_width), F32),
-            jax.ShapeDtypeStruct((2, heads, rows, PACKED), BF16),
-        ],
-        (query, key, value, early, query_a, query_b, query_bias),
-        heads * rows * rows * 1200,
-    )
-
-    per_step = heads // 2
+    num_b, phi_b = local(1)
 
     def hidden(chunk):
+        some = rows // 2
+        numbers = pl.BlockSpec((1, some, heads * HEAD_DIM // 2), lambda i, c: (c[0], i, 0))
+        features = pl.BlockSpec((1, heads // 2, some, PACKED), lambda i, c: (c[0], 0, i, 0))
         return call(
             hidden_kernel,
             chunk.reshape(1),
             (2,),
             [
-                pl.BlockSpec((1, rows, per_step * HEAD_DIM), lambda i, c: (c[0], 0, i)),
-                pl.BlockSpec((1, per_step, rows, PACKED), lambda i, c: (c[0], i, 0, 0)),
-                pl.BlockSpec((per_step, PACKED, HEAD_DIM), lambda i, c: (i, 0, 0)),
-                pl.BlockSpec((1, per_step * HEAD_DIM), lambda i, c: (0, i)),
+                numbers,
+                numbers,
+                features,
+                features,
+                whole((heads, PACKED, HEAD_DIM)),
+                whole((1, heads * HEAD_DIM)),
             ],
-            pl.BlockSpec((rows, per_step * HEAD_DIM), lambda i, c: (0, i)),
+            pl.BlockSpec((some, heads * HEAD_DIM), lambda i, c: (i, 0)),
             jax.ShapeDtypeStruct((rows, heads * HEAD_DIM), BF16),
-            (local, phi, prefix, gain_mine),
+            (num_a, num_b, phi_a, phi_b, prefix, gain_mine),
             rows * heads * HEAD_DIM * 600,
         )
 

time: 234 us -> 236 us (level)
  starting transfers between devices: 7.18 us -> 30.5 us
  waiting for transfers between devices: 55.5 us -> 36.6 us
  between operations: 13.5 us -> 0.24 us
  blocking collectives: 98.4 us -> 107 us
  Pallas kernels: 50.9 us -> 53.8 us
    ppermute x2 -> x16, waiting for transfers between devices: 2.6 us -> 36.6 us  [the longest x9 20.6 us: per_device(): lax.ppermute(slot, 'seq', [(s, s ^ m) for s in range(slabs)])]
    all_gather x2 -> x0, waiting for transfers between devices: 31 us -> none  [the longest x1 31 us: per_device(): value_all = lax.all_gather(value_part, 'z', axis=0, tiled=False)]
    all_to_all x1, waiting for transfers between devices: 21.8 us -> 0.01 us  [per_device(): line = lax.all_to_all(own, 'z', split_axis=0, concat_axis=0, tiled=True)]
    ppermute x2 -> x16, starting transfers between devices: 0.07 us -> 21.1 us  [the longest x9 11.4 us: per_device(): lax.ppermute(slot, 'seq', [(s, s ^ m) for s in range(slabs)])]
    all_to_all x2 -> x1, blocking collectives: 39.5 us -> 48.9 us  [per_device(): lax.all_to_all(tokens.reshape(layers, 2 * rows, width), 'z', split_axis=0...]
    pallas_call x5 -> x6, Pallas kernels: 49 us -> 51.9 us  [call(): pl.pallas_call(kernel, grid_spec=pltpu.PrefetchScalarGridSpec(num_scalar_...]
  transfers between devices with their start and end apart: 7 -> 19, of which waited for: 3 -> 11; matrix products, arithmetic and copies ran while one was open for 1% -> 1% of each run, Pallas kernels for 8% -> 9%
where the time goes in v2:
time: 236 us; the launch traced here: 235 us
  blocking collectives  107 us (45%)
  Pallas kernels  53.8 us (23%)
  waiting for transfers between devices  36.6 us (16%)
  starting transfers between devices  30.5 us (13%)
  local copies, waits for them, and re-layouts  4.67 us (2%)
    pallas_call x6, Pallas kernels, call(): pl.pallas_call(kernel, grid_spec=pltpu.PrefetchScalarGridSpec(num_scalar_...  51.9 us
    all_to_all x1, blocking collectives, per_device(): lax.all_to_all(tokens.reshape(layers, 2 * rows, width), 'z', split_axis=0...  48.9 us
    all_to_all x1, blocking collectives, per_device(): lax.all_to_all(out, ('z', 'core'), split_axis=0, concat_axis=0, tiled=True)  48.6 us
    ppermute x9, waiting for transfers between devices, per_device(): lax.ppermute(slot, 'seq', [(s, s ^ m) for s in range(slabs)])  20.6 us
    ppermute x3, waiting for transfers between devices, per_device(): lax.ppermute(down[k - 1], 'z', [(z, z - 1) for z in range(1, layers - k +...  15.9 us
    ppermute x9, starting transfers between devices, per_device(): lax.ppermute(slot, 'seq', [(s, s ^ m) for s in range(slabs)])  11.4 us
    all_gather x1, blocking collectives, per_device(): totals = lax.all_gather(slab_total, 'seq', axis=0, tiled=False)  9.86 us
    ppermute x3, starting transfers between devices, per_device(): lax.ppermute(up[k - 1], 'z', [(z, z + 1) for z in range(k - 1, layers - 1)])  5.9 us
  transfers between devices with their start and end apart: 19, of which 11 were waited for; matrix products, arithmetic and copies ran while one was open for 1% of the time, Pallas kernels for 9%

profile of v2, /device:TPU:0, one launch (start us, length us, event | category | flops | bytes accessed | tf_op | source)
XLA Modules:
  0.0 234.8 jit_solution(9724702780108573687)
XLA Ops:
  0.0 48.9 %all_to_all.20.refs_0_ = bf16[4,896,256]{2,1,0:T(8,128)(2,1)S(1)} all-to-all(bf16[4,896,256]{2,1,0:T(8,128)(2,1)} %bitcast.13), channel_id=1, replica_groups=mesh['seq'=4,'z'=4,'core'=2] {'z'}, dimensions={0} | all-to-all | bytes 3670016 | tf_op jit(solution)/shard_map/all_to_all | solution.py:258
  50.0 1.3 collective-permute-start.1
  51.3 4.6 %collective-permute-start.2 = (bf16[512,256]{1,0:T(8,128)(2,1)S(1)}, bf16[512,256]{1,0:T(8,128)(2,1)S(1)}, u32[]{:S(2)}, u32[]{:S(2)}) collective-permute-start(bf16[512,256]{1,0:T(8,128)(2,1)S(1)} %constant_dynamic-slice_fusion.1), channel_id=1, source_target_pairs={{0,2},{2,4},{4,6},{1,3},{3,5},{5,7},{8,10},{10,12},{12,14},{9,11},... | collective-permute-start | bytes 786440 | tf_op jit(solution)/shard_map/ppermute | solution.py:266
  55.9 4.6 %collective-permute-done.1 = bf16[512,256]{1,0:T(8,128)(2,1)S(1)} collective-permute-done((bf16[512,256]{1,0:T(8,128)(2,1)S(1)}, bf16[512,256]{1,0:T(8,128)(2,1)S(1)}, u32[]{:S(2)}, u32[]{:S(2)}) %collective-permute-start.1) | collective-permute-done | bytes 262176 | tf_op jit(solution)/shard_map/ppermute | solution.py:267
  60.5 1.3 collective-permute-start.8
  62.5 7.6 %collective-permute-done.8 = bf16[512,256]{1,0:T(8,128)(2,1)S(1)} collective-permute-done((bf16[512,256]{1,0:T(8,128)(2,1)S(1)}, bf16[512,256]{1,0:T(8,128)(2,1)S(1)}, u32[]{:S(2)}, u32[]{:S(2)}) %collective-permute-start.8) | collective-permute-done | bytes 262176 | tf_op jit(solution)/shard_map/ppermute | solution.py:267
  70.1 1.3 collective-permute-start.12
  71.5 1.6 collective-permute-start.10
  73.7 1.5 collective-permute-start.11
  75.2 3.7 %collective-permute-done.12 = bf16[512,256]{1,0:T(8,128)(2,1)} collective-permute-done((bf16[512,256]{1,0:T(8,128)(2,1)S(1)}, bf16[512,256]{1,0:T(8,128)(2,1)}, u32[]{:S(2)}, u32[]{:S(2)}) %collective-permute-start.12) | collective-permute-done | bytes 262176 | tf_op jit(solution)/shard_map/ppermute | solution.py:267
  78.9 1.5 collective-permute-start.9
  81.4 2.7 %collective-permute-done.10.refs_13_ = bf16[512,256]{1,0:T(8,128)(2,1)} collective-permute-done((bf16[512,256]{1,0:T(8,128)(2,1)S(1)}, bf16[512,256]{1,0:T(8,128)(2,1)}, u32[]{:S(2)}, u32[]{:S(2)}) %collective-permute-start.10) | collective-permute-done | bytes 262176 | tf_op jit(solution)/shard_map/ppermute | solution.py:274
  84.1 1.5 collective-permute-start.13
  85.6 1.5 collective-permute-start.14
  88.3 1.5 collective-permute-start.5
  89.8 4.1 %collective-permute-done.13.refs_16_ = bf16[512,256]{1,0:T(8,128)(2,1)} collective-permute-done((bf16[512,256]{1,0:T(8,128)(2,1)S(1)}, bf16[512,256]{1,0:T(8,128)(2,1)}, u32[]{:S(2)}, u32[]{:S(2)}) %collective-permute-start.13) | collective-permute-done | bytes 262176 | tf_op jit(solution)/shard_map/ppermute | solution.py:274
  97.5 2.5 %collective-permute-done.15.refs_18_ = bf16[512,256]{1,0:T(8,128)(2,1)S(1)} collective-permute-done((bf16[512,256]{1,0:T(8,128)(2,1)S(1)}, bf16[512,256]{1,0:T(8,128)(2,1)S(1)}, u32[]{:S(2)}, u32[]{:S(2)}) %collective-permute-start.15) | collective-permute-done | bytes 262176 | tf_op jit(solution)/shard_map/ppermute | solution.py:274
  100.0 5.1 %collective-permute-done.5.refs_8_ = bf16[512,256]{1,0:T(8,128)(2,1)S(1)} collective-permute-done((bf16[512,256]{1,0:T(8,128)(2,1)S(1)}, bf16[512,256]{1,0:T(8,128)(2,1)S(1)}, u32[]{:S(2)}, u32[]{:S(2)}) %collective-permute-start.5) | collective-permute-done | bytes 262176 | tf_op jit(solution)/shard_map/ppermute | solution.py:274
  105.1 2.8 %collective-permute-done.6.refs_9_ = bf16[512,256]{1,0:T(8,128)(2,1)} collective-permute-done((bf16[512,256]{1,0:T(8,128)(2,1)S(1)}, bf16[512,256]{1,0:T(8,128)(2,1)}, u32[]{:S(2)}, u32[]{:S(2)}) %collective-permute-start.6) | collective-permute-done | bytes 262176 | tf_op jit(solution)/shard_map/ppermute | solution.py:274
  107.9 1.7 collective-permute-done.7.refs_10_
  109.6 18.8 %shard_map.109 = (bf16[2,448,256]{2,1,0:T(8,128)(2,1)}, bf16[2,448,256]{2,1,0:T(8,128)(2,1)}, bf16[2,448,1024]{2,1,0:T(8,128)(2,1)}, bf16[8,160,128]{2,1,0:T(8,128)(2,1)}, bf16[8,160,128]{2,1,0:T(8,128)(2,1)}) custom-call(s32[3]{0:T(128)} %pad_add_fusion.at_ref, bf16[4,896,256]{2,1,0:T(8,128)(2,1)} %copy-done.2, ...), custom_call_target="tpu_custom_call" | custom-call | flops 5637144576 | bytes 12582912 | tf_op jit(solution)/shard_map/pallas_call | solution.py:215
  128.4 4.3 %all-to-all-start.1 = ((bf16[4,2,160,128]{3,2,1,0:T(8,128)(2,1)}), bf16[4,2,160,128]{3,2,1,0:T(8,128)(2,1)S(1)}, u32[]{:S(2)}, u32[]{:S(2)}) async-start(bf16[4,2,160,128]{3,2,1,0:T(8,128)(2,1)} %bitcast.15), calls=%async_computation.1 | async-start | bytes 655360 | tf_op jit(solution)/shard_map/all_to_all | solution.py:346
  132.6 8.9 %shard_map.110 = (f32[2,448,512]{2,1,0:T(8,128)}, bf16[2,4,448,160]{3,2,1,0:T(8,128)(2,1)}) custom-call(s32[1]{0:T(128)} %bitcast.core_ref.chunk_ref, bf16[2,448,256]{2,1,0:T(8,128)(2,1)} %get-tuple-element.18.refs_0_, bf16[2,448,256]{2,1,0:T(8,128)(2,1)} %get-tuple-element.19.refs_1_, bf16[2,448,1024]{2,1,0:T(8,128)(2,1)} %get-tuple-element.20.refs_2_, ...), custom_call_target="tpu_custom_call" | custom-call | flops 963379200 | bytes 12582912 | tf_op jit(solution)/shard_map/pallas_call | solution.py:215
  141.6 9.9 %all-gather = bf16[8,160,128]{2,1,0:T(8,128)(2,1)} all-gather(bf16[2,160,128]{2,1,0:T(8,128)(2,1)S(1)} %reduce_sum.12), channel_id=2, replica_groups=mesh['seq'=4,'z'=4,'core'=2] {'seq'}, dimensions={0}, use_global_device_ids=true | all-gather | bytes 409600 | tf_op jit(solution)/shard_map/all_gather | solution.py:350
  151.5 1.9 shard_map.112
  153.4 5.1 %all-to-all-start.2 = ((bf16[4,2,160,128]{3,2,1,0:T(8,128)(2,1)}), bf16[4,2,160,128]{3,2,1,0:T(8,128)(2,1)S(1)}, u32[]{:S(2)}, u32[]{:S(2)}) async-start(bf16[4,2,160,128]{3,2,1,0:T(8,128)(2,1)} %shard_map.112), calls=%async_computation.2 | async-start | bytes 655360 | tf_op jit(solution)/shard_map/all_to_all | solution.py:358
  159.1 9.0 %shard_map.111 = (f32[2,448,512]{2,1,0:T(8,128)}, bf16[2,4,448,160]{3,2,1,0:T(8,128)(2,1)}) custom-call(s32[1]{0:T(128)} %bitcast.core_ref.chunk_ref, bf16[2,448,256]{2,1,0:T(8,128)(2,1)} %get-tuple-element.18.refs_0_, bf16[2,448,256]{2,1,0:T(8,128)(2,1)} %get-tuple-element.19.refs_1_, bf16[2,448,1024]{2,1,0:T(8,128)(2,1)} %get-tuple-element.20.refs_2_, ...), custom_call_target="tpu_custom_call" | custom-call | flops 963379200 | bytes 12582912 | tf_op jit(solution)/shard_map/pallas_call | solution.py:215
  168.8 3.4 %shard_map.114 = bf16[448,1024]{1,0:T(8,128)(2,1)} custom-call(s32[1]{0:T(128)} %bitcast.8.chunk_ref, f32[2,448,512]{2,1,0:T(8,128)} %get-tuple-element.24.num_a, f32[2,448,512]{2,1,0:T(8,128)} %get-tuple-element.25.num_b, bf16[2,4,448,160]{3,2,1,0:T(8,128)(2,1)} %get-tuple-element.26.phi_a, bf16[2,4,448,160]{3,2,1,0:T(8,128)(2,1)} %get-tuple-element.27.phi_b, ...), custom_call_target="tpu_custom_call" | custom-call | flops 275251200 | bytes 12582912 | tf_op jit(solution)/shard_map/pallas_call | solution.py:215
  172.2 3.4 %shard_map.113.refs_0_ = bf16[448,1024]{1,0:T(8,128)(2,1)} custom-call(s32[1]{0:T(128)} %bitcast.core_ref.chunk_ref, f32[2,448,512]{2,1,0:T(8,128)} %get-tuple-element.24.num_a, f32[2,448,512]{2,1,0:T(8,128)} %get-tuple-element.25.num_b, bf16[2,4,448,160]{3,2,1,0:T(8,128)(2,1)} %get-tuple-element.26.phi_a, bf16[2,4,448,160]{3,2,1,0:T(8,128)(2,1)} %get-tuple-element.27.phi_b, ...), custom_call_target="tpu_custom_call" | custom-call | flops 275251200 | bytes 12582912 | tf_op jit(solution)/shard_map/pallas_call | solution.py:215
  176.6 8.4 %shard_map.115 = bf16[8,448,256]{2,1,0:T(8,128)(2,1)} custom-call(s32[1]{0:T(128)} %bitcast.core_ref.chunk_ref, bf16[448,1024]{1,0:T(8,128)(2,1)} %shard_map.113.refs_0_, bf16[448,1024]{1,0:T(8,128)(2,1)} %copy-done.7, bf16[2048,2048]{1,0:T(8,128)(2,1)} %refs_2_.3), custom_call_target="tpu_custom_call" | custom-call | flops 3758096384 | bytes 12582912 | tf_op jit(solution)/shard_map/pallas_call | solution.py:215
  185.0 48.6 %all_to_all.21 = bf16[8,448,256]{2,1,0:T(8,128)(2,1)S(1)} all-to-all(bf16[8,448,256]{2,1,0:T(8,128)(2,1)} %shard_map.115), channel_id=1, replica_groups=mesh['seq'=4,'z'=4,'core'=2] {'z','core'}, dimensions={0} | all-to-all | bytes 3670016 | tf_op jit(solution)/shard_map/all_to_all | solution.py:403
  233.6 1.2 copy.13
  (47 shorter events, 10.6 us)
Async XLA Ops:
  48.9 60.6 %copy-start.2 = (bf16[4,896,256]{2,1,0:T(8,128)(2,1)}, bf16[4,896,256]{2,1,0:T(8,128)(2,1)S(1)}, u32[]{:S(2)}) copy-start(bf16[4,896,256]{2,1,0:T(8,128)(2,1)S(1)} %all_to_all.20.refs_0_) | copy-start | bytes 5505028
  48.9 60.6 %collective-permute-start = (bf16[4,896,256]{2,1,0:T(8,128)(2,1)S(1)}, bf16[4,896,256]{2,1,0:T(8,128)(2,1)}, u32[]{:S(2)}, u32[]{:S(2)}) collective-permute-start(bf16[4,896,256]{2,1,0:T(8,128)(2,1)S(1)} %all_to_all.20.refs_0_), channel_id=1, source_target_pairs={{0,1},{1,0},{2,3},{3,2},{4,5},{5,4},{6,7},{7,6},{8,9},{9,8},{10,11... | collective-permute-start | bytes 5505032 | tf_op jit(solution)/shard_map/ppermute | solution.py:261
  50.0 10.4 %collective-permute-start.1 = (bf16[512,256]{1,0:T(8,128)(2,1)S(1)}, bf16[512,256]{1,0:T(8,128)(2,1)S(1)}, u32[]{:S(2)}, u32[]{:S(2)}) collective-permute-start(bf16[512,256]{1,0:T(8,128)(2,1)S(1)} %constant_dynamic-slice_fusion.1), channel_id=1, source_target_pairs={{2,0},{4,2},{6,4},{3,1},{5,3},{7,5},{10,8},{12,10},{14,12},{11,9},... | collective-permute-start | bytes 786440 | tf_op jit(solution)/shard_map/ppermute | solution.py:267
  51.3 10.4 %collective-permute-start.2 = (bf16[512,256]{1,0:T(8,128)(2,1)S(1)}, bf16[512,256]{1,0:T(8,128)(2,1)S(1)}, u32[]{:S(2)}, u32[]{:S(2)}) collective-permute-start(bf16[512,256]{1,0:T(8,128)(2,1)S(1)} %constant_dynamic-slice_fusion.1), channel_id=1, source_target_pairs={{0,2},{2,4},{4,6},{1,3},{3,5},{5,7},{8,10},{10,12},{12,14},{9,11},... | collective-permute-start | bytes 786440 | tf_op jit(solution)/shard_map/ppermute | solution.py:266
  60.5 9.6 %collective-permute-start.8 = (bf16[512,256]{1,0:T(8,128)(2,1)S(1)}, bf16[512,256]{1,0:T(8,128)(2,1)S(1)}, u32[]{:S(2)}, u32[]{:S(2)}) collective-permute-start(bf16[512,256]{1,0:T(8,128)(2,1)S(1)} %collective-permute-done.1), channel_id=1, source_target_pairs={{2,0},{4,2},{3,1},{5,3},{10,8},{12,10},{11,9},{13,11},{18,16},{20,... | collective-permute-start | bytes 786440 | tf_op jit(solution)/shard_map/ppermute | solution.py:267
  61.8 9.6 %collective-permute-start.3 = (bf16[512,256]{1,0:T(8,128)(2,1)S(1)}, bf16[512,256]{1,0:T(8,128)(2,1)S(1)}, u32[]{:S(2)}, u32[]{:S(2)}) collective-permute-start(bf16[512,256]{1,0:T(8,128)(2,1)S(1)} %collective-permute-done.2), channel_id=1, source_target_pairs={{2,4},{4,6},{3,5},{5,7},{10,12},{12,14},{11,13},{13,15},{18,20},{2... | collective-permute-start | bytes 786440 | tf_op jit(solution)/shard_map/ppermute | solution.py:266
  70.1 8.8 %collective-permute-start.12 = (bf16[512,256]{1,0:T(8,128)(2,1)S(1)}, bf16[512,256]{1,0:T(8,128)(2,1)}, u32[]{:S(2)}, u32[]{:S(2)}) collective-permute-start(bf16[512,256]{1,0:T(8,128)(2,1)S(1)} %collective-permute-done.8), channel_id=1, source_target_pairs={{2,0},{3,1},{10,8},{11,9},{18,16},{19,17},{26,24},{27,25}} | collective-permute-start | bytes 786440 | tf_op jit(solution)/shard_map/ppermute | solution.py:267
  71.5 38.1 %copy-start.3 = (bf16[512,256]{1,0:T(8,128)(2,1)}, bf16[512,256]{1,0:T(8,128)(2,1)S(1)}, u32[]{:S(2)}) copy-start(bf16[512,256]{1,0:T(8,128)(2,1)S(1)} %broadcast_select_fusion.1.refs_11_) | copy-start | bytes 786436
  71.5 12.6 %collective-permute-start.10 = (bf16[512,256]{1,0:T(8,128)(2,1)S(1)}, bf16[512,256]{1,0:T(8,128)(2,1)}, u32[]{:S(2)}, u32[]{:S(2)}) collective-permute-start(bf16[512,256]{1,0:T(8,128)(2,1)S(1)} %broadcast_select_fusion.1.refs_11_), channel_id=1, source_target_pairs={{0,16},{8,24},{16,0},{24,8},{1,17},{9,25},{17,1},{25,9},{2,18},{10... | collective-permute-start | bytes 786440 | tf_op jit(solution)/shard_map/ppermute | solution.py:274
  73.0 12.5 %collective-permute-start.4 = (bf16[512,256]{1,0:T(8,128)(2,1)S(1)}, bf16[512,256]{1,0:T(8,128)(2,1)S(1)}, u32[]{:S(2)}, u32[]{:S(2)}) collective-permute-start(bf16[512,256]{1,0:T(8,128)(2,1)S(1)} %collective-permute-done.3), channel_id=1, source_target_pairs={{4,6},{5,7},{12,14},{13,15},{20,22},{21,23},{28,30},{29,31}} | collective-permute-start | bytes 786440 | tf_op jit(solution)/shard_map/ppermute | solution.py:266
  73.7 13.4 %collective-permute-start.11 = (bf16[512,256]{1,0:T(8,128)(2,1)S(1)}, bf16[512,256]{1,0:T(8,128)(2,1)}, u32[]{:S(2)}, u32[]{:S(2)}) collective-permute-start(bf16[512,256]{1,0:T(8,128)(2,1)S(1)} %broadcast_select_fusion.1.refs_11_), channel_id=1, source_target_pairs={{0,24},{8,16},{16,8},{24,0},{1,25},{9,17},{17,9},{25,1},{2,26},{10... | collective-permute-start | bytes 786440 | tf_op jit(solution)/shard_map/ppermute | solution.py:274
  78.9 9.4 %collective-permute-start.9 = (bf16[512,256]{1,0:T(8,128)(2,1)S(1)}, bf16[512,256]{1,0:T(8,128)(2,1)}, u32[]{:S(2)}, u32[]{:S(2)}) collective-permute-start(bf16[512,256]{1,0:T(8,128)(2,1)S(1)} %broadcast_select_fusion.1.refs_11_), channel_id=1, source_target_pairs={{0,8},{8,0},{16,24},{24,16},{1,9},{9,1},{17,25},{25,17},{2,10},{10... | collective-permute-start | bytes 786440 | tf_op jit(solution)/shard_map/ppermute | solution.py:274
  81.4 28.1 %copy-start.4 = (bf16[512,256]{1,0:T(8,128)(2,1)}, bf16[512,256]{1,0:T(8,128)(2,1)S(1)}, u32[]{:S(2)}) copy-start(bf16[512,256]{1,0:T(8,128)(2,1)S(1)} %broadcast_select_fusion.refs_15_) | copy-start | bytes 786436
  84.1 9.8 %collective-permute-start.13 = (bf16[512,256]{1,0:T(8,128)(2,1)S(1)}, bf16[512,256]{1,0:T(8,128)(2,1)}, u32[]{:S(2)}, u32[]{:S(2)}) collective-permute-start(bf16[512,256]{1,0:T(8,128)(2,1)S(1)} %broadcast_select_fusion.refs_15_), channel_id=1, source_target_pairs={{0,8},{8,0},{16,24},{24,16},{1,9},{9,1},{17,25},{25,17},{2,10},{10... | collective-permute-start | bytes 786440 | tf_op jit(solution)/shard_map/ppermute | solution.py:274
  85.6 10.6 %collective-permute-start.14 = (bf16[512,256]{1,0:T(8,128)(2,1)S(1)}, bf16[512,256]{1,0:T(8,128)(2,1)S(1)}, u32[]{:S(2)}, u32[]{:S(2)}) collective-permute-start(bf16[512,256]{1,0:T(8,128)(2,1)S(1)} %broadcast_select_fusion.refs_15_), channel_id=1, source_target_pairs={{0,16},{8,24},{16,0},{24,8},{1,17},{9,25},{17,1},{25,9},{2,18},{10... | collective-permute-start | bytes 786440 | tf_op jit(solution)/shard_map/ppermute | solution.py:274
  87.1 22.4 %copy-start.5 = (bf16[512,256]{1,0:T(8,128)(2,1)}, bf16[512,256]{1,0:T(8,128)(2,1)S(1)}, u32[]{:S(2)}) copy-start(bf16[512,256]{1,0:T(8,128)(2,1)S(1)} %broadcast_select_fusion.2.refs_7_) | copy-start | bytes 786436
  87.2 12.8 %collective-permute-start.15 = (bf16[512,256]{1,0:T(8,128)(2,1)S(1)}, bf16[512,256]{1,0:T(8,128)(2,1)S(1)}, u32[]{:S(2)}, u32[]{:S(2)}) collective-permute-start(bf16[512,256]{1,0:T(8,128)(2,1)S(1)} %broadcast_select_fusion.refs_15_), channel_id=1, source_target_pairs={{0,24},{8,16},{16,8},{24,0},{1,25},{9,17},{17,9},{25,1},{2,26},{10... | collective-permute-start | bytes 786440 | tf_op jit(solution)/shard_map/ppermute | solution.py:274
  88.3 16.8 %collective-permute-start.5 = (bf16[512,256]{1,0:T(8,128)(2,1)S(1)}, bf16[512,256]{1,0:T(8,128)(2,1)S(1)}, u32[]{:S(2)}, u32[]{:S(2)}) collective-permute-start(bf16[512,256]{1,0:T(8,128)(2,1)S(1)} %broadcast_select_fusion.2.refs_7_), channel_id=1, source_target_pairs={{0,8},{8,0},{16,24},{24,16},{1,9},{9,1},{17,25},{25,17},{2,10},{10... | collective-permute-start | bytes 786440 | tf_op jit(solution)/shard_map/ppermute | solution.py:274
  93.9 14.0 %collective-permute-start.6 = (bf16[512,256]{1,0:T(8,128)(2,1)S(1)}, bf16[512,256]{1,0:T(8,128)(2,1)}, u32[]{:S(2)}, u32[]{:S(2)}) collective-permute-start(bf16[512,256]{1,0:T(8,128)(2,1)S(1)} %broadcast_select_fusion.2.refs_7_), channel_id=1, source_target_pairs={{0,16},{8,24},{16,0},{24,8},{1,17},{9,25},{17,1},{25,9},{2,18},{10... | collective-permute-start | bytes 786440 | tf_op jit(solution)/shard_map/ppermute | solution.py:274
  96.2 13.4 %copy-start.8 = (bf16[512,256]{1,0:T(8,128)(2,1)}, bf16[512,256]{1,0:T(8,128)(2,1)S(1)}, u32[]{:S(2)}) copy-start(bf16[512,256]{1,0:T(8,128)(2,1)S(1)} %collective-permute-done.14.refs_17_) | copy-start | bytes 786436
  96.2 13.4 %collective-permute-start.7 = (bf16[512,256]{1,0:T(8,128)(2,1)S(1)}, bf16[512,256]{1,0:T(8,128)(2,1)}, u32[]{:S(2)}, u32[]{:S(2)}) collective-permute-start(bf16[512,256]{1,0:T(8,128)(2,1)S(1)} %broadcast_select_fusion.2.refs_7_), channel_id=1, source_target_pairs={{0,24},{8,16},{16,8},{24,0},{1,25},{9,17},{17,9},{25,1},{2,26},{10... | collective-permute-start | bytes 786440 | tf_op jit(solution)/shard_map/ppermute | solution.py:274
  100.0 9.6 %copy-start.9 = (bf16[512,256]{1,0:T(8,128)(2,1)}, bf16[512,256]{1,0:T(8,128)(2,1)S(1)}, u32[]{:S(2)}) copy-start(bf16[512,256]{1,0:T(8,128)(2,1)S(1)} %collective-permute-done.15.refs_18_) | copy-start | bytes 786436
  105.1 4.5 %copy-start.10 = (bf16[512,256]{1,0:T(8,128)(2,1)}, bf16[512,256]{1,0:T(8,128)(2,1)S(1)}, u32[]{:S(2)}) copy-start(bf16[512,256]{1,0:T(8,128)(2,1)S(1)} %collective-permute-done.5.refs_8_) | copy-start | bytes 786436
  128.4 13.2 %all-to-all-start.1 = ((bf16[4,2,160,128]{3,2,1,0:T(8,128)(2,1)}), bf16[4,2,160,128]{3,2,1,0:T(8,128)(2,1)S(1)}, u32[]{:S(2)}, u32[]{:S(2)}) async-start(bf16[4,2,160,128]{3,2,1,0:T(8,128)(2,1)} %bitcast.15), calls=%async_computation.1 | async-start | bytes 655360 | tf_op jit(solution)/shard_map/all_to_all | solution.py:346
  141.5 16.9 %copy-start.6 = (f32[2048]{0:T(1024)S(1)}, f32[2048]{0:T(1024)}, u32[]{:S(2)}) copy-start(f32[2048]{0:T(1024)} %param.16) | copy-start | bytes 24580
  141.6 9.9 %copy-start.1 = (bf16[4,2,160,128]{3,2,1,0:T(8,128)(2,1)}, bf16[4,2,160,128]{3,2,1,0:T(8,128)(2,1)S(1)}, u32[]{:S(2)}) copy-start(bf16[4,2,160,128]{3,2,1,0:T(8,128)(2,1)S(1)} %all-to-all-done.1.line_ref) | copy-start | bytes 983044
  153.4 14.7 %all-to-all-start.2 = ((bf16[4,2,160,128]{3,2,1,0:T(8,128)(2,1)}), bf16[4,2,160,128]{3,2,1,0:T(8,128)(2,1)S(1)}, u32[]{:S(2)}, u32[]{:S(2)}) async-start(bf16[4,2,160,128]{3,2,1,0:T(8,128)(2,1)} %shard_map.112), calls=%async_computation.2 | async-start | bytes 655360 | tf_op jit(solution)/shard_map/all_to_all | solution.py:358
  168.1 0.7 copy-start
  172.2 3.4 %collective-permute-start.16 = (bf16[448,1024]{1,0:T(8,128)(2,1)}, bf16[448,1024]{1,0:T(8,128)(2,1)S(1)}, u32[]{:S(2)}, u32[]{:S(2)}) collective-permute-start(bf16[448,1024]{1,0:T(8,128)(2,1)} %shard_map.114), channel_id=1, source_target_pairs={{0,1},{1,0},{2,3},{3,2},{4,5},{5,4},{6,7},{7,6},{8,9},{9,8},{10,11... | collective-permute-start | bytes 2752520 | tf_op jit(solution)/shard_map/ppermute | solution.py:384
  175.6 0.9 copy-start.7

commit v3 on v2

--- a/solution.py
+++ b/solution.py
@@ -59,41 +59,34 @@
     return np.stack([every[places].reshape(-1, LANES) for places in own])
 
 
-def project_kernel(
-    at_ref,
-    per_group,
-    counts,
-    mine_ref,
-    other_ref,
-    wq_ref,
-    wk_ref,
-    table_ref,
-    bias_ref,
-    *rest,
-):
+def project_kernel(at_ref, per_group, counts, layers, *refs):
     n_weights = sum(counts)
-    weights = rest[:n_weights]
-    q_ref, k_ref, v_ref, early_ref, total_ref, row_ref, w_ref, phi_ref, sems = rest[n_weights:]
+    mine, other = refs[:layers], refs[layers : 2 * layers]
+    wq_ref, wk_ref, table_ref, bias_ref = refs[2 * layers : 2 * layers + 4]
+    weights = refs[2 * layers + 4 : 2 * layers + 4 + n_weights]
+    q_ref, k_ref, v_ref, early_ref, *rest = refs[2 * layers + 4 + n_weights :]
+    totals, (row_ref, w_ref, phi_ref, sems) = rest[:layers], rest[layers:]
     core, layer, slab = at_ref[0], at_ref[1], at_ref[2]
-    layers, both, width = mine_ref.shape
+    both, width = other[0].shape
     rows = both // 2
     copies = []
     place = 0
-    for d, count in enumerate(counts):
+    for e, count in enumerate(counts):
         for m in range(count):
             source = weights[place]
             part = source.shape[0]
             start = 0 if count == 1 else pl.multiple_of((slab ^ m) * part, part)
-            copy = pltpu.make_async_copy(source, w_ref.at[d, pl.ds(start, part)], sems.at[place])
+            copy = pltpu.make_async_copy(source, w_ref.at[e, pl.ds(start, part)], sems.at[place])
             copy.start()
-            copies.append((d, copy))
+            copies.append((e, copy))
             place += 1
 
-    for z in range(layers):
+    for d in range(layers):
+        z = lax.rem(layer + layers - d, layers)
         here = pl.multiple_of((2 * z + core) * width, width)
         there = pl.multiple_of((2 * z + 1 - core) * width, width)
-        row_ref[:, pl.ds(here, width)] = mine_ref[z]
-        row_ref[:, pl.ds(there, width)] = other_ref[z]
+        row_ref[:, pl.ds(here, width)] = mine[d][0] if d == 0 else mine[d][...]
+        row_ref[:, pl.ds(there, width)] = other[d][...]
     q = dot(row_ref[...], wq_ref[...]).astype(BF16)
     k = dot(row_ref[...], wk_ref[...]).astype(BF16)
     half = table_ref.shape[1] // 2
@@ -109,35 +102,36 @@
             phi_ref[chunk, to : to + half, :] = (left * right).astype(BF16)
 
     block = v_ref.shape[2] // layers
-    for d in range(layers):
+    for e in range(layers):
         for slot, copy in copies:
-            if slot == d:
+            if slot == e:
                 copy.wait()
-        z = lax.rem(layer + d, layers)
+        z = lax.rem(layer + e, layers)
+        first = []
         for chunk in range(2):
-            value = dot(row_ref[chunk * rows : (chunk + 1) * rows, :], w_ref[d]).astype(BF16)
-            v_ref[chunk, :, pl.ds(pl.multiple_of(z * block, block), block)] = value
+            value = dot(row_ref[chunk * rows : (chunk + 1) * rows, :], w_ref[e]).astype(BF16)
+            v_ref[chunk, :, e * block : (e + 1) * block] = value
             for i in range(per_group):
-                head = z * per_group + i
-                phi = phi_ref[chunk, pl.ds(pl.multiple_of(head * PACKED, PACKED), PACKED), :]
+                at = pl.multiple_of((z * per_group + i) * PACKED, PACKED)
+                phi = phi_ref[chunk, pl.ds(at, PACKED), :]
                 state = dot(phi, value[:, i * HEAD_DIM : (i + 1) * HEAD_DIM])
                 if chunk == 0:
-                    early_ref[head] = state.astype(BF16)
-                    first = state if i == 0 else jnp.concatenate([first, state], axis=0)
+                    early_ref[e * per_group + i] = state.astype(BF16)
+                    first.append(state)
                 else:
-                    total = first[i * PACKED : (i + 1) * PACKED] + state
-                    total_ref[head] = total.astype(BF16)
+                    totals[e][i] = (first[i] + state).astype(BF16)
 
 
 def local_kernel(
-    core_ref, per_group, offset, q_ref, k_ref, v_ref, early_ref, ta_ref, tb_ref, bias_ref, num_ref, phi_ref
+    core_ref, per_group, layers, offset, q_ref, k_ref, v_ref, early_ref, ta_ref, tb_ref, bias_ref, num_ref, phi_ref
 ):
     chunk = pl.program_id(0)
     step = pl.program_id(1) + offset
     rows = q_ref.shape[1]
     half = rows // 2
     for i in range(per_group):
-        head = (2 * step + core_ref[0]) * per_group + i
+        z = lax.rem(core_ref[1] + step, layers)
+        head = (2 * z + core_ref[0]) * per_group + i
         lanes = pl.multiple_of((head // HELD) * LANES, LANES)
         place = lax.rem(head, HELD)
         query = q_ref[0, :, pl.ds(lanes, LANES)]
@@ -162,23 +156,35 @@
             num_ref[0, :, columns] += dot(phi_ref[0, i], early_ref[i])
 
 
-def prefix_kernel(slab_ref, line_ref, totals_ref, out_ref):
+def prefix_kernel(at_ref, layers, *refs):
+    pieces, refs = refs[:layers], refs[layers:]
+    slabs = len(refs) - layers - 1
+    totals, outs, line_ref = refs[:slabs], refs[slabs : slabs + layers], refs[-1]
+    layer, slab = at_ref[1], at_ref[2]
+    for d in range(layers):
+        line_ref[lax.rem(layer + layers - d, layers)] = pieces[d][...].astype(F32)
     run = jnp.zeros(line_ref.shape[1:], F32)
-    for s in range(totals_ref.shape[0]):
-        keep = jnp.where(s < slab_ref[0], 1.0, 0.0)
-        run = run + totals_ref[s].astype(F32) * keep
-    for c in range(line_ref.shape[0]):
-        out_ref[c] = run.astype(BF16)
-        run = run + line_ref[c].astype(F32)
-
-
-def hidden_kernel(chunk_ref, num_a, num_b, phi_a, phi_b, state_ref, gain_ref, out_ref):
+    for m in range(1, slabs):
+        keep = jnp.where((slab ^ m) < slab, 1.0, 0.0)
+        run = run + totals[m][...].astype(F32) * keep
+    for z in range(layers):
+        now = line_ref[z]
+        line_ref[z] = run
+        run = run + now
+    for d in range(layers):
+        outs[d][...] = line_ref[lax.rem(layer + layers - d, layers)].astype(BF16)
+
+
+def hidden_kernel(chunk_ref, layers, num_a, num_b, phi_a, phi_b, gain_ref, *rest):
+    states, out_ref = rest[:layers], rest[layers]
     held = phi_a.shape[1]
+    per_group = 2 * held // layers
     for i in range(2 * held):
         columns = slice(i * HEAD_DIM, (i + 1) * HEAD_DIM)
         num_ref, phi_ref = (num_a, phi_a) if i < held else (num_b, phi_b)
         at = (i % held) * HEAD_DIM
-        num = num_ref[0, :, at : at + HEAD_DIM] + dot(phi_ref[0, i % held], state_ref[i])
+        state = states[i // per_group][i % per_group]
+        num = num_ref[0, :, at : at + HEAD_DIM] + dot(phi_ref[0, i % held], state)
         mean_square = jnp.mean(num * num, axis=1, keepdims=True)
         hidden = num * lax.rsqrt(mean_square + 1e-05) * gain_ref[:, columns]
         out_ref[:, columns] = hidden.astype(BF16)
@@ -190,8 +196,9 @@
     @pl.when(pl.program_id(0) == 0)
     def _():
         block = mine_ref.shape[1] // layers
-        for z in range(layers):
-            columns = slice(z * block, (z + 1) * block)
+        for e in range(layers):
+            z = lax.rem(core_ref[1] + e, layers)
+            columns = slice(e * block, (e + 1) * block)
             here = pl.multiple_of((2 * z + core) * block, block)
             there = pl.multiple_of((2 * z + 1 - core) * block, block)
             hidden_ref[:, pl.ds(here, block)] = mine_ref[:, columns]
@@ -234,7 +241,6 @@
     my_slab = lax.axis_index("seq")
     core = lax.axis_index("core").astype(jnp.int32)
     layer = lax.axis_index("z").astype(jnp.int32)
-    which = core.reshape(1)
     width = tokens.shape[1]
     rows = tokens.shape[0] // groups
     model, value_width = w_value.shape
@@ -253,38 +259,44 @@
     query_b = jnp.asarray(placed(second), BF16)
     query_bias = jnp.asarray(np.stack([first_bias * scale, second_bias]))
     gain_mine = lax.dynamic_index_in_dim(gain.reshape(layers, 2, value_width), core, 1, False)
-    gain_mine = gain_mine.reshape(1, layers * value_width)
-
-    mine = lax.all_to_all(
-        tokens.reshape(layers, 2 * rows, width), "z", split_axis=0, concat_axis=0, tiled=True
-    )
-    other = lax.ppermute(mine, "core", swap)
+    gain_mine = jnp.concatenate([gain_mine, gain_mine])
+    gain_mine = lax.dynamic_slice_in_dim(gain_mine, layer, layers, 0).reshape(1, layers * value_width)
+    turn = lambda d: [(z, (z + d) % layers) for z in range(layers)]
+    flip = lambda m: [(s, s ^ m) for s in range(slabs)]
 
     value_part = lax.dynamic_slice_in_dim(w_value, my_slab * part, part, 0)
     up, down = {0: value_part}, {0: value_part}
     for k in range(1, layers):
         up[k] = lax.ppermute(up[k - 1], "z", [(z, z + 1) for z in range(k - 1, layers - 1)])
         down[k] = lax.ppermute(down[k - 1], "z", [(z, z - 1) for z in range(1, layers - k + 1)])
+
+    blocks = tokens.reshape(layers, 2 * rows, width)
+    send = lambda d: lax.dynamic_index_in_dim(blocks, lax.rem(layer + d, layers), 0, False)
+    mine = [send(0)] + [lax.ppermute(send(d), "z", turn(d)) for d in range(1, layers)]
+    other = [lax.ppermute(piece, "core", swap) for piece in mine]
+
     weights, counts = [w_value], [1]
-    for d in range(1, layers):
-        slot = jnp.where(layer + d < layers, down[d], up[layers - d])
+    for e in range(1, layers):
+        slot = jnp.where(layer + e < layers, down[e], up[layers - e])
         if slabs == 4:
             weights.append(slot)
             for m in range(1, slabs):
-                weights.append(lax.ppermute(slot, "seq", [(s, s ^ m) for s in range(slabs)]))
+                weights.append(lax.ppermute(slot, "seq", flip(m)))
             counts.append(slabs)
         else:
             weights.append(lax.all_gather(slot, "seq", axis=0, tiled=True))
             counts.append(1)
 
     anywhere = pl.BlockSpec(memory_space=pl.ANY)
-    query, key, value, early, total = call(
-        lambda at_ref, *refs: project_kernel(at_ref, per_group, counts, *refs),
-        jnp.stack([core, layer, my_slab.astype(jnp.int32)]),
+    at = jnp.stack([core, layer, my_slab.astype(jnp.int32)])
+    piece_shape = jax.ShapeDtypeStruct((per_group, PACKED, HEAD_DIM), BF16)
+    query, key, value, early, *own = call(
+        lambda at_ref, *refs: project_kernel(at_ref, per_group, counts, layers, *refs),
+        at,
         (1,),
-        [
-            whole((layers, 2 * rows, width)),
-            whole((layers, 2 * rows, width)),
+        [pl.BlockSpec((1, 2 * rows, width), lambda i, at: (at[1], 0, 0))]
+        + [whole((2 * rows, width))] * (2 * layers - 1)
+        + [
             whole((model, narrow)),
             whole((model, narrow)),
             pl.BlockSpec((1,) + key_table.shape[1:], lambda i, at: (at[0], 0, 0)),
@@ -296,16 +308,16 @@
             whole((2, rows, narrow)),
             whole((2, rows, layers * value_width)),
             whole((heads, PACKED, HEAD_DIM)),
-            whole((heads, PACKED, HEAD_DIM)),
-        ],
+        ]
+        + [whole(piece_shape.shape)] * layers,
         [
             jax.ShapeDtypeStruct((2, rows, narrow), BF16),
             jax.ShapeDtypeStruct((2, rows, narrow), BF16),
             jax.ShapeDtypeStruct((2, rows, layers * value_width), BF16),
             jax.ShapeDtypeStruct((heads, PACKED, HEAD_DIM), BF16),
-            jax.ShapeDtypeStruct((heads, PACKED, HEAD_DIM), BF16),
-        ],
-        (mine, other, w_query, w_key, key_table, key_bias, *weights),
+        ]
+        + [piece_shape] * layers,
+        (blocks, *mine[1:], *other, w_query, w_key, key_table, key_bias, *weights),
         4 * rows * model * (model // 2 + 2 * narrow),
         [
             pltpu.VMEM((2 * rows, model), BF16),
@@ -318,8 +330,8 @@
     def local(part_of_heads):
         offset = part_of_heads * (layers // 2)
         return call(
-            lambda core_ref, *refs: local_kernel(core_ref, per_group, offset, *refs),
-            which,
+            lambda core_ref, *refs: local_kernel(core_ref, per_group, layers, offset, *refs),
+            at,
             (2, layers // 2),
             [
                 pl.BlockSpec((1, rows, narrow), lambda c, i, _: (c, 0, 0)),
@@ -342,21 +354,20 @@
             heads * rows * rows * 600,
         )
 
-    own = total.reshape(layers, per_group, PACKED, HEAD_DIM)
-    line = lax.all_to_all(own, "z", split_axis=0, concat_axis=0, tiled=True)
+    pieces = [own[0]] + [lax.ppermute(own[d], "z", turn(d)) for d in range(1, layers)]
     num_a, phi_a = local(0)
-    line, num_a, phi_a = lax.optimization_barrier((line, num_a, phi_a))
-    slab_total = jnp.sum(line.astype(F32), axis=0).astype(BF16)
-    totals = lax.all_gather(slab_total, "seq", axis=0, tiled=False)
+    pieces, num_a, phi_a = lax.optimization_barrier((pieces, num_a, phi_a))
+    slab_total = sum(piece.astype(F32) for piece in pieces).astype(BF16)
+    totals = [slab_total] + [lax.ppermute(slab_total, "seq", flip(m)) for m in range(1, slabs)]
     vmem = pl.BlockSpec(memory_space=pltpu.VMEM)
     prefix = pl.pallas_call(
-        prefix_kernel,
-        in_specs=[pl.BlockSpec(memory_space=pltpu.SMEM), vmem, vmem],
-        out_specs=vmem,
-        out_shape=jax.ShapeDtypeStruct(line.shape, BF16),
-    )(my_slab.reshape(1), line, totals)
-    prefix = lax.all_to_all(prefix, "z", split_axis=0, concat_axis=0, tiled=True)
-    prefix = prefix.reshape(heads, PACKED, HEAD_DIM)
+        lambda at_ref, *refs: prefix_kernel(at_ref, layers, *refs),
+        in_specs=[pl.BlockSpec(memory_space=pltpu.SMEM)] + [vmem] * (layers + slabs),
+        out_specs=[vmem] * layers,
+        out_shape=[piece_shape] * layers,
+        scratch_shapes=[pltpu.VMEM((layers,) + piece_shape.shape, F32)],
+    )(at, *pieces, *totals)
+    prefix = [prefix[0]] + [lax.ppermute(prefix[d], "z", turn(-d)) for d in range(1, layers)]
     num_b, phi_b = local(1)
 
     def hidden(chunk):
@@ -364,20 +375,14 @@
         numbers = pl.BlockSpec((1, some, heads * HEAD_DIM // 2), lambda i, c: (c[0], i, 0))
         features = pl.BlockSpec((1, heads // 2, some, PACKED), lambda i, c: (c[0], 0, i, 0))
         return call(
-            hidden_kernel,
+            lambda chunk_ref, *refs: hidden_kernel(chunk_ref, layers, *refs),
             chunk.reshape(1),
             (2,),
-            [
-                numbers,
-                numbers,
-                features,
-                features,
-                whole((heads, PACKED, HEAD_DIM)),
-                whole((1, heads * HEAD_DIM)),
-            ],
+            [numbers, numbers, features, features, whole((1, heads * HEAD_DIM))]
+            + [whole(piece_shape.shape)] * layers,
             pl.BlockSpec((some, heads * HEAD_DIM), lambda i, c: (i, 0)),
             jax.ShapeDtypeStruct((rows, heads * HEAD_DIM), BF16),
-            (num_a, num_b, phi_a, phi_b, prefix, gain_mine),
+            (num_a, num_b, phi_a, phi_b, gain_mine, *prefix),
             rows * heads * HEAD_DIM * 600,
         )
 
@@ -387,7 +392,7 @@
     per_out = groups // steps
     out = call(
         lambda core_ref, *refs: output_kernel(core_ref, layers, *refs),
-        which,
+        at,
         (steps,),
         [
             whole((rows, heads * HEAD_DIM)),

time: 236 us -> 227 us (0.962)
  blocking collectives: 107 us -> 48.5 us
  starting transfers between devices: 30.5 us -> 54.2 us
  waiting for transfers between devices: 36.6 us -> 59.2 us
  local copies, waits for them, and re-layouts: 4.67 us -> 7.31 us
    all_to_all x1 -> x0, blocking collectives: 48.9 us -> none  [per_device(): lax.all_to_all(tokens.reshape(layers, 2 * rows, width), 'z', split_axis=0...]
    ppermute x10 -> x25, starting transfers between devices: 11.4 us -> 43.4 us  [the longest x9 13.9 us: per_device(): weights.append(lax.ppermute(slot, 'seq', flip(m)))]
    ppermute x10 -> x25, waiting for transfers between devices: 20.6 us -> 37 us  [the longest x3 19.2 us: per_device(): lax.ppermute(send(d), 'z', turn(d))]
    all_gather x1 -> x0, blocking collectives: 9.86 us -> none  [per_device(): totals = lax.all_gather(slab_total, 'seq', axis=0, tiled=False)]
    all_to_all x2 -> x0, starting transfers between devices: 9.35 us -> none  [the longest x1 5.08 us: per_device(): lax.all_to_all(prefix, 'z', split_axis=0, concat_axis=0, tiled=True)]
    ppermute x3, waiting for transfers between devices: 15.9 us -> 22.2 us  [per_device(): lax.ppermute(down[k - 1], 'z', [(z, z - 1) for z in range(1, layers - k +...]
    unnamed x23 -> x51, local copies, waits for them, and re-layouts: 2.93 us -> 4.76 us
  transfers between devices with their start and end apart: 19 -> 32, of which waited for: 11 -> 11; matrix products, arithmetic and copies ran while one was open for 1% -> 1% of each run, Pallas kernels for 9% -> 10%
where the time goes in v3:
time: 227 us; the launch traced here: 226 us
  waiting for transfers between devices  59.2 us (26%)
  Pallas kernels  55.9 us (25%)
  starting transfers between devices  54.2 us (24%)
  blocking collectives  48.5 us (21%)
  local copies, waits for them, and re-layouts  7.31 us (3%)
    pallas_call x6, Pallas kernels, call(): pl.pallas_call(kernel, grid_spec=pltpu.PrefetchScalarGridSpec(num_scalar_...  53.9 us
    all_to_all x1, blocking collectives, per_device(): lax.all_to_all(out, ('z', 'core'), split_axis=0, concat_axis=0, tiled=True)  48.5 us
    ppermute x3, waiting for transfers between devices, per_device(): lax.ppermute(down[k - 1], 'z', [(z, z - 1) for z in range(1, layers - k +...  22.2 us
    ppermute x3, waiting for transfers between devices, per_device(): lax.ppermute(send(d), 'z', turn(d))  19.2 us
    ppermute x9, starting transfers between devices, per_device(): weights.append(lax.ppermute(slot, 'seq', flip(m)))  13.9 us
    ppermute x9, waiting for transfers between devices, per_device(): weights.append(lax.ppermute(slot, 'seq', flip(m)))  13.5 us
    ppermute x3, starting transfers between devices, per_device(): lax.ppermute(own[d], 'z', turn(d))  13.5 us
    ppermute x3, starting transfers between devices, per_device(): lax.ppermute(send(d), 'z', turn(d))  9.32 us
  transfers between devices with their start and end apart: 32, of which 11 were waited for; matrix products, arithmetic and copies ran while one was open for 1% of the time, Pallas kernels for 10%

profile of v3, /device:TPU:0, one launch (start us, length us, event | category | flops | bytes accessed | tf_op | source)
XLA Modules:
  0.0 226.4 jit_solution(3971892500943787579)
XLA Ops:
  2.3 5.6 %collective-permute-start.8 = (bf16[512,256]{1,0:T(8,128)(2,1)S(1)}, bf16[512,256]{1,0:T(8,128)(2,1)S(1)}, u32[]{:S(2)}, u32[]{:S(2)}) collective-permute-start(bf16[512,256]{1,0:T(8,128)(2,1)S(1)} %constant_dynamic-slice_fusion.1), channel_id=1, source_target_pairs={{0,2},{2,4},{4,6},{1,3},{3,5},{5,7},{8,10},{10,12},{12,14},{9,11},... | collective-permute-start | bytes 786440 | tf_op jit(solution)/shard_map/ppermute | solution.py:270
  7.9 4.3 %collective-permute-done.7 = bf16[512,256]{1,0:T(8,128)(2,1)S(1)} collective-permute-done((bf16[512,256]{1,0:T(8,128)(2,1)S(1)}, bf16[512,256]{1,0:T(8,128)(2,1)S(1)}, u32[]{:S(2)}, u32[]{:S(2)}) %collective-permute-start.7) | collective-permute-done | bytes 262176 | tf_op jit(solution)/shard_map/ppermute | solution.py:271
  14.2 1.6 dynamic-slice_bitcast_fusion
  15.8 5.7 %collective-permute-start = (bf16[896,256]{1,0:T(8,128)(2,1)S(1)}, bf16[896,256]{1,0:T(8,128)(2,1)}, u32[]{:S(2)}, u32[]{:S(2)}) collective-permute-start(bf16[896,256]{1,0:T(8,128)(2,1)S(1)} %get-tuple-element.52), channel_id=1, source_target_pairs={{0,2},{2,4},{4,6},{6,0},{1,3},{3,5},{5,7},{7,1},{8,10},{10,12},{12... | collective-permute-start | bytes 1376264 | tf_op jit(solution)/shard_map/ppermute | solution.py:275
  22.2 2.8 %collective-permute-start.2 = (bf16[896,256]{1,0:T(8,128)(2,1)S(1)}, bf16[896,256]{1,0:T(8,128)(2,1)}, u32[]{:S(2)}, u32[]{:S(2)}) collective-permute-start(bf16[896,256]{1,0:T(8,128)(2,1)S(1)} %get-tuple-element.50), channel_id=1, source_target_pairs={{0,6},{2,0},{4,2},{6,4},{1,7},{3,1},{5,3},{7,5},{8,14},{10,8},{12,... | collective-permute-start | bytes 1376264 | tf_op jit(solution)/shard_map/ppermute | solution.py:275
  25.1 7.0 %collective-permute-done.14 = bf16[512,256]{1,0:T(8,128)(2,1)S(1)} collective-permute-done((bf16[512,256]{1,0:T(8,128)(2,1)S(1)}, bf16[512,256]{1,0:T(8,128)(2,1)S(1)}, u32[]{:S(2)}, u32[]{:S(2)}) %collective-permute-start.14) | collective-permute-done | bytes 262176 | tf_op jit(solution)/shard_map/ppermute | solution.py:271
  33.1 1.5 collective-permute-start.16
  34.6 19.2 %collective-permute-done.1.refs_2_ = bf16[896,256]{1,0:T(8,128)(2,1)} collective-permute-done((bf16[896,256]{1,0:T(8,128)(2,1)S(1)}, bf16[896,256]{1,0:T(8,128)(2,1)}, u32[]{:S(2)}, u32[]{:S(2)}) %collective-permute-start.1) | collective-permute-done | bytes 458784 | tf_op jit(solution)/shard_map/ppermute | solution.py:275
  56.5 2.4 %collective-permute-start.17 = (bf16[512,256]{1,0:T(8,128)(2,1)S(1)}, bf16[512,256]{1,0:T(8,128)(2,1)S(1)}, u32[]{:S(2)}, u32[]{:S(2)}) collective-permute-start(bf16[512,256]{1,0:T(8,128)(2,1)S(1)} %broadcast_select_fusion.1.refs_17_), channel_id=1, source_target_pairs={{0,24},{8,16},{16,8},{24,0},{1,25},{9,17},{17,9},{25,1},{2,26},{10... | collective-permute-start | bytes 786440 | tf_op jit(solution)/shard_map/ppermute | solution.py:284
  59.0 10.8 %collective-permute-done.18 = bf16[512,256]{1,0:T(8,128)(2,1)S(1)} collective-permute-done((bf16[512,256]{1,0:T(8,128)(2,1)S(1)}, bf16[512,256]{1,0:T(8,128)(2,1)S(1)}, u32[]{:S(2)}, u32[]{:S(2)}) %collective-permute-start.18) | collective-permute-done | bytes 262176 | tf_op jit(solution)/shard_map/ppermute | solution.py:271
  71.4 1.6 collective-permute-start.12
  73.5 1.5 collective-permute-start.19
  75.0 1.5 collective-permute-start.20
  76.5 2.6 %collective-permute-done.11.refs_14_ = bf16[512,256]{1,0:T(8,128)(2,1)S(1)} collective-permute-done((bf16[512,256]{1,0:T(8,128)(2,1)S(1)}, bf16[512,256]{1,0:T(8,128)(2,1)S(1)}, u32[]{:S(2)}, u32[]{:S(2)}) %collective-permute-start.11) | collective-permute-done | bytes 262176 | tf_op jit(solution)/shard_map/ppermute | solution.py:284
  79.1 2.4 %collective-permute-start.21 = (bf16[512,256]{1,0:T(8,128)(2,1)S(1)}, bf16[512,256]{1,0:T(8,128)(2,1)}, u32[]{:S(2)}, u32[]{:S(2)}) collective-permute-start(bf16[512,256]{1,0:T(8,128)(2,1)S(1)} %broadcast_select_fusion.refs_21_), channel_id=1, source_target_pairs={{0,24},{8,16},{16,8},{24,0},{1,25},{9,17},{17,9},{25,1},{2,26},{10... | collective-permute-start | bytes 786440 | tf_op jit(solution)/shard_map/ppermute | solution.py:284
  82.2 4.1 %collective-permute-done.12.refs_15_ = bf16[512,256]{1,0:T(8,128)(2,1)S(1)} collective-permute-done((bf16[512,256]{1,0:T(8,128)(2,1)S(1)}, bf16[512,256]{1,0:T(8,128)(2,1)S(1)}, u32[]{:S(2)}, u32[]{:S(2)}) %collective-permute-start.12) | collective-permute-done | bytes 262176 | tf_op jit(solution)/shard_map/ppermute | solution.py:284
  86.3 2.8 %collective-permute-done.19.refs_22_ = bf16[512,256]{1,0:T(8,128)(2,1)S(1)} collective-permute-done((bf16[512,256]{1,0:T(8,128)(2,1)S(1)}, bf16[512,256]{1,0:T(8,128)(2,1)S(1)}, u32[]{:S(2)}, u32[]{:S(2)}) %collective-permute-start.19) | collective-permute-done | bytes 262176 | tf_op jit(solution)/shard_map/ppermute | solution.py:284
  89.1 4.1 %collective-permute-done.20.refs_23_ = bf16[512,256]{1,0:T(8,128)(2,1)S(1)} collective-permute-done((bf16[512,256]{1,0:T(8,128)(2,1)S(1)}, bf16[512,256]{1,0:T(8,128)(2,1)S(1)}, u32[]{:S(2)}, u32[]{:S(2)}) %collective-permute-start.20) | collective-permute-done | bytes 262176 | tf_op jit(solution)/shard_map/ppermute | solution.py:284
  93.8 18.6 %shard_map.109 = (bf16[2,448,256]{2,1,0:T(8,128)(2,1)}, bf16[2,448,256]{2,1,0:T(8,128)(2,1)}, bf16[2,448,1024]{2,1,0:T(8,128)(2,1)}, bf16[8,160,128]{2,1,0:T(8,1...) custom-call(s32[3]{0:T(128)} %pad_add_fusion.at_ref.core_ref, ...), custom_call_target="tpu_custom_call" | custom-call | flops 5637144576 | bytes 12582912 | tf_op jit(solution)/shard_map/pallas_call | solution.py:222
  112.5 7.4 %collective-permute-start.22 = (bf16[2,160,128]{2,1,0:T(8,128)(2,1)}, bf16[2,160,128]{2,1,0:T(8,128)(2,1)S(1)}, u32[]{:S(2)}, u32[]{:S(2)}) collective-permute-start(bf16[2,160,128]{2,1,0:T(8,128)(2,1)} %get-tuple-element.28), channel_id=1, source_target_pairs={{0,2},{2,4},{4,6},{6,0},{1,3},{3,5},{5,7},{7,1},{8,10},{10,12},{12... | collective-permute-start | bytes 245768 | tf_op jit(solution)/shard_map/ppermute | solution.py:357
  119.9 5.0 %collective-permute-start.23 = (bf16[2,160,128]{2,1,0:T(8,128)(2,1)}, bf16[2,160,128]{2,1,0:T(8,128)(2,1)S(1)}, u32[]{:S(2)}, u32[]{:S(2)}) collective-permute-start(bf16[2,160,128]{2,1,0:T(8,128)(2,1)} %get-tuple-element.29), channel_id=1, source_target_pairs={{0,4},{2,6},{4,0},{6,2},{1,5},{3,7},{5,1},{7,3},{8,12},{10,14},{12... | collective-permute-start | bytes 245768 | tf_op jit(solution)/shard_map/ppermute | solution.py:357
  126.0 9.7 %shard_map.110 = (f32[2,448,512]{2,1,0:T(8,128)}, bf16[2,4,448,160]{3,2,1,0:T(8,128)(2,1)}) custom-call(s32[3]{0:T(128)} %pad_add_fusion.at_ref.core_ref, bf16[2,448,256]{2,1,0:T(8,128)(2,1)} %get-tuple-element.31.refs_0_, bf16[2,448,256]{2,1,0:T(8,128)(2,1)} %get-tuple-element.32.refs_1_, bf16[2,448,1024]{2,1,0:T(8,128)(2,1)} %get-tuple-element.33.refs_2_, ...), custom_call_target="tpu_custom_call" | custom-call | flops 963379200 | bytes 12582912 | tf_op jit(solution)/shard_map/pallas_call | solution.py:222
  135.8 1.6 collective-permute-start.25
  137.4 1.5 collective-permute-start.26
  141.8 2.4 %collective-permute-done.27.refs_7_ = bf16[2,160,128]{2,1,0:T(8,128)(2,1)S(1)} collective-permute-done((bf16[2,160,128]{2,1,0:T(8,128)(2,1)S(1)}, bf16[2,160,128]{2,1,0:T(8,128)(2,1)S(1)}, u32[]{:S(2)}, u32[]{:S(2)}) %collective-permute-start.27) | collective-permute-done | bytes 81952 | tf_op jit(solution)/shard_map/ppermute | solution.py:361
  144.9 2.0 shard_map.112
  147.3 2.0 collective-permute-start.29
  149.4 9.6 %shard_map.111 = (f32[2,448,512]{2,1,0:T(8,128)}, bf16[2,4,448,160]{3,2,1,0:T(8,128)(2,1)}) custom-call(s32[3]{0:T(128)} %pad_add_fusion.at_ref.core_ref, bf16[2,448,256]{2,1,0:T(8,128)(2,1)} %get-tuple-element.31.refs_0_, bf16[2,448,256]{2,1,0:T(8,128)(2,1)} %get-tuple-element.32.refs_1_, bf16[2,448,1024]{2,1,0:T(8,128)(2,1)} %get-tuple-element.33.refs_2_, ...), custom_call_target="tpu_custom_call" | custom-call | flops 963379200 | bytes 12582912 | tf_op jit(solution)/shard_map/pallas_call | solution.py:222
  159.8 3.4 %shard_map.114 = bf16[448,1024]{1,0:T(8,128)(2,1)} custom-call(s32[1]{0:T(128)} %bitcast.8.chunk_ref, f32[2,448,512]{2,1,0:T(8,128)} %get-tuple-element.37.refs_0_, f32[2,448,512]{2,1,0:T(8,128)} %get-tuple-element.38.refs_1_, bf16[2,4,448,160]{3,2,1,0:T(8,128)(2,1)} %get-tuple-element.39.refs_2_, bf16[2,4,448,160]{3,2,1,0:T(8,128)(2,1)} %get-tuple-element.40.refs_3_, ...), custom_call_target="tpu_custom_call" | custom-call | flops 275251200 | bytes 12582912 | tf_op jit(solution)/shard_map/pallas_call | solution.py:222
  163.2 3.5 %shard_map.113.refs_0_ = bf16[448,1024]{1,0:T(8,128)(2,1)} custom-call(s32[1]{0:T(128)} %bitcast.chunk_ref, f32[2,448,512]{2,1,0:T(8,128)} %get-tuple-element.37.refs_0_, f32[2,448,512]{2,1,0:T(8,128)} %get-tuple-element.38.refs_1_, bf16[2,4,448,160]{3,2,1,0:T(8,128)(2,1)} %get-tuple-element.39.refs_2_, bf16[2,4,448,160]{3,2,1,0:T(8,128)(2,1)} %get-tuple-element.40.refs_3_, ...), custom_call_target="tpu_custom_call" | custom-call | flops 275251200 | bytes 12582912 | tf_op jit(solution)/shard_map/pallas_call | solution.py:222
  167.6 9.1 %shard_map.115 = bf16[8,448,256]{2,1,0:T(8,128)(2,1)} custom-call(s32[3]{0:T(128)} %pad_add_fusion.at_ref.core_ref, bf16[448,1024]{1,0:T(8,128)(2,1)} %shard_map.113.refs_0_, bf16[448,1024]{1,0:T(8,128)(2,1)} %copy-done.15, bf16[2048,2048]{1,0:T(8,128)(2,1)} %refs_2_.1), custom_call_target="tpu_custom_call" | custom-call | flops 3758096384 | bytes 12582912 | tf_op jit(solution)/shard_map/pallas_call | solution.py:222
  176.7 48.5 %all_to_all.5 = bf16[8,448,256]{2,1,0:T(8,128)(2,1)S(1)} all-to-all(bf16[8,448,256]{2,1,0:T(8,128)(2,1)} %shard_map.115), channel_id=1, replica_groups=mesh['seq'=4,'z'=4,'core'=2] {'z','core'}, dimensions={0} | all-to-all | bytes 3670016 | tf_op jit(solution)/shard_map/all_to_all | solution.py:408
  (101 shorter events, 20.0 us)
Async XLA Ops:
  1.0 11.2 %collective-permute-start.7 = (bf16[512,256]{1,0:T(8,128)(2,1)S(1)}, bf16[512,256]{1,0:T(8,128)(2,1)S(1)}, u32[]{:S(2)}, u32[]{:S(2)}) collective-permute-start(bf16[512,256]{1,0:T(8,128)(2,1)S(1)} %constant_dynamic-slice_fusion.1), channel_id=1, source_target_pairs={{2,0},{4,2},{6,4},{3,1},{5,3},{7,5},{10,8},{12,10},{14,12},{11,9},... | collective-permute-start | bytes 786440 | tf_op jit(solution)/shard_map/ppermute | solution.py:271
  2.3 11.2 %collective-permute-start.8 = (bf16[512,256]{1,0:T(8,128)(2,1)S(1)}, bf16[512,256]{1,0:T(8,128)(2,1)S(1)}, u32[]{:S(2)}, u32[]{:S(2)}) collective-permute-start(bf16[512,256]{1,0:T(8,128)(2,1)S(1)} %constant_dynamic-slice_fusion.1), channel_id=1, source_target_pairs={{0,2},{2,4},{4,6},{1,3},{3,5},{5,7},{8,10},{10,12},{12,14},{9,11},... | collective-permute-start | bytes 786440 | tf_op jit(solution)/shard_map/ppermute | solution.py:270
  12.2 19.9 %collective-permute-start.14 = (bf16[512,256]{1,0:T(8,128)(2,1)S(1)}, bf16[512,256]{1,0:T(8,128)(2,1)S(1)}, u32[]{:S(2)}, u32[]{:S(2)}) collective-permute-start(bf16[512,256]{1,0:T(8,128)(2,1)S(1)} %collective-permute-done.7), channel_id=1, source_target_pairs={{2,0},{4,2},{3,1},{5,3},{10,8},{12,10},{11,9},{13,11},{18,16},{20,... | collective-permute-start | bytes 786440 | tf_op jit(solution)/shard_map/ppermute | solution.py:271
  13.5 18.6 %collective-permute-start.9 = (bf16[512,256]{1,0:T(8,128)(2,1)S(1)}, bf16[512,256]{1,0:T(8,128)(2,1)S(1)}, u32[]{:S(2)}, u32[]{:S(2)}) collective-permute-start(bf16[512,256]{1,0:T(8,128)(2,1)S(1)} %collective-permute-done.8), channel_id=1, source_target_pairs={{2,4},{4,6},{3,5},{5,7},{10,12},{12,14},{11,13},{13,15},{18,20},{2... | collective-permute-start | bytes 786440 | tf_op jit(solution)/shard_map/ppermute | solution.py:270
  15.8 17.3 %collective-permute-start = (bf16[896,256]{1,0:T(8,128)(2,1)S(1)}, bf16[896,256]{1,0:T(8,128)(2,1)}, u32[]{:S(2)}, u32[]{:S(2)}) collective-permute-start(bf16[896,256]{1,0:T(8,128)(2,1)S(1)} %get-tuple-element.52), channel_id=1, source_target_pairs={{0,2},{2,4},{4,6},{6,0},{1,3},{3,5},{5,7},{7,1},{8,10},{10,12},{12... | collective-permute-start | bytes 1376264 | tf_op jit(solution)/shard_map/ppermute | solution.py:275
  21.4 32.4 %collective-permute-start.1 = (bf16[896,256]{1,0:T(8,128)(2,1)S(1)}, bf16[896,256]{1,0:T(8,128)(2,1)}, u32[]{:S(2)}, u32[]{:S(2)}) collective-permute-start(bf16[896,256]{1,0:T(8,128)(2,1)S(1)} %get-tuple-element.51), channel_id=1, source_target_pairs={{0,4},{2,6},{4,0},{6,2},{1,5},{3,7},{5,1},{7,3},{8,12},{10,14},{12... | collective-permute-start | bytes 1376264 | tf_op jit(solution)/shard_map/ppermute | solution.py:275
  22.2 32.2 %collective-permute-start.2 = (bf16[896,256]{1,0:T(8,128)(2,1)S(1)}, bf16[896,256]{1,0:T(8,128)(2,1)}, u32[]{:S(2)}, u32[]{:S(2)}) collective-permute-start(bf16[896,256]{1,0:T(8,128)(2,1)S(1)} %get-tuple-element.50), channel_id=1, source_target_pairs={{0,6},{2,0},{4,2},{6,4},{1,7},{3,1},{5,3},{7,5},{8,14},{10,8},{12,... | collective-permute-start | bytes 1376264 | tf_op jit(solution)/shard_map/ppermute | solution.py:275
  32.1 23.7 %collective-permute-start.3 = (bf16[896,256]{1,0:T(8,128)(2,1)S(1)}, bf16[896,256]{1,0:T(8,128)(2,1)}, u32[]{:S(2)}, u32[]{:S(2)}) collective-permute-start(bf16[896,256]{1,0:T(8,128)(2,1)S(1)} %get-tuple-element.49), channel_id=1, source_target_pairs={{0,1},{1,0},{2,3},{3,2},{4,5},{5,4},{6,7},{7,6},{8,9},{9,8},{10,11... | collective-permute-start | bytes 1376264 | tf_op jit(solution)/shard_map/ppermute | solution.py:276
  32.1 23.8 %collective-permute-start.15 = (bf16[512,256]{1,0:T(8,128)(2,1)S(1)}, bf16[512,256]{1,0:T(8,128)(2,1)S(1)}, u32[]{:S(2)}, u32[]{:S(2)}) collective-permute-start(bf16[512,256]{1,0:T(8,128)(2,1)S(1)} %broadcast_select_fusion.1.refs_17_), channel_id=1, source_target_pairs={{0,8},{8,0},{16,24},{24,16},{1,9},{9,1},{17,25},{25,17},{2,10},{10... | collective-permute-start | bytes 786440 | tf_op jit(solution)/shard_map/ppermute | solution.py:284
  33.1 23.3 %collective-permute-start.16 = (bf16[512,256]{1,0:T(8,128)(2,1)S(1)}, bf16[512,256]{1,0:T(8,128)(2,1)}, u32[]{:S(2)}, u32[]{:S(2)}) collective-permute-start(bf16[512,256]{1,0:T(8,128)(2,1)S(1)} %broadcast_select_fusion.1.refs_17_), channel_id=1, source_target_pairs={{0,16},{8,24},{16,0},{24,8},{1,17},{9,25},{17,1},{25,9},{2,18},{10... | collective-permute-start | bytes 786440 | tf_op jit(solution)/shard_map/ppermute | solution.py:284
  53.8 2.7 %collective-permute-start.10 = (bf16[512,256]{1,0:T(8,128)(2,1)S(1)}, bf16[512,256]{1,0:T(8,128)(2,1)S(1)}, u32[]{:S(2)}, u32[]{:S(2)}) collective-permute-start(bf16[512,256]{1,0:T(8,128)(2,1)S(1)} %collective-permute-done.9), channel_id=1, source_target_pairs={{4,6},{5,7},{12,14},{13,15},{20,22},{21,23},{28,30},{29,31}} | collective-permute-start | bytes 786440 | tf_op jit(solution)/shard_map/ppermute | solution.py:270
  54.5 15.3 %collective-permute-start.18 = (bf16[512,256]{1,0:T(8,128)(2,1)S(1)}, bf16[512,256]{1,0:T(8,128)(2,1)S(1)}, u32[]{:S(2)}, u32[]{:S(2)}) collective-permute-start(bf16[512,256]{1,0:T(8,128)(2,1)S(1)} %collective-permute-done.14), channel_id=1, source_target_pairs={{2,0},{3,1},{10,8},{11,9},{18,16},{19,17},{26,24},{27,25}} | collective-permute-start | bytes 786440 | tf_op jit(solution)/shard_map/ppermute | solution.py:271
  55.8 17.2 %collective-permute-start.4 = (bf16[896,256]{1,0:T(8,128)(2,1)}, bf16[896,256]{1,0:T(8,128)(2,1)S(1)}, u32[]{:S(2)}, u32[]{:S(2)}) collective-permute-start(bf16[896,256]{1,0:T(8,128)(2,1)} %collective-permute-done.refs_1_), channel_id=1, source_target_pairs={{0,1},{1,0},{2,3},{3,2},{4,5},{5,4},{6,7},{7,6},{8,9},{9,8},{10,11... | collective-permute-start | bytes 1376264 | tf_op jit(solution)/shard_map/ppermute | solution.py:276
  55.9 17.5 %collective-permute-start.5 = (bf16[896,256]{1,0:T(8,128)(2,1)}, bf16[896,256]{1,0:T(8,128)(2,1)}, u32[]{:S(2)}, u32[]{:S(2)}) collective-permute-start(bf16[896,256]{1,0:T(8,128)(2,1)} %collective-permute-done.1.refs_2_), channel_id=1, source_target_pairs={{0,1},{1,0},{2,3},{3,2},{4,5},{5,4},{6,7},{7,6},{8,9},{9,8},{10,11... | collective-permute-start | bytes 1376264 | tf_op jit(solution)/shard_map/ppermute | solution.py:276
  56.4 18.6 %collective-permute-start.6 = (bf16[896,256]{1,0:T(8,128)(2,1)}, bf16[896,256]{1,0:T(8,128)(2,1)}, u32[]{:S(2)}, u32[]{:S(2)}) collective-permute-start(bf16[896,256]{1,0:T(8,128)(2,1)} %collective-permute-done.2.refs_3_), channel_id=1, source_target_pairs={{0,1},{1,0},{2,3},{3,2},{4,5},{5,4},{6,7},{7,6},{8,9},{9,8},{10,11... | collective-permute-start | bytes 1376264 | tf_op jit(solution)/shard_map/ppermute | solution.py:276
  56.5 14.9 %collective-permute-start.17 = (bf16[512,256]{1,0:T(8,128)(2,1)S(1)}, bf16[512,256]{1,0:T(8,128)(2,1)S(1)}, u32[]{:S(2)}, u32[]{:S(2)}) collective-permute-start(bf16[512,256]{1,0:T(8,128)(2,1)S(1)} %broadcast_select_fusion.1.refs_17_), channel_id=1, source_target_pairs={{0,24},{8,16},{16,8},{24,0},{1,25},{9,17},{17,9},{25,1},{2,26},{10... | collective-permute-start | bytes 786440 | tf_op jit(solution)/shard_map/ppermute | solution.py:284
  69.8 9.2 %collective-permute-start.11 = (bf16[512,256]{1,0:T(8,128)(2,1)S(1)}, bf16[512,256]{1,0:T(8,128)(2,1)S(1)}, u32[]{:S(2)}, u32[]{:S(2)}) collective-permute-start(bf16[512,256]{1,0:T(8,128)(2,1)S(1)} %broadcast_select_fusion.2.refs_13_), channel_id=1, source_target_pairs={{0,8},{8,0},{16,24},{24,16},{1,9},{9,1},{17,25},{25,17},{2,10},{10... | collective-permute-start | bytes 786440 | tf_op jit(solution)/shard_map/ppermute | solution.py:284
  71.4 14.9 %collective-permute-start.12 = (bf16[512,256]{1,0:T(8,128)(2,1)S(1)}, bf16[512,256]{1,0:T(8,128)(2,1)S(1)}, u32[]{:S(2)}, u32[]{:S(2)}) collective-permute-start(bf16[512,256]{1,0:T(8,128)(2,1)S(1)} %broadcast_select_fusion.2.refs_13_), channel_id=1, source_target_pairs={{0,16},{8,24},{16,0},{24,8},{1,17},{9,25},{17,1},{25,9},{2,18},{10... | collective-permute-start | bytes 786440 | tf_op jit(solution)/shard_map/ppermute | solution.py:284
  73.0 13.3 %collective-permute-start.13 = (bf16[512,256]{1,0:T(8,128)(2,1)S(1)}, bf16[512,256]{1,0:T(8,128)(2,1)S(1)}, u32[]{:S(2)}, u32[]{:S(2)}) collective-permute-start(bf16[512,256]{1,0:T(8,128)(2,1)S(1)} %broadcast_select_fusion.2.refs_13_), channel_id=1, source_target_pairs={{0,24},{8,16},{16,8},{24,0},{1,25},{9,17},{17,9},{25,1},{2,26},{10... | collective-permute-start | bytes 786440 | tf_op jit(solution)/shard_map/ppermute | solution.py:284
  73.5 15.6 %collective-permute-start.19 = (bf16[512,256]{1,0:T(8,128)(2,1)S(1)}, bf16[512,256]{1,0:T(8,128)(2,1)S(1)}, u32[]{:S(2)}, u32[]{:S(2)}) collective-permute-start(bf16[512,256]{1,0:T(8,128)(2,1)S(1)} %broadcast_select_fusion.refs_21_), channel_id=1, source_target_pairs={{0,8},{8,0},{16,24},{24,16},{1,9},{9,1},{17,25},{25,17},{2,10},{10... | collective-permute-start | bytes 786440 | tf_op jit(solution)/shard_map/ppermute | solution.py:284
  75.0 18.2 %collective-permute-start.20 = (bf16[512,256]{1,0:T(8,128)(2,1)S(1)}, bf16[512,256]{1,0:T(8,128)(2,1)S(1)}, u32[]{:S(2)}, u32[]{:S(2)}) collective-permute-start(bf16[512,256]{1,0:T(8,128)(2,1)S(1)} %broadcast_select_fusion.refs_21_), channel_id=1, source_target_pairs={{0,16},{8,24},{16,0},{24,8},{1,17},{9,25},{17,1},{25,9},{2,18},{10... | collective-permute-start | bytes 786440 | tf_op jit(solution)/shard_map/ppermute | solution.py:284
  79.1 14.1 %collective-permute-start.21 = (bf16[512,256]{1,0:T(8,128)(2,1)S(1)}, bf16[512,256]{1,0:T(8,128)(2,1)}, u32[]{:S(2)}, u32[]{:S(2)}) collective-permute-start(bf16[512,256]{1,0:T(8,128)(2,1)S(1)} %broadcast_select_fusion.refs_21_), channel_id=1, source_target_pairs={{0,24},{8,16},{16,8},{24,0},{1,25},{9,17},{17,9},{25,1},{2,26},{10... | collective-permute-start | bytes 786440 | tf_op jit(solution)/shard_map/ppermute | solution.py:284
  112.5 23.2 %collective-permute-start.22 = (bf16[2,160,128]{2,1,0:T(8,128)(2,1)}, bf16[2,160,128]{2,1,0:T(8,128)(2,1)S(1)}, u32[]{:S(2)}, u32[]{:S(2)}) collective-permute-start(bf16[2,160,128]{2,1,0:T(8,128)(2,1)} %get-tuple-element.28), channel_id=1, source_target_pairs={{0,2},{2,4},{4,6},{6,0},{1,3},{3,5},{5,7},{7,1},{8,10},{10,12},{12... | collective-permute-start | bytes 245768 | tf_op jit(solution)/shard_map/ppermute | solution.py:357
  119.9 15.9 %collective-permute-start.23 = (bf16[2,160,128]{2,1,0:T(8,128)(2,1)}, bf16[2,160,128]{2,1,0:T(8,128)(2,1)S(1)}, u32[]{:S(2)}, u32[]{:S(2)}) collective-permute-start(bf16[2,160,128]{2,1,0:T(8,128)(2,1)} %get-tuple-element.29), channel_id=1, source_target_pairs={{0,4},{2,6},{4,0},{6,2},{1,5},{3,7},{5,1},{7,3},{8,12},{10,14},{12... | collective-permute-start | bytes 245768 | tf_op jit(solution)/shard_map/ppermute | solution.py:357
  124.9 10.9 %collective-permute-start.24 = (bf16[2,160,128]{2,1,0:T(8,128)(2,1)}, bf16[2,160,128]{2,1,0:T(8,128)(2,1)S(1)}, u32[]{:S(2)}, u32[]{:S(2)}) collective-permute-start(bf16[2,160,128]{2,1,0:T(8,128)(2,1)} %get-tuple-element.30), channel_id=1, source_target_pairs={{0,6},{2,0},{4,2},{6,4},{1,7},{3,1},{5,3},{7,5},{8,14},{10,8},{12,... | collective-permute-start | bytes 245768 | tf_op jit(solution)/shard_map/ppermute | solution.py:357
  135.8 4.5 %collective-permute-start.25 = (bf16[2,160,128]{2,1,0:T(8,128)(2,1)S(1)}, bf16[2,160,128]{2,1,0:T(8,128)(2,1)S(1)}, u32[]{:S(2)}, u32[]{:S(2)}) collective-permute-start(bf16[2,160,128]{2,1,0:T(8,128)(2,1)S(1)} %add_convert_fusion.refs_4_), channel_id=1, source_target_pairs={{0,8},{8,0},{16,24},{24,16},{1,9},{9,1},{17,25},{25,17},{2,10},{10... | collective-permute-start | bytes 245768 | tf_op jit(solution)/shard_map/ppermute | solution.py:361
  137.4 4.4 %collective-permute-start.26 = (bf16[2,160,128]{2,1,0:T(8,128)(2,1)S(1)}, bf16[2,160,128]{2,1,0:T(8,128)(2,1)S(1)}, u32[]{:S(2)}, u32[]{:S(2)}) collective-permute-start(bf16[2,160,128]{2,1,0:T(8,128)(2,1)S(1)} %add_convert_fusion.refs_4_), channel_id=1, source_target_pairs={{0,16},{8,24},{16,0},{24,8},{1,17},{9,25},{17,1},{25,9},{2,18},{10... | collective-permute-start | bytes 245768 | tf_op jit(solution)/shard_map/ppermute | solution.py:361
  138.9 5.3 %collective-permute-start.27 = (bf16[2,160,128]{2,1,0:T(8,128)(2,1)S(1)}, bf16[2,160,128]{2,1,0:T(8,128)(2,1)S(1)}, u32[]{:S(2)}, u32[]{:S(2)}) collective-permute-start(bf16[2,160,128]{2,1,0:T(8,128)(2,1)S(1)} %add_convert_fusion.refs_4_), channel_id=1, source_target_pairs={{0,24},{8,16},{16,8},{24,0},{1,25},{9,17},{17,9},{25,1},{2,26},{10... | collective-permute-start | bytes 245768 | tf_op jit(solution)/shard_map/ppermute | solution.py:361
  147.0 12.1 %collective-permute-start.28 = (bf16[2,160,128]{2,1,0:T(8,128)(2,1)}, bf16[2,160,128]{2,1,0:T(8,128)(2,1)S(1)}, u32[]{:S(2)}, u32[]{:S(2)}) collective-permute-start(bf16[2,160,128]{2,1,0:T(8,128)(2,1)} %get-tuple-element.46), channel_id=1, source_target_pairs={{0,6},{2,0},{4,2},{6,4},{1,7},{3,1},{5,3},{7,5},{8,14},{10,8},{12,... | collective-permute-start | bytes 245768 | tf_op jit(solution)/shard_map/ppermute | solution.py:370
  147.3 11.8 %collective-permute-start.29 = (bf16[2,160,128]{2,1,0:T(8,128)(2,1)}, bf16[2,160,128]{2,1,0:T(8,128)(2,1)S(1)}, u32[]{:S(2)}, u32[]{:S(2)}) collective-permute-start(bf16[2,160,128]{2,1,0:T(8,128)(2,1)} %get-tuple-element.47), channel_id=1, source_target_pairs={{0,4},{2,6},{4,0},{6,2},{1,5},{3,7},{5,1},{7,3},{8,12},{10,14},{12... | collective-permute-start | bytes 245768 | tf_op jit(solution)/shard_map/ppermute | solution.py:370
  149.4 9.7 %collective-permute-start.30 = (bf16[2,160,128]{2,1,0:T(8,128)(2,1)}, bf16[2,160,128]{2,1,0:T(8,128)(2,1)S(1)}, u32[]{:S(2)}, u32[]{:S(2)}) collective-permute-start(bf16[2,160,128]{2,1,0:T(8,128)(2,1)} %get-tuple-element.48), channel_id=1, source_target_pairs={{0,2},{2,4},{4,6},{6,0},{1,3},{3,5},{5,7},{7,1},{8,10},{10,12},{12... | collective-permute-start | bytes 245768 | tf_op jit(solution)/shard_map/ppermute | solution.py:370
  163.1 3.5 %collective-permute-start.31 = (bf16[448,1024]{1,0:T(8,128)(2,1)}, bf16[448,1024]{1,0:T(8,128)(2,1)S(1)}, u32[]{:S(2)}, u32[]{:S(2)}) collective-permute-start(bf16[448,1024]{1,0:T(8,128)(2,1)} %shard_map.114), channel_id=1, source_target_pairs={{0,1},{1,0},{2,3},{3,2},{4,5},{5,4},{6,7},{7,6},{8,9},{9,8},{10,11... | collective-permute-start | bytes 2752520 | tf_op jit(solution)/shard_map/ppermute | solution.py:389
  (24 other events, 348.6 us)

commit v4 on v2

--- a/solution.py
+++ b/solution.py
@@ -59,41 +59,35 @@
     return np.stack([every[places].reshape(-1, LANES) for places in own])
 
 
-def project_kernel(
-    at_ref,
-    per_group,
-    counts,
-    mine_ref,
-    other_ref,
-    wq_ref,
-    wk_ref,
-    table_ref,
-    bias_ref,
-    *rest,
-):
-    n_weights = sum(counts)
-    weights = rest[:n_weights]
-    q_ref, k_ref, v_ref, early_ref, total_ref, row_ref, w_ref, phi_ref, sems = rest[n_weights:]
+def project_kernel(at_ref, per_group, layers, n_weights, gathered, *refs):
+    mine, other = refs[:layers], refs[layers : 2 * layers]
+    wq_ref, wk_ref, table_ref, bias_ref = refs[2 * layers : 2 * layers + 4]
+    weights = refs[2 * layers + 4 : 2 * layers + 4 + n_weights]
+    q_ref, k_ref, v_ref, early_ref, total_ref, row_ref, w_ref, phi_ref, sems = refs[2 * layers + 4 + n_weights :]
     core, layer, slab = at_ref[0], at_ref[1], at_ref[2]
-    layers, both, width = mine_ref.shape
+    both, width = other[0].shape
     rows = both // 2
-    copies = []
-    place = 0
-    for d, count in enumerate(counts):
-        for m in range(count):
-            source = weights[place]
-            part = source.shape[0]
-            start = 0 if count == 1 else pl.multiple_of((slab ^ m) * part, part)
-            copy = pltpu.make_async_copy(source, w_ref.at[d, pl.ds(start, part)], sems.at[place])
-            copy.start()
-            copies.append((d, copy))
-            place += 1
-
-    for z in range(layers):
+    part = weights[1].shape[-2]
+    copies = [pltpu.make_async_copy(weights[0], w_ref.at[0], sems.at[0])]
+    slots = [0]
+    for d in range(1, layers):
+        for m in range(w_ref.shape[1] // part):
+            if gathered:
+                source, start = weights[1].at[m, d - 1], m * part
+            else:
+                source, start = weights[1 + m].at[d - 1], pl.multiple_of((slab ^ m) * part, part)
+            to = w_ref.at[d, pl.ds(start, part)]
+            copies.append(pltpu.make_async_copy(source, to, sems.at[len(copies)]))
+            slots.append(d)
+    for copy in copies:
+        copy.start()
+
+    for d in range(layers):
+        z = lax.rem(layer + layers - d, layers)
         here = pl.multiple_of((2 * z + core) * width, width)
         there = pl.multiple_of((2 * z + 1 - core) * width, width)
-        row_ref[:, pl.ds(here, width)] = mine_ref[z]
-        row_ref[:, pl.ds(there, width)] = other_ref[z]
+        row_ref[:, pl.ds(here, width)] = mine[d][0] if d == 0 else mine[d][...]
+        row_ref[:, pl.ds(there, width)] = other[d][...]
     q = dot(row_ref[...], wq_ref[...]).astype(BF16)
     k = dot(row_ref[...], wk_ref[...]).astype(BF16)
     half = table_ref.shape[1] // 2
@@ -110,10 +104,11 @@
 
     block = v_ref.shape[2] // layers
     for d in range(layers):
-        for slot, copy in copies:
+        for slot, copy in zip(slots, copies):
             if slot == d:
                 copy.wait()
         z = lax.rem(layer + d, layers)
+        first = []
         for chunk in range(2):
             value = dot(row_ref[chunk * rows : (chunk + 1) * rows, :], w_ref[d]).astype(BF16)
             v_ref[chunk, :, pl.ds(pl.multiple_of(z * block, block), block)] = value
@@ -123,10 +118,9 @@
                 state = dot(phi, value[:, i * HEAD_DIM : (i + 1) * HEAD_DIM])
                 if chunk == 0:
                     early_ref[head] = state.astype(BF16)
-                    first = state if i == 0 else jnp.concatenate([first, state], axis=0)
+                    first.append(state)
                 else:
-                    total = first[i * PACKED : (i + 1) * PACKED] + state
-                    total_ref[head] = total.astype(BF16)
+                    total_ref[head] = (first[i] + state).astype(BF16)
 
 
 def local_kernel(
@@ -162,17 +156,18 @@
             num_ref[0, :, columns] += dot(phi_ref[0, i], early_ref[i])
 
 
-def prefix_kernel(slab_ref, line_ref, totals_ref, out_ref):
+def prefix_kernel(at_ref, line_ref, *refs):
+    totals, out_ref = refs[:-1], refs[-1]
+    slab = at_ref[2]
     run = jnp.zeros(line_ref.shape[1:], F32)
-    for s in range(totals_ref.shape[0]):
-        keep = jnp.where(s < slab_ref[0], 1.0, 0.0)
-        run = run + totals_ref[s].astype(F32) * keep
-    for c in range(line_ref.shape[0]):
-        out_ref[c] = run.astype(BF16)
-        run = run + line_ref[c].astype(F32)
-
-
-def hidden_kernel(chunk_ref, num_a, num_b, phi_a, phi_b, state_ref, gain_ref, out_ref):
+    for m, total in enumerate(totals, 1):
+        run = run + total[...].astype(F32) * jnp.where((slab ^ m) < slab, 1.0, 0.0)
+    for z in range(line_ref.shape[0]):
+        out_ref[z] = run.astype(BF16)
+        run = run + line_ref[z].astype(F32)
+
+
+def hidden_kernel(at_ref, num_a, num_b, phi_a, phi_b, state_ref, gain_ref, out_ref):
     held = phi_a.shape[1]
     for i in range(2 * held):
         columns = slice(i * HEAD_DIM, (i + 1) * HEAD_DIM)
@@ -184,23 +179,28 @@
         out_ref[:, columns] = hidden.astype(BF16)
 
 
-def output_kernel(core_ref, layers, mine_ref, other_ref, w_ref, out_ref, hidden_ref):
-    core = core_ref[0]
-
-    @pl.when(pl.program_id(0) == 0)
-    def _():
-        block = mine_ref.shape[1] // layers
-        for z in range(layers):
-            columns = slice(z * block, (z + 1) * block)
-            here = pl.multiple_of((2 * z + core) * block, block)
-            there = pl.multiple_of((2 * z + 1 - core) * block, block)
-            hidden_ref[:, pl.ds(here, block)] = mine_ref[:, columns]
-            hidden_ref[:, pl.ds(there, block)] = other_ref[:, columns]
-
-    width = out_ref.shape[2]
-    for c in range(out_ref.shape[0]):
-        part = dot(hidden_ref[...], w_ref[:, c * width : (c + 1) * width])
-        out_ref[c] = part.astype(BF16)
+def output_kernel(at_ref, *refs):
+    chunks, w_mine, w_other, out_ref = refs[:-3], refs[-3], refs[-2], refs[-1]
+    rows, depth = chunks[0].shape
+    width = out_ref.shape[1]
+    for i in range(len(chunks) // 2):
+        part = dot(chunks[2 * i][...], w_mine[...].reshape(depth, width))
+        part = part + dot(chunks[2 * i + 1][...], w_other[...].reshape(depth, width))
+        out_ref[i * rows : (i + 1) * rows, :] = part.astype(BF16)
+
+
+def place_kernel(at_ref, *refs):
+    pieces, out_ref, sems = refs[:-2], refs[-2], refs[-1]
+    layers = len(pieces)
+    copies = []
+    for d, piece in enumerate(pieces):
+        z = lax.rem(at_ref[1] + layers - d, layers)
+        to = out_ref.at[pl.ds(pl.multiple_of(z * piece.shape[0], piece.shape[0]), piece.shape[0])]
+        copies.append(pltpu.make_async_copy(piece, to, sems.at[d]))
+    for copy in copies:
+        copy.start()
+    for copy in copies:
+        copy.wait()
 
 
 def whole(shape):
@@ -211,7 +211,7 @@
     return pltpu.CompilerParams(vmem_limit_bytes=mib * MIB)
 
 
-def call(kernel, scalar, grid, in_specs, out_specs, out_shape, args, flops, scratch=(), mib=60):
+def call(kernel, scalar, grid, in_specs, out_specs, out_shape, args, flops, scratch=()):
     return pl.pallas_call(
         kernel,
         grid_spec=pltpu.PrefetchScalarGridSpec(
@@ -222,7 +222,7 @@
             scratch_shapes=list(scratch),
         ),
         out_shape=out_shape,
-        compiler_params=params(mib),
+        compiler_params=params(60),
         cost_estimate=pl.CostEstimate(flops=flops, bytes_accessed=12 * MIB, transcendentals=0),
     )(scalar, *args)
 
@@ -255,36 +255,37 @@
     gain_mine = lax.dynamic_index_in_dim(gain.reshape(layers, 2, value_width), core, 1, False)
     gain_mine = gain_mine.reshape(1, layers * value_width)
 
-    mine = lax.all_to_all(
-        tokens.reshape(layers, 2 * rows, width), "z", split_axis=0, concat_axis=0, tiled=True
-    )
-    other = lax.ppermute(mine, "core", swap)
+    flip = lambda m: [(s, s ^ m) for s in range(slabs)]
+    turn = lambda d: [(z, (z + d) % layers) for z in range(layers)]
+    anywhere = pl.BlockSpec(memory_space=pl.ANY)
+    vmem = pl.BlockSpec(memory_space=pltpu.VMEM)
+    at = jnp.stack([core, layer, my_slab.astype(jnp.int32)])
 
     value_part = lax.dynamic_slice_in_dim(w_value, my_slab * part, part, 0)
     up, down = {0: value_part}, {0: value_part}
+    blocks = tokens.reshape(layers, 2 * rows, width)
+    sent = [lax.dynamic_index_in_dim(blocks, lax.rem(layer + d, layers), 0, False) for d in range(layers)]
     for k in range(1, layers):
         up[k] = lax.ppermute(up[k - 1], "z", [(z, z + 1) for z in range(k - 1, layers - 1)])
         down[k] = lax.ppermute(down[k - 1], "z", [(z, z - 1) for z in range(1, layers - k + 1)])
-    weights, counts = [w_value], [1]
-    for d in range(1, layers):
-        slot = jnp.where(layer + d < layers, down[d], up[layers - d])
-        if slabs == 4:
-            weights.append(slot)
-            for m in range(1, slabs):
-                weights.append(lax.ppermute(slot, "seq", [(s, s ^ m) for s in range(slabs)]))
-            counts.append(slabs)
-        else:
-            weights.append(lax.all_gather(slot, "seq", axis=0, tiled=True))
-            counts.append(1)
-
-    anywhere = pl.BlockSpec(memory_space=pl.ANY)
+        if k == layers - 2:
+            up[k], down[k], sent = lax.optimization_barrier((up[k], down[k], sent))
+    slots = jnp.stack([jnp.where(layer + d < layers, down[d], up[layers - d]) for d in range(1, layers)])
+    mine = [sent[0]] + [lax.ppermute(sent[d], "z", turn(d)) for d in range(1, layers)]
+    if slabs == 4:
+        weights = [w_value, slots] + [lax.ppermute(slots, "seq", flip(m)) for m in range(1, slabs)]
+    else:
+        weights = [w_value, lax.all_gather(slots, "seq", axis=0, tiled=False)]
+    mine, weights[2:] = lax.optimization_barrier((mine, weights[2:]))
+    other = [lax.ppermute(piece, "core", swap) for piece in mine]
+
     query, key, value, early, total = call(
-        lambda at_ref, *refs: project_kernel(at_ref, per_group, counts, *refs),
-        jnp.stack([core, layer, my_slab.astype(jnp.int32)]),
+        lambda at_ref, *refs: project_kernel(at_ref, per_group, layers, len(weights), slabs != 4, *refs),
+        at,
         (1,),
-        [
-            whole((layers, 2 * rows, width)),
-            whole((layers, 2 * rows, width)),
+        [pl.BlockSpec((1, 2 * rows, width), lambda i, at: (at[1], 0, 0))]
+        + [whole((2 * rows, width))] * (2 * layers - 1)
+        + [
             whole((model, narrow)),
             whole((model, narrow)),
             pl.BlockSpec((1,) + key_table.shape[1:], lambda i, at: (at[0], 0, 0)),
@@ -305,13 +306,13 @@
             jax.ShapeDtypeStruct((heads, PACKED, HEAD_DIM), BF16),
             jax.ShapeDtypeStruct((heads, PACKED, HEAD_DIM), BF16),
         ],
-        (mine, other, w_query, w_key, key_table, key_bias, *weights),
+        (blocks, *mine[1:], *other, w_query, w_key, key_table, key_bias, *weights),
         4 * rows * model * (model // 2 + 2 * narrow),
         [
             pltpu.VMEM((2 * rows, model), BF16),
             pltpu.VMEM((layers, model, value_width), BF16),
             pltpu.VMEM((2, heads * PACKED, rows), BF16),
-            pltpu.SemaphoreType.DMA((len(weights),)),
+            pltpu.SemaphoreType.DMA((1 + (layers - 1) * slabs,)),
         ],
     )
 
@@ -319,7 +320,7 @@
         offset = part_of_heads * (layers // 2)
         return call(
             lambda core_ref, *refs: local_kernel(core_ref, per_group, offset, *refs),
-            which,
+            at,
             (2, layers // 2),
             [
                 pl.BlockSpec((1, rows, narrow), lambda c, i, _: (c, 0, 0)),
@@ -347,25 +348,24 @@
     num_a, phi_a = local(0)
     line, num_a, phi_a = lax.optimization_barrier((line, num_a, phi_a))
     slab_total = jnp.sum(line.astype(F32), axis=0).astype(BF16)
-    totals = lax.all_gather(slab_total, "seq", axis=0, tiled=False)
-    vmem = pl.BlockSpec(memory_space=pltpu.VMEM)
+    totals = [lax.ppermute(slab_total, "seq", flip(m)) for m in range(1, slabs)]
     prefix = pl.pallas_call(
         prefix_kernel,
-        in_specs=[pl.BlockSpec(memory_space=pltpu.SMEM), vmem, vmem],
+        in_specs=[pl.BlockSpec(memory_space=pltpu.SMEM)] + [vmem] * slabs,
         out_specs=vmem,
         out_shape=jax.ShapeDtypeStruct(line.shape, BF16),
-    )(my_slab.reshape(1), line, totals)
+    )(at, line, *totals)
     prefix = lax.all_to_all(prefix, "z", split_axis=0, concat_axis=0, tiled=True)
     prefix = prefix.reshape(heads, PACKED, HEAD_DIM)
     num_b, phi_b = local(1)
 
     def hidden(chunk):
         some = rows // 2
-        numbers = pl.BlockSpec((1, some, heads * HEAD_DIM // 2), lambda i, c: (c[0], i, 0))
-        features = pl.BlockSpec((1, heads // 2, some, PACKED), lambda i, c: (c[0], 0, i, 0))
+        numbers = pl.BlockSpec((1, some, heads * HEAD_DIM // 2), lambda i, _: (chunk, i, 0))
+        features = pl.BlockSpec((1, heads // 2, some, PACKED), lambda i, _: (chunk, 0, i, 0))
         return call(
             hidden_kernel,
-            chunk.reshape(1),
+            at,
             (2,),
             [
                 numbers,
@@ -375,33 +375,50 @@
                 whole((heads, PACKED, HEAD_DIM)),
                 whole((1, heads * HEAD_DIM)),
             ],
-            pl.BlockSpec((some, heads * HEAD_DIM), lambda i, c: (i, 0)),
+            pl.BlockSpec((some, heads * HEAD_DIM), lambda i, _: (i, 0)),
             jax.ShapeDtypeStruct((rows, heads * HEAD_DIM), BF16),
             (num_a, num_b, phi_a, phi_b, prefix, gain_mine),
             rows * heads * HEAD_DIM * 600,
         )
 
-    received = lax.ppermute(hidden(1 - core), "core", swap)
-    kept = hidden(core)
-    steps = 4
-    per_out = groups // steps
-    out = call(
-        lambda core_ref, *refs: output_kernel(core_ref, layers, *refs),
-        which,
-        (steps,),
-        [
-            whole((rows, heads * HEAD_DIM)),
-            whole((rows, heads * HEAD_DIM)),
-            pl.BlockSpec((model, per_out * width), lambda i, _: (0, i)),
-        ],
-        pl.BlockSpec((per_out, rows, width), lambda i, _: (i, 0, 0)),
-        jax.ShapeDtypeStruct((groups, rows, width), BF16),
-        (kept, received, w_out),
-        2 * rows * model * model,
-        [pltpu.VMEM((rows, model), BF16)],
+    w_rows = w_out.reshape(layers, 2, value_width, model)
+
+    def project_out(d):
+        columns = lambda at: 2 * lax.rem(at[1] + d, layers) + at[0]
+        return call(
+            output_kernel,
+            at,
+            (1,),
+            [whole((rows, heads * HEAD_DIM))] * len(chunks)
+            + [
+                pl.BlockSpec((layers, 1, value_width, width), lambda i, at: (0, at[0], 0, columns(at))),
+                pl.BlockSpec((layers, 1, value_width, width), lambda i, at: (0, 1 - at[0], 0, columns(at))),
+            ],
+            whole((2 * rows, width)),
+            jax.ShapeDtypeStruct((2 * rows, width), BF16),
+            (*chunks, w_rows, w_rows),
+            4 * rows * model * width,
+        )
+
+    chunks = []
+    for chunk in range(2):
+        kept = hidden(chunk)
+        chunks += [kept, lax.ppermute(kept, "core", swap)]
+    pieces = {}
+    for d in list(range(1, layers)) + [0]:
+        part_out = project_out(d)
+        pieces[d] = lax.ppermute(part_out, "z", turn(d)) if d else part_out
+    return call(
+        place_kernel,
+        at,
+        (1,),
+        [anywhere] * layers,
+        anywhere,
+        jax.ShapeDtypeStruct((groups * rows, width), BF16),
+        tuple(pieces[d] for d in range(layers)),
+        0,
+        [pltpu.SemaphoreType.DMA((layers,))],
     )
-    out = lax.all_to_all(out, ("z", "core"), split_axis=0, concat_axis=0, tiled=True)
-    return out.reshape(groups * rows, width)
 
 
 def solution(mesh):

time: 236 us -> 263 us (1.11)
  blocking collectives: 107 us -> 0 us
  Pallas kernels: 53.8 us -> 125 us
  waiting for transfers between devices: 36.6 us -> 92.5 us
  starting transfers between devices: 30.5 us -> 35.9 us
  local copies, waits for them, and re-layouts: 4.67 us -> 7.42 us
    all_to_all x2 -> x0, blocking collectives: 97.5 us -> none  [the longest x1 48.9 us: per_device(): lax.all_to_all(tokens.reshape(layers, 2 * rows, width), 'z', split_axis=0...]
    pallas_call x6 -> x10, Pallas kernels: 51.9 us -> 123 us  [call(): pl.pallas_call(kernel, grid_spec=pltpu.PrefetchScalarGridSpec(num_scalar_...]
    ppermute x11 -> x18, waiting for transfers between devices: 20.6 us -> 64.7 us  [the longest x3 24.1 us: per_device(): pieces[d] = lax.ppermute(part_out, 'z', turn(d)) if d else part_out]
    all_gather x1 -> x0, blocking collectives: 9.86 us -> none  [per_device(): totals = lax.all_gather(slab_total, 'seq', axis=0, tiled=False)]
    ppermute x11 -> x18, starting transfers between devices: 11.4 us -> 18.2 us  [the longest x3 4.95 us: per_device(): pieces[d] = lax.ppermute(part_out, 'z', turn(d)) if d else part_out]
    ppermute x3, waiting for transfers between devices: 15.9 us -> 22.6 us  [per_device(): lax.ppermute(down[k - 1], 'z', [(z, z - 1) for z in range(1, layers - k +...]
    ppermute x3, waiting for transfers between devices: 0.01 us -> 4.24 us  [per_device(): lax.ppermute(up[k - 1], 'z', [(z, z + 1) for z in range(k - 1, layers - 1)])]
  transfers between devices with their start and end apart: 19 -> 26, of which waited for: 11 -> 16; matrix products, arithmetic and copies ran while one was open for 1% -> 1% of each run, Pallas kernels for 9% -> 13%
where the time goes in v4:
time: 263 us; the launch traced here: 262 us
  Pallas kernels  125 us (48%)
  waiting for transfers between devices  92.5 us (35%)
  starting transfers between devices  35.9 us (14%)
  local copies, waits for them, and re-layouts  7.42 us (3%)
    pallas_call x10, Pallas kernels, call(): pl.pallas_call(kernel, grid_spec=pltpu.PrefetchScalarGridSpec(num_scalar_...  123 us
    ppermute x3, waiting for transfers between devices, per_device(): pieces[d] = lax.ppermute(part_out, 'z', turn(d)) if d else part_out  24.1 us
    ppermute x3, waiting for transfers between devices, per_device(): lax.ppermute(down[k - 1], 'z', [(z, z - 1) for z in range(1, layers - k +...  22.6 us
    ppermute x3, waiting for transfers between devices, per_device(): lax.ppermute(sent[d], 'z', turn(d))  17.6 us
    ppermute x3, waiting for transfers between devices, per_device(): lax.ppermute(slots, 'seq', flip(m))  12.5 us
    ppermute x3, starting transfers between devices, per_device(): lax.ppermute(up[k - 1], 'z', [(z, z + 1) for z in range(k - 1, layers - 1)])  6.29 us
  transfers between devices with their start and end apart: 26, of which 16 were waited for; matrix products, arithmetic and copies ran while one was open for 1% of the time, Pallas kernels for 13%

profile of v4, /device:TPU:0, one launch (start us, length us, event | category | flops | bytes accessed | tf_op | source)
XLA Modules:
  0.0 262.0 jit_solution(12333004100653083999)
XLA Ops:
  1.0 4.9 %collective-permute-start = (bf16[512,256]{1,0:T(8,128)(2,1)S(1)}, bf16[512,256]{1,0:T(8,128)(2,1)S(1)}, u32[]{:S(2)}, u32[]{:S(2)}) collective-permute-start(bf16[512,256]{1,0:T(8,128)(2,1)S(1)} %constant_dynamic-slice_fusion.1), channel_id=1, source_target_pairs={{0,2},{2,4},{4,6},{1,3},{3,5},{5,7},{8,10},{10,12},{12,14},{9,11},... | collective-permute-start | bytes 786440 | tf_op jit(solution)/shard_map/ppermute | solution.py:269
  7.2 4.2 %collective-permute-done = bf16[512,256]{1,0:T(8,128)(2,1)S(1)} collective-permute-done((bf16[512,256]{1,0:T(8,128)(2,1)S(1)}, bf16[512,256]{1,0:T(8,128)(2,1)S(1)}, u32[]{:S(2)}, u32[]{:S(2)}) %collective-permute-start) | collective-permute-done | bytes 262176 | tf_op jit(solution)/shard_map/ppermute | solution.py:269
  12.1 3.5 %collective-permute-done.2 = bf16[512,256]{1,0:T(8,128)(2,1)S(1)} collective-permute-done((bf16[512,256]{1,0:T(8,128)(2,1)S(1)}, bf16[512,256]{1,0:T(8,128)(2,1)S(1)}, u32[]{:S(2)}, u32[]{:S(2)}) %collective-permute-start.2) | collective-permute-done | bytes 262176 | tf_op jit(solution)/shard_map/ppermute | solution.py:270
  16.9 1.6 dynamic-slice_bitcast_fusion
  18.5 6.0 %collective-permute-done.3 = bf16[512,256]{1,0:T(8,128)(2,1)S(1)} collective-permute-done((bf16[512,256]{1,0:T(8,128)(2,1)S(1)}, bf16[512,256]{1,0:T(8,128)(2,1)S(1)}, u32[]{:S(2)}, u32[]{:S(2)}) %collective-permute-start.3) | collective-permute-done | bytes 262176 | tf_op jit(solution)/shard_map/ppermute | solution.py:270
  26.5 2.7 %collective-permute-start.4 = (bf16[896,256]{1,0:T(8,128)(2,1)S(1)}, bf16[896,256]{1,0:T(8,128)(2,1)}, u32[]{:S(2)}, u32[]{:S(2)}) collective-permute-start(bf16[896,256]{1,0:T(8,128)(2,1)S(1)} %get-tuple-element.31), channel_id=1, source_target_pairs={{0,2},{2,4},{4,6},{6,0},{1,3},{3,5},{5,7},{7,1},{8,10},{10,12},{12... | collective-permute-start | bytes 1376264 | tf_op jit(solution)/shard_map/ppermute | solution.py:274
  29.2 13.1 %collective-permute-done.8 = bf16[512,256]{1,0:T(8,128)(2,1)S(1)} collective-permute-done((bf16[512,256]{1,0:T(8,128)(2,1)S(1)}, bf16[512,256]{1,0:T(8,128)(2,1)S(1)}, u32[]{:S(2)}, u32[]{:S(2)}) %collective-permute-start.8) | collective-permute-done | bytes 262176 | tf_op jit(solution)/shard_map/ppermute | solution.py:270
  42.5 1.6 collective-permute-start.10
  46.1 1.9 collective-permute-start.6
  48.0 17.6 %collective-permute-done.5.refs_2_ = bf16[896,256]{1,0:T(8,128)(2,1)} collective-permute-done((bf16[896,256]{1,0:T(8,128)(2,1)S(1)}, bf16[896,256]{1,0:T(8,128)(2,1)}, u32[]{:S(2)}, u32[]{:S(2)}) %collective-permute-start.5) | collective-permute-done | bytes 458784 | tf_op jit(solution)/shard_map/ppermute | solution.py:274
  65.6 11.3 %collective-permute-done.10.refs_15_ = bf16[3,512,256]{2,1,0:T(8,128)(2,1)S(1)} collective-permute-done((bf16[3,512,256]{2,1,0:T(8,128)(2,1)S(1)}, bf16[3,512,256]{2,1,0:T(8,128)(2,1)S(1)}, u32[]{:S(2)}, u32[]{:S(2)}) %collective-permute-start.10) | collective-permute-done | bytes 786464 | tf_op jit(solution)/shard_map/ppermute | solution.py:276
  80.8 1.4 collective-permute-done.14.refs_6_
  82.2 18.8 %shard_map.109 = (bf16[2,448,256]{2,1,0:T(8,128)(2,1)}, bf16[2,448,256]{2,1,0:T(8,128)(2,1)}, bf16[2,448,1024]{2,1,0:T(8,128)(2,1)}, bf16[8,160,128]{2,1,0:T(8,128)(2,1)}, bf16[8,160,128]{2,1,0:T(8,128)(2,1)}) custom-call(s32[3]{0:T(128)} %pad_add_fusion.at_ref.core_ref, bf16[4,896,256]{2,1,0:T(8,128)(2,1)} %bitcast.33, ...), custom_call_target="tpu_custom_call" | custom-call | flops 5637144576 | bytes 12582912 | tf_op jit(solution)/shard_map/pallas_call | solution.py:215
  101.0 3.6 %all-to-all-start = ((bf16[4,2,160,128]{3,2,1,0:T(8,128)(2,1)}), bf16[4,2,160,128]{3,2,1,0:T(8,128)(2,1)S(1)}, u32[]{:S(2)}, u32[]{:S(2)}) async-start(bf16[4,2,160,128]{3,2,1,0:T(8,128)(2,1)} %bitcast.34), calls=%async_computation | async-start | bytes 655360 | tf_op jit(solution)/shard_map/all_to_all | solution.py:347
  104.7 9.6 %shard_map.110 = (f32[2,448,512]{2,1,0:T(8,128)}, bf16[2,4,448,160]{3,2,1,0:T(8,128)(2,1)}) custom-call(s32[3]{0:T(128)} %pad_add_fusion.at_ref.core_ref, bf16[2,448,256]{2,1,0:T(8,128)(2,1)} %get-tuple-element.44.refs_0_, bf16[2,448,256]{2,1,0:T(8,128)(2,1)} %get-tuple-element.45.refs_1_, bf16[2,448,1024]{2,1,0:T(8,128)(2,1)} %get-tuple-element.46.refs_2_, ...), custom_call_target="tpu_custom_call" | custom-call | flops 963379200 | bytes 12582912 | tf_op jit(solution)/shard_map/pallas_call | solution.py:215
  115.3 1.6 collective-permute-start.16
  116.9 1.5 collective-permute-start.17
  120.0 2.2 collective-permute-done.17.refs_1_
  122.2 1.5 collective-permute-done.18.refs_2_
  124.4 1.9 shard_map.112
  126.3 3.9 %all-to-all-start.1 = ((bf16[4,2,160,128]{3,2,1,0:T(8,128)(2,1)}), bf16[4,2,160,128]{3,2,1,0:T(8,128)(2,1)S(1)}, u32[]{:S(2)}, u32[]{:S(2)}) async-start(bf16[4,2,160,128]{3,2,1,0:T(8,128)(2,1)} %shard_map.112), calls=%async_computation.1 | async-start | bytes 655360 | tf_op jit(solution)/shard_map/all_to_all | solution.py:358
  130.8 9.6 %shard_map.111 = (f32[2,448,512]{2,1,0:T(8,128)}, bf16[2,4,448,160]{3,2,1,0:T(8,128)(2,1)}) custom-call(s32[3]{0:T(128)} %pad_add_fusion.at_ref.core_ref, bf16[2,448,256]{2,1,0:T(8,128)(2,1)} %get-tuple-element.44.refs_0_, bf16[2,448,256]{2,1,0:T(8,128)(2,1)} %get-tuple-element.45.refs_1_, bf16[2,448,1024]{2,1,0:T(8,128)(2,1)} %get-tuple-element.46.refs_2_, ...), custom_call_target="tpu_custom_call" | custom-call | flops 963379200 | bytes 12582912 | tf_op jit(solution)/shard_map/pallas_call | solution.py:215
  141.2 4.1 %shard_map.114.refs_2_ = bf16[448,1024]{1,0:T(8,128)(2,1)} custom-call(s32[3]{0:T(128)} %pad_add_fusion.at_ref.core_ref, f32[2,448,512]{2,1,0:T(8,128)} %get-tuple-element.50.num_a, f32[2,448,512]{2,1,0:T(8,128)} %get-tuple-element.51.num_b, bf16[2,4,448,160]{3,2,1,0:T(8,128)(2,1)} %get-tuple-element.52.phi_a, ...), custom_call_target="tpu_custom_call" | custom-call | flops 275251200 | bytes 12582912 | tf_op jit(solution)/shard_map/pallas_call | solution.py:215
  145.2 4.2 %shard_map.113.refs_0_ = bf16[448,1024]{1,0:T(8,128)(2,1)} custom-call(s32[3]{0:T(128)} %pad_add_fusion.at_ref.core_ref, f32[2,448,512]{2,1,0:T(8,128)} %get-tuple-element.50.num_a, f32[2,448,512]{2,1,0:T(8,128)} %get-tuple-element.51.num_b, bf16[2,4,448,160]{3,2,1,0:T(8,128)(2,1)} %get-tuple-element.52.phi_a, ...), custom_call_target="tpu_custom_call" | custom-call | flops 275251200 | bytes 12582912 | tf_op jit(solution)/shard_map/pallas_call | solution.py:215
  149.9 2.5 collective-permute-done.20.refs_3_
  154.3 4.9 %shard_map.118 = bf16[896,256]{1,0:T(8,128)(2,1)} custom-call(s32[3]{0:T(128)} %pad_add_fusion.at_ref.core_ref, bf16[448,1024]{1,0:T(8,128)(2,1)} %shard_map.113.refs_0_, bf16[448,1024]{1,0:T(8,128)(2,1)} %copy-done.2, bf16[448,1024]{1,0:T(8,128)(2,1)} %shard_map.114.refs_2_, bf16[448,1024]{1,0:T(8,128)(2,1)} %copy-done.1, ...), custom_call_target="tpu_custom_call" | custom-call | flops 939524096 | bytes 12582912 | tf_op jit(solution)/shard_map/pallas_call | solution.py:215
  159.2 3.8 %collective-permute-start.23 = (bf16[896,256]{1,0:T(8,128)(2,1)}, bf16[896,256]{1,0:T(8,128)(2,1)S(1)}, u32[]{:S(2)}, u32[]{:S(2)}) collective-permute-start(bf16[896,256]{1,0:T(8,128)(2,1)} %shard_map.118), channel_id=1, source_target_pairs={{0,6},{2,0},{4,2},{6,4},{1,7},{3,1},{5,3},{7,5},{8,14},{10,8},{12,... | collective-permute-start | bytes 1376264 | tf_op jit(solution)/shard_map/ppermute | solution.py:410
  163.0 4.9 %shard_map.117 = bf16[896,256]{1,0:T(8,128)(2,1)} custom-call(s32[3]{0:T(128)} %pad_add_fusion.at_ref.core_ref, bf16[448,1024]{1,0:T(8,128)(2,1)} %shard_map.113.refs_0_, bf16[448,1024]{1,0:T(8,128)(2,1)} %copy-done.2, bf16[448,1024]{1,0:T(8,128)(2,1)} %shard_map.114.refs_2_, bf16[448,1024]{1,0:T(8,128)(2,1)} %copy-done.1, ...), custom_call_target="tpu_custom_call" | custom-call | flops 939524096 | bytes 12582912 | tf_op jit(solution)/shard_map/pallas_call | solution.py:215
  167.9 4.9 %shard_map.116 = bf16[896,256]{1,0:T(8,128)(2,1)} custom-call(s32[3]{0:T(128)} %pad_add_fusion.at_ref.core_ref, bf16[448,1024]{1,0:T(8,128)(2,1)} %shard_map.113.refs_0_, bf16[448,1024]{1,0:T(8,128)(2,1)} %copy-done.2, bf16[448,1024]{1,0:T(8,128)(2,1)} %shard_map.114.refs_2_, bf16[448,1024]{1,0:T(8,128)(2,1)} %copy-done.1, ...), custom_call_target="tpu_custom_call" | custom-call | flops 939524096 | bytes 12582912 | tf_op jit(solution)/shard_map/pallas_call | solution.py:215
  173.9 4.9 %shard_map.115.refs_0_ = bf16[896,256]{1,0:T(8,128)(2,1)} custom-call(s32[3]{0:T(128)} %pad_add_fusion.at_ref.core_ref, bf16[448,1024]{1,0:T(8,128)(2,1)} %shard_map.113.refs_0_, bf16[448,1024]{1,0:T(8,128)(2,1)} %copy-done.2, bf16[448,1024]{1,0:T(8,128)(2,1)} %shard_map.114.refs_2_, bf16[448,1024]{1,0:T(8,128)(2,1)} %copy-done.1, ...), custom_call_target="tpu_custom_call" | custom-call | flops 939524096 | bytes 12582912 | tf_op jit(solution)/shard_map/pallas_call | solution.py:215
  178.8 24.1 %collective-permute-done.22.refs_2_ = bf16[896,256]{1,0:T(8,128)(2,1)S(1)} collective-permute-done((bf16[896,256]{1,0:T(8,128)(2,1)}, bf16[896,256]{1,0:T(8,128)(2,1)S(1)}, u32[]{:S(2)}, u32[]{:S(2)}) %collective-permute-start.22) | collective-permute-done | bytes 458784 | tf_op jit(solution)/shard_map/ppermute | solution.py:410
  204.5 57.4 %shard_map.119 = bf16[3584,256]{1,0:T(8,128)(2,1)} custom-call(s32[3]{0:T(128)} %pad_add_fusion.at_ref.core_ref, bf16[896,256]{1,0:T(8,128)(2,1)} %shard_map.115.refs_0_, bf16[896,256]{1,0:T(8,128)(2,1)} %copy-done.8, bf16[896,256]{1,0:T(8,128)(2,1)} %copy-done.7, bf16[896,256]{1,0:T(8,128)(2,1)} %copy-done.6), custom_call_target="tpu_custom_call" | custom-call | bytes 12582912 | tf_op jit(solution)/shard_map/pallas_call | solution.py:215
  (79 shorter events, 22.0 us)
Async XLA Ops:
  1.0 10.5 %collective-permute-start = (bf16[512,256]{1,0:T(8,128)(2,1)S(1)}, bf16[512,256]{1,0:T(8,128)(2,1)S(1)}, u32[]{:S(2)}, u32[]{:S(2)}) collective-permute-start(bf16[512,256]{1,0:T(8,128)(2,1)S(1)} %constant_dynamic-slice_fusion.1), channel_id=1, source_target_pairs={{0,2},{2,4},{4,6},{1,3},{3,5},{5,7},{8,10},{10,12},{12,14},{9,11},... | collective-permute-start | bytes 786440 | tf_op jit(solution)/shard_map/ppermute | solution.py:269
  5.9 9.7 %collective-permute-start.2 = (bf16[512,256]{1,0:T(8,128)(2,1)S(1)}, bf16[512,256]{1,0:T(8,128)(2,1)S(1)}, u32[]{:S(2)}, u32[]{:S(2)}) collective-permute-start(bf16[512,256]{1,0:T(8,128)(2,1)S(1)} %constant_dynamic-slice_fusion.1), channel_id=1, source_target_pairs={{2,0},{4,2},{6,4},{3,1},{5,3},{7,5},{10,8},{12,10},{14,12},{11,9},... | collective-permute-start | bytes 786440 | tf_op jit(solution)/shard_map/ppermute | solution.py:270
  11.5 7.0 %collective-permute-start.1 = (bf16[512,256]{1,0:T(8,128)(2,1)S(1)}, bf16[512,256]{1,0:T(8,128)(2,1)S(1)}, u32[]{:S(2)}, u32[]{:S(2)}) collective-permute-start(bf16[512,256]{1,0:T(8,128)(2,1)S(1)} %collective-permute-done), channel_id=1, source_target_pairs={{2,4},{4,6},{3,5},{5,7},{10,12},{12,14},{11,13},{13,15},{18,20},{2... | collective-permute-start | bytes 786440 | tf_op jit(solution)/shard_map/ppermute | solution.py:269
  15.6 8.9 %collective-permute-start.3 = (bf16[512,256]{1,0:T(8,128)(2,1)S(1)}, bf16[512,256]{1,0:T(8,128)(2,1)S(1)}, u32[]{:S(2)}, u32[]{:S(2)}) collective-permute-start(bf16[512,256]{1,0:T(8,128)(2,1)S(1)} %collective-permute-done.2), channel_id=1, source_target_pairs={{2,0},{4,2},{3,1},{5,3},{10,8},{12,10},{11,9},{13,11},{18,16},{20,... | collective-permute-start | bytes 786440 | tf_op jit(solution)/shard_map/ppermute | solution.py:270
  24.5 17.8 %collective-permute-start.8 = (bf16[512,256]{1,0:T(8,128)(2,1)S(1)}, bf16[512,256]{1,0:T(8,128)(2,1)S(1)}, u32[]{:S(2)}, u32[]{:S(2)}) collective-permute-start(bf16[512,256]{1,0:T(8,128)(2,1)S(1)} %collective-permute-done.3), channel_id=1, source_target_pairs={{2,0},{3,1},{10,8},{11,9},{18,16},{19,17},{26,24},{27,25}} | collective-permute-start | bytes 786440 | tf_op jit(solution)/shard_map/ppermute | solution.py:270
  25.8 16.6 %collective-permute-start.7 = (bf16[512,256]{1,0:T(8,128)(2,1)S(1)}, bf16[512,256]{1,0:T(8,128)(2,1)S(1)}, u32[]{:S(2)}, u32[]{:S(2)}) collective-permute-start(bf16[512,256]{1,0:T(8,128)(2,1)S(1)} %collective-permute-done.1), channel_id=1, source_target_pairs={{4,6},{5,7},{12,14},{13,15},{20,22},{21,23},{28,30},{29,31}} | collective-permute-start | bytes 786440 | tf_op jit(solution)/shard_map/ppermute | solution.py:269
  26.5 19.6 %collective-permute-start.4 = (bf16[896,256]{1,0:T(8,128)(2,1)S(1)}, bf16[896,256]{1,0:T(8,128)(2,1)}, u32[]{:S(2)}, u32[]{:S(2)}) collective-permute-start(bf16[896,256]{1,0:T(8,128)(2,1)S(1)} %get-tuple-element.31), channel_id=1, source_target_pairs={{0,2},{2,4},{4,6},{6,0},{1,3},{3,5},{5,7},{7,1},{8,10},{10,12},{12... | collective-permute-start | bytes 1376264 | tf_op jit(solution)/shard_map/ppermute | solution.py:274
  42.5 39.7 %copy-start.5 = (bf16[3,512,256]{2,1,0:T(8,128)(2,1)}, bf16[3,512,256]{2,1,0:T(8,128)(2,1)S(1)}, u32[]{:S(2)}) copy-start(bf16[3,512,256]{2,1,0:T(8,128)(2,1)S(1)} %pad_maximum_fusion.refs_13_) | copy-start | bytes 2359300
  42.5 34.3 %collective-permute-start.10 = (bf16[3,512,256]{2,1,0:T(8,128)(2,1)S(1)}, bf16[3,512,256]{2,1,0:T(8,128)(2,1)S(1)}, u32[]{:S(2)}, u32[]{:S(2)}) collective-permute-start(bf16[3,512,256]{2,1,0:T(8,128)(2,1)S(1)} %pad_maximum_fusion.refs_13_), channel_id=1, source_target_pairs={{0,16},{8,24},{16,0},{24,8},{1,17},{9,25},{17,1},{25,9},{2,18},{10... | collective-permute-start | bytes 2359304 | tf_op jit(solution)/shard_map/ppermute | solution.py:276
  44.1 32.7 %collective-permute-start.11 = (bf16[3,512,256]{2,1,0:T(8,128)(2,1)S(1)}, bf16[3,512,256]{2,1,0:T(8,128)(2,1)S(1)}, u32[]{:S(2)}, u32[]{:S(2)}) collective-permute-start(bf16[3,512,256]{2,1,0:T(8,128)(2,1)S(1)} %pad_maximum_fusion.refs_13_), channel_id=1, source_target_pairs={{0,24},{8,16},{16,8},{24,0},{1,25},{9,17},{17,9},{25,1},{2,26},{10... | collective-permute-start | bytes 2359304 | tf_op jit(solution)/shard_map/ppermute | solution.py:276
  45.5 32.5 %collective-permute-start.9 = (bf16[3,512,256]{2,1,0:T(8,128)(2,1)S(1)}, bf16[3,512,256]{2,1,0:T(8,128)(2,1)S(1)}, u32[]{:S(2)}, u32[]{:S(2)}) collective-permute-start(bf16[3,512,256]{2,1,0:T(8,128)(2,1)S(1)} %pad_maximum_fusion.refs_13_), channel_id=1, source_target_pairs={{0,8},{8,0},{16,24},{24,16},{1,9},{9,1},{17,25},{25,17},{2,10},{10... | collective-permute-start | bytes 2359304 | tf_op jit(solution)/shard_map/ppermute | solution.py:276
  46.1 19.5 %collective-permute-start.5 = (bf16[896,256]{1,0:T(8,128)(2,1)S(1)}, bf16[896,256]{1,0:T(8,128)(2,1)}, u32[]{:S(2)}, u32[]{:S(2)}) collective-permute-start(bf16[896,256]{1,0:T(8,128)(2,1)S(1)} %get-tuple-element.32), channel_id=1, source_target_pairs={{0,4},{2,6},{4,0},{6,2},{1,5},{3,7},{5,1},{7,3},{8,12},{10,14},{12... | collective-permute-start | bytes 1376264 | tf_op jit(solution)/shard_map/ppermute | solution.py:274
  46.1 19.5 %collective-permute-start.6 = (bf16[896,256]{1,0:T(8,128)(2,1)S(1)}, bf16[896,256]{1,0:T(8,128)(2,1)S(1)}, u32[]{:S(2)}, u32[]{:S(2)}) collective-permute-start(bf16[896,256]{1,0:T(8,128)(2,1)S(1)} %get-tuple-element.33), channel_id=1, source_target_pairs={{0,6},{2,0},{4,2},{6,4},{1,7},{3,1},{5,3},{7,5},{8,14},{10,8},{12,... | collective-permute-start | bytes 1376264 | tf_op jit(solution)/shard_map/ppermute | solution.py:274
  65.6 16.6 %copy-start.16 = (bf16[896,256]{1,0:T(8,128)(2,1)}, bf16[896,256]{1,0:T(8,128)(2,1)S(1)}, u32[]{:S(2)}) copy-start(bf16[896,256]{1,0:T(8,128)(2,1)S(1)} %collective-permute-done.6.refs_3_) | copy-start | bytes 1376260
  76.8 5.4 %copy-start.13 = (bf16[3,512,256]{2,1,0:T(8,128)(2,1)}, bf16[3,512,256]{2,1,0:T(8,128)(2,1)S(1)}, u32[]{:S(2)}) copy-start(bf16[3,512,256]{2,1,0:T(8,128)(2,1)S(1)} %collective-permute-done.10.refs_15_) | copy-start | bytes 2359300
  78.1 2.0 collective-permute-start.12
  78.1 2.7 %collective-permute-start.13 = (bf16[896,256]{1,0:T(8,128)(2,1)}, bf16[896,256]{1,0:T(8,128)(2,1)S(1)}, u32[]{:S(2)}, u32[]{:S(2)}) collective-permute-start(bf16[896,256]{1,0:T(8,128)(2,1)} %collective-permute-done.4.refs_1_), channel_id=1, source_target_pairs={{0,1},{1,0},{2,3},{3,2},{4,5},{5,4},{6,7},{7,6},{8,9},{9,8},{10,11... | collective-permute-start | bytes 1376264 | tf_op jit(solution)/shard_map/ppermute | solution.py:280
  79.0 3.2 %collective-permute-start.14 = (bf16[896,256]{1,0:T(8,128)(2,1)}, bf16[896,256]{1,0:T(8,128)(2,1)}, u32[]{:S(2)}, u32[]{:S(2)}) collective-permute-start(bf16[896,256]{1,0:T(8,128)(2,1)} %collective-permute-done.5.refs_2_), channel_id=1, source_target_pairs={{0,1},{1,0},{2,3},{3,2},{4,5},{5,4},{6,7},{7,6},{8,9},{9,8},{10,11... | collective-permute-start | bytes 1376264 | tf_op jit(solution)/shard_map/ppermute | solution.py:280
  79.0 3.2 %collective-permute-start.15 = (bf16[896,256]{1,0:T(8,128)(2,1)S(1)}, bf16[896,256]{1,0:T(8,128)(2,1)}, u32[]{:S(2)}, u32[]{:S(2)}) collective-permute-start(bf16[896,256]{1,0:T(8,128)(2,1)S(1)} %collective-permute-done.6.refs_3_), channel_id=1, source_target_pairs={{0,1},{1,0},{2,3},{3,2},{4,5},{5,4},{6,7},{7,6},{8,9},{9,8},{10,11... | collective-permute-start | bytes 1376264 | tf_op jit(solution)/shard_map/ppermute | solution.py:280
  101.0 14.3 %all-to-all-start = ((bf16[4,2,160,128]{3,2,1,0:T(8,128)(2,1)}), bf16[4,2,160,128]{3,2,1,0:T(8,128)(2,1)S(1)}, u32[]{:S(2)}, u32[]{:S(2)}) async-start(bf16[4,2,160,128]{3,2,1,0:T(8,128)(2,1)} %bitcast.34), calls=%async_computation | async-start | bytes 655360 | tf_op jit(solution)/shard_map/all_to_all | solution.py:347
  114.3 15.9 %copy-start.12 = (f32[2048]{0:T(1024)S(1)}, f32[2048]{0:T(1024)}, u32[]{:S(2)}) copy-start(f32[2048]{0:T(1024)} %param.16) | copy-start | bytes 24580
  115.3 8.5 %copy-start.4 = (bf16[4,2,160,128]{3,2,1,0:T(8,128)(2,1)}, bf16[4,2,160,128]{3,2,1,0:T(8,128)(2,1)S(1)}, u32[]{:S(2)}) copy-start(bf16[4,2,160,128]{3,2,1,0:T(8,128)(2,1)S(1)} %all-to-all-done.line_ref) | copy-start | bytes 983044
  115.3 4.7 %collective-permute-start.16 = (bf16[2,160,128]{2,1,0:T(8,128)(2,1)S(1)}, bf16[2,160,128]{2,1,0:T(8,128)(2,1)S(1)}, u32[]{:S(2)}, u32[]{:S(2)}) collective-permute-start(bf16[2,160,128]{2,1,0:T(8,128)(2,1)S(1)} %reduce_sum.12), channel_id=1, source_target_pairs={{0,8},{8,0},{16,24},{24,16},{1,9},{9,1},{17,25},{25,17},{2,10},{10... | collective-permute-start | bytes 245768 | tf_op jit(solution)/shard_map/ppermute | solution.py:351
  116.9 5.3 %collective-permute-start.17 = (bf16[2,160,128]{2,1,0:T(8,128)(2,1)S(1)}, bf16[2,160,128]{2,1,0:T(8,128)(2,1)S(1)}, u32[]{:S(2)}, u32[]{:S(2)}) collective-permute-start(bf16[2,160,128]{2,1,0:T(8,128)(2,1)S(1)} %reduce_sum.12), channel_id=1, source_target_pairs={{0,16},{8,24},{16,0},{24,8},{1,17},{9,25},{17,1},{25,9},{2,18},{10... | collective-permute-start | bytes 245768 | tf_op jit(solution)/shard_map/ppermute | solution.py:351
  118.4 5.3 %collective-permute-start.18 = (bf16[2,160,128]{2,1,0:T(8,128)(2,1)S(1)}, bf16[2,160,128]{2,1,0:T(8,128)(2,1)S(1)}, u32[]{:S(2)}, u32[]{:S(2)}) collective-permute-start(bf16[2,160,128]{2,1,0:T(8,128)(2,1)S(1)} %reduce_sum.12), channel_id=1, source_target_pairs={{0,24},{8,16},{16,8},{24,0},{1,25},{9,17},{17,9},{25,1},{2,26},{10... | collective-permute-start | bytes 245768 | tf_op jit(solution)/shard_map/ppermute | solution.py:351
  126.3 14.1 %all-to-all-start.1 = ((bf16[4,2,160,128]{3,2,1,0:T(8,128)(2,1)}), bf16[4,2,160,128]{3,2,1,0:T(8,128)(2,1)S(1)}, u32[]{:S(2)}, u32[]{:S(2)}) async-start(bf16[4,2,160,128]{3,2,1,0:T(8,128)(2,1)} %shard_map.112), calls=%async_computation.1 | async-start | bytes 655360 | tf_op jit(solution)/shard_map/all_to_all | solution.py:358
  149.4 3.0 %collective-permute-start.20 = (bf16[448,1024]{1,0:T(8,128)(2,1)S(1)}, bf16[448,1024]{1,0:T(8,128)(2,1)S(1)}, u32[]{:S(2)}, u32[]{:S(2)}) collective-permute-start(bf16[448,1024]{1,0:T(8,128)(2,1)S(1)} %copy-done), channel_id=1, source_target_pairs={{0,1},{1,0},{2,3},{3,2},{4,5},{5,4},{6,7},{7,6},{8,9},{9,8},{10,11... | collective-permute-start | bytes 2752520 | tf_op jit(solution)/shard_map/ppermute | solution.py:406
  149.4 4.0 %collective-permute-start.19 = (bf16[448,1024]{1,0:T(8,128)(2,1)}, bf16[448,1024]{1,0:T(8,128)(2,1)S(1)}, u32[]{:S(2)}, u32[]{:S(2)}) collective-permute-start(bf16[448,1024]{1,0:T(8,128)(2,1)} %shard_map.113.refs_0_), channel_id=1, source_target_pairs={{0,1},{1,0},{2,3},{3,2},{4,5},{5,4},{6,7},{7,6},{8,9},{9,8},{10,11... | collective-permute-start | bytes 2752520 | tf_op jit(solution)/shard_map/ppermute | solution.py:406
  159.2 19.6 %collective-permute-start.23 = (bf16[896,256]{1,0:T(8,128)(2,1)}, bf16[896,256]{1,0:T(8,128)(2,1)S(1)}, u32[]{:S(2)}, u32[]{:S(2)}) collective-permute-start(bf16[896,256]{1,0:T(8,128)(2,1)} %shard_map.118), channel_id=1, source_target_pairs={{0,6},{2,0},{4,2},{6,4},{1,7},{3,1},{5,3},{7,5},{8,14},{10,8},{12,... | collective-permute-start | bytes 1376264 | tf_op jit(solution)/shard_map/ppermute | solution.py:410
  167.9 35.0 %collective-permute-start.22 = (bf16[896,256]{1,0:T(8,128)(2,1)}, bf16[896,256]{1,0:T(8,128)(2,1)S(1)}, u32[]{:S(2)}, u32[]{:S(2)}) collective-permute-start(bf16[896,256]{1,0:T(8,128)(2,1)} %shard_map.117), channel_id=1, source_target_pairs={{0,4},{2,6},{4,0},{6,2},{1,5},{3,7},{5,1},{7,3},{8,12},{10,14},{12... | collective-permute-start | bytes 1376264 | tf_op jit(solution)/shard_map/ppermute | solution.py:410
  172.8 30.2 %collective-permute-start.21 = (bf16[896,256]{1,0:T(8,128)(2,1)}, bf16[896,256]{1,0:T(8,128)(2,1)S(1)}, u32[]{:S(2)}, u32[]{:S(2)}) collective-permute-start(bf16[896,256]{1,0:T(8,128)(2,1)} %shard_map.116), channel_id=1, source_target_pairs={{0,2},{2,4},{4,6},{6,0},{1,3},{3,5},{5,7},{7,1},{8,10},{10,12},{12... | collective-permute-start | bytes 1376264 | tf_op jit(solution)/shard_map/ppermute | solution.py:410
  178.8 24.1 %copy-start.6 = (bf16[896,256]{1,0:T(8,128)(2,1)}, bf16[896,256]{1,0:T(8,128)(2,1)S(1)}, u32[]{:S(2)}) copy-start(bf16[896,256]{1,0:T(8,128)(2,1)S(1)} %collective-permute-done.23.refs_3_) | copy-start | bytes 1376260
  (13 other events, 20.0 us)

commit v5 on v4

--- a/solution.py
+++ b/solution.py
@@ -59,28 +59,42 @@
     return np.stack([every[places].reshape(-1, LANES) for places in own])
 
 
-def project_kernel(at_ref, per_group, layers, n_weights, gathered, *refs):
+def project_kernel(at_ref, per_group, layers, gathered, *refs):
     mine, other = refs[:layers], refs[layers : 2 * layers]
-    wq_ref, wk_ref, table_ref, bias_ref = refs[2 * layers : 2 * layers + 4]
-    weights = refs[2 * layers + 4 : 2 * layers + 4 + n_weights]
-    q_ref, k_ref, v_ref, early_ref, total_ref, row_ref, w_ref, phi_ref, sems = refs[2 * layers + 4 + n_weights :]
+    table_ref, bias_ref, wq_ref, wk_ref, own_ref = refs[2 * layers : 2 * layers + 5]
+    rest = refs[2 * layers + 5 :]
+    weights, rest = rest[:-10], rest[-10:]
+    q_ref, k_ref, v_ref, early_ref, total_ref, row_ref, narrow_ref, w_ref, phi_ref, sems = rest
+    inner, outer = weights[: len(weights) // 2], weights[len(weights) // 2 :]
     core, layer, slab = at_ref[0], at_ref[1], at_ref[2]
     both, width = other[0].shape
     rows = both // 2
-    part = weights[1].shape[-2]
-    copies = [pltpu.make_async_copy(weights[0], w_ref.at[0], sems.at[0])]
-    slots = [0]
+    model = row_ref.shape[1]
+    part = inner[0].shape[-2]
+    block = v_ref.shape[2] // layers
+    narrow = wq_ref.shape[1]
+    copies = []
+
+    def fetch(slot, source, to):
+        copies.append((slot, pltpu.make_async_copy(source, to, sems.at[len(copies)])))
+        copies[-1][1].start()
+
+    fetch(-1, wq_ref, narrow_ref.at[:, pl.ds(0, narrow)])
+    fetch(-1, wk_ref, narrow_ref.at[:, pl.ds(narrow, narrow)])
+    fetch(0, own_ref, w_ref.at[0, :, pl.ds(0, block)])
     for d in range(1, layers):
-        for m in range(w_ref.shape[1] // part):
+        group, index = (outer, 0 if d == 1 else 1) if d in (1, layers - 1) else (inner, d - 2)
+        for m in range(model // part):
             if gathered:
-                source, start = weights[1].at[m, d - 1], m * part
+                source, start = group[0].at[m, index], m * part
             else:
-                source, start = weights[1 + m].at[d - 1], pl.multiple_of((slab ^ m) * part, part)
-            to = w_ref.at[d, pl.ds(start, part)]
-            copies.append(pltpu.make_async_copy(source, to, sems.at[len(copies)]))
-            slots.append(d)
-    for copy in copies:
-        copy.start()
+                source, start = group[m].at[index], pl.multiple_of((slab ^ m) * part, part)
+            fetch(d, source, w_ref.at[d // 2, pl.ds(start, part), pl.ds((d % 2) * block, block)])
+
+    def arrived(slots):
+        for slot, copy in copies:
+            if slot in slots:
+                copy.wait()
 
     for d in range(layers):
         z = lax.rem(layer + layers - d, layers)
@@ -88,39 +102,40 @@
         there = pl.multiple_of((2 * z + 1 - core) * width, width)
         row_ref[:, pl.ds(here, width)] = mine[d][0] if d == 0 else mine[d][...]
         row_ref[:, pl.ds(there, width)] = other[d][...]
-    q = dot(row_ref[...], wq_ref[...]).astype(BF16)
-    k = dot(row_ref[...], wk_ref[...]).astype(BF16)
+    arrived((-1,))
     half = table_ref.shape[1] // 2
     for chunk in range(2):
         at = slice(chunk * rows, (chunk + 1) * rows)
-        q_ref[chunk] = q[at]
-        k_ref[chunk] = k[at]
-        for lanes in range(0, k.shape[1], LANES):
-            product = dot(table_ref[0], k[at, lanes : lanes + LANES], NT)
+        both_narrow = dot(row_ref[at, :], narrow_ref[...]).astype(BF16)
+        q_ref[chunk] = both_narrow[:, :narrow]
+        k_ref[chunk] = both_narrow[:, narrow:]
+        for lanes in range(0, narrow, LANES):
+            product = dot(table_ref[0], both_narrow[:, narrow + lanes : narrow + lanes + LANES], NT)
             left = product[:half] + bias_ref[:, 0:1]
             right = product[half:] + bias_ref[:, 1:2]
             to = (lanes // LANES) * half
             phi_ref[chunk, to : to + half, :] = (left * right).astype(BF16)
 
-    block = v_ref.shape[2] // layers
-    for d in range(layers):
-        for slot, copy in zip(slots, copies):
-            if slot == d:
-                copy.wait()
-        z = lax.rem(layer + d, layers)
+    for pair in range(layers // 2):
+        arrived((2 * pair, 2 * pair + 1))
         first = []
         for chunk in range(2):
-            value = dot(row_ref[chunk * rows : (chunk + 1) * rows, :], w_ref[d]).astype(BF16)
-            v_ref[chunk, :, pl.ds(pl.multiple_of(z * block, block), block)] = value
-            for i in range(per_group):
-                head = z * per_group + i
-                phi = phi_ref[chunk, pl.ds(pl.multiple_of(head * PACKED, PACKED), PACKED), :]
-                state = dot(phi, value[:, i * HEAD_DIM : (i + 1) * HEAD_DIM])
-                if chunk == 0:
-                    early_ref[head] = state.astype(BF16)
-                    first.append(state)
-                else:
-                    total_ref[head] = (first[i] + state).astype(BF16)
+            at = slice(chunk * rows, (chunk + 1) * rows)
+            value = dot(row_ref[at, :], w_ref[pair]).astype(BF16)
+            for d in (2 * pair, 2 * pair + 1):
+                z = lax.rem(layer + d, layers)
+                side = (d % 2) * block
+                v_ref[chunk, :, pl.ds(pl.multiple_of(z * block, block), block)] = value[:, side : side + block]
+                for i in range(per_group):
+                    head = z * per_group + i
+                    phi = phi_ref[chunk, pl.ds(pl.multiple_of(head * PACKED, PACKED), PACKED), :]
+                    lanes = side + i * HEAD_DIM
+                    state = dot(phi, value[:, lanes : lanes + HEAD_DIM])
+                    if chunk == 0:
+                        early_ref[head] = state.astype(BF16)
+                        first.append(state)
+                    else:
+                        total_ref[head] = (first.pop(0) + state).astype(BF16)
 
 
 def local_kernel(
@@ -167,36 +182,37 @@
         run = run + line_ref[z].astype(F32)
 
 
-def hidden_kernel(at_ref, num_a, num_b, phi_a, phi_b, state_ref, gain_ref, out_ref):
-    held = phi_a.shape[1]
-    for i in range(2 * held):
+def hidden_kernel(at_ref, state_ref, gain_ref, *refs):
+    parts, out_ref = refs[:-1], refs[-1]
+    numbers, features = parts[: len(parts) // 2], parts[len(parts) // 2 :]
+    held = features[0].shape[1]
+    for i in range(held * len(features)):
         columns = slice(i * HEAD_DIM, (i + 1) * HEAD_DIM)
-        num_ref, phi_ref = (num_a, phi_a) if i < held else (num_b, phi_b)
         at = (i % held) * HEAD_DIM
-        num = num_ref[0, :, at : at + HEAD_DIM] + dot(phi_ref[0, i % held], state_ref[i])
+        num = numbers[i // held][0, :, at : at + HEAD_DIM]
+        num = num + dot(features[i // held][0, i % held], state_ref[i])
         mean_square = jnp.mean(num * num, axis=1, keepdims=True)
         hidden = num * lax.rsqrt(mean_square + 1e-05) * gain_ref[:, columns]
         out_ref[:, columns] = hidden.astype(BF16)
 
 
-def output_kernel(at_ref, *refs):
-    chunks, w_mine, w_other, out_ref = refs[:-3], refs[-3], refs[-2], refs[-1]
-    rows, depth = chunks[0].shape
+def output_kernel(at_ref, mine_ref, other_ref, w_mine, w_other, out_ref):
+    depth = mine_ref.shape[1]
     width = out_ref.shape[1]
-    for i in range(len(chunks) // 2):
-        part = dot(chunks[2 * i][...], w_mine[...].reshape(depth, width))
-        part = part + dot(chunks[2 * i + 1][...], w_other[...].reshape(depth, width))
-        out_ref[i * rows : (i + 1) * rows, :] = part.astype(BF16)
+    part = dot(mine_ref[...], w_mine[...].reshape(depth, width))
+    part = part + dot(other_ref[...], w_other[...].reshape(depth, width))
+    out_ref[...] = part.astype(BF16)
 
 
 def place_kernel(at_ref, *refs):
     pieces, out_ref, sems = refs[:-2], refs[-2], refs[-1]
-    layers = len(pieces)
+    layers = len(pieces) // 2
     copies = []
-    for d, piece in enumerate(pieces):
-        z = lax.rem(at_ref[1] + layers - d, layers)
-        to = out_ref.at[pl.ds(pl.multiple_of(z * piece.shape[0], piece.shape[0]), piece.shape[0])]
-        copies.append(pltpu.make_async_copy(piece, to, sems.at[d]))
+    for i, piece in enumerate(pieces):
+        rows = piece.shape[0]
+        z = lax.rem(at_ref[1] + layers - i // 2, layers)
+        to = out_ref.at[pl.ds(pl.multiple_of((2 * z + i % 2) * rows, rows), rows)]
+        copies.append(pltpu.make_async_copy(piece, to, sems.at[i]))
     for copy in copies:
         copy.start()
     for copy in copies:
@@ -211,7 +227,7 @@
     return pltpu.CompilerParams(vmem_limit_bytes=mib * MIB)
 
 
-def call(kernel, scalar, grid, in_specs, out_specs, out_shape, args, flops, scratch=()):
+def call(kernel, scalar, grid, in_specs, out_specs, out_shape, args, flops, scratch=(), mib=60):
     return pl.pallas_call(
         kernel,
         grid_spec=pltpu.PrefetchScalarGridSpec(
@@ -222,7 +238,7 @@
             scratch_shapes=list(scratch),
         ),
         out_shape=out_shape,
-        compiler_params=params(60),
+        compiler_params=params(mib),
         cost_estimate=pl.CostEstimate(flops=flops, bytes_accessed=12 * MIB, transcendentals=0),
     )(scalar, *args)
 
@@ -270,28 +286,33 @@
         down[k] = lax.ppermute(down[k - 1], "z", [(z, z - 1) for z in range(1, layers - k + 1)])
         if k == layers - 2:
             up[k], down[k], sent = lax.optimization_barrier((up[k], down[k], sent))
-    slots = jnp.stack([jnp.where(layer + d < layers, down[d], up[layers - d]) for d in range(1, layers)])
+    slot = lambda d: jnp.where(layer + d < layers, down[d], up[layers - d])
+
+    def to_lines(chosen):
+        stack = jnp.stack([slot(d) for d in chosen])
+        if slabs == 4:
+            return [stack] + [lax.ppermute(stack, "seq", flip(m)) for m in range(1, slabs)]
+        return [lax.all_gather(stack, "seq", axis=0, tiled=False)]
+
     mine = [sent[0]] + [lax.ppermute(sent[d], "z", turn(d)) for d in range(1, layers)]
-    if slabs == 4:
-        weights = [w_value, slots] + [lax.ppermute(slots, "seq", flip(m)) for m in range(1, slabs)]
-    else:
-        weights = [w_value, lax.all_gather(slots, "seq", axis=0, tiled=False)]
-    mine, weights[2:] = lax.optimization_barrier((mine, weights[2:]))
+    inner = to_lines(range(2, layers - 1))
+    outer = to_lines((1, layers - 1))
+    far = layers // 2
+    mine[far], outer[-1] = lax.optimization_barrier((mine[far], outer[-1]))
     other = [lax.ppermute(piece, "core", swap) for piece in mine]
+    weights = inner + outer
 
     query, key, value, early, total = call(
-        lambda at_ref, *refs: project_kernel(at_ref, per_group, layers, len(weights), slabs != 4, *refs),
+        lambda at_ref, *refs: project_kernel(at_ref, per_group, layers, slabs != 4, *refs),
         at,
         (1,),
         [pl.BlockSpec((1, 2 * rows, width), lambda i, at: (at[1], 0, 0))]
         + [whole((2 * rows, width))] * (2 * layers - 1)
         + [
-            whole((model, narrow)),
-            whole((model, narrow)),
             pl.BlockSpec((1,) + key_table.shape[1:], lambda i, at: (at[0], 0, 0)),
             whole(key_bias.shape),
         ]
-        + [anywhere] * len(weights),
+        + [anywhere] * (3 + len(weights)),
         [
             whole((2, rows, narrow)),
             whole((2, rows, narrow)),
@@ -306,22 +327,26 @@
             jax.ShapeDtypeStruct((heads, PACKED, HEAD_DIM), BF16),
             jax.ShapeDtypeStruct((heads, PACKED, HEAD_DIM), BF16),
         ],
-        (blocks, *mine[1:], *other, w_query, w_key, key_table, key_bias, *weights),
+        (blocks, *mine[1:], *other, key_table, key_bias, w_query, w_key, w_value, *weights),
         4 * rows * model * (model // 2 + 2 * narrow),
         [
             pltpu.VMEM((2 * rows, model), BF16),
-            pltpu.VMEM((layers, model, value_width), BF16),
+            pltpu.VMEM((model, 2 * narrow), BF16),
+            pltpu.VMEM((layers // 2, model, 2 * value_width), BF16),
             pltpu.VMEM((2, heads * PACKED, rows), BF16),
-            pltpu.SemaphoreType.DMA((1 + (layers - 1) * slabs,)),
+            pltpu.SemaphoreType.DMA((3 + (layers - 1) * slabs,)),
         ],
     )
 
-    def local(part_of_heads):
-        offset = part_of_heads * (layers // 2)
+    parts = 4
+    some_layers = layers // parts
+
+    def local(index):
+        offset = index * some_layers
         return call(
             lambda core_ref, *refs: local_kernel(core_ref, per_group, offset, *refs),
             at,
-            (2, layers // 2),
+            (2, some_layers),
             [
                 pl.BlockSpec((1, rows, narrow), lambda c, i, _: (c, 0, 0)),
                 pl.BlockSpec((1, rows, narrow), lambda c, i, _: (c, 0, 0)),
@@ -336,19 +361,21 @@
                 pl.BlockSpec((1, per_group, rows, PACKED), lambda c, i, _: (c, i, 0, 0)),
             ],
             [
-                jax.ShapeDtypeStruct((2, rows, layers * value_width // 2), F32),
-                jax.ShapeDtypeStruct((2, heads // 2, rows, PACKED), BF16),
+                jax.ShapeDtypeStruct((2, rows, some_layers * value_width), F32),
+                jax.ShapeDtypeStruct((2, heads // parts, rows, PACKED), BF16),
             ],
             (query, key, value, early, query_a, query_b, query_bias),
-            heads * rows * rows * 600,
+            heads * rows * rows * 300,
         )
 
     own = total.reshape(layers, per_group, PACKED, HEAD_DIM)
     line = lax.all_to_all(own, "z", split_axis=0, concat_axis=0, tiled=True)
-    num_a, phi_a = local(0)
-    line, num_a, phi_a = lax.optimization_barrier((line, num_a, phi_a))
+    locals_ = [local(0), local(1)]
+    line, locals_ = lax.optimization_barrier((line, locals_))
     slab_total = jnp.sum(line.astype(F32), axis=0).astype(BF16)
     totals = [lax.ppermute(slab_total, "seq", flip(m)) for m in range(1, slabs)]
+    third = local(2)
+    totals, third = lax.optimization_barrier((totals, third))
     prefix = pl.pallas_call(
         prefix_kernel,
         in_specs=[pl.BlockSpec(memory_space=pltpu.SMEM)] + [vmem] * slabs,
@@ -357,67 +384,65 @@
     )(at, line, *totals)
     prefix = lax.all_to_all(prefix, "z", split_axis=0, concat_axis=0, tiled=True)
     prefix = prefix.reshape(heads, PACKED, HEAD_DIM)
-    num_b, phi_b = local(1)
+    locals_ = locals_ + [third, local(3)]
 
     def hidden(chunk):
         some = rows // 2
-        numbers = pl.BlockSpec((1, some, heads * HEAD_DIM // 2), lambda i, _: (chunk, i, 0))
-        features = pl.BlockSpec((1, heads // 2, some, PACKED), lambda i, _: (chunk, 0, i, 0))
+        numbers = pl.BlockSpec((1, some, heads * HEAD_DIM // parts), lambda i, _: (chunk, i, 0))
+        features = pl.BlockSpec((1, heads // parts, some, PACKED), lambda i, _: (chunk, 0, i, 0))
         return call(
             hidden_kernel,
             at,
             (2,),
-            [
-                numbers,
-                numbers,
-                features,
-                features,
-                whole((heads, PACKED, HEAD_DIM)),
-                whole((1, heads * HEAD_DIM)),
-            ],
+            [whole((heads, PACKED, HEAD_DIM)), whole((1, heads * HEAD_DIM))]
+            + [numbers] * parts
+            + [features] * parts,
             pl.BlockSpec((some, heads * HEAD_DIM), lambda i, _: (i, 0)),
             jax.ShapeDtypeStruct((rows, heads * HEAD_DIM), BF16),
-            (num_a, num_b, phi_a, phi_b, prefix, gain_mine),
+            (prefix, gain_mine, *(num for num, _ in locals_), *(phi for _, phi in locals_)),
             rows * heads * HEAD_DIM * 600,
         )
 
     w_rows = w_out.reshape(layers, 2, value_width, model)
 
-    def project_out(d):
+    def project_out(kept, received, d):
         columns = lambda at: 2 * lax.rem(at[1] + d, layers) + at[0]
         return call(
             output_kernel,
             at,
             (1,),
-            [whole((rows, heads * HEAD_DIM))] * len(chunks)
-            + [
+            [
+                whole((rows, heads * HEAD_DIM)),
+                whole((rows, heads * HEAD_DIM)),
                 pl.BlockSpec((layers, 1, value_width, width), lambda i, at: (0, at[0], 0, columns(at))),
                 pl.BlockSpec((layers, 1, value_width, width), lambda i, at: (0, 1 - at[0], 0, columns(at))),
             ],
-            whole((2 * rows, width)),
-            jax.ShapeDtypeStruct((2 * rows, width), BF16),
-            (*chunks, w_rows, w_rows),
-            4 * rows * model * width,
+            whole((rows, width)),
+            jax.ShapeDtypeStruct((rows, width), BF16),
+            (kept, received, w_rows, w_rows),
+            2 * rows * model * width,
         )
 
-    chunks = []
+    kept = [hidden(chunk) for chunk in range(2)]
+    received = [lax.ppermute(half, "core", swap) for half in kept]
+    pieces = {}
     for chunk in range(2):
-        kept = hidden(chunk)
-        chunks += [kept, lax.ppermute(kept, "core", swap)]
-    pieces = {}
-    for d in list(range(1, layers)) + [0]:
-        part_out = project_out(d)
-        pieces[d] = lax.ppermute(part_out, "z", turn(d)) if d else part_out
+        for d in range(1, layers):
+            piece = project_out(kept[chunk], received[chunk], d)
+            pieces[d, chunk] = lax.ppermute(piece, "z", turn(d))
+    for chunk in range(2):
+        pieces[0, chunk] = project_out(kept[chunk], received[chunk], 0)
     return call(
         place_kernel,
         at,
         (1,),
-        [anywhere] * layers,
+        [vmem] * (2 * layers),
         anywhere,
         jax.ShapeDtypeStruct((groups * rows, width), BF16),
-        tuple(pieces[d] for d in range(layers)),
+        tuple(pieces[d, chunk] for d in range(layers) for chunk in range(2)),
         0,
-        [pltpu.SemaphoreType.DMA((layers,))],
+        [pltpu.SemaphoreType.DMA((2 * layers,))],
+        mib=8,
     )
 
 

time: 263 us -> 200 us (0.76)
  Pallas kernels: 125 us -> 82.3 us
  waiting for transfers between devices: 92.5 us -> 63 us
  starting transfers between devices: 35.9 us -> 42 us
    pallas_call x10 -> x16, Pallas kernels: 123 us -> 80.4 us  [call(): pl.pallas_call(kernel, grid_spec=pltpu.PrefetchScalarGridSpec(num_scalar_...]
    ppermute x8 -> x14, waiting for transfers between devices: 40.1 us -> 29.3 us  [the longest x6 20 us: to_lines(): lax.ppermute(stack, 'seq', flip(m))]
    ppermute x3, waiting for transfers between devices: 22.6 us -> 12.1 us  [per_device(): lax.ppermute(down[k - 1], 'z', [(z, z - 1) for z in range(1, layers - k +...]
    ppermute x8 -> x14, starting transfers between devices: 9.01 us -> 15.9 us  [the longest x6 8.29 us: per_device(): pieces[d, chunk] = lax.ppermute(piece, 'z', turn(d))]
    ppermute x3, waiting for transfers between devices: 4.85 us -> 0.01 us  [per_device(): totals = [lax.ppermute(slab_total, 'seq', flip(m)) for m in range(1, slabs)]]
    unnamed x38 -> x44, local copies, waits for them, and re-layouts: 4.27 us -> 6.7 us
  transfers between devices with their start and end apart: 26 -> 32, of which waited for: 16 -> 13; matrix products, arithmetic and copies ran while one was open for 1% -> 2% of each run, Pallas kernels for 13% -> 30%
where the time goes in v5:
time: 200 us; the launch traced here: 198 us
  Pallas kernels  82.3 us (41%)
  waiting for transfers between devices  63 us (32%)
  starting transfers between devices  42 us (21%)
  local copies, waits for them, and re-layouts  9.84 us (5%)
    pallas_call x16, Pallas kernels, call(): pl.pallas_call(kernel, grid_spec=pltpu.PrefetchScalarGridSpec(num_scalar_...  80.4 us
    ppermute x6, waiting for transfers between devices, to_lines(): lax.ppermute(stack, 'seq', flip(m))  20 us
    ppermute x3, waiting for transfers between devices, per_device(): lax.ppermute(sent[d], 'z', turn(d))  16.8 us
    ppermute x3, waiting for transfers between devices, per_device(): lax.ppermute(down[k - 1], 'z', [(z, z - 1) for z in range(1, layers - k +...  12.1 us
    ppermute x6, waiting for transfers between devices, per_device(): pieces[d, chunk] = lax.ppermute(piece, 'z', turn(d))  9.25 us
    ppermute x6, starting transfers between devices, per_device(): pieces[d, chunk] = lax.ppermute(piece, 'z', turn(d))  8.29 us
    ppermute x6, starting transfers between devices, to_lines(): lax.ppermute(stack, 'seq', flip(m))  7.11 us
    unnamed x44, local copies, waits for them, and re-layouts  6.7 us
  transfers between devices with their start and end apart: 32, of which 13 were waited for; matrix products, arithmetic and copies ran while one was open for 2% of the time, Pallas kernels for 30%

profile of v5, /device:TPU:0, one launch (start us, length us, event | category | flops | bytes accessed | tf_op | source)
XLA Modules:
  0.0 198.5 jit_solution(8673583820573685716)
XLA Ops:
  1.0 4.9 %collective-permute-start = (bf16[512,256]{1,0:T(8,128)(2,1)S(1)}, bf16[512,256]{1,0:T(8,128)(2,1)S(1)}, u32[]{:S(2)}, u32[]{:S(2)}) collective-permute-start(bf16[512,256]{1,0:T(8,128)(2,1)S(1)} %constant_dynamic-slice_fusion.1), channel_id=1, source_target_pairs={{0,2},{2,4},{4,6},{1,3},{3,5},{5,7},{8,10},{10,12},{12,14},{9,11},... | collective-permute-start | bytes 786440 | tf_op jit(solution)/shard_map/ppermute | solution.py:285
  7.2 4.2 %collective-permute-done = bf16[512,256]{1,0:T(8,128)(2,1)S(1)} collective-permute-done((bf16[512,256]{1,0:T(8,128)(2,1)S(1)}, bf16[512,256]{1,0:T(8,128)(2,1)S(1)}, u32[]{:S(2)}, u32[]{:S(2)}) %collective-permute-start) | collective-permute-done | bytes 262176 | tf_op jit(solution)/shard_map/ppermute | solution.py:285
  12.1 3.5 %collective-permute-done.2 = bf16[512,256]{1,0:T(8,128)(2,1)S(1)} collective-permute-done((bf16[512,256]{1,0:T(8,128)(2,1)S(1)}, bf16[512,256]{1,0:T(8,128)(2,1)S(1)}, u32[]{:S(2)}, u32[]{:S(2)}) %collective-permute-start.2) | collective-permute-done | bytes 262176 | tf_op jit(solution)/shard_map/ppermute | solution.py:286
  18.5 6.0 %collective-permute-done.3 = bf16[512,256]{1,0:T(8,128)(2,1)S(1)} collective-permute-done((bf16[512,256]{1,0:T(8,128)(2,1)S(1)}, bf16[512,256]{1,0:T(8,128)(2,1)S(1)}, u32[]{:S(2)}, u32[]{:S(2)}) %collective-permute-start.3) | collective-permute-done | bytes 262176 | tf_op jit(solution)/shard_map/ppermute | solution.py:286
  30.1 2.7 %collective-permute-done.7 = bf16[512,256]{1,0:T(8,128)(2,1)S(1)} collective-permute-done((bf16[512,256]{1,0:T(8,128)(2,1)S(1)}, bf16[512,256]{1,0:T(8,128)(2,1)S(1)}, u32[]{:S(2)}, u32[]{:S(2)}) %collective-permute-start.7) | collective-permute-done | bytes 262176 | tf_op jit(solution)/shard_map/ppermute | solution.py:286
  32.9 2.5 %collective-permute-start.8 = (bf16[2,512,256]{2,1,0:T(8,128)(2,1)S(1)}, bf16[2,512,256]{2,1,0:T(8,128)(2,1)S(1)}, u32[]{:S(2)}, u32[]{:S(2)}) collective-permute-start(bf16[2,512,256]{2,1,0:T(8,128)(2,1)S(1)} %pad_maximum_fusion.refs_17_), channel_id=1, source_target_pairs={{0,24},{8,16},{16,8},{24,0},{1,25},{9,17},{17,9},{25,1},{2,26},{10... | collective-permute-start | bytes 1572872 | tf_op jit(solution)/shard_map/ppermute | solution.py:294
  35.8 2.7 %collective-permute-start.4 = (bf16[896,256]{1,0:T(8,128)(2,1)S(1)}, bf16[896,256]{1,0:T(8,128)(2,1)}, u32[]{:S(2)}, u32[]{:S(2)}) collective-permute-start(bf16[896,256]{1,0:T(8,128)(2,1)S(1)} %get-tuple-element.36), channel_id=1, source_target_pairs={{0,2},{2,4},{4,6},{6,0},{1,3},{3,5},{5,7},{7,1},{8,10},{10,12},{12... | collective-permute-start | bytes 1376264 | tf_op jit(solution)/shard_map/ppermute | solution.py:297
  38.5 12.3 %collective-permute-done.15.refs_15_ = bf16[1,512,256]{2,1,0:T(8,128)(2,1)S(1)} collective-permute-done((bf16[1,512,256]{2,1,0:T(8,128)(2,1)S(1)}, bf16[1,512,256]{2,1,0:T(8,128)(2,1)S(1)}, u32[]{:S(2)}, u32[]{:S(2)}) %collective-permute-start.15) | collective-permute-done | bytes 262176 | tf_op jit(solution)/shard_map/ppermute | solution.py:294
  51.5 13.1 %collective-permute-done.5.refs_2_ = bf16[896,256]{1,0:T(8,128)(2,1)} collective-permute-done((bf16[896,256]{1,0:T(8,128)(2,1)S(1)}, bf16[896,256]{1,0:T(8,128)(2,1)}, u32[]{:S(2)}, u32[]{:S(2)}) %collective-permute-start.5) | collective-permute-done | bytes 458784 | tf_op jit(solution)/shard_map/ppermute | solution.py:297
  65.6 3.7 %collective-permute-done.9.refs_3_ = bf16[896,256]{1,0:T(8,128)(2,1)} collective-permute-done((bf16[896,256]{1,0:T(8,128)(2,1)S(1)}, bf16[896,256]{1,0:T(8,128)(2,1)}, u32[]{:S(2)}, u32[]{:S(2)}) %collective-permute-start.9) | collective-permute-done | bytes 458784 | tf_op jit(solution)/shard_map/ppermute | solution.py:297
  71.3 7.0 %collective-permute-done.17.refs_18_ = bf16[2,512,256]{2,1,0:T(8,128)(2,1)S(1)} collective-permute-done((bf16[2,512,256]{2,1,0:T(8,128)(2,1)S(1)}, bf16[2,512,256]{2,1,0:T(8,128)(2,1)S(1)}, u32[]{:S(2)}, u32[]{:S(2)}) %collective-permute-start.17) | collective-permute-done | bytes 524320 | tf_op jit(solution)/shard_map/ppermute | solution.py:294
  80.4 14.6 %shard_map.109 = (bf16[2,448,256]{2,1,0:T(8,128)(2,1)}, bf16[2,448,256]{2,1,0:T(8,128)(2,1)}, bf16[2,448,1024]{2,1,0:T(8,128)(2,1)}, bf16[8,160,128]{2,1,0:T(8,128)(2,1)}, bf16[8,160,128]{2,1,0:T(8,128)(2,1)}) custom-call(s32[3]{0:T(128)} %pad_add_fusion.at_ref.core_ref, bf16[4,896,256]{2,1,0:T(8,128)(2,1)} %bitcast.41, ...), custom_call_target="tpu_custom_call" | custom-call | flops 5637144576 | bytes 12582912 | tf_op jit(solution)/shard_map/pallas_call | solution.py:231
  95.0 3.6 %all-to-all-start = ((bf16[4,2,160,128]{3,2,1,0:T(8,128)(2,1)}), bf16[4,2,160,128]{3,2,1,0:T(8,128)(2,1)S(1)}, u32[]{:S(2)}, u32[]{:S(2)}) async-start(bf16[4,2,160,128]{3,2,1,0:T(8,128)(2,1)} %bitcast.42), calls=%async_computation | async-start | bytes 655360 | tf_op jit(solution)/shard_map/all_to_all | solution.py:372
  98.7 6.3 %shard_map.111 = (f32[2,448,256]{2,1,0:T(8,128)}, bf16[2,2,448,160]{3,2,1,0:T(8,128)(2,1)}) custom-call(s32[3]{0:T(128)} %pad_add_fusion.at_ref.core_ref, bf16[2,448,256]{2,1,0:T(8,128)(2,1)} %get-tuple-element.45.refs_0_, bf16[2,448,256]{2,1,0:T(8,128)(2,1)} %get-tuple-element.46.refs_1_, bf16[2,448,1024]{2,1,0:T(8,128)(2,1)} %get-tuple-element.47.refs_2_, ...), custom_call_target="tpu_custom_call" | custom-call | flops 481689600 | bytes 12582912 | tf_op jit(solution)/shard_map/pallas_call | solution.py:231
  105.0 6.3 %shard_map.110 = (f32[2,448,256]{2,1,0:T(8,128)}, bf16[2,2,448,160]{3,2,1,0:T(8,128)(2,1)}) custom-call(s32[3]{0:T(128)} %pad_add_fusion.at_ref.core_ref, bf16[2,448,256]{2,1,0:T(8,128)(2,1)} %get-tuple-element.45.refs_0_, bf16[2,448,256]{2,1,0:T(8,128)(2,1)} %get-tuple-element.46.refs_1_, bf16[2,448,1024]{2,1,0:T(8,128)(2,1)} %get-tuple-element.47.refs_2_, ...), custom_call_target="tpu_custom_call" | custom-call | flops 481689600 | bytes 12582912 | tf_op jit(solution)/shard_map/pallas_call | solution.py:231
  114.9 6.3 %shard_map.112 = (f32[2,448,256]{2,1,0:T(8,128)}, bf16[2,2,448,160]{3,2,1,0:T(8,128)(2,1)}) custom-call(s32[3]{0:T(128)} %pad_add_fusion.at_ref.core_ref, bf16[2,448,256]{2,1,0:T(8,128)(2,1)} %get-tuple-element.45.refs_0_, bf16[2,448,256]{2,1,0:T(8,128)(2,1)} %get-tuple-element.46.refs_1_, bf16[2,448,1024]{2,1,0:T(8,128)(2,1)} %get-tuple-element.47.refs_2_, ...), custom_call_target="tpu_custom_call" | custom-call | flops 481689600 | bytes 12582912 | tf_op jit(solution)/shard_map/pallas_call | solution.py:231
  123.8 4.9 %all-to-all-start.1 = ((bf16[4,2,160,128]{3,2,1,0:T(8,128)(2,1)}), bf16[4,2,160,128]{3,2,1,0:T(8,128)(2,1)S(1)}, u32[]{:S(2)}, u32[]{:S(2)}) async-start(bf16[4,2,160,128]{3,2,1,0:T(8,128)(2,1)} %shard_map.113), calls=%async_computation.1 | async-start | bytes 655360 | tf_op jit(solution)/shard_map/all_to_all | solution.py:385
  129.3 6.3 %shard_map.114 = (f32[2,448,256]{2,1,0:T(8,128)}, bf16[2,2,448,160]{3,2,1,0:T(8,128)(2,1)}) custom-call(s32[3]{0:T(128)} %pad_add_fusion.at_ref.core_ref, bf16[2,448,256]{2,1,0:T(8,128)(2,1)} %get-tuple-element.45.refs_0_, bf16[2,448,256]{2,1,0:T(8,128)(2,1)} %get-tuple-element.46.refs_1_, bf16[2,448,1024]{2,1,0:T(8,128)(2,1)} %get-tuple-element.47.refs_2_, ...), custom_call_target="tpu_custom_call" | custom-call | flops 481689600 | bytes 12582912 | tf_op jit(solution)/shard_map/pallas_call | solution.py:231
  136.9 4.2 %shard_map.117.mine_ref = bf16[448,1024]{1,0:T(8,128)(2,1)} custom-call(s32[3]{0:T(128)} %pad_add_fusion.at_ref.core_ref, bf16[8,160,128]{2,1,0:T(8,128)(2,1)} %bitcast.38, f32[1,1024]{1,0:T(1,128)} %bitcast.43, f32[2,448,256]{2,1,0:T(8,128)} %get-tuple-element.59.refs_0_, f32[2,448,256]{2,1,0:T(8,128)} %get-tuple-element.60.refs_1_, ...), custom_call_target="tpu_custom_call" | custom-call | flops 275251200 | bytes 12582912 | tf_op jit(solution)/shard_map/pallas_call | solution.py:231
  141.1 4.2 %shard_map.115.mine_ref = bf16[448,1024]{1,0:T(8,128)(2,1)} custom-call(s32[3]{0:T(128)} %pad_add_fusion.at_ref.core_ref, bf16[8,160,128]{2,1,0:T(8,128)(2,1)} %bitcast.39, f32[1,1024]{1,0:T(1,128)} %bitcast.44, f32[2,448,256]{2,1,0:T(8,128)} %get-tuple-element.59.refs_0_, f32[2,448,256]{2,1,0:T(8,128)} %get-tuple-element.60.refs_1_, ...), custom_call_target="tpu_custom_call" | custom-call | flops 275251200 | bytes 12582912 | tf_op jit(solution)/shard_map/pallas_call | solution.py:231
  146.7 3.8 %shard_map.124 = bf16[448,256]{1,0:T(8,128)(2,1)} custom-call(s32[3]{0:T(128)} %pad_add_fusion.at_ref.core_ref, bf16[448,1024]{1,0:T(8,128)(2,1)} %shard_map.117.mine_ref, bf16[448,1024]{1,0:T(8,128)(2,1)} %copy-done.3, bf16[4,2,256,2048]{3,2,1,0:T(8,128)(2,1)} %bitcast.22, bf16[4,2,256,2048]{3,2,1,0:T(8,128)(2,1)} %bitcast.23), custom_call_target="tpu_custom_call" | custom-call | flops 469762048 | bytes 12582912 | tf_op jit(solution)/shard_map/pallas_call | solution.py:231
  150.5 3.3 %collective-permute-start.29 = (bf16[448,256]{1,0:T(8,128)(2,1)}, bf16[448,256]{1,0:T(8,128)(2,1)S(1)}, u32[]{:S(2)}, u32[]{:S(2)}) collective-permute-start(bf16[448,256]{1,0:T(8,128)(2,1)} %shard_map.124), channel_id=1, source_target_pairs={{0,6},{2,0},{4,2},{6,4},{1,7},{3,1},{5,3},{7,5},{8,14},{10,8},{12,... | collective-permute-start | bytes 688136 | tf_op jit(solution)/shard_map/ppermute | solution.py:432
  154.8 3.8 %shard_map.123 = bf16[448,256]{1,0:T(8,128)(2,1)} custom-call(s32[3]{0:T(128)} %pad_add_fusion.at_ref.core_ref, bf16[448,1024]{1,0:T(8,128)(2,1)} %shard_map.115.mine_ref, bf16[448,1024]{1,0:T(8,128)(2,1)} %copy-done.4, bf16[4,2,256,2048]{3,2,1,0:T(8,128)(2,1)} %bitcast.24, bf16[4,2,256,2048]{3,2,1,0:T(8,128)(2,1)} %bitcast.25), custom_call_target="tpu_custom_call" | custom-call | flops 469762048 | bytes 12582912 | tf_op jit(solution)/shard_map/pallas_call | solution.py:231
  159.1 3.8 %shard_map.122 = bf16[448,256]{1,0:T(8,128)(2,1)} custom-call(s32[3]{0:T(128)} %pad_add_fusion.at_ref.core_ref, bf16[448,1024]{1,0:T(8,128)(2,1)} %shard_map.117.mine_ref, bf16[448,1024]{1,0:T(8,128)(2,1)} %copy-done.3, bf16[4,2,256,2048]{3,2,1,0:T(8,128)(2,1)} %bitcast.26, bf16[4,2,256,2048]{3,2,1,0:T(8,128)(2,1)} %bitcast.27), custom_call_target="tpu_custom_call" | custom-call | flops 469762048 | bytes 12582912 | tf_op jit(solution)/shard_map/pallas_call | solution.py:231
  162.9 3.8 %shard_map.121 = bf16[448,256]{1,0:T(8,128)(2,1)} custom-call(s32[3]{0:T(128)} %pad_add_fusion.at_ref.core_ref, bf16[448,1024]{1,0:T(8,128)(2,1)} %shard_map.115.mine_ref, bf16[448,1024]{1,0:T(8,128)(2,1)} %copy-done.4, bf16[4,2,256,2048]{3,2,1,0:T(8,128)(2,1)} %bitcast.28, bf16[4,2,256,2048]{3,2,1,0:T(8,128)(2,1)} %bitcast.29), custom_call_target="tpu_custom_call" | custom-call | flops 469762048 | bytes 12582912 | tf_op jit(solution)/shard_map/pallas_call | solution.py:231
  166.6 2.9 %collective-permute-start.26 = (bf16[448,256]{1,0:T(8,128)(2,1)}, bf16[448,256]{1,0:T(8,128)(2,1)S(1)}, u32[]{:S(2)}, u32[]{:S(2)}) collective-permute-start(bf16[448,256]{1,0:T(8,128)(2,1)} %shard_map.121), channel_id=1, source_target_pairs={{0,4},{2,6},{4,0},{6,2},{1,5},{3,7},{5,1},{7,3},{8,12},{10,14},{12... | collective-permute-start | bytes 688136 | tf_op jit(solution)/shard_map/ppermute | solution.py:432
  169.6 3.8 %shard_map.120 = bf16[448,256]{1,0:T(8,128)(2,1)} custom-call(s32[3]{0:T(128)} %pad_add_fusion.at_ref.core_ref, bf16[448,1024]{1,0:T(8,128)(2,1)} %shard_map.117.mine_ref, bf16[448,1024]{1,0:T(8,128)(2,1)} %copy-done.3, bf16[4,2,256,2048]{3,2,1,0:T(8,128)(2,1)} %bitcast.30, bf16[4,2,256,2048]{3,2,1,0:T(8,128)(2,1)} %bitcast.31), custom_call_target="tpu_custom_call" | custom-call | flops 469762048 | bytes 12582912 | tf_op jit(solution)/shard_map/pallas_call | solution.py:231
  174.8 3.8 %shard_map.119 = bf16[448,256]{1,0:T(8,128)(2,1)} custom-call(s32[3]{0:T(128)} %pad_add_fusion.at_ref.core_ref, bf16[448,1024]{1,0:T(8,128)(2,1)} %shard_map.115.mine_ref, bf16[448,1024]{1,0:T(8,128)(2,1)} %copy-done.4, bf16[4,2,256,2048]{3,2,1,0:T(8,128)(2,1)} %bitcast.32, bf16[4,2,256,2048]{3,2,1,0:T(8,128)(2,1)} %bitcast.33), custom_call_target="tpu_custom_call" | custom-call | flops 469762048 | bytes 12582912 | tf_op jit(solution)/shard_map/pallas_call | solution.py:231
  178.6 3.8 %shard_map.118.refs_1_ = bf16[448,256]{1,0:T(8,128)(2,1)} custom-call(s32[3]{0:T(128)} %pad_add_fusion.at_ref.core_ref, bf16[448,1024]{1,0:T(8,128)(2,1)} %shard_map.117.mine_ref, bf16[448,1024]{1,0:T(8,128)(2,1)} %copy-done.3, bf16[4,2,256,2048]{3,2,1,0:T(8,128)(2,1)} %bitcast.34, bf16[4,2,256,2048]{3,2,1,0:T(8,128)(2,1)} %bitcast.35), custom_call_target="tpu_custom_call" | custom-call | flops 469762048 | bytes 12582912 | tf_op jit(solution)/shard_map/pallas_call | solution.py:231
  182.4 3.9 %shard_map.116.refs_0_ = bf16[448,256]{1,0:T(8,128)(2,1)} custom-call(s32[3]{0:T(128)} %pad_add_fusion.at_ref.core_ref, bf16[448,1024]{1,0:T(8,128)(2,1)} %shard_map.115.mine_ref, bf16[448,1024]{1,0:T(8,128)(2,1)} %copy-done.4, bf16[4,2,256,2048]{3,2,1,0:T(8,128)(2,1)} %bitcast.36, bf16[4,2,256,2048]{3,2,1,0:T(8,128)(2,1)} %bitcast.37), custom_call_target="tpu_custom_call" | custom-call | flops 469762048 | bytes 12582912 | tf_op jit(solution)/shard_map/pallas_call | solution.py:231
  186.3 5.4 %collective-permute-done.27.refs_5_ = bf16[448,256]{1,0:T(8,128)(2,1)S(1)} collective-permute-done((bf16[448,256]{1,0:T(8,128)(2,1)}, bf16[448,256]{1,0:T(8,128)(2,1)S(1)}, u32[]{:S(2)}, u32[]{:S(2)}) %collective-permute-start.27) | collective-permute-done | bytes 229408 | tf_op jit(solution)/shard_map/ppermute | solution.py:432
  191.7 3.9 %collective-permute-done.26.refs_4_ = bf16[448,256]{1,0:T(8,128)(2,1)S(1)} collective-permute-done((bf16[448,256]{1,0:T(8,128)(2,1)}, bf16[448,256]{1,0:T(8,128)(2,1)S(1)}, u32[]{:S(2)}, u32[]{:S(2)}) %collective-permute-start.26) | collective-permute-done | bytes 229408 | tf_op jit(solution)/shard_map/ppermute | solution.py:432
  (103 shorter events, 32.8 us)
Async XLA Ops:
  1.0 10.5 %collective-permute-start = (bf16[512,256]{1,0:T(8,128)(2,1)S(1)}, bf16[512,256]{1,0:T(8,128)(2,1)S(1)}, u32[]{:S(2)}, u32[]{:S(2)}) collective-permute-start(bf16[512,256]{1,0:T(8,128)(2,1)S(1)} %constant_dynamic-slice_fusion.1), channel_id=1, source_target_pairs={{0,2},{2,4},{4,6},{1,3},{3,5},{5,7},{8,10},{10,12},{12,14},{9,11},... | collective-permute-start | bytes 786440 | tf_op jit(solution)/shard_map/ppermute | solution.py:285
  5.9 9.7 %collective-permute-start.2 = (bf16[512,256]{1,0:T(8,128)(2,1)S(1)}, bf16[512,256]{1,0:T(8,128)(2,1)S(1)}, u32[]{:S(2)}, u32[]{:S(2)}) collective-permute-start(bf16[512,256]{1,0:T(8,128)(2,1)S(1)} %constant_dynamic-slice_fusion.1), channel_id=1, source_target_pairs={{2,0},{4,2},{6,4},{3,1},{5,3},{7,5},{10,8},{12,10},{14,12},{11,9},... | collective-permute-start | bytes 786440 | tf_op jit(solution)/shard_map/ppermute | solution.py:286
  11.5 7.0 %collective-permute-start.1 = (bf16[512,256]{1,0:T(8,128)(2,1)S(1)}, bf16[512,256]{1,0:T(8,128)(2,1)S(1)}, u32[]{:S(2)}, u32[]{:S(2)}) collective-permute-start(bf16[512,256]{1,0:T(8,128)(2,1)S(1)} %collective-permute-done), channel_id=1, source_target_pairs={{2,4},{4,6},{3,5},{5,7},{10,12},{12,14},{11,13},{13,15},{18,20},{2... | collective-permute-start | bytes 786440 | tf_op jit(solution)/shard_map/ppermute | solution.py:285
  15.6 8.9 %collective-permute-start.3 = (bf16[512,256]{1,0:T(8,128)(2,1)S(1)}, bf16[512,256]{1,0:T(8,128)(2,1)S(1)}, u32[]{:S(2)}, u32[]{:S(2)}) collective-permute-start(bf16[512,256]{1,0:T(8,128)(2,1)S(1)} %collective-permute-done.2), channel_id=1, source_target_pairs={{2,0},{4,2},{3,1},{5,3},{10,8},{12,10},{11,9},{13,11},{18,16},{20,... | collective-permute-start | bytes 786440 | tf_op jit(solution)/shard_map/ppermute | solution.py:286
  24.5 8.3 %collective-permute-start.7 = (bf16[512,256]{1,0:T(8,128)(2,1)S(1)}, bf16[512,256]{1,0:T(8,128)(2,1)S(1)}, u32[]{:S(2)}, u32[]{:S(2)}) collective-permute-start(bf16[512,256]{1,0:T(8,128)(2,1)S(1)} %collective-permute-done.3), channel_id=1, source_target_pairs={{2,0},{3,1},{10,8},{11,9},{18,16},{19,17},{26,24},{27,25}} | collective-permute-start | bytes 786440 | tf_op jit(solution)/shard_map/ppermute | solution.py:286
  25.8 7.0 %collective-permute-start.6 = (bf16[512,256]{1,0:T(8,128)(2,1)S(1)}, bf16[512,256]{1,0:T(8,128)(2,1)S(1)}, u32[]{:S(2)}, u32[]{:S(2)}) collective-permute-start(bf16[512,256]{1,0:T(8,128)(2,1)S(1)} %collective-permute-done.1), channel_id=1, source_target_pairs={{4,6},{5,7},{12,14},{13,15},{20,22},{21,23},{28,30},{29,31}} | collective-permute-start | bytes 786440 | tf_op jit(solution)/shard_map/ppermute | solution.py:285
  26.5 9.3 %collective-permute-start.14 = (bf16[1,512,256]{2,1,0:T(8,128)(2,1)S(1)}, bf16[1,512,256]{2,1,0:T(8,128)(2,1)S(1)}, u32[]{:S(2)}, u32[]{:S(2)}) collective-permute-start(bf16[1,512,256]{2,1,0:T(8,128)(2,1)S(1)} %select_bitcast_fusion.refs_13_), channel_id=1, source_target_pairs={{0,8},{8,0},{16,24},{24,16},{1,9},{9,1},{17,25},{25,17},{2,10},{10... | collective-permute-start | bytes 786440 | tf_op jit(solution)/shard_map/ppermute | solution.py:294
  28.1 22.7 %collective-permute-start.15 = (bf16[1,512,256]{2,1,0:T(8,128)(2,1)S(1)}, bf16[1,512,256]{2,1,0:T(8,128)(2,1)S(1)}, u32[]{:S(2)}, u32[]{:S(2)}) collective-permute-start(bf16[1,512,256]{2,1,0:T(8,128)(2,1)S(1)} %select_bitcast_fusion.refs_13_), channel_id=1, source_target_pairs={{0,16},{8,24},{16,0},{24,8},{1,17},{9,25},{17,1},{25,9},{2,18},{10... | collective-permute-start | bytes 786440 | tf_op jit(solution)/shard_map/ppermute | solution.py:294
  29.6 21.8 %collective-permute-start.16 = (bf16[1,512,256]{2,1,0:T(8,128)(2,1)S(1)}, bf16[1,512,256]{2,1,0:T(8,128)(2,1)S(1)}, u32[]{:S(2)}, u32[]{:S(2)}) collective-permute-start(bf16[1,512,256]{2,1,0:T(8,128)(2,1)S(1)} %select_bitcast_fusion.refs_13_), channel_id=1, source_target_pairs={{0,24},{8,16},{16,8},{24,0},{1,25},{9,17},{17,9},{25,1},{2,26},{10... | collective-permute-start | bytes 786440 | tf_op jit(solution)/shard_map/ppermute | solution.py:294
  32.9 32.2 %collective-permute-start.8 = (bf16[2,512,256]{2,1,0:T(8,128)(2,1)S(1)}, bf16[2,512,256]{2,1,0:T(8,128)(2,1)S(1)}, u32[]{:S(2)}, u32[]{:S(2)}) collective-permute-start(bf16[2,512,256]{2,1,0:T(8,128)(2,1)S(1)} %pad_maximum_fusion.refs_17_), channel_id=1, source_target_pairs={{0,24},{8,16},{16,8},{24,0},{1,25},{9,17},{17,9},{25,1},{2,26},{10... | collective-permute-start | bytes 1572872 | tf_op jit(solution)/shard_map/ppermute | solution.py:294
  35.4 29.1 %collective-permute-start.5 = (bf16[896,256]{1,0:T(8,128)(2,1)S(1)}, bf16[896,256]{1,0:T(8,128)(2,1)}, u32[]{:S(2)}, u32[]{:S(2)}) collective-permute-start(bf16[896,256]{1,0:T(8,128)(2,1)S(1)} %get-tuple-element.37), channel_id=1, source_target_pairs={{0,4},{2,6},{4,0},{6,2},{1,5},{3,7},{5,1},{7,3},{8,12},{10,14},{12... | collective-permute-start | bytes 1376264 | tf_op jit(solution)/shard_map/ppermute | solution.py:297
  35.8 29.8 %collective-permute-start.4 = (bf16[896,256]{1,0:T(8,128)(2,1)S(1)}, bf16[896,256]{1,0:T(8,128)(2,1)}, u32[]{:S(2)}, u32[]{:S(2)}) collective-permute-start(bf16[896,256]{1,0:T(8,128)(2,1)S(1)} %get-tuple-element.36), channel_id=1, source_target_pairs={{0,2},{2,4},{4,6},{6,0},{1,3},{3,5},{5,7},{7,1},{8,10},{10,12},{12... | collective-permute-start | bytes 1376264 | tf_op jit(solution)/shard_map/ppermute | solution.py:297
  50.8 18.6 %collective-permute-start.9 = (bf16[896,256]{1,0:T(8,128)(2,1)S(1)}, bf16[896,256]{1,0:T(8,128)(2,1)}, u32[]{:S(2)}, u32[]{:S(2)}) collective-permute-start(bf16[896,256]{1,0:T(8,128)(2,1)S(1)} %get-tuple-element.41), channel_id=1, source_target_pairs={{0,6},{2,0},{4,2},{6,4},{1,7},{3,1},{5,3},{7,5},{8,14},{10,8},{12,... | collective-permute-start | bytes 1376264 | tf_op jit(solution)/shard_map/ppermute | solution.py:297
  51.4 17.9 %collective-permute-start.10 = (bf16[896,256]{1,0:T(8,128)(2,1)S(1)}, bf16[896,256]{1,0:T(8,128)(2,1)S(1)}, u32[]{:S(2)}, u32[]{:S(2)}) collective-permute-start(bf16[896,256]{1,0:T(8,128)(2,1)S(1)} %get-tuple-element.42), channel_id=1, source_target_pairs={{0,1},{1,0},{2,3},{3,2},{4,5},{5,4},{6,7},{7,6},{8,9},{9,8},{10,11... | collective-permute-start | bytes 1376264 | tf_op jit(solution)/shard_map/ppermute | solution.py:302
  64.6 13.8 %collective-permute-start.17 = (bf16[2,512,256]{2,1,0:T(8,128)(2,1)S(1)}, bf16[2,512,256]{2,1,0:T(8,128)(2,1)S(1)}, u32[]{:S(2)}, u32[]{:S(2)}) collective-permute-start(bf16[2,512,256]{2,1,0:T(8,128)(2,1)S(1)} %pad_maximum_fusion.refs_17_), channel_id=1, source_target_pairs={{0,8},{8,0},{16,24},{24,16},{1,9},{9,1},{17,25},{25,17},{2,10},{10... | collective-permute-start | bytes 1572872 | tf_op jit(solution)/shard_map/ppermute | solution.py:294
  65.1 13.6 %collective-permute-start.18 = (bf16[2,512,256]{2,1,0:T(8,128)(2,1)S(1)}, bf16[2,512,256]{2,1,0:T(8,128)(2,1)}, u32[]{:S(2)}, u32[]{:S(2)}) collective-permute-start(bf16[2,512,256]{2,1,0:T(8,128)(2,1)S(1)} %pad_maximum_fusion.refs_17_), channel_id=1, source_target_pairs={{0,16},{8,24},{16,0},{24,8},{1,17},{9,25},{17,1},{25,9},{2,18},{10... | collective-permute-start | bytes 1572872 | tf_op jit(solution)/shard_map/ppermute | solution.py:294
  65.6 13.1 %collective-permute-start.11 = (bf16[896,256]{1,0:T(8,128)(2,1)}, bf16[896,256]{1,0:T(8,128)(2,1)S(1)}, u32[]{:S(2)}, u32[]{:S(2)}) collective-permute-start(bf16[896,256]{1,0:T(8,128)(2,1)} %collective-permute-done.4.refs_1_), channel_id=1, source_target_pairs={{0,1},{1,0},{2,3},{3,2},{4,5},{5,4},{6,7},{7,6},{8,9},{9,8},{10,11... | collective-permute-start | bytes 1376264 | tf_op jit(solution)/shard_map/ppermute | solution.py:302
  69.3 9.3 %collective-permute-start.13 = (bf16[896,256]{1,0:T(8,128)(2,1)}, bf16[896,256]{1,0:T(8,128)(2,1)S(1)}, u32[]{:S(2)}, u32[]{:S(2)}) collective-permute-start(bf16[896,256]{1,0:T(8,128)(2,1)} %collective-permute-done.9.refs_3_), channel_id=1, source_target_pairs={{0,1},{1,0},{2,3},{3,2},{4,5},{5,4},{6,7},{7,6},{8,9},{9,8},{10,11... | collective-permute-start | bytes 1376264 | tf_op jit(solution)/shard_map/ppermute | solution.py:302
  70.2 8.6 %collective-permute-start.12 = (bf16[896,256]{1,0:T(8,128)(2,1)}, bf16[896,256]{1,0:T(8,128)(2,1)S(1)}, u32[]{:S(2)}, u32[]{:S(2)}) collective-permute-start(bf16[896,256]{1,0:T(8,128)(2,1)} %collective-permute-done.5.refs_2_), channel_id=1, source_target_pairs={{0,1},{1,0},{2,3},{3,2},{4,5},{5,4},{6,7},{7,6},{8,9},{9,8},{10,11... | collective-permute-start | bytes 1376264 | tf_op jit(solution)/shard_map/ppermute | solution.py:302
  95.0 16.3 %all-to-all-start = ((bf16[4,2,160,128]{3,2,1,0:T(8,128)(2,1)}), bf16[4,2,160,128]{3,2,1,0:T(8,128)(2,1)S(1)}, u32[]{:S(2)}, u32[]{:S(2)}) async-start(bf16[4,2,160,128]{3,2,1,0:T(8,128)(2,1)} %bitcast.42), calls=%async_computation | async-start | bytes 655360 | tf_op jit(solution)/shard_map/all_to_all | solution.py:372
  111.4 9.9 %collective-permute-start.19 = (bf16[2,160,128]{2,1,0:T(8,128)(2,1)S(1)}, bf16[2,160,128]{2,1,0:T(8,128)(2,1)S(1)}, u32[]{:S(2)}, u32[]{:S(2)}) collective-permute-start(bf16[2,160,128]{2,1,0:T(8,128)(2,1)S(1)} %reduce_sum.12), channel_id=1, source_target_pairs={{0,8},{8,0},{16,24},{24,16},{1,9},{9,1},{17,25},{25,17},{2,10},{10... | collective-permute-start | bytes 245768 | tf_op jit(solution)/shard_map/ppermute | solution.py:376
  112.9 8.3 %collective-permute-start.20 = (bf16[2,160,128]{2,1,0:T(8,128)(2,1)S(1)}, bf16[2,160,128]{2,1,0:T(8,128)(2,1)S(1)}, u32[]{:S(2)}, u32[]{:S(2)}) collective-permute-start(bf16[2,160,128]{2,1,0:T(8,128)(2,1)S(1)} %reduce_sum.12), channel_id=1, source_target_pairs={{0,16},{8,24},{16,0},{24,8},{1,17},{9,25},{17,1},{25,9},{2,18},{10... | collective-permute-start | bytes 245768 | tf_op jit(solution)/shard_map/ppermute | solution.py:376
  113.4 7.8 %collective-permute-start.21 = (bf16[2,160,128]{2,1,0:T(8,128)(2,1)S(1)}, bf16[2,160,128]{2,1,0:T(8,128)(2,1)S(1)}, u32[]{:S(2)}, u32[]{:S(2)}) collective-permute-start(bf16[2,160,128]{2,1,0:T(8,128)(2,1)S(1)} %reduce_sum.12), channel_id=1, source_target_pairs={{0,24},{8,16},{16,8},{24,0},{1,25},{9,17},{17,9},{25,1},{2,26},{10... | collective-permute-start | bytes 245768 | tf_op jit(solution)/shard_map/ppermute | solution.py:376
  123.8 12.3 %all-to-all-start.1 = ((bf16[4,2,160,128]{3,2,1,0:T(8,128)(2,1)}), bf16[4,2,160,128]{3,2,1,0:T(8,128)(2,1)S(1)}, u32[]{:S(2)}, u32[]{:S(2)}) async-start(bf16[4,2,160,128]{3,2,1,0:T(8,128)(2,1)} %shard_map.113), calls=%async_computation.1 | async-start | bytes 655360 | tf_op jit(solution)/shard_map/all_to_all | solution.py:385
  141.1 4.7 %collective-permute-start.23 = (bf16[448,1024]{1,0:T(8,128)(2,1)}, bf16[448,1024]{1,0:T(8,128)(2,1)S(1)}, u32[]{:S(2)}, u32[]{:S(2)}) collective-permute-start(bf16[448,1024]{1,0:T(8,128)(2,1)} %shard_map.117.mine_ref), channel_id=1, source_target_pairs={{0,1},{1,0},{2,3},{3,2},{4,5},{5,4},{6,7},{7,6},{8,9},{9,8},{10,11... | collective-permute-start | bytes 2752520 | tf_op jit(solution)/shard_map/ppermute | solution.py:427
  145.2 8.6 %collective-permute-start.22 = (bf16[448,1024]{1,0:T(8,128)(2,1)}, bf16[448,1024]{1,0:T(8,128)(2,1)S(1)}, u32[]{:S(2)}, u32[]{:S(2)}) collective-permute-start(bf16[448,1024]{1,0:T(8,128)(2,1)} %shard_map.115.mine_ref), channel_id=1, source_target_pairs={{0,1},{1,0},{2,3},{3,2},{4,5},{5,4},{6,7},{7,6},{8,9},{9,8},{10,11... | collective-permute-start | bytes 2752520 | tf_op jit(solution)/shard_map/ppermute | solution.py:427
  150.5 28.1 %collective-permute-start.29 = (bf16[448,256]{1,0:T(8,128)(2,1)}, bf16[448,256]{1,0:T(8,128)(2,1)S(1)}, u32[]{:S(2)}, u32[]{:S(2)}) collective-permute-start(bf16[448,256]{1,0:T(8,128)(2,1)} %shard_map.124), channel_id=1, source_target_pairs={{0,6},{2,0},{4,2},{6,4},{1,7},{3,1},{5,3},{7,5},{8,14},{10,8},{12,... | collective-permute-start | bytes 688136 | tf_op jit(solution)/shard_map/ppermute | solution.py:432
  158.5 27.8 %collective-permute-start.28 = (bf16[448,256]{1,0:T(8,128)(2,1)}, bf16[448,256]{1,0:T(8,128)(2,1)S(1)}, u32[]{:S(2)}, u32[]{:S(2)}) collective-permute-start(bf16[448,256]{1,0:T(8,128)(2,1)} %shard_map.123), channel_id=1, source_target_pairs={{0,6},{2,0},{4,2},{6,4},{1,7},{3,1},{5,3},{7,5},{8,14},{10,8},{12,... | collective-permute-start | bytes 688136 | tf_op jit(solution)/shard_map/ppermute | solution.py:432
  162.9 28.8 %collective-permute-start.27 = (bf16[448,256]{1,0:T(8,128)(2,1)}, bf16[448,256]{1,0:T(8,128)(2,1)S(1)}, u32[]{:S(2)}, u32[]{:S(2)}) collective-permute-start(bf16[448,256]{1,0:T(8,128)(2,1)} %shard_map.122), channel_id=1, source_target_pairs={{0,4},{2,6},{4,0},{6,2},{1,5},{3,7},{5,1},{7,3},{8,12},{10,14},{12... | collective-permute-start | bytes 688136 | tf_op jit(solution)/shard_map/ppermute | solution.py:432
  166.6 28.9 %collective-permute-start.26 = (bf16[448,256]{1,0:T(8,128)(2,1)}, bf16[448,256]{1,0:T(8,128)(2,1)S(1)}, u32[]{:S(2)}, u32[]{:S(2)}) collective-permute-start(bf16[448,256]{1,0:T(8,128)(2,1)} %shard_map.121), channel_id=1, source_target_pairs={{0,4},{2,6},{4,0},{6,2},{1,5},{3,7},{5,1},{7,3},{8,12},{10,14},{12... | collective-permute-start | bytes 688136 | tf_op jit(solution)/shard_map/ppermute | solution.py:432
  173.3 22.2 %collective-permute-start.25 = (bf16[448,256]{1,0:T(8,128)(2,1)}, bf16[448,256]{1,0:T(8,128)(2,1)S(1)}, u32[]{:S(2)}, u32[]{:S(2)}) collective-permute-start(bf16[448,256]{1,0:T(8,128)(2,1)} %shard_map.120), channel_id=1, source_target_pairs={{0,2},{2,4},{4,6},{6,0},{1,3},{3,5},{5,7},{7,1},{8,10},{10,12},{12... | collective-permute-start | bytes 688136 | tf_op jit(solution)/shard_map/ppermute | solution.py:432
  178.6 16.9 %collective-permute-start.24 = (bf16[448,256]{1,0:T(8,128)(2,1)}, bf16[448,256]{1,0:T(8,128)(2,1)S(1)}, u32[]{:S(2)}, u32[]{:S(2)}) collective-permute-start(bf16[448,256]{1,0:T(8,128)(2,1)} %shard_map.119), channel_id=1, source_target_pairs={{0,2},{2,4},{4,6},{6,0},{1,3},{3,5},{5,7},{7,1},{8,10},{10,12},{12... | collective-permute-start | bytes 688136 | tf_op jit(solution)/shard_map/ppermute | solution.py:432
  (22 other events, 244.9 us)

commit v6 on v5

--- a/solution.py
+++ b/solution.py
@@ -65,12 +65,11 @@
     rest = refs[2 * layers + 5 :]
     weights, rest = rest[:-10], rest[-10:]
     q_ref, k_ref, v_ref, early_ref, total_ref, row_ref, narrow_ref, w_ref, phi_ref, sems = rest
-    inner, outer = weights[: len(weights) // 2], weights[len(weights) // 2 :]
     core, layer, slab = at_ref[0], at_ref[1], at_ref[2]
     both, width = other[0].shape
     rows = both // 2
     model = row_ref.shape[1]
-    part = inner[0].shape[-2]
+    part = weights[0].shape[-2]
     block = v_ref.shape[2] // layers
     narrow = wq_ref.shape[1]
     copies = []
@@ -83,12 +82,11 @@
     fetch(-1, wk_ref, narrow_ref.at[:, pl.ds(narrow, narrow)])
     fetch(0, own_ref, w_ref.at[0, :, pl.ds(0, block)])
     for d in range(1, layers):
-        group, index = (outer, 0 if d == 1 else 1) if d in (1, layers - 1) else (inner, d - 2)
         for m in range(model // part):
             if gathered:
-                source, start = group[0].at[m, index], m * part
+                source, start = weights[0].at[m, d - 1], m * part
             else:
-                source, start = group[m].at[index], pl.multiple_of((slab ^ m) * part, part)
+                source, start = weights[m].at[d - 1], pl.multiple_of((slab ^ m) * part, part)
             fetch(d, source, w_ref.at[d // 2, pl.ds(start, part), pl.ds((d % 2) * block, block)])
 
     def arrived(slots):
@@ -138,33 +136,35 @@
                         total_ref[head] = (first.pop(0) + state).astype(BF16)
 
 
-def local_kernel(
-    core_ref, per_group, offset, q_ref, k_ref, v_ref, early_ref, ta_ref, tb_ref, bias_ref, num_ref, phi_ref
-):
+def local_kernel(core_ref, per_group, offset, q_ref, k_ref, v_ref, early_ref, table_ref, bias_ref, num_ref, phi_ref):
     chunk = pl.program_id(0)
     step = pl.program_id(1) + offset
     rows = q_ref.shape[1]
-    half = rows // 2
+    cut = LANES * -(-rows // (2 * LANES))
+    wide = table_ref.shape[2] // 2
     for i in range(per_group):
         head = (2 * step + core_ref[0]) * per_group + i
         lanes = pl.multiple_of((head // HELD) * LANES, LANES)
         place = lax.rem(head, HELD)
         query = q_ref[0, :, pl.ds(lanes, LANES)]
         key = k_ref[0, :, pl.ds(lanes, LANES)]
-        left = dot(query, ta_ref[place]) + bias_ref[0:1]
-        right = dot(query, tb_ref[place]) + bias_ref[1:2]
-        phi_ref[0, i] = (left * right).astype(BF16)
+        sides = dot(query, table_ref[place]) + bias_ref[...]
+        phi_ref[0, i] = (sides[:, :PACKED] * sides[:, wide : wide + PACKED]).astype(BF16)
         lane = lax.broadcasted_iota(jnp.int32, (rows, LANES), 1)
         mine = jnp.where(lane // FEAT == place, query * jnp.asarray(0.25, BF16), jnp.zeros_like(query))
         columns = slice(i * HEAD_DIM, (i + 1) * HEAD_DIM)
-        for low in (0, half):
-            seen = low + half
-            s = dot(mine[low:seen], key[:seen], NT)
-            weight = 1.0 + s + 0.5 * s * s
-            t_at = lax.broadcasted_iota(jnp.int32, (half, seen), 0) + low
-            j_at = lax.broadcasted_iota(jnp.int32, (half, seen), 1)
-            weight = jnp.where(t_at >= j_at, weight, 0.0).astype(BF16)
-            num_ref[0, low:seen, columns] = dot(weight, v_ref[0, :seen, columns])
+        for low, high in ((0, cut), (cut, rows)):
+            span = high - low
+            s = dot(mine[low:high], key[low:high], NT)
+            t_at = lax.broadcasted_iota(jnp.int32, (span, span), 0)
+            j_at = lax.broadcasted_iota(jnp.int32, (span, span), 1)
+            weight = jnp.where(t_at >= j_at, (0.5 * s + 1.0) * s + 1.0, 0.0).astype(BF16)
+            num = dot(weight, v_ref[0, low:high, columns])
+            if low > 0:
+                s = dot(mine[low:high], key[:low], NT)
+                weight = ((0.5 * s + 1.0) * s + 1.0).astype(BF16)
+                num = num + dot(weight, v_ref[0, :low, columns])
+            num_ref[0, low:high, columns] = num
 
         @pl.when(chunk == 1)
         def _():
@@ -186,22 +186,25 @@
     parts, out_ref = refs[:-1], refs[-1]
     numbers, features = parts[: len(parts) // 2], parts[len(parts) // 2 :]
     held = features[0].shape[1]
+    ones = jnp.full((HEAD_DIM, HEAD_DIM), 1.0 / HEAD_DIM, BF16)
     for i in range(held * len(features)):
         columns = slice(i * HEAD_DIM, (i + 1) * HEAD_DIM)
         at = (i % held) * HEAD_DIM
         num = numbers[i // held][0, :, at : at + HEAD_DIM]
         num = num + dot(features[i // held][0, i % held], state_ref[i])
-        mean_square = jnp.mean(num * num, axis=1, keepdims=True)
+        mean_square = dot((num * num).astype(BF16), ones)
         hidden = num * lax.rsqrt(mean_square + 1e-05) * gain_ref[:, columns]
         out_ref[:, columns] = hidden.astype(BF16)
 
 
-def output_kernel(at_ref, mine_ref, other_ref, w_mine, w_other, out_ref):
-    depth = mine_ref.shape[1]
-    width = out_ref.shape[1]
-    part = dot(mine_ref[...], w_mine[...].reshape(depth, width))
-    part = part + dot(other_ref[...], w_other[...].reshape(depth, width))
-    out_ref[...] = part.astype(BF16)
+def output_kernel(at_ref, mine_ref, other_ref, *refs):
+    outs = refs[len(refs) * 2 // 3 :]
+    weights = [w[...].reshape(mine_ref.shape[1], -1) for w in refs[: 2 * len(outs)]]
+    width = weights[0].shape[1]
+    part = dot(mine_ref[...], jnp.concatenate(weights[0::2], axis=1))
+    part = part + dot(other_ref[...], jnp.concatenate(weights[1::2], axis=1))
+    for i, out_ref in enumerate(outs):
+        out_ref[...] = part[:, i * width : (i + 1) * width].astype(BF16)
 
 
 def place_kernel(at_ref, *refs):
@@ -265,9 +268,14 @@
     key_table = jnp.asarray(np.concatenate(sides, axis=1), BF16)
     repeat = HELD // 2
     key_bias = jnp.asarray(np.stack([np.tile(first_bias, repeat), np.tile(second_bias, repeat)], axis=1))
-    query_a = jnp.asarray(placed(first * scale), BF16)
-    query_b = jnp.asarray(placed(second), BF16)
-    query_bias = jnp.asarray(np.stack([first_bias * scale, second_bias]))
+    wide = 2 * LANES
+    query_table = np.zeros((HELD, LANES, 2 * wide), np.float32)
+    query_bias = np.zeros((1, 2 * wide), np.float32)
+    query_table[:, :, :PACKED] = placed(first * scale)
+    query_table[:, :, wide : wide + PACKED] = placed(second)
+    query_bias[0, :PACKED] = first_bias * scale
+    query_bias[0, wide : wide + PACKED] = second_bias
+    query_table, query_bias = jnp.asarray(query_table, BF16), jnp.asarray(query_bias)
     gain_mine = lax.dynamic_index_in_dim(gain.reshape(layers, 2, value_width), core, 1, False)
     gain_mine = gain_mine.reshape(1, layers * value_width)
 
@@ -284,23 +292,17 @@
     for k in range(1, layers):
         up[k] = lax.ppermute(up[k - 1], "z", [(z, z + 1) for z in range(k - 1, layers - 1)])
         down[k] = lax.ppermute(down[k - 1], "z", [(z, z - 1) for z in range(1, layers - k + 1)])
-        if k == layers - 2:
-            up[k], down[k], sent = lax.optimization_barrier((up[k], down[k], sent))
-    slot = lambda d: jnp.where(layer + d < layers, down[d], up[layers - d])
-
-    def to_lines(chosen):
-        stack = jnp.stack([slot(d) for d in chosen])
-        if slabs == 4:
-            return [stack] + [lax.ppermute(stack, "seq", flip(m)) for m in range(1, slabs)]
-        return [lax.all_gather(stack, "seq", axis=0, tiled=False)]
-
-    mine = [sent[0]] + [lax.ppermute(sent[d], "z", turn(d)) for d in range(1, layers)]
-    inner = to_lines(range(2, layers - 1))
-    outer = to_lines((1, layers - 1))
+    stack = jnp.stack([jnp.where(layer + d < layers, down[d], up[layers - d]) for d in range(1, layers)])
+    stack, sent = lax.optimization_barrier((stack, sent))
+    if slabs == 4:
+        weights = [stack] + [lax.ppermute(stack, "seq", flip(m)) for m in range(1, slabs)]
+    else:
+        weights = [lax.all_gather(stack, "seq", axis=0, tiled=False)]
     far = layers // 2
-    mine[far], outer[-1] = lax.optimization_barrier((mine[far], outer[-1]))
+    mine = {d: lax.ppermute(sent[d], "z", turn(d)) for d in [far] + [d for d in range(1, layers) if d != far]}
+    mine = [sent[0]] + [mine[d] for d in range(1, layers)]
+    mine[far], weights[1:] = lax.optimization_barrier((mine[far], weights[1:]))
     other = [lax.ppermute(piece, "core", swap) for piece in mine]
-    weights = inner + outer
 
     query, key, value, early, total = call(
         lambda at_ref, *refs: project_kernel(at_ref, per_group, layers, slabs != 4, *refs),
@@ -352,9 +354,8 @@
                 pl.BlockSpec((1, rows, narrow), lambda c, i, _: (c, 0, 0)),
                 pl.BlockSpec((1, rows, value_width), lambda c, i, _: (c, 0, i + offset)),
                 pl.BlockSpec((per_group, PACKED, HEAD_DIM), lambda c, i, _: (i + offset, 0, 0)),
-                whole((HELD, LANES, PACKED)),
-                whole((HELD, LANES, PACKED)),
-                whole((2, PACKED)),
+                whole(query_table.shape),
+                whole(query_bias.shape),
             ],
             [
                 pl.BlockSpec((1, rows, value_width), lambda c, i, _: (c, 0, i)),
@@ -364,7 +365,7 @@
                 jax.ShapeDtypeStruct((2, rows, some_layers * value_width), F32),
                 jax.ShapeDtypeStruct((2, heads // parts, rows, PACKED), BF16),
             ],
-            (query, key, value, early, query_a, query_b, query_bias),
+            (query, key, value, early, query_table, query_bias),
             heads * rows * rows * 300,
         )
 
@@ -405,33 +406,33 @@
 
     w_rows = w_out.reshape(layers, 2, value_width, model)
 
-    def project_out(kept, received, d):
-        columns = lambda at: 2 * lax.rem(at[1] + d, layers) + at[0]
+    def project_out(kept, received, to):
+        block = (layers, 1, value_width, width)
+        specs = []
+        for d in to:
+            columns = lambda at, d=d: 2 * lax.rem(at[1] + d, layers) + at[0]
+            specs.append(pl.BlockSpec(block, lambda i, at, columns=columns: (0, at[0], 0, columns(at))))
+            specs.append(pl.BlockSpec(block, lambda i, at, columns=columns: (0, 1 - at[0], 0, columns(at))))
         return call(
             output_kernel,
             at,
             (1,),
-            [
-                whole((rows, heads * HEAD_DIM)),
-                whole((rows, heads * HEAD_DIM)),
-                pl.BlockSpec((layers, 1, value_width, width), lambda i, at: (0, at[0], 0, columns(at))),
-                pl.BlockSpec((layers, 1, value_width, width), lambda i, at: (0, 1 - at[0], 0, columns(at))),
-            ],
-            whole((rows, width)),
-            jax.ShapeDtypeStruct((rows, width), BF16),
-            (kept, received, w_rows, w_rows),
-            2 * rows * model * width,
+            [whole((rows, heads * HEAD_DIM))] * 2 + specs,
+            [whole((rows, width))] * len(to),
+            [jax.ShapeDtypeStruct((rows, width), BF16)] * len(to),
+            (kept, received, *[w_rows] * len(specs)),
+            2 * rows * model * width * len(to),
         )
 
     kept = [hidden(chunk) for chunk in range(2)]
     received = [lax.ppermute(half, "core", swap) for half in kept]
+    order = [far] + [d for d in range(1, layers) if d != far] + [0]
     pieces = {}
-    for chunk in range(2):
-        for d in range(1, layers):
-            piece = project_out(kept[chunk], received[chunk], d)
-            pieces[d, chunk] = lax.ppermute(piece, "z", turn(d))
-    for chunk in range(2):
-        pieces[0, chunk] = project_out(kept[chunk], received[chunk], 0)
+    for start in range(0, layers, 2):
+        to = order[start : start + 2]
+        for chunk in range(2):
+            for d, piece in zip(to, project_out(kept[chunk], received[chunk], to)):
+                pieces[d, chunk] = lax.ppermute(piece, "z", turn(d)) if d else piece
     return call(
         place_kernel,
         at,

time: 200 us -> 197 us (0.985)
  Pallas kernels: 82.3 us -> 74.5 us
  waiting for transfers between devices: 63 us -> 70.1 us
  starting transfers between devices: 42 us -> 39.8 us
    ppermute x3, waiting for transfers between devices: 16.8 us -> 31.2 us  [per_device(): lax.ppermute(sent[d], 'z', turn(d))]
    ppermute x12 -> x9, waiting for transfers between devices: 29.3 us -> 15.4 us  [the longest x6 15.4 us: per_device(): pieces[d, chunk] = lax.ppermute(piece, 'z', turn(d)) if d else piece]
    pallas_call x16 -> x12, Pallas kernels: 80.4 us -> 72.6 us  [call(): pl.pallas_call(kernel, grid_spec=pltpu.PrefetchScalarGridSpec(num_scalar_...]
    ppermute x3, waiting for transfers between devices: 12.1 us -> 15.7 us  [per_device(): lax.ppermute(down[k - 1], 'z', [(z, z - 1) for z in range(1, layers - k +...]
    ppermute x12 -> x9, starting transfers between devices: 15.4 us -> 12.3 us  [the longest x6 8.77 us: per_device(): pieces[d, chunk] = lax.ppermute(piece, 'z', turn(d)) if d else piece]
    all_to_all x1, starting transfers between devices: 3.65 us -> 6.24 us  [per_device(): line = lax.all_to_all(own, 'z', split_axis=0, concat_axis=0, tiled=True)]
    ppermute x3, starting transfers between devices: 3.33 us -> 1.33 us  [per_device(): lax.ppermute(sent[d], 'z', turn(d))]
    unnamed x44 -> x36, local copies, waits for them, and re-layouts: 6.7 us -> 6.01 us
  transfers between devices with their start and end apart: 32 -> 29, of which waited for: 13 -> 11; matrix products, arithmetic and copies ran while one was open for 2% -> 1% of each run, Pallas kernels for 30% -> 26%
where the time goes in v6:
time: 197 us; the launch traced here: 195 us
  Pallas kernels  74.5 us (38%)
  waiting for transfers between devices  70.1 us (36%)
  starting transfers between devices  39.8 us (20%)
  local copies, waits for them, and re-layouts  9.15 us (5%)
    pallas_call x12, Pallas kernels, call(): pl.pallas_call(kernel, grid_spec=pltpu.PrefetchScalarGridSpec(num_scalar_...  72.6 us
    ppermute x3, waiting for transfers between devices, per_device(): lax.ppermute(sent[d], 'z', turn(d))  31.2 us
    ppermute x3, waiting for transfers between devices, per_device(): lax.ppermute(down[k - 1], 'z', [(z, z - 1) for z in range(1, layers - k +...  15.7 us
    ppermute x6, waiting for transfers between devices, per_device(): pieces[d, chunk] = lax.ppermute(piece, 'z', turn(d)) if d else piece  15.4 us
    ppermute x6, starting transfers between devices, per_device(): pieces[d, chunk] = lax.ppermute(piece, 'z', turn(d)) if d else piece  8.77 us
    ppermute x3, starting transfers between devices, per_device(): lax.ppermute(up[k - 1], 'z', [(z, z + 1) for z in range(k - 1, layers - 1)])  6.29 us
    all_to_all x1, starting transfers between devices, per_device(): line = lax.all_to_all(own, 'z', split_axis=0, concat_axis=0, tiled=True)  6.24 us
    unnamed x36, local copies, waits for them, and re-layouts  6.01 us
  transfers between devices with their start and end apart: 29, of which 11 were waited for; matrix products, arithmetic and copies ran while one was open for 1% of the time, Pallas kernels for 26%

profile of v6, /device:TPU:0, one launch (start us, length us, event | category | flops | bytes accessed | tf_op | source)
XLA Modules:
  0.0 195.0 jit_solution(895636938393377728)
XLA Ops:
  1.0 4.9 %collective-permute-start.1 = (bf16[512,256]{1,0:T(8,128)(2,1)S(1)}, bf16[512,256]{1,0:T(8,128)(2,1)S(1)}, u32[]{:S(2)}, u32[]{:S(2)}) collective-permute-start(bf16[512,256]{1,0:T(8,128)(2,1)S(1)} %constant_dynamic-slice_fusion.1), channel_id=1, source_target_pairs={{0,2},{2,4},{4,6},{1,3},{3,5},{5,7},{8,10},{10,12},{12,14},{9,11},... | collective-permute-start | bytes 786440 | tf_op jit(solution)/shard_map/ppermute | solution.py:293
  7.2 4.2 %collective-permute-done.1 = bf16[512,256]{1,0:T(8,128)(2,1)S(1)} collective-permute-done((bf16[512,256]{1,0:T(8,128)(2,1)S(1)}, bf16[512,256]{1,0:T(8,128)(2,1)S(1)}, u32[]{:S(2)}, u32[]{:S(2)}) %collective-permute-start.1) | collective-permute-done | bytes 262176 | tf_op jit(solution)/shard_map/ppermute | solution.py:293
  12.1 3.5 %collective-permute-done = bf16[512,256]{1,0:T(8,128)(2,1)S(1)} collective-permute-done((bf16[512,256]{1,0:T(8,128)(2,1)S(1)}, bf16[512,256]{1,0:T(8,128)(2,1)S(1)}, u32[]{:S(2)}, u32[]{:S(2)}) %collective-permute-start) | collective-permute-done | bytes 262176 | tf_op jit(solution)/shard_map/ppermute | solution.py:294
  17.6 1.6 dynamic-slice_bitcast_fusion
  19.2 5.3 %collective-permute-done.4 = bf16[512,256]{1,0:T(8,128)(2,1)S(1)} collective-permute-done((bf16[512,256]{1,0:T(8,128)(2,1)S(1)}, bf16[512,256]{1,0:T(8,128)(2,1)S(1)}, u32[]{:S(2)}, u32[]{:S(2)}) %collective-permute-start.4) | collective-permute-done | bytes 262176 | tf_op jit(solution)/shard_map/ppermute | solution.py:294
  25.9 6.9 %collective-permute-done.5 = bf16[512,256]{1,0:T(8,128)(2,1)S(1)} collective-permute-done((bf16[512,256]{1,0:T(8,128)(2,1)S(1)}, bf16[512,256]{1,0:T(8,128)(2,1)S(1)}, u32[]{:S(2)}, u32[]{:S(2)}) %collective-permute-start.5) | collective-permute-done | bytes 262176 | tf_op jit(solution)/shard_map/ppermute | solution.py:294
  33.0 2.5 %collective-permute-start.10 = (bf16[3,512,256]{2,1,0:T(8,128)(2,1)S(1)}, bf16[3,512,256]{2,1,0:T(8,128)(2,1)S(1)}, u32[]{:S(2)}, u32[]{:S(2)}) collective-permute-start(bf16[3,512,256]{2,1,0:T(8,128)(2,1)S(1)} %pad_maximum_fusion.refs_13_), channel_id=1, source_target_pairs={{0,24},{8,16},{16,8},{24,0},{1,25},{9,17},{17,9},{25,1},{2,26},{10... | collective-permute-start | bytes 2359304 | tf_op jit(solution)/shard_map/ppermute | solution.py:298
  37.8 10.6 %collective-permute-done.6.refs_1_ = bf16[896,256]{1,0:T(8,128)(2,1)} collective-permute-done((bf16[896,256]{1,0:T(8,128)(2,1)S(1)}, bf16[896,256]{1,0:T(8,128)(2,1)}, u32[]{:S(2)}, u32[]{:S(2)}) %collective-permute-start.6) | collective-permute-done | bytes 458784 | tf_op jit(solution)/shard_map/ppermute | solution.py:302
  48.4 15.4 %collective-permute-done.7.refs_2_ = bf16[896,256]{1,0:T(8,128)(2,1)} collective-permute-done((bf16[896,256]{1,0:T(8,128)(2,1)S(1)}, bf16[896,256]{1,0:T(8,128)(2,1)}, u32[]{:S(2)}, u32[]{:S(2)}) %collective-permute-start.7) | collective-permute-done | bytes 458784 | tf_op jit(solution)/shard_map/ppermute | solution.py:302
  63.8 5.2 %collective-permute-done.11.refs_3_ = bf16[896,256]{1,0:T(8,128)(2,1)S(1)} collective-permute-done((bf16[896,256]{1,0:T(8,128)(2,1)S(1)}, bf16[896,256]{1,0:T(8,128)(2,1)S(1)}, u32[]{:S(2)}, u32[]{:S(2)}) %collective-permute-start.11) | collective-permute-done | bytes 458784 | tf_op jit(solution)/shard_map/ppermute | solution.py:302
  73.5 14.8 %shard_map.100 = (bf16[2,448,256]{2,1,0:T(8,128)(2,1)}, bf16[2,448,256]{2,1,0:T(8,128)(2,1)}, bf16[2,448,1024]{2,1,0:T(8,128)(2,1)}, bf16[8,160,128]{2,1,0:T(8,128)(2,1)}, bf16[8,160,128]{2,1,0:T(8,128)(2,1)}) custom-call(s32[3]{0:T(128)} %pad_add_fusion.at_ref.core_ref, bf16[4,896,256]{2,1,0:T(8,128)(2,1)} %bitcast.41, ...), custom_call_target="tpu_custom_call" | custom-call | flops 5637144576 | bytes 12582912 | tf_op jit(solution)/shard_map/pallas_call | solution.py:234
  88.3 6.2 %all-to-all-start = ((bf16[4,2,160,128]{3,2,1,0:T(8,128)(2,1)}), bf16[4,2,160,128]{3,2,1,0:T(8,128)(2,1)S(1)}, u32[]{:S(2)}, u32[]{:S(2)}) async-start(bf16[4,2,160,128]{3,2,1,0:T(8,128)(2,1)} %bitcast.42), calls=%async_computation | async-start | bytes 655360 | tf_op jit(solution)/shard_map/all_to_all | solution.py:373
  94.5 6.3 %shard_map.102 = (f32[2,448,256]{2,1,0:T(8,128)}, bf16[2,2,448,160]{3,2,1,0:T(8,128)(2,1)}) custom-call(s32[3]{0:T(128)} %pad_add_fusion.at_ref.core_ref, bf16[2,448,256]{2,1,0:T(8,128)(2,1)} %get-tuple-element.55.refs_0_, bf16[2,448,256]{2,1,0:T(8,128)(2,1)} %get-tuple-element.56.refs_1_, bf16[2,448,1024]{2,1,0:T(8,128)(2,1)} %get-tuple-element.57.refs_2_, ...), custom_call_target="tpu_custom_call" | custom-call | flops 481689600 | bytes 12582912 | tf_op jit(solution)/shard_map/pallas_call | solution.py:234
  100.8 6.3 %shard_map.101 = (f32[2,448,256]{2,1,0:T(8,128)}, bf16[2,2,448,160]{3,2,1,0:T(8,128)(2,1)}) custom-call(s32[3]{0:T(128)} %pad_add_fusion.at_ref.core_ref, bf16[2,448,256]{2,1,0:T(8,128)(2,1)} %get-tuple-element.55.refs_0_, bf16[2,448,256]{2,1,0:T(8,128)(2,1)} %get-tuple-element.56.refs_1_, bf16[2,448,1024]{2,1,0:T(8,128)(2,1)} %get-tuple-element.57.refs_2_, ...), custom_call_target="tpu_custom_call" | custom-call | flops 481689600 | bytes 12582912 | tf_op jit(solution)/shard_map/pallas_call | solution.py:234
  107.2 2.5 %collective-permute-start.18 = (bf16[2,160,128]{2,1,0:T(8,128)(2,1)S(1)}, bf16[2,160,128]{2,1,0:T(8,128)(2,1)S(1)}, u32[]{:S(2)}, u32[]{:S(2)}) collective-permute-start(bf16[2,160,128]{2,1,0:T(8,128)(2,1)S(1)} %reduce_sum.12), channel_id=1, source_target_pairs={{0,24},{8,16},{16,8},{24,0},{1,25},{9,17},{17,9},{25,1},{2,26},{10... | collective-permute-start | bytes 245768 | tf_op jit(solution)/shard_map/ppermute | solution.py:377
  110.7 6.3 %shard_map.103 = (f32[2,448,256]{2,1,0:T(8,128)}, bf16[2,2,448,160]{3,2,1,0:T(8,128)(2,1)}) custom-call(s32[3]{0:T(128)} %pad_add_fusion.at_ref.core_ref, bf16[2,448,256]{2,1,0:T(8,128)(2,1)} %get-tuple-element.55.refs_0_, bf16[2,448,256]{2,1,0:T(8,128)(2,1)} %get-tuple-element.56.refs_1_, bf16[2,448,1024]{2,1,0:T(8,128)(2,1)} %get-tuple-element.57.refs_2_, ...), custom_call_target="tpu_custom_call" | custom-call | flops 481689600 | bytes 12582912 | tf_op jit(solution)/shard_map/pallas_call | solution.py:234
  117.7 1.9 shard_map.104
  119.6 5.1 %all-to-all-start.1 = ((bf16[4,2,160,128]{3,2,1,0:T(8,128)(2,1)}), bf16[4,2,160,128]{3,2,1,0:T(8,128)(2,1)S(1)}, u32[]{:S(2)}, u32[]{:S(2)}) async-start(bf16[4,2,160,128]{3,2,1,0:T(8,128)(2,1)} %shard_map.104), calls=%async_computation.1 | async-start | bytes 655360 | tf_op jit(solution)/shard_map/all_to_all | solution.py:386
  125.3 6.3 %shard_map.105 = (f32[2,448,256]{2,1,0:T(8,128)}, bf16[2,2,448,160]{3,2,1,0:T(8,128)(2,1)}) custom-call(s32[3]{0:T(128)} %pad_add_fusion.at_ref.core_ref, bf16[2,448,256]{2,1,0:T(8,128)(2,1)} %get-tuple-element.55.refs_0_, bf16[2,448,256]{2,1,0:T(8,128)(2,1)} %get-tuple-element.56.refs_1_, bf16[2,448,1024]{2,1,0:T(8,128)(2,1)} %get-tuple-element.57.refs_2_, ...), custom_call_target="tpu_custom_call" | custom-call | flops 481689600 | bytes 12582912 | tf_op jit(solution)/shard_map/pallas_call | solution.py:234
  131.6 2.3 %all-to-all-done.1 = bf16[4,2,160,128]{3,2,1,0:T(8,128)(2,1)S(1)} async-done(((bf16[4,2,160,128]{3,2,1,0:T(8,128)(2,1)}), bf16[4,2,160,128]{3,2,1,0:T(8,128)(2,1)S(1)}, u32[]{:S(2)}, u32[]{:S(2)}) %all-to-all-start.1) | async-done | bytes 327712 | tf_op jit(solution)/shard_map/all_to_all | solution.py:386
  134.6 6.1 %shard_map.106.mine_ref = bf16[448,1024]{1,0:T(8,128)(2,1)} custom-call(s32[3]{0:T(128)} %pad_add_fusion.at_ref.core_ref, bf16[8,160,128]{2,1,0:T(8,128)(2,1)} %bitcast.38, f32[1,1024]{1,0:T(1,128)} %bitcast.43, f32[2,448,256]{2,1,0:T(8,128)} %get-tuple-element.69.refs_0_, f32[2,448,256]{2,1,0:T(8,128)} %get-tuple-element.70.refs_1_, ...), custom_call_target="tpu_custom_call" | custom-call | flops 275251200 | bytes 12582912 | tf_op jit(solution)/shard_map/pallas_call | solution.py:234
  140.7 6.1 %shard_map.108.mine_ref = bf16[448,1024]{1,0:T(8,128)(2,1)} custom-call(s32[3]{0:T(128)} %pad_add_fusion.at_ref.core_ref, bf16[8,160,128]{2,1,0:T(8,128)(2,1)} %bitcast.39, f32[1,1024]{1,0:T(1,128)} %bitcast.44, f32[2,448,256]{2,1,0:T(8,128)} %get-tuple-element.69.refs_0_, f32[2,448,256]{2,1,0:T(8,128)} %get-tuple-element.70.refs_1_, ...), custom_call_target="tpu_custom_call" | custom-call | flops 275251200 | bytes 12582912 | tf_op jit(solution)/shard_map/pallas_call | solution.py:234
  148.2 4.7 %shard_map.110 = (bf16[448,256]{1,0:T(8,128)(2,1)}, bf16[448,256]{1,0:T(8,128)(2,1)}) custom-call(s32[3]{0:T(128)} %pad_add_fusion.at_ref.core_ref, bf16[448,1024]{1,0:T(8,128)(2,1)} %shard_map.106.mine_ref, bf16[448,1024]{1,0:T(8,128)(2,1)} %copy-done.4, bf16[4,2,256,2048]{3,2,1,0:T(8,128)(2,1)} %bitcast.22, bf16[4,2,256,2048]{3,2,1,0:T(8,128)(2,1)} %bitcast.23, ...), custom_call_target="tpu_custom_call" | custom-call | flops 939524096 | bytes 12582912 | tf_op jit(solution)/shard_map/pallas_call | solution.py:234
  152.9 2.1 %collective-permute-start.23 = (bf16[448,256]{1,0:T(8,128)(2,1)}, bf16[448,256]{1,0:T(8,128)(2,1)S(1)}, u32[]{:S(2)}, u32[]{:S(2)}) collective-permute-start(bf16[448,256]{1,0:T(8,128)(2,1)} %get-tuple-element.81), channel_id=1, source_target_pairs={{0,4},{2,6},{4,0},{6,2},{1,5},{3,7},{5,1},{7,3},{8,12},{10,14},{12... | collective-permute-start | bytes 688136 | tf_op jit(solution)/shard_map/ppermute | solution.py:435
  155.0 4.7 %shard_map.107 = (bf16[448,256]{1,0:T(8,128)(2,1)}, bf16[448,256]{1,0:T(8,128)(2,1)}) custom-call(s32[3]{0:T(128)} %pad_add_fusion.at_ref.core_ref, bf16[448,1024]{1,0:T(8,128)(2,1)} %shard_map.106.mine_ref, bf16[448,1024]{1,0:T(8,128)(2,1)} %copy-done.4, bf16[4,2,256,2048]{3,2,1,0:T(8,128)(2,1)} %bitcast.26, bf16[4,2,256,2048]{3,2,1,0:T(8,128)(2,1)} %bitcast.27, ...), custom_call_target="tpu_custom_call" | custom-call | flops 939524096 | bytes 12582912 | tf_op jit(solution)/shard_map/pallas_call | solution.py:234
  159.7 1.7 collective-permute-start.25
  162.3 4.7 %shard_map.111 = (bf16[448,256]{1,0:T(8,128)(2,1)}, bf16[448,256]{1,0:T(8,128)(2,1)}) custom-call(s32[3]{0:T(128)} %pad_add_fusion.at_ref.core_ref, bf16[448,1024]{1,0:T(8,128)(2,1)} %shard_map.108.mine_ref, bf16[448,1024]{1,0:T(8,128)(2,1)} %copy-done.3, bf16[4,2,256,2048]{3,2,1,0:T(8,128)(2,1)} %bitcast.30, bf16[4,2,256,2048]{3,2,1,0:T(8,128)(2,1)} %bitcast.31, ...), custom_call_target="tpu_custom_call" | custom-call | flops 939524096 | bytes 12582912 | tf_op jit(solution)/shard_map/pallas_call | solution.py:234
  169.1 4.7 %shard_map.109 = (bf16[448,256]{1,0:T(8,128)(2,1)}, bf16[448,256]{1,0:T(8,128)(2,1)}) custom-call(s32[3]{0:T(128)} %pad_add_fusion.at_ref.core_ref, bf16[448,1024]{1,0:T(8,128)(2,1)} %shard_map.108.mine_ref, bf16[448,1024]{1,0:T(8,128)(2,1)} %copy-done.3, bf16[4,2,256,2048]{3,2,1,0:T(8,128)(2,1)} %bitcast.34, bf16[4,2,256,2048]{3,2,1,0:T(8,128)(2,1)} %bitcast.35, ...), custom_call_target="tpu_custom_call" | custom-call | flops 939524096 | bytes 12582912 | tf_op jit(solution)/shard_map/pallas_call | solution.py:234
  173.8 2.9 %collective-permute-start.26 = (bf16[448,256]{1,0:T(8,128)(2,1)}, bf16[448,256]{1,0:T(8,128)(2,1)S(1)}, u32[]{:S(2)}, u32[]{:S(2)}) collective-permute-start(bf16[448,256]{1,0:T(8,128)(2,1)} %get-tuple-element.84), channel_id=1, source_target_pairs={{0,6},{2,0},{4,2},{6,4},{1,7},{3,1},{5,3},{7,5},{8,14},{10,8},{12,... | collective-permute-start | bytes 688136 | tf_op jit(solution)/shard_map/ppermute | solution.py:435
  176.7 1.6 collective-permute-done.22.refs_3_
  178.3 13.7 %collective-permute-done.24.refs_5_ = bf16[448,256]{1,0:T(8,128)(2,1)S(1)} collective-permute-done((bf16[448,256]{1,0:T(8,128)(2,1)}, bf16[448,256]{1,0:T(8,128)(2,1)S(1)}, u32[]{:S(2)}, u32[]{:S(2)}) %collective-permute-start.24) | collective-permute-done | bytes 229408 | tf_op jit(solution)/shard_map/ppermute | solution.py:435
  193.0 1.8 shard_map.112
  (85 shorter events, 21.7 us)
Async XLA Ops:
  1.0 10.5 %collective-permute-start.1 = (bf16[512,256]{1,0:T(8,128)(2,1)S(1)}, bf16[512,256]{1,0:T(8,128)(2,1)S(1)}, u32[]{:S(2)}, u32[]{:S(2)}) collective-permute-start(bf16[512,256]{1,0:T(8,128)(2,1)S(1)} %constant_dynamic-slice_fusion.1), channel_id=1, source_target_pairs={{0,2},{2,4},{4,6},{1,3},{3,5},{5,7},{8,10},{10,12},{12,14},{9,11},... | collective-permute-start | bytes 786440 | tf_op jit(solution)/shard_map/ppermute | solution.py:293
  5.9 9.7 %collective-permute-start = (bf16[512,256]{1,0:T(8,128)(2,1)S(1)}, bf16[512,256]{1,0:T(8,128)(2,1)S(1)}, u32[]{:S(2)}, u32[]{:S(2)}) collective-permute-start(bf16[512,256]{1,0:T(8,128)(2,1)S(1)} %constant_dynamic-slice_fusion.1), channel_id=1, source_target_pairs={{2,0},{4,2},{6,4},{3,1},{5,3},{7,5},{10,8},{12,10},{14,12},{11,9},... | collective-permute-start | bytes 786440 | tf_op jit(solution)/shard_map/ppermute | solution.py:294
  11.5 5.4 %collective-permute-start.2 = (bf16[512,256]{1,0:T(8,128)(2,1)S(1)}, bf16[512,256]{1,0:T(8,128)(2,1)S(1)}, u32[]{:S(2)}, u32[]{:S(2)}) collective-permute-start(bf16[512,256]{1,0:T(8,128)(2,1)S(1)} %collective-permute-done.1), channel_id=1, source_target_pairs={{2,4},{4,6},{3,5},{5,7},{10,12},{12,14},{11,13},{13,15},{18,20},{2... | collective-permute-start | bytes 786440 | tf_op jit(solution)/shard_map/ppermute | solution.py:293
  15.6 8.9 %collective-permute-start.4 = (bf16[512,256]{1,0:T(8,128)(2,1)S(1)}, bf16[512,256]{1,0:T(8,128)(2,1)S(1)}, u32[]{:S(2)}, u32[]{:S(2)}) collective-permute-start(bf16[512,256]{1,0:T(8,128)(2,1)S(1)} %collective-permute-done), channel_id=1, source_target_pairs={{2,0},{4,2},{3,1},{5,3},{10,8},{12,10},{11,9},{13,11},{18,16},{20,... | collective-permute-start | bytes 786440 | tf_op jit(solution)/shard_map/ppermute | solution.py:294
  16.9 8.9 %collective-permute-start.3 = (bf16[512,256]{1,0:T(8,128)(2,1)S(1)}, bf16[512,256]{1,0:T(8,128)(2,1)S(1)}, u32[]{:S(2)}, u32[]{:S(2)}) collective-permute-start(bf16[512,256]{1,0:T(8,128)(2,1)S(1)} %collective-permute-done.2), channel_id=1, source_target_pairs={{4,6},{5,7},{12,14},{13,15},{20,22},{21,23},{28,30},{29,31}} | collective-permute-start | bytes 786440 | tf_op jit(solution)/shard_map/ppermute | solution.py:293
  24.5 8.3 %collective-permute-start.5 = (bf16[512,256]{1,0:T(8,128)(2,1)S(1)}, bf16[512,256]{1,0:T(8,128)(2,1)S(1)}, u32[]{:S(2)}, u32[]{:S(2)}) collective-permute-start(bf16[512,256]{1,0:T(8,128)(2,1)S(1)} %collective-permute-done.4), channel_id=1, source_target_pairs={{2,0},{3,1},{10,8},{11,9},{18,16},{19,17},{26,24},{27,25}} | collective-permute-start | bytes 786440 | tf_op jit(solution)/shard_map/ppermute | solution.py:294
  32.9 40.6 %copy-start.7 = (bf16[3,512,256]{2,1,0:T(8,128)(2,1)}, bf16[3,512,256]{2,1,0:T(8,128)(2,1)S(1)}, u32[]{:S(2)}) copy-start(bf16[3,512,256]{2,1,0:T(8,128)(2,1)S(1)} %pad_maximum_fusion.refs_13_) | copy-start | bytes 2359300
  32.9 15.5 %collective-permute-start.6 = (bf16[896,256]{1,0:T(8,128)(2,1)S(1)}, bf16[896,256]{1,0:T(8,128)(2,1)}, u32[]{:S(2)}, u32[]{:S(2)}) collective-permute-start(bf16[896,256]{1,0:T(8,128)(2,1)S(1)} %get-tuple-element.45), channel_id=1, source_target_pairs={{0,2},{2,4},{4,6},{6,0},{1,3},{3,5},{5,7},{7,1},{8,10},{10,12},{12... | collective-permute-start | bytes 1376264 | tf_op jit(solution)/shard_map/ppermute | solution.py:302
  33.0 36.1 %collective-permute-start.10 = (bf16[3,512,256]{2,1,0:T(8,128)(2,1)S(1)}, bf16[3,512,256]{2,1,0:T(8,128)(2,1)S(1)}, u32[]{:S(2)}, u32[]{:S(2)}) collective-permute-start(bf16[3,512,256]{2,1,0:T(8,128)(2,1)S(1)} %pad_maximum_fusion.refs_13_), channel_id=1, source_target_pairs={{0,24},{8,16},{16,8},{24,0},{1,25},{9,17},{17,9},{25,1},{2,26},{10... | collective-permute-start | bytes 2359304 | tf_op jit(solution)/shard_map/ppermute | solution.py:298
  35.5 34.1 %collective-permute-start.9 = (bf16[3,512,256]{2,1,0:T(8,128)(2,1)S(1)}, bf16[3,512,256]{2,1,0:T(8,128)(2,1)S(1)}, u32[]{:S(2)}, u32[]{:S(2)}) collective-permute-start(bf16[3,512,256]{2,1,0:T(8,128)(2,1)S(1)} %pad_maximum_fusion.refs_13_), channel_id=1, source_target_pairs={{0,16},{8,24},{16,0},{24,8},{1,17},{9,25},{17,1},{25,9},{2,18},{10... | collective-permute-start | bytes 2359304 | tf_op jit(solution)/shard_map/ppermute | solution.py:298
  36.0 33.6 %collective-permute-start.8 = (bf16[3,512,256]{2,1,0:T(8,128)(2,1)S(1)}, bf16[3,512,256]{2,1,0:T(8,128)(2,1)S(1)}, u32[]{:S(2)}, u32[]{:S(2)}) collective-permute-start(bf16[3,512,256]{2,1,0:T(8,128)(2,1)S(1)} %pad_maximum_fusion.refs_13_), channel_id=1, source_target_pairs={{0,8},{8,0},{16,24},{24,16},{1,9},{9,1},{17,25},{25,17},{2,10},{10... | collective-permute-start | bytes 2359304 | tf_op jit(solution)/shard_map/ppermute | solution.py:298
  36.5 27.3 %collective-permute-start.7 = (bf16[896,256]{1,0:T(8,128)(2,1)S(1)}, bf16[896,256]{1,0:T(8,128)(2,1)}, u32[]{:S(2)}, u32[]{:S(2)}) collective-permute-start(bf16[896,256]{1,0:T(8,128)(2,1)S(1)} %get-tuple-element.46), channel_id=1, source_target_pairs={{0,4},{2,6},{4,0},{6,2},{1,5},{3,7},{5,1},{7,3},{8,12},{10,14},{12... | collective-permute-start | bytes 1376264 | tf_op jit(solution)/shard_map/ppermute | solution.py:302
  48.4 20.6 %collective-permute-start.11 = (bf16[896,256]{1,0:T(8,128)(2,1)S(1)}, bf16[896,256]{1,0:T(8,128)(2,1)S(1)}, u32[]{:S(2)}, u32[]{:S(2)}) collective-permute-start(bf16[896,256]{1,0:T(8,128)(2,1)S(1)} %get-tuple-element.49), channel_id=1, source_target_pairs={{0,6},{2,0},{4,2},{6,4},{1,7},{3,1},{5,3},{7,5},{8,14},{10,8},{12,... | collective-permute-start | bytes 1376264 | tf_op jit(solution)/shard_map/ppermute | solution.py:302
  63.8 8.3 %collective-permute-start.12 = (bf16[896,256]{1,0:T(8,128)(2,1)S(1)}, bf16[896,256]{1,0:T(8,128)(2,1)S(1)}, u32[]{:S(2)}, u32[]{:S(2)}) collective-permute-start(bf16[896,256]{1,0:T(8,128)(2,1)S(1)} %get-tuple-element.50), channel_id=1, source_target_pairs={{0,1},{1,0},{2,3},{3,2},{4,5},{5,4},{6,7},{7,6},{8,9},{9,8},{10,11... | collective-permute-start | bytes 1376264 | tf_op jit(solution)/shard_map/ppermute | solution.py:305
  69.0 3.1 %collective-permute-start.13 = (bf16[896,256]{1,0:T(8,128)(2,1)}, bf16[896,256]{1,0:T(8,128)(2,1)S(1)}, u32[]{:S(2)}, u32[]{:S(2)}) collective-permute-start(bf16[896,256]{1,0:T(8,128)(2,1)} %collective-permute-done.6.refs_1_), channel_id=1, source_target_pairs={{0,1},{1,0},{2,3},{3,2},{4,5},{5,4},{6,7},{7,6},{8,9},{9,8},{10,11... | collective-permute-start | bytes 1376264 | tf_op jit(solution)/shard_map/ppermute | solution.py:305
  69.0 3.1 %collective-permute-start.15 = (bf16[896,256]{1,0:T(8,128)(2,1)S(1)}, bf16[896,256]{1,0:T(8,128)(2,1)}, u32[]{:S(2)}, u32[]{:S(2)}) collective-permute-start(bf16[896,256]{1,0:T(8,128)(2,1)S(1)} %collective-permute-done.11.refs_3_), channel_id=1, source_target_pairs={{0,1},{1,0},{2,3},{3,2},{4,5},{5,4},{6,7},{7,6},{8,9},{9,8},{10,11... | collective-permute-start | bytes 1376264 | tf_op jit(solution)/shard_map/ppermute | solution.py:305
  71.3 2.2 %collective-permute-start.14 = (bf16[896,256]{1,0:T(8,128)(2,1)}, bf16[896,256]{1,0:T(8,128)(2,1)}, u32[]{:S(2)}, u32[]{:S(2)}) collective-permute-start(bf16[896,256]{1,0:T(8,128)(2,1)} %collective-permute-done.7.refs_2_), channel_id=1, source_target_pairs={{0,1},{1,0},{2,3},{3,2},{4,5},{5,4},{6,7},{7,6},{8,9},{9,8},{10,11... | collective-permute-start | bytes 1376264 | tf_op jit(solution)/shard_map/ppermute | solution.py:305
  88.3 18.8 %all-to-all-start = ((bf16[4,2,160,128]{3,2,1,0:T(8,128)(2,1)}), bf16[4,2,160,128]{3,2,1,0:T(8,128)(2,1)S(1)}, u32[]{:S(2)}, u32[]{:S(2)}) async-start(bf16[4,2,160,128]{3,2,1,0:T(8,128)(2,1)} %bitcast.42), calls=%async_computation | async-start | bytes 655360 | tf_op jit(solution)/shard_map/all_to_all | solution.py:373
  107.2 9.8 %collective-permute-start.18 = (bf16[2,160,128]{2,1,0:T(8,128)(2,1)S(1)}, bf16[2,160,128]{2,1,0:T(8,128)(2,1)S(1)}, u32[]{:S(2)}, u32[]{:S(2)}) collective-permute-start(bf16[2,160,128]{2,1,0:T(8,128)(2,1)S(1)} %reduce_sum.12), channel_id=1, source_target_pairs={{0,24},{8,16},{16,8},{24,0},{1,25},{9,17},{17,9},{25,1},{2,26},{10... | collective-permute-start | bytes 245768 | tf_op jit(solution)/shard_map/ppermute | solution.py:377
  109.7 7.3 %collective-permute-start.17 = (bf16[2,160,128]{2,1,0:T(8,128)(2,1)S(1)}, bf16[2,160,128]{2,1,0:T(8,128)(2,1)S(1)}, u32[]{:S(2)}, u32[]{:S(2)}) collective-permute-start(bf16[2,160,128]{2,1,0:T(8,128)(2,1)S(1)} %reduce_sum.12), channel_id=1, source_target_pairs={{0,16},{8,24},{16,0},{24,8},{1,17},{9,25},{17,1},{25,9},{2,18},{10... | collective-permute-start | bytes 245768 | tf_op jit(solution)/shard_map/ppermute | solution.py:377
  110.2 6.8 %collective-permute-start.16 = (bf16[2,160,128]{2,1,0:T(8,128)(2,1)S(1)}, bf16[2,160,128]{2,1,0:T(8,128)(2,1)S(1)}, u32[]{:S(2)}, u32[]{:S(2)}) collective-permute-start(bf16[2,160,128]{2,1,0:T(8,128)(2,1)S(1)} %reduce_sum.12), channel_id=1, source_target_pairs={{0,8},{8,0},{16,24},{24,16},{1,9},{9,1},{17,25},{25,17},{2,10},{10... | collective-permute-start | bytes 245768 | tf_op jit(solution)/shard_map/ppermute | solution.py:377
  119.6 14.3 %all-to-all-start.1 = ((bf16[4,2,160,128]{3,2,1,0:T(8,128)(2,1)}), bf16[4,2,160,128]{3,2,1,0:T(8,128)(2,1)S(1)}, u32[]{:S(2)}, u32[]{:S(2)}) async-start(bf16[4,2,160,128]{3,2,1,0:T(8,128)(2,1)} %shard_map.104), calls=%async_computation.1 | async-start | bytes 655360 | tf_op jit(solution)/shard_map/all_to_all | solution.py:386
  140.7 6.6 %collective-permute-start.19 = (bf16[448,1024]{1,0:T(8,128)(2,1)}, bf16[448,1024]{1,0:T(8,128)(2,1)S(1)}, u32[]{:S(2)}, u32[]{:S(2)}) collective-permute-start(bf16[448,1024]{1,0:T(8,128)(2,1)} %shard_map.106.mine_ref), channel_id=1, source_target_pairs={{0,1},{1,0},{2,3},{3,2},{4,5},{5,4},{6,7},{7,6},{8,9},{9,8},{10,11... | collective-permute-start | bytes 2752520 | tf_op jit(solution)/shard_map/ppermute | solution.py:428
  146.8 14.6 %collective-permute-start.20 = (bf16[448,1024]{1,0:T(8,128)(2,1)}, bf16[448,1024]{1,0:T(8,128)(2,1)S(1)}, u32[]{:S(2)}, u32[]{:S(2)}) collective-permute-start(bf16[448,1024]{1,0:T(8,128)(2,1)} %shard_map.108.mine_ref), channel_id=1, source_target_pairs={{0,1},{1,0},{2,3},{3,2},{4,5},{5,4},{6,7},{7,6},{8,9},{9,8},{10,11... | collective-permute-start | bytes 2752520 | tf_op jit(solution)/shard_map/ppermute | solution.py:428
  152.9 20.9 %collective-permute-start.21 = (bf16[448,256]{1,0:T(8,128)(2,1)}, bf16[448,256]{1,0:T(8,128)(2,1)S(1)}, u32[]{:S(2)}, u32[]{:S(2)}) collective-permute-start(bf16[448,256]{1,0:T(8,128)(2,1)} %get-tuple-element.79), channel_id=1, source_target_pairs={{0,2},{2,4},{4,6},{6,0},{1,3},{3,5},{5,7},{7,1},{8,10},{10,12},{12... | collective-permute-start | bytes 688136 | tf_op jit(solution)/shard_map/ppermute | solution.py:435
  152.9 23.7 %collective-permute-start.23 = (bf16[448,256]{1,0:T(8,128)(2,1)}, bf16[448,256]{1,0:T(8,128)(2,1)S(1)}, u32[]{:S(2)}, u32[]{:S(2)}) collective-permute-start(bf16[448,256]{1,0:T(8,128)(2,1)} %get-tuple-element.81), channel_id=1, source_target_pairs={{0,4},{2,6},{4,0},{6,2},{1,5},{3,7},{5,1},{7,3},{8,12},{10,14},{12... | collective-permute-start | bytes 688136 | tf_op jit(solution)/shard_map/ppermute | solution.py:435
  159.7 17.0 %collective-permute-start.25 = (bf16[448,256]{1,0:T(8,128)(2,1)}, bf16[448,256]{1,0:T(8,128)(2,1)S(1)}, u32[]{:S(2)}, u32[]{:S(2)}) collective-permute-start(bf16[448,256]{1,0:T(8,128)(2,1)} %get-tuple-element.83), channel_id=1, source_target_pairs={{0,6},{2,0},{4,2},{6,4},{1,7},{3,1},{5,3},{7,5},{8,14},{10,8},{12,... | collective-permute-start | bytes 688136 | tf_op jit(solution)/shard_map/ppermute | solution.py:435
  167.0 11.2 %collective-permute-start.22 = (bf16[448,256]{1,0:T(8,128)(2,1)}, bf16[448,256]{1,0:T(8,128)(2,1)S(1)}, u32[]{:S(2)}, u32[]{:S(2)}) collective-permute-start(bf16[448,256]{1,0:T(8,128)(2,1)} %get-tuple-element.80), channel_id=1, source_target_pairs={{0,2},{2,4},{4,6},{6,0},{1,3},{3,5},{5,7},{7,1},{8,10},{10,12},{12... | collective-permute-start | bytes 688136 | tf_op jit(solution)/shard_map/ppermute | solution.py:435
  167.6 24.4 %copy-start = (bf16[448,256]{1,0:T(8,128)(2,1)S(1)}, bf16[448,256]{1,0:T(8,128)(2,1)}, u32[]{:S(2)}) copy-start(bf16[448,256]{1,0:T(8,128)(2,1)} %get-tuple-element.77.refs_0_) | copy-start | bytes 688132
  167.6 24.4 %copy-start.2 = (s32[3]{0:T(128)S(1)}, s32[3]{0:T(128)}, u32[]{:S(2)}) copy-start(s32[3]{0:T(128)} %pad_add_fusion.at_ref.core_ref) | copy-start | bytes 40
  167.6 24.4 %collective-permute-start.24 = (bf16[448,256]{1,0:T(8,128)(2,1)}, bf16[448,256]{1,0:T(8,128)(2,1)S(1)}, u32[]{:S(2)}, u32[]{:S(2)}) collective-permute-start(bf16[448,256]{1,0:T(8,128)(2,1)} %get-tuple-element.82), channel_id=1, source_target_pairs={{0,4},{2,6},{4,0},{6,2},{1,5},{3,7},{5,1},{7,3},{8,12},{10,14},{12... | collective-permute-start | bytes 688136 | tf_op jit(solution)/shard_map/ppermute | solution.py:435
  173.8 18.2 %collective-permute-start.26 = (bf16[448,256]{1,0:T(8,128)(2,1)}, bf16[448,256]{1,0:T(8,128)(2,1)S(1)}, u32[]{:S(2)}, u32[]{:S(2)}) collective-permute-start(bf16[448,256]{1,0:T(8,128)(2,1)} %get-tuple-element.84), channel_id=1, source_target_pairs={{0,6},{2,0},{4,2},{6,4},{1,7},{3,1},{5,3},{7,5},{8,14},{10,8},{12,... | collective-permute-start | bytes 688136 | tf_op jit(solution)/shard_map/ppermute | solution.py:435
  (15 other events, 46.4 us)

commit v7 on v6

--- a/solution.py
+++ b/solution.py
@@ -102,13 +102,13 @@
         row_ref[:, pl.ds(there, width)] = other[d][...]
     arrived((-1,))
     half = table_ref.shape[1] // 2
+    both_narrow = dot(row_ref[...], narrow_ref[...]).astype(BF16)
     for chunk in range(2):
         at = slice(chunk * rows, (chunk + 1) * rows)
-        both_narrow = dot(row_ref[at, :], narrow_ref[...]).astype(BF16)
-        q_ref[chunk] = both_narrow[:, :narrow]
-        k_ref[chunk] = both_narrow[:, narrow:]
+        q_ref[chunk] = both_narrow[at, :narrow]
+        k_ref[chunk] = both_narrow[at, narrow:]
         for lanes in range(0, narrow, LANES):
-            product = dot(table_ref[0], both_narrow[:, narrow + lanes : narrow + lanes + LANES], NT)
+            product = dot(table_ref[0], both_narrow[at, narrow + lanes : narrow + lanes + LANES], NT)
             left = product[:half] + bias_ref[:, 0:1]
             right = product[half:] + bias_ref[:, 1:2]
             to = (lanes // LANES) * half
@@ -116,83 +116,84 @@
 
     for pair in range(layers // 2):
         arrived((2 * pair, 2 * pair + 1))
-        first = []
-        for chunk in range(2):
-            at = slice(chunk * rows, (chunk + 1) * rows)
-            value = dot(row_ref[at, :], w_ref[pair]).astype(BF16)
-            for d in (2 * pair, 2 * pair + 1):
-                z = lax.rem(layer + d, layers)
-                side = (d % 2) * block
-                v_ref[chunk, :, pl.ds(pl.multiple_of(z * block, block), block)] = value[:, side : side + block]
-                for i in range(per_group):
-                    head = z * per_group + i
-                    phi = phi_ref[chunk, pl.ds(pl.multiple_of(head * PACKED, PACKED), PACKED), :]
-                    lanes = side + i * HEAD_DIM
-                    state = dot(phi, value[:, lanes : lanes + HEAD_DIM])
-                    if chunk == 0:
-                        early_ref[head] = state.astype(BF16)
-                        first.append(state)
-                    else:
-                        total_ref[head] = (first.pop(0) + state).astype(BF16)
-
-
-def local_kernel(core_ref, per_group, offset, q_ref, k_ref, v_ref, early_ref, table_ref, bias_ref, num_ref, phi_ref):
-    chunk = pl.program_id(0)
-    step = pl.program_id(1) + offset
+        value = dot(row_ref[...], w_ref[pair]).astype(BF16)
+        for d in (2 * pair, 2 * pair + 1):
+            z = lax.rem(layer + d, layers)
+            side = (d % 2) * block
+            lanes = pl.multiple_of(z * block, block)
+            for chunk in range(2):
+                at = slice(chunk * rows, (chunk + 1) * rows)
+                v_ref[chunk, :, pl.ds(lanes, block)] = value[at, side : side + block]
+            for i in range(per_group):
+                head = z * per_group + i
+                place = pl.multiple_of(head * PACKED, PACKED)
+                column = side + i * HEAD_DIM
+                early = dot(phi_ref[0, pl.ds(place, PACKED), :], value[:rows, column : column + HEAD_DIM])
+                late = dot(phi_ref[1, pl.ds(place, PACKED), :], value[rows:, column : column + HEAD_DIM])
+                early_ref[head] = early.astype(BF16)
+                total_ref[head] = (early + late).astype(BF16)
+
+
+def local_kernel(at_ref, per_group, offset, q_ref, k_ref, v_ref, early_ref, table_ref, bias_ref, num_ref, phi_ref):
     rows = q_ref.shape[1]
     cut = LANES * -(-rows // (2 * LANES))
     wide = table_ref.shape[2] // 2
-    for i in range(per_group):
-        head = (2 * step + core_ref[0]) * per_group + i
+    lane = lax.broadcasted_iota(jnp.int32, (rows, LANES), 1) // FEAT
+    for i in range(early_ref.shape[0]):
+        head = (2 * (i // per_group + offset) + at_ref[0]) * per_group + i % per_group
         lanes = pl.multiple_of((head // HELD) * LANES, LANES)
         place = lax.rem(head, HELD)
-        query = q_ref[0, :, pl.ds(lanes, LANES)]
-        key = k_ref[0, :, pl.ds(lanes, LANES)]
-        sides = dot(query, table_ref[place]) + bias_ref[...]
-        phi_ref[0, i] = (sides[:, :PACKED] * sides[:, wide : wide + PACKED]).astype(BF16)
-        lane = lax.broadcasted_iota(jnp.int32, (rows, LANES), 1)
-        mine = jnp.where(lane // FEAT == place, query * jnp.asarray(0.25, BF16), jnp.zeros_like(query))
         columns = slice(i * HEAD_DIM, (i + 1) * HEAD_DIM)
-        for low, high in ((0, cut), (cut, rows)):
-            span = high - low
-            s = dot(mine[low:high], key[low:high], NT)
-            t_at = lax.broadcasted_iota(jnp.int32, (span, span), 0)
-            j_at = lax.broadcasted_iota(jnp.int32, (span, span), 1)
-            weight = jnp.where(t_at >= j_at, (0.5 * s + 1.0) * s + 1.0, 0.0).astype(BF16)
-            num = dot(weight, v_ref[0, low:high, columns])
-            if low > 0:
-                s = dot(mine[low:high], key[:low], NT)
-                weight = ((0.5 * s + 1.0) * s + 1.0).astype(BF16)
-                num = num + dot(weight, v_ref[0, :low, columns])
-            num_ref[0, low:high, columns] = num
-
-        @pl.when(chunk == 1)
-        def _():
-            num_ref[0, :, columns] += dot(phi_ref[0, i], early_ref[i])
+        for chunk in range(2):
+            query = q_ref[chunk, :, pl.ds(lanes, LANES)]
+            key = k_ref[chunk, :, pl.ds(lanes, LANES)]
+            sides = dot(query, table_ref[place]) + bias_ref[...]
+            phi = (sides[:, :PACKED] * sides[:, wide : wide + PACKED]).astype(BF16)
+            phi_ref[chunk, i] = phi
+            mine = jnp.where(lane == place, query * jnp.asarray(0.25, BF16), jnp.zeros_like(query))
+            for low, high in ((0, cut), (cut, rows)):
+                span = high - low
+                s = dot(mine[low:high], key[low:high], NT)
+                t_at = lax.broadcasted_iota(jnp.int32, (span, span), 0)
+                j_at = lax.broadcasted_iota(jnp.int32, (span, span), 1)
+                weight = jnp.where(t_at >= j_at, (0.5 * s + 1.0) * s + 1.0, 0.0).astype(BF16)
+                num = dot(weight, v_ref[chunk, low:high, columns])
+                if low > 0:
+                    s = dot(mine[low:high], key[:low], NT)
+                    weight = ((0.5 * s + 1.0) * s + 1.0).astype(BF16)
+                    num = num + dot(weight, v_ref[chunk, :low, columns])
+                if chunk > 0:
+                    num = num + dot(phi[low:high], early_ref[i])
+                num_ref[chunk, low:high, columns] = num
 
 
 def prefix_kernel(at_ref, line_ref, *refs):
-    totals, out_ref = refs[:-1], refs[-1]
-    slab = at_ref[2]
+    layers = line_ref.shape[0]
+    totals, outs, sum_ref = refs[: -layers - 1], refs[-layers - 1 : -1], refs[-1]
+    layer, slab = at_ref[1], at_ref[2]
     run = jnp.zeros(line_ref.shape[1:], F32)
     for m, total in enumerate(totals, 1):
         run = run + total[...].astype(F32) * jnp.where((slab ^ m) < slab, 1.0, 0.0)
-    for z in range(line_ref.shape[0]):
-        out_ref[z] = run.astype(BF16)
+    for z in range(layers):
+        sum_ref[z] = run.astype(BF16)
         run = run + line_ref[z].astype(F32)
-
-
-def hidden_kernel(at_ref, state_ref, gain_ref, *refs):
-    parts, out_ref = refs[:-1], refs[-1]
+    for d in range(layers):
+        outs[d][...] = sum_ref[lax.rem(layer + layers - d, layers)]
+
+
+def hidden_kernel(at_ref, layers, gain_ref, *refs):
+    pieces, parts, out_ref, state_ref = refs[:layers], refs[layers:-2], refs[-2], refs[-1]
     numbers, features = parts[: len(parts) // 2], parts[len(parts) // 2 :]
     held = features[0].shape[1]
-    ones = jnp.full((HEAD_DIM, HEAD_DIM), 1.0 / HEAD_DIM, BF16)
+    group = pieces[0].shape[0]
+    for d in range(layers):
+        state_ref[lax.rem(at_ref[1] + d, layers)] = pieces[d][...]
     for i in range(held * len(features)):
         columns = slice(i * HEAD_DIM, (i + 1) * HEAD_DIM)
         at = (i % held) * HEAD_DIM
         num = numbers[i // held][0, :, at : at + HEAD_DIM]
-        num = num + dot(features[i // held][0, i % held], state_ref[i])
-        mean_square = dot((num * num).astype(BF16), ones)
+        num = num + dot(features[i // held][0, i % held], state_ref[i // group, i % group])
+        mean_square = jnp.mean(num * num, axis=1, keepdims=True)
         hidden = num * lax.rsqrt(mean_square + 1e-05) * gain_ref[:, columns]
         out_ref[:, columns] = hidden.astype(BF16)
 
@@ -286,13 +287,9 @@
     at = jnp.stack([core, layer, my_slab.astype(jnp.int32)])
 
     value_part = lax.dynamic_slice_in_dim(w_value, my_slab * part, part, 0)
-    up, down = {0: value_part}, {0: value_part}
     blocks = tokens.reshape(layers, 2 * rows, width)
     sent = [lax.dynamic_index_in_dim(blocks, lax.rem(layer + d, layers), 0, False) for d in range(layers)]
-    for k in range(1, layers):
-        up[k] = lax.ppermute(up[k - 1], "z", [(z, z + 1) for z in range(k - 1, layers - 1)])
-        down[k] = lax.ppermute(down[k - 1], "z", [(z, z - 1) for z in range(1, layers - k + 1)])
-    stack = jnp.stack([jnp.where(layer + d < layers, down[d], up[layers - d]) for d in range(1, layers)])
+    stack = jnp.stack([lax.ppermute(value_part, "z", turn(-d)) for d in range(1, layers)])
     stack, sent = lax.optimization_barrier((stack, sent))
     if slabs == 4:
         weights = [stack] + [lax.ppermute(stack, "seq", flip(m)) for m in range(1, slabs)]
@@ -348,18 +345,18 @@
         return call(
             lambda core_ref, *refs: local_kernel(core_ref, per_group, offset, *refs),
             at,
-            (2, some_layers),
+            (1,),
             [
-                pl.BlockSpec((1, rows, narrow), lambda c, i, _: (c, 0, 0)),
-                pl.BlockSpec((1, rows, narrow), lambda c, i, _: (c, 0, 0)),
-                pl.BlockSpec((1, rows, value_width), lambda c, i, _: (c, 0, i + offset)),
-                pl.BlockSpec((per_group, PACKED, HEAD_DIM), lambda c, i, _: (i + offset, 0, 0)),
+                whole((2, rows, narrow)),
+                whole((2, rows, narrow)),
+                pl.BlockSpec((2, rows, some_layers * value_width), lambda i, _: (0, 0, index)),
+                pl.BlockSpec((heads // parts, PACKED, HEAD_DIM), lambda i, _: (index, 0, 0)),
                 whole(query_table.shape),
                 whole(query_bias.shape),
             ],
             [
-                pl.BlockSpec((1, rows, value_width), lambda c, i, _: (c, 0, i)),
-                pl.BlockSpec((1, per_group, rows, PACKED), lambda c, i, _: (c, i, 0, 0)),
+                whole((2, rows, some_layers * value_width)),
+                whole((2, heads // parts, rows, PACKED)),
             ],
             [
                 jax.ShapeDtypeStruct((2, rows, some_layers * value_width), F32),
@@ -377,14 +374,15 @@
     totals = [lax.ppermute(slab_total, "seq", flip(m)) for m in range(1, slabs)]
     third = local(2)
     totals, third = lax.optimization_barrier((totals, third))
+    piece_shape = (per_group, PACKED, HEAD_DIM)
     prefix = pl.pallas_call(
         prefix_kernel,
         in_specs=[pl.BlockSpec(memory_space=pltpu.SMEM)] + [vmem] * slabs,
-        out_specs=vmem,
-        out_shape=jax.ShapeDtypeStruct(line.shape, BF16),
+        out_specs=[vmem] * layers,
+        out_shape=[jax.ShapeDtypeStruct(piece_shape, BF16)] * layers,
+        scratch_shapes=[pltpu.VMEM((layers,) + piece_shape, BF16)],
     )(at, line, *totals)
-    prefix = lax.all_to_all(prefix, "z", split_axis=0, concat_axis=0, tiled=True)
-    prefix = prefix.reshape(heads, PACKED, HEAD_DIM)
+    prefix = [prefix[0]] + [lax.ppermute(prefix[d], "z", turn(-d)) for d in range(1, layers)]
     locals_ = locals_ + [third, local(3)]
 
     def hidden(chunk):
@@ -392,16 +390,18 @@
         numbers = pl.BlockSpec((1, some, heads * HEAD_DIM // parts), lambda i, _: (chunk, i, 0))
         features = pl.BlockSpec((1, heads // parts, some, PACKED), lambda i, _: (chunk, 0, i, 0))
         return call(
-            hidden_kernel,
+            lambda at_ref, *refs: hidden_kernel(at_ref, layers, *refs),
             at,
             (2,),
-            [whole((heads, PACKED, HEAD_DIM)), whole((1, heads * HEAD_DIM))]
+            [whole((1, heads * HEAD_DIM))]
+            + [whole(piece_shape)] * layers
             + [numbers] * parts
             + [features] * parts,
             pl.BlockSpec((some, heads * HEAD_DIM), lambda i, _: (i, 0)),
             jax.ShapeDtypeStruct((rows, heads * HEAD_DIM), BF16),
-            (prefix, gain_mine, *(num for num, _ in locals_), *(phi for _, phi in locals_)),
+            (gain_mine, *prefix, *(num for num, _ in locals_), *(phi for _, phi in locals_)),
             rows * heads * HEAD_DIM * 600,
+            [pltpu.VMEM((layers,) + piece_shape, BF16)],
         )
 
     w_rows = w_out.reshape(layers, 2, value_width, model)
@@ -422,6 +422,7 @@
             [jax.ShapeDtypeStruct((rows, width), BF16)] * len(to),
             (kept, received, *[w_rows] * len(specs)),
             2 * rows * model * width * len(to),
+            mib=20,
         )
 
     kept = [hidden(chunk) for chunk in range(2)]

time: 197 us -> 185 us (0.939)
  Pallas kernels: 74.5 us -> 55 us
  starting transfers between devices: 39.8 us -> 44.6 us
  waiting for transfers between devices: 70.1 us -> 72.3 us
    pallas_call x12, Pallas kernels: 72.6 us -> 53.1 us  [call(): pl.pallas_call(kernel, grid_spec=pltpu.PrefetchScalarGridSpec(num_scalar_...]
    ppermute x6, waiting for transfers between devices: 15.4 us -> 25 us  [per_device(): pieces[d, chunk] = lax.ppermute(piece, 'z', turn(d)) if d else piece]
    ppermute x3, starting transfers between devices: 1.33 us -> 7.73 us  [per_device(): lax.ppermute(sent[d], 'z', turn(d))]
    ppermute x6, waiting for transfers between devices: 19.9 us -> 14.2 us  [the longest x3 14.2 us: per_device(): lax.ppermute(value_part, 'z', turn(-d))]
    all_to_all x1 -> x0, starting transfers between devices: 5.08 us -> none  [per_device(): lax.all_to_all(prefix, 'z', split_axis=0, concat_axis=0, tiled=True)]
    ppermute x3, waiting for transfers between devices: 0.01 us -> 4.34 us  [per_device(): lax.ppermute(stack, 'seq', flip(m))]
    ppermute x3, waiting for transfers between devices: 31.2 us -> 27.1 us  [per_device(): lax.ppermute(sent[d], 'z', turn(d))]
    all_to_all x1 -> x0, waiting for transfers between devices: 2.28 us -> none  [per_device(): lax.all_to_all(prefix, 'z', split_axis=0, concat_axis=0, tiled=True)]
  transfers between devices with their start and end apart: 29 -> 28, of which waited for: 11 -> 11; matrix products, arithmetic and copies ran while one was open for 1% -> 2% of each run, Pallas kernels for 26% -> 18%
where the time goes in v7:
time: 185 us; the launch traced here: 182 us
  waiting for transfers between devices  72.3 us (39%)
  Pallas kernels  55 us (30%)
  starting transfers between devices  44.6 us (24%)
  local copies, waits for them, and re-layouts  8.84 us (5%)
    pallas_call x12, Pallas kernels, call(): pl.pallas_call(kernel, grid_spec=pltpu.PrefetchScalarGridSpec(num_scalar_...  53.1 us
    ppermute x3, waiting for transfers between devices, per_device(): lax.ppermute(sent[d], 'z', turn(d))  27.1 us
    ppermute x6, waiting for transfers between devices, per_device(): pieces[d, chunk] = lax.ppermute(piece, 'z', turn(d)) if d else piece  25 us
    ppermute x3, waiting for transfers between devices, per_device(): lax.ppermute(value_part, 'z', turn(-d))  14.2 us
    ppermute x6, starting transfers between devices, per_device(): pieces[d, chunk] = lax.ppermute(piece, 'z', turn(d)) if d else piece  8.99 us
    all_to_all x1, starting transfers between devices, per_device(): line = lax.all_to_all(own, 'z', split_axis=0, concat_axis=0, tiled=True)  7.9 us
    ppermute x3, starting transfers between devices, per_device(): lax.ppermute(sent[d], 'z', turn(d))  7.73 us
    ppermute x3, starting transfers between devices, per_device(): lax.ppermute(value_part, 'z', turn(-d))  7.01 us
  transfers between devices with their start and end apart: 28, of which 11 were waited for; matrix products, arithmetic and copies ran while one was open for 2% of the time, Pallas kernels for 18%

profile of v7, /device:TPU:0, one launch (start us, length us, event | category | flops | bytes accessed | tf_op | source)
XLA Modules:
  0.0 181.8 jit_solution(18380851375842524004)
XLA Ops:
  1.0 3.1 %collective-permute-start.2 = (bf16[512,256]{1,0:T(8,128)(2,1)S(1)}, bf16[512,256]{1,0:T(8,128)(2,1)S(1)}, u32[]{:S(2)}, u32[]{:S(2)}) collective-permute-start(bf16[512,256]{1,0:T(8,128)(2,1)S(1)} %constant_dynamic-slice_fusion), channel_id=1, source_target_pairs={{0,2},{2,4},{4,6},{6,0},{1,3},{3,5},{5,7},{7,1},{8,10},{10,12},{12... | collective-permute-start | bytes 786440 | tf_op jit(solution)/shard_map/ppermute | solution.py:292
  4.0 2.6 %collective-permute-start.1 = (bf16[512,256]{1,0:T(8,128)(2,1)S(1)}, bf16[512,256]{1,0:T(8,128)(2,1)S(1)}, u32[]{:S(2)}, u32[]{:S(2)}) collective-permute-start(bf16[512,256]{1,0:T(8,128)(2,1)S(1)} %constant_dynamic-slice_fusion), channel_id=1, source_target_pairs={{0,4},{2,6},{4,0},{6,2},{1,5},{3,7},{5,1},{7,3},{8,12},{10,14},{12... | collective-permute-start | bytes 786440 | tf_op jit(solution)/shard_map/ppermute | solution.py:292
  9.5 3.8 %collective-permute-done.2 = bf16[512,256]{1,0:T(8,128)(2,1)S(1)} collective-permute-done((bf16[512,256]{1,0:T(8,128)(2,1)S(1)}, bf16[512,256]{1,0:T(8,128)(2,1)S(1)}, u32[]{:S(2)}, u32[]{:S(2)}) %collective-permute-start.2) | collective-permute-done | bytes 262176 | tf_op jit(solution)/shard_map/ppermute | solution.py:292
  13.3 10.4 %collective-permute-done.1 = bf16[512,256]{1,0:T(8,128)(2,1)S(1)} collective-permute-done((bf16[512,256]{1,0:T(8,128)(2,1)S(1)}, bf16[512,256]{1,0:T(8,128)(2,1)S(1)}, u32[]{:S(2)}, u32[]{:S(2)}) %collective-permute-start.1) | collective-permute-done | bytes 262176 | tf_op jit(solution)/shard_map/ppermute | solution.py:292
  23.9 6.1 %collective-permute-start.3 = (bf16[896,256]{1,0:T(8,128)(2,1)S(1)}, bf16[896,256]{1,0:T(8,128)(2,1)S(1)}, u32[]{:S(2)}, u32[]{:S(2)}) collective-permute-start(bf16[896,256]{1,0:T(8,128)(2,1)S(1)} %get-tuple-element.49), channel_id=1, source_target_pairs={{0,2},{2,4},{4,6},{6,0},{1,3},{3,5},{5,7},{7,1},{8,10},{10,12},{12... | collective-permute-start | bytes 1376264 | tf_op jit(solution)/shard_map/ppermute | solution.py:299
  30.0 2.4 %collective-permute-start.7 = (bf16[3,512,256]{2,1,0:T(8,128)(2,1)S(1)}, bf16[3,512,256]{2,1,0:T(8,128)(2,1)S(1)}, u32[]{:S(2)}, u32[]{:S(2)}) collective-permute-start(bf16[3,512,256]{2,1,0:T(8,128)(2,1)S(1)} %pad_maximum_fusion.refs_13_), channel_id=1, source_target_pairs={{0,24},{8,16},{16,8},{24,0},{1,25},{9,17},{17,9},{25,1},{2,26},{10... | collective-permute-start | bytes 2359304 | tf_op jit(solution)/shard_map/ppermute | solution.py:295
  35.1 7.5 %collective-permute-done.3.refs_1_ = bf16[896,256]{1,0:T(8,128)(2,1)S(1)} collective-permute-done((bf16[896,256]{1,0:T(8,128)(2,1)S(1)}, bf16[896,256]{1,0:T(8,128)(2,1)S(1)}, u32[]{:S(2)}, u32[]{:S(2)}) %collective-permute-start.3) | collective-permute-done | bytes 458784 | tf_op jit(solution)/shard_map/ppermute | solution.py:299
  42.6 18.0 %collective-permute-done.4.refs_2_ = bf16[896,256]{1,0:T(8,128)(2,1)} collective-permute-done((bf16[896,256]{1,0:T(8,128)(2,1)S(1)}, bf16[896,256]{1,0:T(8,128)(2,1)}, u32[]{:S(2)}, u32[]{:S(2)}) %collective-permute-start.4) | collective-permute-done | bytes 458784 | tf_op jit(solution)/shard_map/ppermute | solution.py:299
  62.7 4.2 %collective-permute-done.6.refs_15_ = bf16[3,512,256]{2,1,0:T(8,128)(2,1)S(1)} collective-permute-done((bf16[3,512,256]{2,1,0:T(8,128)(2,1)S(1)}, bf16[3,512,256]{2,1,0:T(8,128)(2,1)S(1)}, u32[]{:S(2)}, u32[]{:S(2)}) %collective-permute-start.6) | collective-permute-done | bytes 786464 | tf_op jit(solution)/shard_map/ppermute | solution.py:295
  70.2 14.1 %shard_map.100 = (bf16[2,448,256]{2,1,0:T(8,128)(2,1)}, bf16[2,448,256]{2,1,0:T(8,128)(2,1)}, bf16[2,448,1024]{2,1,0:T(8,128)(2,1)}, bf16[8,160,128]{2,1,0:T(8,128)(2,1)}, bf16[8,160,128]{2,1,0:T(8,128)(2,1)}) custom-call(s32[3]{0:T(128)} %pad_add_fusion.at_ref.core_ref, bf16[4,896,256]{2,1,0:T(8,128)(2,1)} %bitcast.37, bf16[896,256]{1,0:T(8,128)(2,1)} %copy-done.16, ...), custom_call_target="tpu_custom_call" | custom-call | flops 5637144576 | bytes 12582912 | tf_op jit(solution)/shard_map/pallas_call | solution.py:235
  84.3 7.9 %all-to-all-start = ((bf16[4,2,160,128]{3,2,1,0:T(8,128)(2,1)}), bf16[4,2,160,128]{3,2,1,0:T(8,128)(2,1)S(1)}, u32[]{:S(2)}, u32[]{:S(2)}) async-start(bf16[4,2,160,128]{3,2,1,0:T(8,128)(2,1)} %bitcast.38), calls=%async_computation | async-start | bytes 655360 | tf_op jit(solution)/shard_map/all_to_all | solution.py:370
  92.2 5.4 %shard_map.102 = (f32[2,448,256]{2,1,0:T(8,128)}, bf16[2,2,448,160]{3,2,1,0:T(8,128)(2,1)}) custom-call(s32[3]{0:T(128)} %pad_add_fusion.at_ref.core_ref, bf16[2,448,256]{2,1,0:T(8,128)(2,1)} %get-tuple-element.59.refs_0_, bf16[2,448,256]{2,1,0:T(8,128)(2,1)} %get-tuple-element.60.refs_1_, bf16[2,448,1024]{2,1,0:T(8,128)(2,1)} %get-tuple-element.61.refs_2_, ...), custom_call_target="tpu_custom_call" | custom-call | flops 481689600 | bytes 12582912 | tf_op jit(solution)/shard_map/pallas_call | solution.py:235
  97.6 5.5 %shard_map.101 = (f32[2,448,256]{2,1,0:T(8,128)}, bf16[2,2,448,160]{3,2,1,0:T(8,128)(2,1)}) custom-call(s32[3]{0:T(128)} %pad_add_fusion.at_ref.core_ref, bf16[2,448,256]{2,1,0:T(8,128)(2,1)} %get-tuple-element.59.refs_0_, bf16[2,448,256]{2,1,0:T(8,128)(2,1)} %get-tuple-element.60.refs_1_, bf16[2,448,1024]{2,1,0:T(8,128)(2,1)} %get-tuple-element.61.refs_2_, ...), custom_call_target="tpu_custom_call" | custom-call | flops 481689600 | bytes 12582912 | tf_op jit(solution)/shard_map/pallas_call | solution.py:235
  103.3 2.5 %collective-permute-start.15 = (bf16[2,160,128]{2,1,0:T(8,128)(2,1)S(1)}, bf16[2,160,128]{2,1,0:T(8,128)(2,1)S(1)}, u32[]{:S(2)}, u32[]{:S(2)}) collective-permute-start(bf16[2,160,128]{2,1,0:T(8,128)(2,1)S(1)} %reduce_sum.12), channel_id=1, source_target_pairs={{0,24},{8,16},{16,8},{24,0},{1,25},{9,17},{17,9},{25,1},{2,26},{10... | collective-permute-start | bytes 245768 | tf_op jit(solution)/shard_map/ppermute | solution.py:374
  106.8 5.4 %shard_map.103 = (f32[2,448,256]{2,1,0:T(8,128)}, bf16[2,2,448,160]{3,2,1,0:T(8,128)(2,1)}) custom-call(s32[3]{0:T(128)} %pad_add_fusion.at_ref.core_ref, bf16[2,448,256]{2,1,0:T(8,128)(2,1)} %get-tuple-element.59.refs_0_, bf16[2,448,256]{2,1,0:T(8,128)(2,1)} %get-tuple-element.60.refs_1_, bf16[2,448,1024]{2,1,0:T(8,128)(2,1)} %get-tuple-element.61.refs_2_, ...), custom_call_target="tpu_custom_call" | custom-call | flops 481689600 | bytes 12582912 | tf_op jit(solution)/shard_map/pallas_call | solution.py:235
  112.9 1.9 %shard_map.104 = (bf16[2,160,128]{2,1,0:T(8,128)(2,1)}, bf16[2,160,128]{2,1,0:T(8,128)(2,1)}, bf16[2,160,128]{2,1,0:T(8,128)(2,1)}, bf16[2,160,128]{2,1,0:T(8,128)(2,1)}) custom-call(s32[3]{0:T(128)} %pad_add_fusion.at_ref.core_ref, bf16[4,2,160,128]{3,2,1,0:T(8,128)(2,1)} %copy-done.4, bf16[2,160,128]{2,1,0:T(8,128)(2,1)} %copy-done.11, ...), custom_call_target="tpu_custom_call" | custom-call | tf_op jit(solution)/shard_map/pallas_call | solution.py:378
  114.8 3.8 %collective-permute-start.16 = (bf16[2,160,128]{2,1,0:T(8,128)(2,1)}, bf16[2,160,128]{2,1,0:T(8,128)(2,1)S(1)}, u32[]{:S(2)}, u32[]{:S(2)}) collective-permute-start(bf16[2,160,128]{2,1,0:T(8,128)(2,1)} %get-tuple-element.74), channel_id=1, source_target_pairs={{0,6},{2,0},{4,2},{6,4},{1,7},{3,1},{5,3},{7,5},{8,14},{10,8},{12,... | collective-permute-start | bytes 245768 | tf_op jit(solution)/shard_map/ppermute | solution.py:385
  120.4 5.4 %shard_map.105 = (f32[2,448,256]{2,1,0:T(8,128)}, bf16[2,2,448,160]{3,2,1,0:T(8,128)(2,1)}) custom-call(s32[3]{0:T(128)} %pad_add_fusion.at_ref.core_ref, bf16[2,448,256]{2,1,0:T(8,128)(2,1)} %get-tuple-element.59.refs_0_, bf16[2,448,256]{2,1,0:T(8,128)(2,1)} %get-tuple-element.60.refs_1_, bf16[2,448,1024]{2,1,0:T(8,128)(2,1)} %get-tuple-element.61.refs_2_, ...), custom_call_target="tpu_custom_call" | custom-call | flops 481689600 | bytes 12582912 | tf_op jit(solution)/shard_map/pallas_call | solution.py:235
  126.5 4.2 %shard_map.106.mine_ref = bf16[448,1024]{1,0:T(8,128)(2,1)} custom-call(s32[3]{0:T(128)} %pad_add_fusion.at_ref.core_ref, f32[1,1024]{1,0:T(1,128)} %bitcast.42, bf16[2,160,128]{2,1,0:T(8,128)(2,1)} %get-tuple-element.73.refs_1_, bf16[2,160,128]{2,1,0:T(8,128)(2,1)} %copy-done.6, bf16[2,160,128]{2,1,0:T(8,128)(2,1)} %copy-done.7, ...), custom_call_target="tpu_custom_call" | custom-call | flops 275251200 | bytes 12582912 | tf_op jit(solution)/shard_map/pallas_call | solution.py:235
  130.8 4.4 %shard_map.108.mine_ref = bf16[448,1024]{1,0:T(8,128)(2,1)} custom-call(s32[3]{0:T(128)} %pad_add_fusion.at_ref.core_ref, f32[1,1024]{1,0:T(1,128)} %bitcast.43, bf16[2,160,128]{2,1,0:T(8,128)(2,1)} %get-tuple-element.73.refs_1_, bf16[2,160,128]{2,1,0:T(8,128)(2,1)} %copy-done.6, bf16[2,160,128]{2,1,0:T(8,128)(2,1)} %copy-done.7, ...), custom_call_target="tpu_custom_call" | custom-call | flops 275251200 | bytes 12582912 | tf_op jit(solution)/shard_map/pallas_call | solution.py:235
  135.6 3.4 %copy-done = bf16[2048,2048]{1,0:T(8,128)(2,1)S(1)} copy-done((bf16[2048,2048]{1,0:T(8,128)(2,1)S(1)}, bf16[2048,2048]{1,0:T(8,128)(2,1)}, u32[]{:S(2)}) %copy-start) | copy-done | bytes 8388632
  139.0 1.7 shard_map.110
  140.7 2.4 %collective-permute-start.21 = (bf16[448,256]{1,0:T(8,128)(2,1)S(1)}, bf16[448,256]{1,0:T(8,128)(2,1)S(1)}, u32[]{:S(2)}, u32[]{:S(2)}) collective-permute-start(bf16[448,256]{1,0:T(8,128)(2,1)S(1)} %get-tuple-element.87), channel_id=1, source_target_pairs={{0,2},{2,4},{4,6},{6,0},{1,3},{3,5},{5,7},{7,1},{8,10},{10,12},{12... | collective-permute-start | bytes 688136 | tf_op jit(solution)/shard_map/ppermute | solution.py:436
  144.0 1.7 shard_map.107
  145.7 1.6 collective-permute-start.25
  147.4 1.7 shard_map.111
  149.5 2.0 %collective-permute-start.24 = (bf16[448,256]{1,0:T(8,128)(2,1)S(1)}, bf16[448,256]{1,0:T(8,128)(2,1)S(1)}, u32[]{:S(2)}, u32[]{:S(2)}) collective-permute-start(bf16[448,256]{1,0:T(8,128)(2,1)S(1)} %get-tuple-element.90), channel_id=1, source_target_pairs={{0,4},{2,6},{4,0},{6,2},{1,5},{3,7},{5,1},{7,3},{8,12},{10,14},{12... | collective-permute-start | bytes 688136 | tf_op jit(solution)/shard_map/ppermute | solution.py:436
  151.6 1.7 shard_map.109
  154.8 6.2 %collective-permute-done.23.refs_4_ = bf16[448,256]{1,0:T(8,128)(2,1)S(1)} collective-permute-done((bf16[448,256]{1,0:T(8,128)(2,1)S(1)}, bf16[448,256]{1,0:T(8,128)(2,1)S(1)}, u32[]{:S(2)}, u32[]{:S(2)}) %collective-permute-start.23) | collective-permute-done | bytes 229408 | tf_op jit(solution)/shard_map/ppermute | solution.py:436
  161.0 4.9 %collective-permute-done.22.refs_3_ = bf16[448,256]{1,0:T(8,128)(2,1)S(1)} collective-permute-done((bf16[448,256]{1,0:T(8,128)(2,1)S(1)}, bf16[448,256]{1,0:T(8,128)(2,1)S(1)}, u32[]{:S(2)}, u32[]{:S(2)}) %collective-permute-start.22) | collective-permute-done | bytes 229408 | tf_op jit(solution)/shard_map/ppermute | solution.py:436
  165.9 13.9 %collective-permute-done.24.refs_5_ = bf16[448,256]{1,0:T(8,128)(2,1)S(1)} collective-permute-done((bf16[448,256]{1,0:T(8,128)(2,1)S(1)}, bf16[448,256]{1,0:T(8,128)(2,1)S(1)}, u32[]{:S(2)}, u32[]{:S(2)}) %collective-permute-start.24) | collective-permute-done | bytes 229408 | tf_op jit(solution)/shard_map/ppermute | solution.py:436
  179.8 1.8 %shard_map.112 = bf16[3584,256]{1,0:T(8,128)(2,1)} custom-call(s32[3]{0:T(128)S(1)} %copy-done.3, bf16[448,256]{1,0:T(8,128)(2,1)S(1)} %get-tuple-element.85.refs_0_, bf16[448,256]{1,0:T(8,128)(2,1)S(1)} %get-tuple-element.86.refs_1_, bf16[448,256]{1,0:T(8,128)(2,1)S(1)} %collective-permute-done.21.refs_2_, ...), custom_call_target="tpu_custom_call" | custom-call | bytes 12582912 | tf_op jit(solution)/shard_map/pallas_call | solution.py:235
  (83 shorter events, 19.5 us)
Async XLA Ops:
  1.0 12.4 %collective-permute-start.2 = (bf16[512,256]{1,0:T(8,128)(2,1)S(1)}, bf16[512,256]{1,0:T(8,128)(2,1)S(1)}, u32[]{:S(2)}, u32[]{:S(2)}) collective-permute-start(bf16[512,256]{1,0:T(8,128)(2,1)S(1)} %constant_dynamic-slice_fusion), channel_id=1, source_target_pairs={{0,2},{2,4},{4,6},{6,0},{1,3},{3,5},{5,7},{7,1},{8,10},{10,12},{12... | collective-permute-start | bytes 786440 | tf_op jit(solution)/shard_map/ppermute | solution.py:292
  4.0 19.7 %collective-permute-start.1 = (bf16[512,256]{1,0:T(8,128)(2,1)S(1)}, bf16[512,256]{1,0:T(8,128)(2,1)S(1)}, u32[]{:S(2)}, u32[]{:S(2)}) collective-permute-start(bf16[512,256]{1,0:T(8,128)(2,1)S(1)} %constant_dynamic-slice_fusion), channel_id=1, source_target_pairs={{0,4},{2,6},{4,0},{6,2},{1,5},{3,7},{5,1},{7,3},{8,12},{10,14},{12... | collective-permute-start | bytes 786440 | tf_op jit(solution)/shard_map/ppermute | solution.py:292
  6.6 17.1 %collective-permute-start = (bf16[512,256]{1,0:T(8,128)(2,1)S(1)}, bf16[512,256]{1,0:T(8,128)(2,1)S(1)}, u32[]{:S(2)}, u32[]{:S(2)}) collective-permute-start(bf16[512,256]{1,0:T(8,128)(2,1)S(1)} %constant_dynamic-slice_fusion), channel_id=1, source_target_pairs={{0,6},{2,0},{4,2},{6,4},{1,7},{3,1},{5,3},{7,5},{8,14},{10,8},{12,... | collective-permute-start | bytes 786440 | tf_op jit(solution)/shard_map/ppermute | solution.py:292
  23.8 46.3 %copy-start.5 = (bf16[3,512,256]{2,1,0:T(8,128)(2,1)}, bf16[3,512,256]{2,1,0:T(8,128)(2,1)S(1)}, u32[]{:S(2)}) copy-start(bf16[3,512,256]{2,1,0:T(8,128)(2,1)S(1)} %pad_maximum_fusion.refs_13_) | copy-start | bytes 2359300
  23.9 18.7 %collective-permute-start.3 = (bf16[896,256]{1,0:T(8,128)(2,1)S(1)}, bf16[896,256]{1,0:T(8,128)(2,1)S(1)}, u32[]{:S(2)}, u32[]{:S(2)}) collective-permute-start(bf16[896,256]{1,0:T(8,128)(2,1)S(1)} %get-tuple-element.49), channel_id=1, source_target_pairs={{0,2},{2,4},{4,6},{6,0},{1,3},{3,5},{5,7},{7,1},{8,10},{10,12},{12... | collective-permute-start | bytes 1376264 | tf_op jit(solution)/shard_map/ppermute | solution.py:299
  30.0 32.2 %collective-permute-start.7 = (bf16[3,512,256]{2,1,0:T(8,128)(2,1)S(1)}, bf16[3,512,256]{2,1,0:T(8,128)(2,1)S(1)}, u32[]{:S(2)}, u32[]{:S(2)}) collective-permute-start(bf16[3,512,256]{2,1,0:T(8,128)(2,1)S(1)} %pad_maximum_fusion.refs_13_), channel_id=1, source_target_pairs={{0,24},{8,16},{16,8},{24,0},{1,25},{9,17},{17,9},{25,1},{2,26},{10... | collective-permute-start | bytes 2359304 | tf_op jit(solution)/shard_map/ppermute | solution.py:295
  32.4 34.5 %collective-permute-start.6 = (bf16[3,512,256]{2,1,0:T(8,128)(2,1)S(1)}, bf16[3,512,256]{2,1,0:T(8,128)(2,1)S(1)}, u32[]{:S(2)}, u32[]{:S(2)}) collective-permute-start(bf16[3,512,256]{2,1,0:T(8,128)(2,1)S(1)} %pad_maximum_fusion.refs_13_), channel_id=1, source_target_pairs={{0,16},{8,24},{16,0},{24,8},{1,17},{9,25},{17,1},{25,9},{2,18},{10... | collective-permute-start | bytes 2359304 | tf_op jit(solution)/shard_map/ppermute | solution.py:295
  32.9 34.1 %collective-permute-start.5 = (bf16[3,512,256]{2,1,0:T(8,128)(2,1)S(1)}, bf16[3,512,256]{2,1,0:T(8,128)(2,1)S(1)}, u32[]{:S(2)}, u32[]{:S(2)}) collective-permute-start(bf16[3,512,256]{2,1,0:T(8,128)(2,1)S(1)} %pad_maximum_fusion.refs_13_), channel_id=1, source_target_pairs={{0,8},{8,0},{16,24},{24,16},{1,9},{9,1},{17,25},{25,17},{2,10},{10... | collective-permute-start | bytes 2359304 | tf_op jit(solution)/shard_map/ppermute | solution.py:295
  33.5 27.1 %collective-permute-start.4 = (bf16[896,256]{1,0:T(8,128)(2,1)S(1)}, bf16[896,256]{1,0:T(8,128)(2,1)}, u32[]{:S(2)}, u32[]{:S(2)}) collective-permute-start(bf16[896,256]{1,0:T(8,128)(2,1)S(1)} %get-tuple-element.50), channel_id=1, source_target_pairs={{0,4},{2,6},{4,0},{6,2},{1,5},{3,7},{5,1},{7,3},{8,12},{10,14},{12... | collective-permute-start | bytes 1376264 | tf_op jit(solution)/shard_map/ppermute | solution.py:299
  42.6 27.6 %copy-start.16 = (bf16[896,256]{1,0:T(8,128)(2,1)}, bf16[896,256]{1,0:T(8,128)(2,1)S(1)}, u32[]{:S(2)}) copy-start(bf16[896,256]{1,0:T(8,128)(2,1)S(1)} %collective-permute-done.3.refs_1_) | copy-start | bytes 1376260
  42.6 19.6 %collective-permute-start.8 = (bf16[896,256]{1,0:T(8,128)(2,1)S(1)}, bf16[896,256]{1,0:T(8,128)(2,1)}, u32[]{:S(2)}, u32[]{:S(2)}) collective-permute-start(bf16[896,256]{1,0:T(8,128)(2,1)S(1)} %get-tuple-element.53), channel_id=1, source_target_pairs={{0,6},{2,0},{4,2},{6,4},{1,7},{3,1},{5,3},{7,5},{8,14},{10,8},{12,... | collective-permute-start | bytes 1376264 | tf_op jit(solution)/shard_map/ppermute | solution.py:299
  60.6 8.0 %collective-permute-start.9 = (bf16[896,256]{1,0:T(8,128)(2,1)S(1)}, bf16[896,256]{1,0:T(8,128)(2,1)}, u32[]{:S(2)}, u32[]{:S(2)}) collective-permute-start(bf16[896,256]{1,0:T(8,128)(2,1)S(1)} %get-tuple-element.54), channel_id=1, source_target_pairs={{0,1},{1,0},{2,3},{3,2},{4,5},{5,4},{6,7},{7,6},{8,9},{9,8},{10,11... | collective-permute-start | bytes 1376264 | tf_op jit(solution)/shard_map/ppermute | solution.py:302
  62.2 6.4 %collective-permute-start.10 = (bf16[896,256]{1,0:T(8,128)(2,1)S(1)}, bf16[896,256]{1,0:T(8,128)(2,1)}, u32[]{:S(2)}, u32[]{:S(2)}) collective-permute-start(bf16[896,256]{1,0:T(8,128)(2,1)S(1)} %collective-permute-done.3.refs_1_), channel_id=1, source_target_pairs={{0,1},{1,0},{2,3},{3,2},{4,5},{5,4},{6,7},{7,6},{8,9},{9,8},{10,11... | collective-permute-start | bytes 1376264 | tf_op jit(solution)/shard_map/ppermute | solution.py:302
  62.2 6.4 %collective-permute-start.12 = (bf16[896,256]{1,0:T(8,128)(2,1)}, bf16[896,256]{1,0:T(8,128)(2,1)}, u32[]{:S(2)}, u32[]{:S(2)}) collective-permute-start(bf16[896,256]{1,0:T(8,128)(2,1)} %collective-permute-done.8.refs_3_), channel_id=1, source_target_pairs={{0,1},{1,0},{2,3},{3,2},{4,5},{5,4},{6,7},{7,6},{8,9},{9,8},{10,11... | collective-permute-start | bytes 1376264 | tf_op jit(solution)/shard_map/ppermute | solution.py:302
  68.0 2.2 %collective-permute-start.11 = (bf16[896,256]{1,0:T(8,128)(2,1)}, bf16[896,256]{1,0:T(8,128)(2,1)}, u32[]{:S(2)}, u32[]{:S(2)}) collective-permute-start(bf16[896,256]{1,0:T(8,128)(2,1)} %collective-permute-done.4.refs_2_), channel_id=1, source_target_pairs={{0,1},{1,0},{2,3},{3,2},{4,5},{5,4},{6,7},{7,6},{8,9},{9,8},{10,11... | collective-permute-start | bytes 1376264 | tf_op jit(solution)/shard_map/ppermute | solution.py:302
  84.3 18.9 %all-to-all-start = ((bf16[4,2,160,128]{3,2,1,0:T(8,128)(2,1)}), bf16[4,2,160,128]{3,2,1,0:T(8,128)(2,1)S(1)}, u32[]{:S(2)}, u32[]{:S(2)}) async-start(bf16[4,2,160,128]{3,2,1,0:T(8,128)(2,1)} %bitcast.38), calls=%async_computation | async-start | bytes 655360 | tf_op jit(solution)/shard_map/all_to_all | solution.py:370
  97.6 9.2 %copy-start.12 = (f32[2048]{0:T(1024)S(1)}, f32[2048]{0:T(1024)}, u32[]{:S(2)}) copy-start(f32[2048]{0:T(1024)} %param.15) | copy-start | bytes 24580
  103.2 9.0 %copy-start.4 = (bf16[4,2,160,128]{3,2,1,0:T(8,128)(2,1)}, bf16[4,2,160,128]{3,2,1,0:T(8,128)(2,1)S(1)}, u32[]{:S(2)}) copy-start(bf16[4,2,160,128]{3,2,1,0:T(8,128)(2,1)S(1)} %all-to-all-done.line_ref) | copy-start | bytes 983044
  103.3 9.0 %collective-permute-start.15 = (bf16[2,160,128]{2,1,0:T(8,128)(2,1)S(1)}, bf16[2,160,128]{2,1,0:T(8,128)(2,1)S(1)}, u32[]{:S(2)}, u32[]{:S(2)}) collective-permute-start(bf16[2,160,128]{2,1,0:T(8,128)(2,1)S(1)} %reduce_sum.12), channel_id=1, source_target_pairs={{0,24},{8,16},{16,8},{24,0},{1,25},{9,17},{17,9},{25,1},{2,26},{10... | collective-permute-start | bytes 245768 | tf_op jit(solution)/shard_map/ppermute | solution.py:374
  105.8 6.5 %collective-permute-start.14 = (bf16[2,160,128]{2,1,0:T(8,128)(2,1)S(1)}, bf16[2,160,128]{2,1,0:T(8,128)(2,1)S(1)}, u32[]{:S(2)}, u32[]{:S(2)}) collective-permute-start(bf16[2,160,128]{2,1,0:T(8,128)(2,1)S(1)} %reduce_sum.12), channel_id=1, source_target_pairs={{0,16},{8,24},{16,0},{24,8},{1,17},{9,25},{17,1},{25,9},{2,18},{10... | collective-permute-start | bytes 245768 | tf_op jit(solution)/shard_map/ppermute | solution.py:374
  106.3 6.0 %collective-permute-start.13 = (bf16[2,160,128]{2,1,0:T(8,128)(2,1)S(1)}, bf16[2,160,128]{2,1,0:T(8,128)(2,1)S(1)}, u32[]{:S(2)}, u32[]{:S(2)}) collective-permute-start(bf16[2,160,128]{2,1,0:T(8,128)(2,1)S(1)} %reduce_sum.12), channel_id=1, source_target_pairs={{0,8},{8,0},{16,24},{24,16},{1,9},{9,1},{17,25},{25,17},{2,10},{10... | collective-permute-start | bytes 245768 | tf_op jit(solution)/shard_map/ppermute | solution.py:374
  114.8 11.0 %collective-permute-start.16 = (bf16[2,160,128]{2,1,0:T(8,128)(2,1)}, bf16[2,160,128]{2,1,0:T(8,128)(2,1)S(1)}, u32[]{:S(2)}, u32[]{:S(2)}) collective-permute-start(bf16[2,160,128]{2,1,0:T(8,128)(2,1)} %get-tuple-element.74), channel_id=1, source_target_pairs={{0,6},{2,0},{4,2},{6,4},{1,7},{3,1},{5,3},{7,5},{8,14},{10,8},{12,... | collective-permute-start | bytes 245768 | tf_op jit(solution)/shard_map/ppermute | solution.py:385
  118.7 7.2 %collective-permute-start.17 = (bf16[2,160,128]{2,1,0:T(8,128)(2,1)}, bf16[2,160,128]{2,1,0:T(8,128)(2,1)S(1)}, u32[]{:S(2)}, u32[]{:S(2)}) collective-permute-start(bf16[2,160,128]{2,1,0:T(8,128)(2,1)} %get-tuple-element.75), channel_id=1, source_target_pairs={{0,4},{2,6},{4,0},{6,2},{1,5},{3,7},{5,1},{7,3},{8,12},{10,14},{12... | collective-permute-start | bytes 245768 | tf_op jit(solution)/shard_map/ppermute | solution.py:385
  118.7 7.2 %collective-permute-start.18 = (bf16[2,160,128]{2,1,0:T(8,128)(2,1)}, bf16[2,160,128]{2,1,0:T(8,128)(2,1)S(1)}, u32[]{:S(2)}, u32[]{:S(2)}) collective-permute-start(bf16[2,160,128]{2,1,0:T(8,128)(2,1)} %get-tuple-element.76), channel_id=1, source_target_pairs={{0,2},{2,4},{4,6},{6,0},{1,3},{3,5},{5,7},{7,1},{8,10},{10,12},{12... | collective-permute-start | bytes 245768 | tf_op jit(solution)/shard_map/ppermute | solution.py:385
  130.8 4.8 %collective-permute-start.19 = (bf16[448,1024]{1,0:T(8,128)(2,1)}, bf16[448,1024]{1,0:T(8,128)(2,1)S(1)}, u32[]{:S(2)}, u32[]{:S(2)}) collective-permute-start(bf16[448,1024]{1,0:T(8,128)(2,1)} %shard_map.106.mine_ref), channel_id=1, source_target_pairs={{0,1},{1,0},{2,3},{3,2},{4,5},{5,4},{6,7},{7,6},{8,9},{9,8},{10,11... | collective-permute-start | bytes 2752520 | tf_op jit(solution)/shard_map/ppermute | solution.py:429
  135.2 12.1 %collective-permute-start.20 = (bf16[448,1024]{1,0:T(8,128)(2,1)}, bf16[448,1024]{1,0:T(8,128)(2,1)S(1)}, u32[]{:S(2)}, u32[]{:S(2)}) collective-permute-start(bf16[448,1024]{1,0:T(8,128)(2,1)} %shard_map.108.mine_ref), channel_id=1, source_target_pairs={{0,1},{1,0},{2,3},{3,2},{4,5},{5,4},{6,7},{7,6},{8,9},{9,8},{10,11... | collective-permute-start | bytes 2752520 | tf_op jit(solution)/shard_map/ppermute | solution.py:429
  140.7 12.6 %collective-permute-start.21 = (bf16[448,256]{1,0:T(8,128)(2,1)S(1)}, bf16[448,256]{1,0:T(8,128)(2,1)S(1)}, u32[]{:S(2)}, u32[]{:S(2)}) collective-permute-start(bf16[448,256]{1,0:T(8,128)(2,1)S(1)} %get-tuple-element.87), channel_id=1, source_target_pairs={{0,2},{2,4},{4,6},{6,0},{1,3},{3,5},{5,7},{7,1},{8,10},{10,12},{12... | collective-permute-start | bytes 688136 | tf_op jit(solution)/shard_map/ppermute | solution.py:436
  143.1 17.9 %collective-permute-start.23 = (bf16[448,256]{1,0:T(8,128)(2,1)S(1)}, bf16[448,256]{1,0:T(8,128)(2,1)S(1)}, u32[]{:S(2)}, u32[]{:S(2)}) collective-permute-start(bf16[448,256]{1,0:T(8,128)(2,1)S(1)} %get-tuple-element.89), channel_id=1, source_target_pairs={{0,4},{2,6},{4,0},{6,2},{1,5},{3,7},{5,1},{7,3},{8,12},{10,14},{12... | collective-permute-start | bytes 688136 | tf_op jit(solution)/shard_map/ppermute | solution.py:436
  145.7 15.3 %collective-permute-start.25 = (bf16[448,256]{1,0:T(8,128)(2,1)S(1)}, bf16[448,256]{1,0:T(8,128)(2,1)S(1)}, u32[]{:S(2)}, u32[]{:S(2)}) collective-permute-start(bf16[448,256]{1,0:T(8,128)(2,1)S(1)} %get-tuple-element.91), channel_id=1, source_target_pairs={{0,6},{2,0},{4,2},{6,4},{1,7},{3,1},{5,3},{7,5},{8,14},{10,8},{12,... | collective-permute-start | bytes 688136 | tf_op jit(solution)/shard_map/ppermute | solution.py:436
  149.0 16.8 %collective-permute-start.22 = (bf16[448,256]{1,0:T(8,128)(2,1)S(1)}, bf16[448,256]{1,0:T(8,128)(2,1)S(1)}, u32[]{:S(2)}, u32[]{:S(2)}) collective-permute-start(bf16[448,256]{1,0:T(8,128)(2,1)S(1)} %get-tuple-element.88), channel_id=1, source_target_pairs={{0,2},{2,4},{4,6},{6,0},{1,3},{3,5},{5,7},{7,1},{8,10},{10,12},{12... | collective-permute-start | bytes 688136 | tf_op jit(solution)/shard_map/ppermute | solution.py:436
  149.5 30.3 %collective-permute-start.24 = (bf16[448,256]{1,0:T(8,128)(2,1)S(1)}, bf16[448,256]{1,0:T(8,128)(2,1)S(1)}, u32[]{:S(2)}, u32[]{:S(2)}) collective-permute-start(bf16[448,256]{1,0:T(8,128)(2,1)S(1)} %get-tuple-element.90), channel_id=1, source_target_pairs={{0,4},{2,6},{4,0},{6,2},{1,5},{3,7},{5,1},{7,3},{8,12},{10,14},{12... | collective-permute-start | bytes 688136 | tf_op jit(solution)/shard_map/ppermute | solution.py:436
  153.3 26.6 %collective-permute-start.26 = (bf16[448,256]{1,0:T(8,128)(2,1)S(1)}, bf16[448,256]{1,0:T(8,128)(2,1)S(1)}, u32[]{:S(2)}, u32[]{:S(2)}) collective-permute-start(bf16[448,256]{1,0:T(8,128)(2,1)S(1)} %get-tuple-element.92), channel_id=1, source_target_pairs={{0,6},{2,0},{4,2},{6,4},{1,7},{3,1},{5,3},{7,5},{8,14},{10,8},{12,... | collective-permute-start | bytes 688136 | tf_op jit(solution)/shard_map/ppermute | solution.py:436
  (15 other events, 41.9 us)

commit v8 on v7

--- a/solution.py
+++ b/solution.py
@@ -231,7 +231,7 @@
     return pltpu.CompilerParams(vmem_limit_bytes=mib * MIB)
 
 
-def call(kernel, scalar, grid, in_specs, out_specs, out_shape, args, flops, scratch=(), mib=60):
+def call(kernel, scalar, grid, in_specs, out_specs, out_shape, args, flops, scratch=(), *, mib):
     return pl.pallas_call(
         kernel,
         grid_spec=pltpu.PrefetchScalarGridSpec(
@@ -335,6 +335,7 @@
             pltpu.VMEM((2, heads * PACKED, rows), BF16),
             pltpu.SemaphoreType.DMA((3 + (layers - 1) * slabs,)),
         ],
+        mib=36,
     )
 
     parts = 4
@@ -364,6 +365,7 @@
             ],
             (query, key, value, early, query_table, query_bias),
             heads * rows * rows * 300,
+            mib=20,
         )
 
     own = total.reshape(layers, per_group, PACKED, HEAD_DIM)
@@ -402,6 +404,7 @@
             (gain_mine, *prefix, *(num for num, _ in locals_), *(phi for _, phi in locals_)),
             rows * heads * HEAD_DIM * 600,
             [pltpu.VMEM((layers,) + piece_shape, BF16)],
+            mib=16,
         )
 
     w_rows = w_out.reshape(layers, 2, value_width, model)

time: 185 us -> 201 us (1.086)
  local copies, waits for them, and re-layouts: 8.84 us -> 45 us
  Pallas kernels: 55 us -> 35.9 us
  waiting for transfers between devices: 72.3 us -> 67.2 us
  starting transfers between devices: 44.6 us -> 47.2 us
    unnamed x38 -> x112, local copies, waits for them, and re-layouts: 5.72 us -> 41.7 us
    pallas_call x12, Pallas kernels: 53.1 us -> 34 us  [call(): pl.pallas_call(kernel, grid_spec=pltpu.PrefetchScalarGridSpec(num_scalar_...]
    all_to_all x1, starting transfers between devices: 7.9 us -> 10.4 us  [per_device(): line = lax.all_to_all(own, 'z', split_axis=0, concat_axis=0, tiled=True)]
    ppermute x3, waiting for transfers between devices: 4.34 us -> 1.9 us  [per_device(): lax.ppermute(stack, 'seq', flip(m))]
  transfers between devices with their start and end apart: 28 -> 28, of which waited for: 11 -> 11; matrix products, arithmetic and copies ran while one was open for 2% -> 1% of each run, Pallas kernels for 18% -> 10%
where the time goes in v8:
time: 201 us; the launch traced here: 197 us
  waiting for transfers between devices  67.2 us (33%)
  starting transfers between devices  47.2 us (23%)
  local copies, waits for them, and re-layouts  45 us (22%)
  Pallas kernels  35.9 us (18%)
    unnamed x112, local copies, waits for them, and re-layouts  41.7 us
    pallas_call x12, Pallas kernels, call(): pl.pallas_call(kernel, grid_spec=pltpu.PrefetchScalarGridSpec(num_scalar_...  34 us
    ppermute x3, waiting for transfers between devices, per_device(): lax.ppermute(sent[d], 'z', turn(d))  26.1 us
    ppermute x6, waiting for transfers between devices, per_device(): pieces[d, chunk] = lax.ppermute(piece, 'z', turn(d)) if d else piece  25.1 us
    ppermute x3, waiting for transfers between devices, per_device(): lax.ppermute(value_part, 'z', turn(-d))  13.4 us
    all_to_all x1, starting transfers between devices, per_device(): line = lax.all_to_all(own, 'z', split_axis=0, concat_axis=0, tiled=True)  10.4 us
    ppermute x6, starting transfers between devices, per_device(): pieces[d, chunk] = lax.ppermute(piece, 'z', turn(d)) if d else piece  8.98 us
    ppermute x3, starting transfers between devices, per_device(): lax.ppermute(sent[d], 'z', turn(d))  7.73 us
  transfers between devices with their start and end apart: 28, of which 11 were waited for; matrix products, arithmetic and copies ran while one was open for 1% of the time, Pallas kernels for 10%

profile of v8, /device:TPU:0, one launch (start us, length us, event | category | flops | bytes accessed | tf_op | source)
XLA Modules:
  0.0 197.0 jit_solution(14801473719718855573)
XLA Ops:
  1.0 3.1 %collective-permute-start.2 = (bf16[512,256]{1,0:T(8,128)(2,1)S(1)}, bf16[512,256]{1,0:T(8,128)(2,1)S(1)}, u32[]{:S(2)}, u32[]{:S(2)}) collective-permute-start(bf16[512,256]{1,0:T(8,128)(2,1)S(1)} %constant_dynamic-slice_fusion), channel_id=1, source_target_pairs={{0,2},{2,4},{4,6},{6,0},{1,3},{3,5},{5,7},{7,1},{8,10},{10,12},{12... | collective-permute-start | bytes 786440 | tf_op jit(solution)/shard_map/ppermute | solution.py:292
  4.0 2.6 %collective-permute-start.1 = (bf16[512,256]{1,0:T(8,128)(2,1)S(1)}, bf16[512,256]{1,0:T(8,128)(2,1)S(1)}, u32[]{:S(2)}, u32[]{:S(2)}) collective-permute-start(bf16[512,256]{1,0:T(8,128)(2,1)S(1)} %constant_dynamic-slice_fusion), channel_id=1, source_target_pairs={{0,4},{2,6},{4,0},{6,2},{1,5},{3,7},{5,1},{7,3},{8,12},{10,14},{12... | collective-permute-start | bytes 786440 | tf_op jit(solution)/shard_map/ppermute | solution.py:292
  8.0 2.3 %dynamic-slice_bitcast_fusion = (bf16[896,256]{1,0:T(8,128)(2,1)S(1)}, bf16[896,256]{1,0:T(8,128)(2,1)S(1)}, bf16[896,256]{1,0:T(8,128)(2,1)S(1)}, bf16[896,256]{1,0:T(8,128)(2,1)}) fusion(bf16[4,896,256]{2,1,0:T(8,128)(2,1)} %bitcast.36, s32[]{:T(128)S(6)} %select_n.25, s32[]{:T(128)S(6)} %select_n.24, s32[]{:T(128)S(6)} %select_n.23, s32[]{:T(128)S(6)} %select_n.22), kind=kLoop, calls=%fused_computation.1 | loop fusion | bytes 3670032 | tf_op jit(solution)/shard_map/jit(dynamic_index_in_dim)/squeeze | solution.py:291
  10.3 3.0 %collective-permute-done.2 = bf16[512,256]{1,0:T(8,128)(2,1)S(1)} collective-permute-done((bf16[512,256]{1,0:T(8,128)(2,1)S(1)}, bf16[512,256]{1,0:T(8,128)(2,1)S(1)}, u32[]{:S(2)}, u32[]{:S(2)}) %collective-permute-start.2) | collective-permute-done | bytes 262176 | tf_op jit(solution)/shard_map/ppermute | solution.py:292
  13.3 10.4 %collective-permute-done.1 = bf16[512,256]{1,0:T(8,128)(2,1)S(1)} collective-permute-done((bf16[512,256]{1,0:T(8,128)(2,1)S(1)}, bf16[512,256]{1,0:T(8,128)(2,1)S(1)}, u32[]{:S(2)}, u32[]{:S(2)}) %collective-permute-start.1) | collective-permute-done | bytes 262176 | tf_op jit(solution)/shard_map/ppermute | solution.py:292
  23.8 6.1 %collective-permute-start.3 = (bf16[896,256]{1,0:T(8,128)(2,1)S(1)}, bf16[896,256]{1,0:T(8,128)(2,1)S(1)}, u32[]{:S(2)}, u32[]{:S(2)}) collective-permute-start(bf16[896,256]{1,0:T(8,128)(2,1)S(1)} %get-tuple-element.49), channel_id=1, source_target_pairs={{0,2},{2,4},{4,6},{6,0},{1,3},{3,5},{5,7},{7,1},{8,10},{10,12},{12... | collective-permute-start | bytes 1376264 | tf_op jit(solution)/shard_map/ppermute | solution.py:299
  30.0 2.4 %collective-permute-start.7 = (bf16[3,512,256]{2,1,0:T(8,128)(2,1)S(1)}, bf16[3,512,256]{2,1,0:T(8,128)(2,1)S(1)}, u32[]{:S(2)}, u32[]{:S(2)}) collective-permute-start(bf16[3,512,256]{2,1,0:T(8,128)(2,1)S(1)} %pad_maximum_fusion.refs_13_), channel_id=1, source_target_pairs={{0,24},{8,16},{16,8},{24,0},{1,25},{9,17},{17,9},{25,1},{2,26},{10... | collective-permute-start | bytes 2359304 | tf_op jit(solution)/shard_map/ppermute | solution.py:295
  35.9 6.6 %collective-permute-done.3.refs_1_ = bf16[896,256]{1,0:T(8,128)(2,1)S(1)} collective-permute-done((bf16[896,256]{1,0:T(8,128)(2,1)S(1)}, bf16[896,256]{1,0:T(8,128)(2,1)S(1)}, u32[]{:S(2)}, u32[]{:S(2)}) %collective-permute-start.3) | collective-permute-done | bytes 458784 | tf_op jit(solution)/shard_map/ppermute | solution.py:299
  42.5 17.9 %collective-permute-done.4.refs_2_ = bf16[896,256]{1,0:T(8,128)(2,1)S(1)} collective-permute-done((bf16[896,256]{1,0:T(8,128)(2,1)S(1)}, bf16[896,256]{1,0:T(8,128)(2,1)S(1)}, u32[]{:S(2)}, u32[]{:S(2)}) %collective-permute-start.4) | collective-permute-done | bytes 458784 | tf_op jit(solution)/shard_map/ppermute | solution.py:299
  65.0 1.9 collective-permute-done.6.refs_15_
  88.0 11.2 %shard_map.100 = (bf16[2,448,256]{2,1,0:T(8,128)(2,1)S(1)}, bf16[2,448,256]{2,1,0:T(8,128)(2,1)S(1)}, bf16[2,448,1024]{2,1,0:T(8,128)(2,1)S(1)}, bf16[8,160,128]...) custom-call(s32[3]{0:T(128)S(1)} %pad_add_fusion.at_ref.core_ref, bf16[4,896,256]{2,1,0:T(8,128)(2,1)S(1)} %bitcast.37, ...), custom_call_target="tpu_custom_call" | custom-call | flops 5637144576 | bytes 12582912 | tf_op jit(solution)/shard_map/pallas_call | solution.py:235
  101.5 10.4 %all-to-all-start = ((bf16[4,2,160,128]{3,2,1,0:T(8,128)(2,1)}), bf16[4,2,160,128]{3,2,1,0:T(8,128)(2,1)}, u32[]{:S(2)}, u32[]{:S(2)}) async-start(bf16[4,2,160,128]{3,2,1,0:T(8,128)(2,1)} %bitcast.38), calls=%async_computation | async-start | bytes 655360 | tf_op jit(solution)/shard_map/all_to_all | solution.py:372
  113.9 2.7 %shard_map.102 = (f32[2,448,256]{2,1,0:T(8,128)S(1)}, bf16[2,2,448,160]{3,2,1,0:T(8,128)(2,1)S(1)}) custom-call(s32[3]{0:T(128)S(1)} %pad_add_fusion.at_ref.core_ref, bf16[2,448,256]{2,1,0:T(8,128)(2,1)S(1)} %get-tuple-element.59.refs_0_, bf16[2,448,256]{2,1,0:T(8,128)(2,1)S(1)} %copy-done.2, bf16[2,448,1024]{2,1,0:T(8,128)(2,1)S(1)} %get-tuple-element.61.refs_2_, ...), custom_call_target="tpu_custom_call" | custom-call | flops 481689600 | bytes 12582912 | tf_op jit(solution)/shard_map/pallas_call | solution.py:235
  118.4 2.7 %shard_map.101 = (f32[2,448,256]{2,1,0:T(8,128)S(1)}, bf16[2,2,448,160]{3,2,1,0:T(8,128)(2,1)S(1)}) custom-call(s32[3]{0:T(128)S(1)} %pad_add_fusion.at_ref.core_ref, bf16[2,448,256]{2,1,0:T(8,128)(2,1)S(1)} %get-tuple-element.59.refs_0_, bf16[2,448,256]{2,1,0:T(8,128)(2,1)S(1)} %copy-done.2, bf16[2,448,1024]{2,1,0:T(8,128)(2,1)S(1)} %get-tuple-element.61.refs_2_, ...), custom_call_target="tpu_custom_call" | custom-call | flops 481689600 | bytes 12582912 | tf_op jit(solution)/shard_map/pallas_call | solution.py:235
  124.0 2.5 %collective-permute-start.15 = (bf16[2,160,128]{2,1,0:T(8,128)(2,1)S(1)}, bf16[2,160,128]{2,1,0:T(8,128)(2,1)S(1)}, u32[]{:S(2)}, u32[]{:S(2)}) collective-permute-start(bf16[2,160,128]{2,1,0:T(8,128)(2,1)S(1)} %reduce_sum.12), channel_id=1, source_target_pairs={{0,24},{8,16},{16,8},{24,0},{1,25},{9,17},{17,9},{25,1},{2,26},{10... | collective-permute-start | bytes 245768 | tf_op jit(solution)/shard_map/ppermute | solution.py:376
  129.6 2.7 %shard_map.103 = (f32[2,448,256]{2,1,0:T(8,128)S(1)}, bf16[2,2,448,160]{3,2,1,0:T(8,128)(2,1)S(1)}) custom-call(s32[3]{0:T(128)S(1)} %pad_add_fusion.at_ref.core_ref, bf16[2,448,256]{2,1,0:T(8,128)(2,1)S(1)} %get-tuple-element.59.refs_0_, bf16[2,448,256]{2,1,0:T(8,128)(2,1)S(1)} %copy-done.3, bf16[2,448,1024]{2,1,0:T(8,128)(2,1)S(1)} %get-tuple-element.61.refs_2_, ...), custom_call_target="tpu_custom_call" | custom-call | flops 481689600 | bytes 12582912 | tf_op jit(solution)/shard_map/pallas_call | solution.py:235
  134.8 1.9 shard_map.104
  136.7 3.8 %collective-permute-start.16 = (bf16[2,160,128]{2,1,0:T(8,128)(2,1)}, bf16[2,160,128]{2,1,0:T(8,128)(2,1)S(1)}, u32[]{:S(2)}, u32[]{:S(2)}) collective-permute-start(bf16[2,160,128]{2,1,0:T(8,128)(2,1)} %get-tuple-element.74), channel_id=1, source_target_pairs={{0,6},{2,0},{4,2},{6,4},{1,7},{3,1},{5,3},{7,5},{8,14},{10,8},{12,... | collective-permute-start | bytes 245768 | tf_op jit(solution)/shard_map/ppermute | solution.py:387
  144.3 2.7 %shard_map.105 = (f32[2,448,256]{2,1,0:T(8,128)S(1)}, bf16[2,2,448,160]{3,2,1,0:T(8,128)(2,1)S(1)}) custom-call(s32[3]{0:T(128)S(1)} %copy-done.28, bf16[2,448,256]{2,1,0:T(8,128)(2,1)S(1)} %get-tuple-element.59.refs_0_, bf16[2,448,256]{2,1,0:T(8,128)(2,1)S(1)} %copy-done.4, bf16[2,448,1024]{2,1,0:T(8,128)(2,1)S(1)} %get-tuple-element.61.refs_2_, ...), custom_call_target="tpu_custom_call" | custom-call | flops 481689600 | bytes 12582912 | tf_op jit(solution)/shard_map/pallas_call | solution.py:235
  149.9 1.8 shard_map.106.mine_ref
  151.7 1.8 shard_map.108.mine_ref
  154.2 1.7 shard_map.110
  155.9 2.0 %collective-permute-start.21 = (bf16[448,256]{1,0:T(8,128)(2,1)S(1)}, bf16[448,256]{1,0:T(8,128)(2,1)S(1)}, u32[]{:S(2)}, u32[]{:S(2)}) collective-permute-start(bf16[448,256]{1,0:T(8,128)(2,1)S(1)} %get-tuple-element.87), channel_id=1, source_target_pairs={{0,2},{2,4},{4,6},{6,0},{1,3},{3,5},{5,7},{7,1},{8,10},{10,12},{12... | collective-permute-start | bytes 688136 | tf_op jit(solution)/shard_map/ppermute | solution.py:439
  158.7 1.7 shard_map.107
  160.4 1.9 collective-permute-start.25
  164.2 2.0 %collective-permute-start.24 = (bf16[448,256]{1,0:T(8,128)(2,1)S(1)}, bf16[448,256]{1,0:T(8,128)(2,1)S(1)}, u32[]{:S(2)}, u32[]{:S(2)}) collective-permute-start(bf16[448,256]{1,0:T(8,128)(2,1)S(1)} %get-tuple-element.90), channel_id=1, source_target_pairs={{0,4},{2,6},{4,0},{6,2},{1,5},{3,7},{5,1},{7,3},{8,12},{10,14},{12... | collective-permute-start | bytes 688136 | tf_op jit(solution)/shard_map/ppermute | solution.py:439
  166.3 1.7 shard_map.109
  168.0 2.0 collective-permute-start.26
  169.9 6.3 %collective-permute-done.23.refs_4_ = bf16[448,256]{1,0:T(8,128)(2,1)S(1)} collective-permute-done((bf16[448,256]{1,0:T(8,128)(2,1)S(1)}, bf16[448,256]{1,0:T(8,128)(2,1)S(1)}, u32[]{:S(2)}, u32[]{:S(2)}) %collective-permute-start.23) | collective-permute-done | bytes 229408 | tf_op jit(solution)/shard_map/ppermute | solution.py:439
  176.2 4.9 %collective-permute-done.22.refs_3_ = bf16[448,256]{1,0:T(8,128)(2,1)S(1)} collective-permute-done((bf16[448,256]{1,0:T(8,128)(2,1)S(1)}, bf16[448,256]{1,0:T(8,128)(2,1)S(1)}, u32[]{:S(2)}, u32[]{:S(2)}) %collective-permute-start.22) | collective-permute-done | bytes 229408 | tf_op jit(solution)/shard_map/ppermute | solution.py:439
  181.1 13.9 %collective-permute-done.24.refs_5_ = bf16[448,256]{1,0:T(8,128)(2,1)S(1)} collective-permute-done((bf16[448,256]{1,0:T(8,128)(2,1)S(1)}, bf16[448,256]{1,0:T(8,128)(2,1)S(1)}, u32[]{:S(2)}, u32[]{:S(2)}) %collective-permute-start.24) | collective-permute-done | bytes 229408 | tf_op jit(solution)/shard_map/ppermute | solution.py:439
  195.1 1.8 shard_map.112
  (157 shorter events, 56.2 us)
Async XLA Ops:
  1.0 12.4 %collective-permute-start.2 = (bf16[512,256]{1,0:T(8,128)(2,1)S(1)}, bf16[512,256]{1,0:T(8,128)(2,1)S(1)}, u32[]{:S(2)}, u32[]{:S(2)}) collective-permute-start(bf16[512,256]{1,0:T(8,128)(2,1)S(1)} %constant_dynamic-slice_fusion), channel_id=1, source_target_pairs={{0,2},{2,4},{4,6},{6,0},{1,3},{3,5},{5,7},{7,1},{8,10},{10,12},{12... | collective-permute-start | bytes 786440 | tf_op jit(solution)/shard_map/ppermute | solution.py:292
  4.0 19.7 %collective-permute-start.1 = (bf16[512,256]{1,0:T(8,128)(2,1)S(1)}, bf16[512,256]{1,0:T(8,128)(2,1)S(1)}, u32[]{:S(2)}, u32[]{:S(2)}) collective-permute-start(bf16[512,256]{1,0:T(8,128)(2,1)S(1)} %constant_dynamic-slice_fusion), channel_id=1, source_target_pairs={{0,4},{2,6},{4,0},{6,2},{1,5},{3,7},{5,1},{7,3},{8,12},{10,14},{12... | collective-permute-start | bytes 786440 | tf_op jit(solution)/shard_map/ppermute | solution.py:292
  6.6 17.1 %collective-permute-start = (bf16[512,256]{1,0:T(8,128)(2,1)S(1)}, bf16[512,256]{1,0:T(8,128)(2,1)S(1)}, u32[]{:S(2)}, u32[]{:S(2)}) collective-permute-start(bf16[512,256]{1,0:T(8,128)(2,1)S(1)} %constant_dynamic-slice_fusion), channel_id=1, source_target_pairs={{0,6},{2,0},{4,2},{6,4},{1,7},{3,1},{5,3},{7,5},{8,14},{10,8},{12,... | collective-permute-start | bytes 786440 | tf_op jit(solution)/shard_map/ppermute | solution.py:292
  23.8 18.7 %collective-permute-start.3 = (bf16[896,256]{1,0:T(8,128)(2,1)S(1)}, bf16[896,256]{1,0:T(8,128)(2,1)S(1)}, u32[]{:S(2)}, u32[]{:S(2)}) collective-permute-start(bf16[896,256]{1,0:T(8,128)(2,1)S(1)} %get-tuple-element.49), channel_id=1, source_target_pairs={{0,2},{2,4},{4,6},{6,0},{1,3},{3,5},{5,7},{7,1},{8,10},{10,12},{12... | collective-permute-start | bytes 1376264 | tf_op jit(solution)/shard_map/ppermute | solution.py:299
  30.0 32.9 %collective-permute-start.7 = (bf16[3,512,256]{2,1,0:T(8,128)(2,1)S(1)}, bf16[3,512,256]{2,1,0:T(8,128)(2,1)S(1)}, u32[]{:S(2)}, u32[]{:S(2)}) collective-permute-start(bf16[3,512,256]{2,1,0:T(8,128)(2,1)S(1)} %pad_maximum_fusion.refs_13_), channel_id=1, source_target_pairs={{0,24},{8,16},{16,8},{24,0},{1,25},{9,17},{17,9},{25,1},{2,26},{10... | collective-permute-start | bytes 2359304 | tf_op jit(solution)/shard_map/ppermute | solution.py:295
  32.4 34.5 %collective-permute-start.6 = (bf16[3,512,256]{2,1,0:T(8,128)(2,1)S(1)}, bf16[3,512,256]{2,1,0:T(8,128)(2,1)S(1)}, u32[]{:S(2)}, u32[]{:S(2)}) collective-permute-start(bf16[3,512,256]{2,1,0:T(8,128)(2,1)S(1)} %pad_maximum_fusion.refs_13_), channel_id=1, source_target_pairs={{0,16},{8,24},{16,0},{24,8},{1,17},{9,25},{17,1},{25,9},{2,18},{10... | collective-permute-start | bytes 2359304 | tf_op jit(solution)/shard_map/ppermute | solution.py:295
  32.9 34.9 %collective-permute-start.5 = (bf16[3,512,256]{2,1,0:T(8,128)(2,1)S(1)}, bf16[3,512,256]{2,1,0:T(8,128)(2,1)S(1)}, u32[]{:S(2)}, u32[]{:S(2)}) collective-permute-start(bf16[3,512,256]{2,1,0:T(8,128)(2,1)S(1)} %pad_maximum_fusion.refs_13_), channel_id=1, source_target_pairs={{0,8},{8,0},{16,24},{24,16},{1,9},{9,1},{17,25},{25,17},{2,10},{10... | collective-permute-start | bytes 2359304 | tf_op jit(solution)/shard_map/ppermute | solution.py:295
  34.4 26.1 %collective-permute-start.4 = (bf16[896,256]{1,0:T(8,128)(2,1)S(1)}, bf16[896,256]{1,0:T(8,128)(2,1)S(1)}, u32[]{:S(2)}, u32[]{:S(2)}) collective-permute-start(bf16[896,256]{1,0:T(8,128)(2,1)S(1)} %get-tuple-element.50), channel_id=1, source_target_pairs={{0,4},{2,6},{4,0},{6,2},{1,5},{3,7},{5,1},{7,3},{8,12},{10,14},{12... | collective-permute-start | bytes 1376264 | tf_op jit(solution)/shard_map/ppermute | solution.py:299
  42.5 19.5 %collective-permute-start.8 = (bf16[896,256]{1,0:T(8,128)(2,1)S(1)}, bf16[896,256]{1,0:T(8,128)(2,1)S(1)}, u32[]{:S(2)}, u32[]{:S(2)}) collective-permute-start(bf16[896,256]{1,0:T(8,128)(2,1)S(1)} %get-tuple-element.53), channel_id=1, source_target_pairs={{0,6},{2,0},{4,2},{6,4},{1,7},{3,1},{5,3},{7,5},{8,14},{10,8},{12,... | collective-permute-start | bytes 1376264 | tf_op jit(solution)/shard_map/ppermute | solution.py:299
  60.5 9.1 %collective-permute-start.9 = (bf16[896,256]{1,0:T(8,128)(2,1)}, bf16[896,256]{1,0:T(8,128)(2,1)S(1)}, u32[]{:S(2)}, u32[]{:S(2)}) collective-permute-start(bf16[896,256]{1,0:T(8,128)(2,1)} %get-tuple-element.54), channel_id=1, source_target_pairs={{0,1},{1,0},{2,3},{3,2},{4,5},{5,4},{6,7},{7,6},{8,9},{9,8},{10,11... | collective-permute-start | bytes 1376264 | tf_op jit(solution)/shard_map/ppermute | solution.py:302
  62.1 8.3 %collective-permute-start.10 = (bf16[896,256]{1,0:T(8,128)(2,1)S(1)}, bf16[896,256]{1,0:T(8,128)(2,1)S(1)}, u32[]{:S(2)}, u32[]{:S(2)}) collective-permute-start(bf16[896,256]{1,0:T(8,128)(2,1)S(1)} %collective-permute-done.3.refs_1_), channel_id=1, source_target_pairs={{0,1},{1,0},{2,3},{3,2},{4,5},{5,4},{6,7},{7,6},{8,9},{9,8},{10,11... | collective-permute-start | bytes 1376264 | tf_op jit(solution)/shard_map/ppermute | solution.py:302
  63.7 7.4 %collective-permute-start.12 = (bf16[896,256]{1,0:T(8,128)(2,1)S(1)}, bf16[896,256]{1,0:T(8,128)(2,1)}, u32[]{:S(2)}, u32[]{:S(2)}) collective-permute-start(bf16[896,256]{1,0:T(8,128)(2,1)S(1)} %collective-permute-done.8.refs_3_), channel_id=1, source_target_pairs={{0,1},{1,0},{2,3},{3,2},{4,5},{5,4},{6,7},{7,6},{8,9},{9,8},{10,11... | collective-permute-start | bytes 1376264 | tf_op jit(solution)/shard_map/ppermute | solution.py:302
  68.7 2.5 %collective-permute-start.11 = (bf16[896,256]{1,0:T(8,128)(2,1)S(1)}, bf16[896,256]{1,0:T(8,128)(2,1)}, u32[]{:S(2)}, u32[]{:S(2)}) collective-permute-start(bf16[896,256]{1,0:T(8,128)(2,1)S(1)} %collective-permute-done.4.refs_2_), channel_id=1, source_target_pairs={{0,1},{1,0},{2,3},{3,2},{4,5},{5,4},{6,7},{7,6},{8,9},{9,8},{10,11... | collective-permute-start | bytes 1376264 | tf_op jit(solution)/shard_map/ppermute | solution.py:302
  69.5 42.4 %copy-start.31 = (f32[1,512]{1,0:T(1,128)S(1)}, f32[1,512]{1,0:T(1,128)}, u32[]{:S(2)}) copy-start(f32[1,512]{1,0:T(1,128)} %constant.61.clone.refs_5_) | copy-start | bytes 6148
  69.6 58.0 %copy-start.27 = (s32[3]{0:T(128)}, s32[3]{0:T(128)S(1)}, u32[]{:S(2)}) copy-start(s32[3]{0:T(128)S(1)} %pad_add_fusion.at_ref.core_ref) | copy-start | bytes 40
  69.6 42.3 %copy-start = (bf16[8,128,512]{2,1,0:T(8,128)(2,1)S(1)}, bf16[8,128,512]{2,1,0:T(8,128)(2,1)}, u32[]{:S(2)}) copy-start(bf16[8,128,512]{2,1,0:T(8,128)(2,1)} %constant.60.clone.refs_4_) | copy-start | bytes 3145732
  101.5 21.4 %all-to-all-start = ((bf16[4,2,160,128]{3,2,1,0:T(8,128)(2,1)}), bf16[4,2,160,128]{3,2,1,0:T(8,128)(2,1)}, u32[]{:S(2)}, u32[]{:S(2)}) async-start(bf16[4,2,160,128]{3,2,1,0:T(8,128)(2,1)} %bitcast.38), calls=%async_computation | async-start | bytes 655360 | tf_op jit(solution)/shard_map/all_to_all | solution.py:372
  118.4 9.1 %copy-start.53 = (f32[2048]{0:T(1024)S(1)}, f32[2048]{0:T(1024)}, u32[]{:S(2)}) copy-start(f32[2048]{0:T(1024)} %param.15) | copy-start | bytes 24580
  124.0 10.1 %collective-permute-start.15 = (bf16[2,160,128]{2,1,0:T(8,128)(2,1)S(1)}, bf16[2,160,128]{2,1,0:T(8,128)(2,1)S(1)}, u32[]{:S(2)}, u32[]{:S(2)}) collective-permute-start(bf16[2,160,128]{2,1,0:T(8,128)(2,1)S(1)} %reduce_sum.12), channel_id=1, source_target_pairs={{0,24},{8,16},{16,8},{24,0},{1,25},{9,17},{17,9},{25,1},{2,26},{10... | collective-permute-start | bytes 245768 | tf_op jit(solution)/shard_map/ppermute | solution.py:376
  126.5 7.6 %collective-permute-start.14 = (bf16[2,160,128]{2,1,0:T(8,128)(2,1)S(1)}, bf16[2,160,128]{2,1,0:T(8,128)(2,1)}, u32[]{:S(2)}, u32[]{:S(2)}) collective-permute-start(bf16[2,160,128]{2,1,0:T(8,128)(2,1)S(1)} %reduce_sum.12), channel_id=1, source_target_pairs={{0,16},{8,24},{16,0},{24,8},{1,17},{9,25},{17,1},{25,9},{2,18},{10... | collective-permute-start | bytes 245768 | tf_op jit(solution)/shard_map/ppermute | solution.py:376
  127.0 7.1 %collective-permute-start.13 = (bf16[2,160,128]{2,1,0:T(8,128)(2,1)S(1)}, bf16[2,160,128]{2,1,0:T(8,128)(2,1)}, u32[]{:S(2)}, u32[]{:S(2)}) collective-permute-start(bf16[2,160,128]{2,1,0:T(8,128)(2,1)S(1)} %reduce_sum.12), channel_id=1, source_target_pairs={{0,8},{8,0},{16,24},{24,16},{1,9},{9,1},{17,25},{25,17},{2,10},{10... | collective-permute-start | bytes 245768 | tf_op jit(solution)/shard_map/ppermute | solution.py:376
  136.7 10.3 %collective-permute-start.16 = (bf16[2,160,128]{2,1,0:T(8,128)(2,1)}, bf16[2,160,128]{2,1,0:T(8,128)(2,1)S(1)}, u32[]{:S(2)}, u32[]{:S(2)}) collective-permute-start(bf16[2,160,128]{2,1,0:T(8,128)(2,1)} %get-tuple-element.74), channel_id=1, source_target_pairs={{0,6},{2,0},{4,2},{6,4},{1,7},{3,1},{5,3},{7,5},{8,14},{10,8},{12,... | collective-permute-start | bytes 245768 | tf_op jit(solution)/shard_map/ppermute | solution.py:387
  140.5 7.0 %collective-permute-start.17 = (bf16[2,160,128]{2,1,0:T(8,128)(2,1)}, bf16[2,160,128]{2,1,0:T(8,128)(2,1)S(1)}, u32[]{:S(2)}, u32[]{:S(2)}) collective-permute-start(bf16[2,160,128]{2,1,0:T(8,128)(2,1)} %get-tuple-element.75), channel_id=1, source_target_pairs={{0,4},{2,6},{4,0},{6,2},{1,5},{3,7},{5,1},{7,3},{8,12},{10,14},{12... | collective-permute-start | bytes 245768 | tf_op jit(solution)/shard_map/ppermute | solution.py:387
  140.5 7.0 %collective-permute-start.18 = (bf16[2,160,128]{2,1,0:T(8,128)(2,1)}, bf16[2,160,128]{2,1,0:T(8,128)(2,1)S(1)}, u32[]{:S(2)}, u32[]{:S(2)}) collective-permute-start(bf16[2,160,128]{2,1,0:T(8,128)(2,1)} %get-tuple-element.76), channel_id=1, source_target_pairs={{0,2},{2,4},{4,6},{6,0},{1,3},{3,5},{5,7},{7,1},{8,10},{10,12},{12... | collective-permute-start | bytes 245768 | tf_op jit(solution)/shard_map/ppermute | solution.py:387
  151.6 2.5 %collective-permute-start.19 = (bf16[448,1024]{1,0:T(8,128)(2,1)S(1)}, bf16[448,1024]{1,0:T(8,128)(2,1)S(1)}, u32[]{:S(2)}, u32[]{:S(2)}) collective-permute-start(bf16[448,1024]{1,0:T(8,128)(2,1)S(1)} %shard_map.106.mine_ref), channel_id=1, source_target_pairs={{0,1},{1,0},{2,3},{3,2},{4,5},{5,4},{6,7},{7,6},{8,9},{9,8},{10,11... | collective-permute-start | bytes 2752520 | tf_op jit(solution)/shard_map/ppermute | solution.py:432
  153.5 8.8 %collective-permute-start.20 = (bf16[448,1024]{1,0:T(8,128)(2,1)S(1)}, bf16[448,1024]{1,0:T(8,128)(2,1)S(1)}, u32[]{:S(2)}, u32[]{:S(2)}) collective-permute-start(bf16[448,1024]{1,0:T(8,128)(2,1)S(1)} %shard_map.108.mine_ref), channel_id=1, source_target_pairs={{0,1},{1,0},{2,3},{3,2},{4,5},{5,4},{6,7},{7,6},{8,9},{9,8},{10,11... | collective-permute-start | bytes 2752520 | tf_op jit(solution)/shard_map/ppermute | solution.py:432
  155.9 12.1 %collective-permute-start.21 = (bf16[448,256]{1,0:T(8,128)(2,1)S(1)}, bf16[448,256]{1,0:T(8,128)(2,1)S(1)}, u32[]{:S(2)}, u32[]{:S(2)}) collective-permute-start(bf16[448,256]{1,0:T(8,128)(2,1)S(1)} %get-tuple-element.87), channel_id=1, source_target_pairs={{0,2},{2,4},{4,6},{6,0},{1,3},{3,5},{5,7},{7,1},{8,10},{10,12},{12... | collective-permute-start | bytes 688136 | tf_op jit(solution)/shard_map/ppermute | solution.py:439
  157.8 18.3 %collective-permute-start.23 = (bf16[448,256]{1,0:T(8,128)(2,1)S(1)}, bf16[448,256]{1,0:T(8,128)(2,1)S(1)}, u32[]{:S(2)}, u32[]{:S(2)}) collective-permute-start(bf16[448,256]{1,0:T(8,128)(2,1)S(1)} %get-tuple-element.89), channel_id=1, source_target_pairs={{0,4},{2,6},{4,0},{6,2},{1,5},{3,7},{5,1},{7,3},{8,12},{10,14},{12... | collective-permute-start | bytes 688136 | tf_op jit(solution)/shard_map/ppermute | solution.py:439
  160.4 15.8 %collective-permute-start.25 = (bf16[448,256]{1,0:T(8,128)(2,1)S(1)}, bf16[448,256]{1,0:T(8,128)(2,1)S(1)}, u32[]{:S(2)}, u32[]{:S(2)}) collective-permute-start(bf16[448,256]{1,0:T(8,128)(2,1)S(1)} %get-tuple-element.91), channel_id=1, source_target_pairs={{0,6},{2,0},{4,2},{6,4},{1,7},{3,1},{5,3},{7,5},{8,14},{10,8},{12,... | collective-permute-start | bytes 688136 | tf_op jit(solution)/shard_map/ppermute | solution.py:439
  164.0 17.1 %collective-permute-start.22 = (bf16[448,256]{1,0:T(8,128)(2,1)S(1)}, bf16[448,256]{1,0:T(8,128)(2,1)S(1)}, u32[]{:S(2)}, u32[]{:S(2)}) collective-permute-start(bf16[448,256]{1,0:T(8,128)(2,1)S(1)} %get-tuple-element.88), channel_id=1, source_target_pairs={{0,2},{2,4},{4,6},{6,0},{1,3},{3,5},{5,7},{7,1},{8,10},{10,12},{12... | collective-permute-start | bytes 688136 | tf_op jit(solution)/shard_map/ppermute | solution.py:439
  164.2 30.8 %collective-permute-start.24 = (bf16[448,256]{1,0:T(8,128)(2,1)S(1)}, bf16[448,256]{1,0:T(8,128)(2,1)S(1)}, u32[]{:S(2)}, u32[]{:S(2)}) collective-permute-start(bf16[448,256]{1,0:T(8,128)(2,1)S(1)} %get-tuple-element.90), channel_id=1, source_target_pairs={{0,4},{2,6},{4,0},{6,2},{1,5},{3,7},{5,1},{7,3},{8,12},{10,14},{12... | collective-permute-start | bytes 688136 | tf_op jit(solution)/shard_map/ppermute | solution.py:439
  168.0 27.1 %collective-permute-start.26 = (bf16[448,256]{1,0:T(8,128)(2,1)S(1)}, bf16[448,256]{1,0:T(8,128)(2,1)S(1)}, u32[]{:S(2)}, u32[]{:S(2)}) collective-permute-start(bf16[448,256]{1,0:T(8,128)(2,1)S(1)} %get-tuple-element.92), channel_id=1, source_target_pairs={{0,6},{2,0},{4,2},{6,4},{1,7},{3,1},{5,3},{7,5},{8,14},{10,8},{12,... | collective-permute-start | bytes 688136 | tf_op jit(solution)/shard_map/ppermute | solution.py:439
  (52 other events, 69.8 us)

commit v9 on v7

--- a/solution.py
+++ b/solution.py
@@ -138,33 +138,32 @@
     rows = q_ref.shape[1]
     cut = LANES * -(-rows // (2 * LANES))
     wide = table_ref.shape[2] // 2
+    local_head = pl.program_id(0) + offset
+    head = (2 * (local_head // per_group) + at_ref[0]) * per_group + lax.rem(local_head, per_group)
+    lanes = pl.multiple_of((head // HELD) * LANES, LANES)
+    place = lax.rem(head, HELD)
     lane = lax.broadcasted_iota(jnp.int32, (rows, LANES), 1) // FEAT
-    for i in range(early_ref.shape[0]):
-        head = (2 * (i // per_group + offset) + at_ref[0]) * per_group + i % per_group
-        lanes = pl.multiple_of((head // HELD) * LANES, LANES)
-        place = lax.rem(head, HELD)
-        columns = slice(i * HEAD_DIM, (i + 1) * HEAD_DIM)
-        for chunk in range(2):
-            query = q_ref[chunk, :, pl.ds(lanes, LANES)]
-            key = k_ref[chunk, :, pl.ds(lanes, LANES)]
-            sides = dot(query, table_ref[place]) + bias_ref[...]
-            phi = (sides[:, :PACKED] * sides[:, wide : wide + PACKED]).astype(BF16)
-            phi_ref[chunk, i] = phi
-            mine = jnp.where(lane == place, query * jnp.asarray(0.25, BF16), jnp.zeros_like(query))
-            for low, high in ((0, cut), (cut, rows)):
-                span = high - low
-                s = dot(mine[low:high], key[low:high], NT)
-                t_at = lax.broadcasted_iota(jnp.int32, (span, span), 0)
-                j_at = lax.broadcasted_iota(jnp.int32, (span, span), 1)
-                weight = jnp.where(t_at >= j_at, (0.5 * s + 1.0) * s + 1.0, 0.0).astype(BF16)
-                num = dot(weight, v_ref[chunk, low:high, columns])
-                if low > 0:
-                    s = dot(mine[low:high], key[:low], NT)
-                    weight = ((0.5 * s + 1.0) * s + 1.0).astype(BF16)
-                    num = num + dot(weight, v_ref[chunk, :low, columns])
-                if chunk > 0:
-                    num = num + dot(phi[low:high], early_ref[i])
-                num_ref[chunk, low:high, columns] = num
+    for chunk in range(2):
+        query = q_ref[chunk, :, pl.ds(lanes, LANES)]
+        key = k_ref[chunk, :, pl.ds(lanes, LANES)]
+        sides = dot(query, table_ref[place]) + bias_ref[...]
+        phi = (sides[:, :PACKED] * sides[:, wide : wide + PACKED]).astype(BF16)
+        phi_ref[chunk, 0] = phi
+        mine = jnp.where(lane == place, query * jnp.asarray(0.25, BF16), jnp.zeros_like(query))
+        for low, high in ((0, cut), (cut, rows)):
+            span = high - low
+            s = dot(mine[low:high], key[low:high], NT)
+            t_at = lax.broadcasted_iota(jnp.int32, (span, span), 0)
+            j_at = lax.broadcasted_iota(jnp.int32, (span, span), 1)
+            weight = jnp.where(t_at >= j_at, (0.5 * s + 1.0) * s + 1.0, 0.0).astype(BF16)
+            num = dot(weight, v_ref[chunk, low:high, :])
+            if low > 0:
+                s = dot(mine[low:high], key[:low], NT)
+                weight = ((0.5 * s + 1.0) * s + 1.0).astype(BF16)
+                num = num + dot(weight, v_ref[chunk, :low, :])
+            if chunk > 0:
+                num = num + dot(phi[low:high], early_ref[0])
+            num_ref[chunk, low:high, :] = num
 
 
 def prefix_kernel(at_ref, line_ref, *refs):
@@ -183,19 +182,19 @@
 
 def hidden_kernel(at_ref, layers, gain_ref, *refs):
     pieces, parts, out_ref, state_ref = refs[:layers], refs[layers:-2], refs[-2], refs[-1]
-    numbers, features = parts[: len(parts) // 2], parts[len(parts) // 2 :]
-    held = features[0].shape[1]
     group = pieces[0].shape[0]
     for d in range(layers):
         state_ref[lax.rem(at_ref[1] + d, layers)] = pieces[d][...]
-    for i in range(held * len(features)):
-        columns = slice(i * HEAD_DIM, (i + 1) * HEAD_DIM)
-        at = (i % held) * HEAD_DIM
-        num = numbers[i // held][0, :, at : at + HEAD_DIM]
-        num = num + dot(features[i // held][0, i % held], state_ref[i // group, i % group])
-        mean_square = jnp.mean(num * num, axis=1, keepdims=True)
-        hidden = num * lax.rsqrt(mean_square + 1e-05) * gain_ref[:, columns]
-        out_ref[:, columns] = hidden.astype(BF16)
+    head = 0
+    for num_ref, phi_ref in zip(parts[0::2], parts[1::2]):
+        for i in range(phi_ref.shape[1]):
+            columns = slice(head * HEAD_DIM, (head + 1) * HEAD_DIM)
+            num = num_ref[0, :, i * HEAD_DIM : (i + 1) * HEAD_DIM]
+            num = num + dot(phi_ref[0, i], state_ref[head // group, head % group])
+            mean_square = jnp.mean(num * num, axis=1, keepdims=True)
+            hidden = num * lax.rsqrt(mean_square + 1e-05) * gain_ref[:, columns]
+            out_ref[:, columns] = hidden.astype(BF16)
+            head += 1
 
 
 def output_kernel(at_ref, mine_ref, other_ref, *refs):
@@ -298,7 +297,7 @@
     far = layers // 2
     mine = {d: lax.ppermute(sent[d], "z", turn(d)) for d in [far] + [d for d in range(1, layers) if d != far]}
     mine = [sent[0]] + [mine[d] for d in range(1, layers)]
-    mine[far], weights[1:] = lax.optimization_barrier((mine[far], weights[1:]))
+    mine[1:], weights[1:] = lax.optimization_barrier((mine[1:], weights[1:]))
     other = [lax.ppermute(piece, "core", swap) for piece in mine]
 
     query, key, value, early, total = call(
@@ -337,42 +336,38 @@
         ],
     )
 
-    parts = 4
-    some_layers = layers // parts
-
-    def local(index):
-        offset = index * some_layers
+    def local(offset, count):
         return call(
             lambda core_ref, *refs: local_kernel(core_ref, per_group, offset, *refs),
             at,
-            (1,),
+            (count,),
             [
                 whole((2, rows, narrow)),
                 whole((2, rows, narrow)),
-                pl.BlockSpec((2, rows, some_layers * value_width), lambda i, _: (0, 0, index)),
-                pl.BlockSpec((heads // parts, PACKED, HEAD_DIM), lambda i, _: (index, 0, 0)),
+                pl.BlockSpec((2, rows, HEAD_DIM), lambda i, _: (0, 0, i + offset)),
+                pl.BlockSpec((1, PACKED, HEAD_DIM), lambda i, _: (i + offset, 0, 0)),
                 whole(query_table.shape),
                 whole(query_bias.shape),
             ],
             [
-                whole((2, rows, some_layers * value_width)),
-                whole((2, heads // parts, rows, PACKED)),
+                pl.BlockSpec((2, rows, HEAD_DIM), lambda i, _: (0, 0, i)),
+                pl.BlockSpec((2, 1, rows, PACKED), lambda i, _: (0, i, 0, 0)),
             ],
             [
-                jax.ShapeDtypeStruct((2, rows, some_layers * value_width), F32),
-                jax.ShapeDtypeStruct((2, heads // parts, rows, PACKED), BF16),
+                jax.ShapeDtypeStruct((2, rows, count * HEAD_DIM), F32),
+                jax.ShapeDtypeStruct((2, count, rows, PACKED), BF16),
             ],
             (query, key, value, early, query_table, query_bias),
-            heads * rows * rows * 300,
+            count * rows * rows * 1200,
         )
 
     own = total.reshape(layers, per_group, PACKED, HEAD_DIM)
     line = lax.all_to_all(own, "z", split_axis=0, concat_axis=0, tiled=True)
-    locals_ = [local(0), local(1)]
+    locals_ = [local(0, heads // 2)]
     line, locals_ = lax.optimization_barrier((line, locals_))
     slab_total = jnp.sum(line.astype(F32), axis=0).astype(BF16)
     totals = [lax.ppermute(slab_total, "seq", flip(m)) for m in range(1, slabs)]
-    third = local(2)
+    third = local(heads // 2, heads // 4)
     totals, third = lax.optimization_barrier((totals, third))
     piece_shape = (per_group, PACKED, HEAD_DIM)
     prefix = pl.pallas_call(
@@ -383,25 +378,27 @@
         scratch_shapes=[pltpu.VMEM((layers,) + piece_shape, BF16)],
     )(at, line, *totals)
     prefix = [prefix[0]] + [lax.ppermute(prefix[d], "z", turn(-d)) for d in range(1, layers)]
-    locals_ = locals_ + [third, local(3)]
+    locals_ = locals_ + [third, local(3 * heads // 4, heads // 4)]
 
     def hidden(chunk):
         some = rows // 2
-        numbers = pl.BlockSpec((1, some, heads * HEAD_DIM // parts), lambda i, _: (chunk, i, 0))
-        features = pl.BlockSpec((1, heads // parts, some, PACKED), lambda i, _: (chunk, 0, i, 0))
+        specs, arrays = [], []
+        for num, phi in locals_:
+            count = phi.shape[1]
+            specs.append(pl.BlockSpec((1, some, count * HEAD_DIM), lambda i, _: (chunk, i, 0)))
+            specs.append(pl.BlockSpec((1, count, some, PACKED), lambda i, _: (chunk, 0, i, 0)))
+            arrays += [num, phi]
         return call(
             lambda at_ref, *refs: hidden_kernel(at_ref, layers, *refs),
             at,
             (2,),
-            [whole((1, heads * HEAD_DIM))]
-            + [whole(piece_shape)] * layers
-            + [numbers] * parts
-            + [features] * parts,
+            [whole((1, heads * HEAD_DIM))] + [whole(piece_shape)] * layers + specs,
             pl.BlockSpec((some, heads * HEAD_DIM), lambda i, _: (i, 0)),
             jax.ShapeDtypeStruct((rows, heads * HEAD_DIM), BF16),
-            (gain_mine, *prefix, *(num for num, _ in locals_), *(phi for _, phi in locals_)),
+            (gain_mine, *prefix, *arrays),
             rows * heads * HEAD_DIM * 600,
             [pltpu.VMEM((layers,) + piece_shape, BF16)],
+            mib=16,
         )
 
     w_rows = w_out.reshape(layers, 2, value_width, model)

time: 185 us -> 179 us (0.968)
  Pallas kernels: 55 us -> 47.9 us
  waiting for transfers between devices: 72.3 us -> 76.5 us
  starting transfers between devices: 44.6 us -> 41.5 us
    pallas_call x12 -> x11, Pallas kernels: 53.1 us -> 46 us  [call(): pl.pallas_call(kernel, grid_spec=pltpu.PrefetchScalarGridSpec(num_scalar_...]
    all_to_all x1, waiting for transfers between devices: 0.01 us -> 2.61 us  [per_device(): line = lax.all_to_all(own, 'z', split_axis=0, concat_axis=0, tiled=True)]
    ppermute x3, starting transfers between devices: 4.95 us -> 2.35 us  [per_device(): lax.ppermute(prefix[d], 'z', turn(-d))]
    unnamed x38 -> x42, local copies, waits for them, and re-layouts: 5.72 us -> 6.38 us
  transfers between devices with their start and end apart: 28 -> 28, of which waited for: 11 -> 16; matrix products, arithmetic and copies ran while one was open for 2% -> 1% of each run, Pallas kernels for 18% -> 16%
where the time goes in v9:
time: 179 us; the launch traced here: 176 us
  waiting for transfers between devices  76.5 us (43%)
  Pallas kernels  47.9 us (27%)
  starting transfers between devices  41.5 us (23%)
  local copies, waits for them, and re-layouts  8.92 us (5%)
    pallas_call x11, Pallas kernels, call(): pl.pallas_call(kernel, grid_spec=pltpu.PrefetchScalarGridSpec(num_scalar_...  46 us
    ppermute x3, waiting for transfers between devices, per_device(): lax.ppermute(sent[d], 'z', turn(d))  27.1 us
    ppermute x6, waiting for transfers between devices, per_device(): pieces[d, chunk] = lax.ppermute(piece, 'z', turn(d)) if d else piece  24.9 us
    ppermute x3, waiting for transfers between devices, per_device(): lax.ppermute(value_part, 'z', turn(-d))  14.2 us
    ppermute x6, starting transfers between devices, per_device(): pieces[d, chunk] = lax.ppermute(piece, 'z', turn(d)) if d else piece  9.2 us
    ppermute x3, starting transfers between devices, per_device(): lax.ppermute(sent[d], 'z', turn(d))  7.73 us
    all_to_all x1, starting transfers between devices, per_device(): line = lax.all_to_all(own, 'z', split_axis=0, concat_axis=0, tiled=True)  7.03 us
    ppermute x3, starting transfers between devices, per_device(): lax.ppermute(value_part, 'z', turn(-d))  7.01 us
  transfers between devices with their start and end apart: 28, of which 16 were waited for; matrix products, arithmetic and copies ran while one was open for 1% of the time, Pallas kernels for 16%

profile of v9, /device:TPU:0, one launch (start us, length us, event | category | flops | bytes accessed | tf_op | source)
XLA Modules:
  0.0 176.0 jit_solution(6002908617977683013)
XLA Ops:
  1.0 3.1 %collective-permute-start.2 = (bf16[512,256]{1,0:T(8,128)(2,1)S(1)}, bf16[512,256]{1,0:T(8,128)(2,1)S(1)}, u32[]{:S(2)}, u32[]{:S(2)}) collective-permute-start(bf16[512,256]{1,0:T(8,128)(2,1)S(1)} %constant_dynamic-slice_fusion), channel_id=1, source_target_pairs={{0,2},{2,4},{4,6},{6,0},{1,3},{3,5},{5,7},{7,1},{8,10},{10,12},{12... | collective-permute-start | bytes 786440 | tf_op jit(solution)/shard_map/ppermute | solution.py:291
  4.0 2.6 %collective-permute-start.1 = (bf16[512,256]{1,0:T(8,128)(2,1)S(1)}, bf16[512,256]{1,0:T(8,128)(2,1)S(1)}, u32[]{:S(2)}, u32[]{:S(2)}) collective-permute-start(bf16[512,256]{1,0:T(8,128)(2,1)S(1)} %constant_dynamic-slice_fusion), channel_id=1, source_target_pairs={{0,4},{2,6},{4,0},{6,2},{1,5},{3,7},{5,1},{7,3},{8,12},{10,14},{12... | collective-permute-start | bytes 786440 | tf_op jit(solution)/shard_map/ppermute | solution.py:291
  9.5 3.8 %collective-permute-done.2 = bf16[512,256]{1,0:T(8,128)(2,1)S(1)} collective-permute-done((bf16[512,256]{1,0:T(8,128)(2,1)S(1)}, bf16[512,256]{1,0:T(8,128)(2,1)S(1)}, u32[]{:S(2)}, u32[]{:S(2)}) %collective-permute-start.2) | collective-permute-done | bytes 262176 | tf_op jit(solution)/shard_map/ppermute | solution.py:291
  13.3 10.4 %collective-permute-done.1 = bf16[512,256]{1,0:T(8,128)(2,1)S(1)} collective-permute-done((bf16[512,256]{1,0:T(8,128)(2,1)S(1)}, bf16[512,256]{1,0:T(8,128)(2,1)S(1)}, u32[]{:S(2)}, u32[]{:S(2)}) %collective-permute-start.1) | collective-permute-done | bytes 262176 | tf_op jit(solution)/shard_map/ppermute | solution.py:291
  23.9 6.1 %collective-permute-start.3 = (bf16[896,256]{1,0:T(8,128)(2,1)S(1)}, bf16[896,256]{1,0:T(8,128)(2,1)S(1)}, u32[]{:S(2)}, u32[]{:S(2)}) collective-permute-start(bf16[896,256]{1,0:T(8,128)(2,1)S(1)} %get-tuple-element.47), channel_id=1, source_target_pairs={{0,2},{2,4},{4,6},{6,0},{1,3},{3,5},{5,7},{7,1},{8,10},{10,12},{12... | collective-permute-start | bytes 1376264 | tf_op jit(solution)/shard_map/ppermute | solution.py:298
  30.0 2.4 %collective-permute-start.8 = (bf16[3,512,256]{2,1,0:T(8,128)(2,1)S(1)}, bf16[3,512,256]{2,1,0:T(8,128)(2,1)S(1)}, u32[]{:S(2)}, u32[]{:S(2)}) collective-permute-start(bf16[3,512,256]{2,1,0:T(8,128)(2,1)S(1)} %pad_maximum_fusion.refs_13_), channel_id=1, source_target_pairs={{0,24},{8,16},{16,8},{24,0},{1,25},{9,17},{17,9},{25,1},{2,26},{10... | collective-permute-start | bytes 2359304 | tf_op jit(solution)/shard_map/ppermute | solution.py:294
  35.1 7.5 %collective-permute-done.3.refs_1_ = bf16[896,256]{1,0:T(8,128)(2,1)S(1)} collective-permute-done((bf16[896,256]{1,0:T(8,128)(2,1)S(1)}, bf16[896,256]{1,0:T(8,128)(2,1)S(1)}, u32[]{:S(2)}, u32[]{:S(2)}) %collective-permute-start.3) | collective-permute-done | bytes 458784 | tf_op jit(solution)/shard_map/ppermute | solution.py:298
  42.6 18.0 %collective-permute-done.4.refs_2_ = bf16[896,256]{1,0:T(8,128)(2,1)} collective-permute-done((bf16[896,256]{1,0:T(8,128)(2,1)S(1)}, bf16[896,256]{1,0:T(8,128)(2,1)}, u32[]{:S(2)}, u32[]{:S(2)}) %collective-permute-start.4) | collective-permute-done | bytes 458784 | tf_op jit(solution)/shard_map/ppermute | solution.py:298
  60.6 1.6 collective-permute-done.5.refs_3_
  62.2 4.7 %collective-permute-done.7.refs_15_ = bf16[3,512,256]{2,1,0:T(8,128)(2,1)S(1)} collective-permute-done((bf16[3,512,256]{2,1,0:T(8,128)(2,1)S(1)}, bf16[3,512,256]{2,1,0:T(8,128)(2,1)S(1)}, u32[]{:S(2)}, u32[]{:S(2)}) %collective-permute-start.7) | collective-permute-done | bytes 786464 | tf_op jit(solution)/shard_map/ppermute | solution.py:294
  71.5 14.1 %shard_map.100 = (bf16[2,448,256]{2,1,0:T(8,128)(2,1)}, bf16[2,448,256]{2,1,0:T(8,128)(2,1)}, bf16[2,448,1024]{2,1,0:T(8,128)(2,1)}, bf16[8,160,128]{2,1,0:T(8,128)(2,1)}, bf16[8,160,128]{2,1,0:T(8,128)(2,1)}) custom-call(s32[3]{0:T(128)} %pad_add_fusion.at_ref.core_ref, bf16[4,896,256]{2,1,0:T(8,128)(2,1)} %bitcast.39, bf16[896,256]{1,0:T(8,128)(2,1)} %copy-done.18, ...), custom_call_target="tpu_custom_call" | custom-call | flops 5637144576 | bytes 12582912 | tf_op jit(solution)/shard_map/pallas_call | solution.py:234
  85.6 7.0 %all-to-all-start = ((bf16[4,2,160,128]{3,2,1,0:T(8,128)(2,1)}), bf16[4,2,160,128]{3,2,1,0:T(8,128)(2,1)S(1)}, u32[]{:S(2)}, u32[]{:S(2)}) async-start(bf16[4,2,160,128]{3,2,1,0:T(8,128)(2,1)} %bitcast.40), calls=%async_computation | async-start | bytes 655360 | tf_op jit(solution)/shard_map/all_to_all | solution.py:365
  92.7 8.2 %shard_map.101 = (f32[2,448,512]{2,1,0:T(8,128)}, bf16[2,4,448,160]{3,2,1,0:T(8,128)(2,1)}) custom-call(s32[3]{0:T(128)} %pad_add_fusion.at_ref.core_ref, bf16[2,448,256]{2,1,0:T(8,128)(2,1)} %get-tuple-element.59.refs_0_, bf16[2,448,256]{2,1,0:T(8,128)(2,1)} %get-tuple-element.60.refs_1_, bf16[2,448,1024]{2,1,0:T(8,128)(2,1)} %get-tuple-element.61.refs_2_, ...), custom_call_target="tpu_custom_call" | custom-call | flops 963379200 | bytes 12582912 | tf_op jit(solution)/shard_map/pallas_call | solution.py:234
  100.9 2.6 %all-to-all-done.line_ref = bf16[4,2,160,128]{3,2,1,0:T(8,128)(2,1)S(1)} async-done(((bf16[4,2,160,128]{3,2,1,0:T(8,128)(2,1)}), bf16[4,2,160,128]{3,2,1,0:T(8,128)(2,1)S(1)}, u32[]{:S(2)}, u32[]{:S(2)}) %all-to-all-start) | async-done | bytes 327712 | tf_op jit(solution)/shard_map/all_to_all | solution.py:365
  103.5 2.5 %collective-permute-start.15 = (bf16[2,160,128]{2,1,0:T(8,128)(2,1)S(1)}, bf16[2,160,128]{2,1,0:T(8,128)(2,1)S(1)}, u32[]{:S(2)}, u32[]{:S(2)}) collective-permute-start(bf16[2,160,128]{2,1,0:T(8,128)(2,1)S(1)} %reduce_sum.12), channel_id=1, source_target_pairs={{0,24},{8,16},{16,8},{24,0},{1,25},{9,17},{17,9},{25,1},{2,26},{10... | collective-permute-start | bytes 245768 | tf_op jit(solution)/shard_map/ppermute | solution.py:369
  107.1 5.6 %shard_map.102 = (f32[2,448,256]{2,1,0:T(8,128)}, bf16[2,2,448,160]{3,2,1,0:T(8,128)(2,1)}) custom-call(s32[3]{0:T(128)} %pad_add_fusion.at_ref.core_ref, bf16[2,448,256]{2,1,0:T(8,128)(2,1)} %get-tuple-element.59.refs_0_, bf16[2,448,256]{2,1,0:T(8,128)(2,1)} %get-tuple-element.60.refs_1_, bf16[2,448,1024]{2,1,0:T(8,128)(2,1)} %get-tuple-element.61.refs_2_, ...), custom_call_target="tpu_custom_call" | custom-call | flops 481689600 | bytes 12582912 | tf_op jit(solution)/shard_map/pallas_call | solution.py:234
  113.4 1.9 %shard_map.103 = (bf16[2,160,128]{2,1,0:T(8,128)(2,1)}, bf16[2,160,128]{2,1,0:T(8,128)(2,1)}, bf16[2,160,128]{2,1,0:T(8,128)(2,1)}, bf16[2,160,128]{2,1,0:T(8,128)(2,1)}) custom-call(s32[3]{0:T(128)} %pad_add_fusion.at_ref.core_ref, bf16[4,2,160,128]{3,2,1,0:T(8,128)(2,1)} %copy-done.9, bf16[2,160,128]{2,1,0:T(8,128)(2,1)} %copy-done.13, ...), custom_call_target="tpu_custom_call" | custom-call | tf_op jit(solution)/shard_map/pallas_call | solution.py:373
  117.7 6.0 %shard_map.104 = (f32[2,448,256]{2,1,0:T(8,128)}, bf16[2,2,448,160]{3,2,1,0:T(8,128)(2,1)}) custom-call(s32[3]{0:T(128)} %pad_add_fusion.at_ref.core_ref, bf16[2,448,256]{2,1,0:T(8,128)(2,1)} %get-tuple-element.59.refs_0_, bf16[2,448,256]{2,1,0:T(8,128)(2,1)} %get-tuple-element.60.refs_1_, bf16[2,448,1024]{2,1,0:T(8,128)(2,1)} %get-tuple-element.61.refs_2_, ...), custom_call_target="tpu_custom_call" | custom-call | flops 481689600 | bytes 12582912 | tf_op jit(solution)/shard_map/pallas_call | solution.py:234
  128.8 1.8 %shard_map.105.mine_ref = bf16[448,1024]{1,0:T(8,128)(2,1)S(1)} custom-call(s32[3]{0:T(128)S(1)} %copy-done.8, f32[1,1024]{1,0:T(1,128)S(1)} %bitcast.36, bf16[2,160,128]{2,1,0:T(8,128)(2,1)S(1)} %copy-done.7, bf16[2,160,128]{2,1,0:T(8,128)(2,1)S(1)} %collective-permute-done.16.refs_2_, bf16[2,160,128]{2,1,0:T(8,128)(2,1)S(1)} %collective-permute-done.17.refs_3_, ...), custom_call_target="tpu_custom_call" | custom-call | flops 275251200 | bytes 12582912 | tf_op jit(solution)/shard_map/pallas_call | solution.py:234
  130.7 1.8 %shard_map.107.mine_ref = bf16[448,1024]{1,0:T(8,128)(2,1)S(1)} custom-call(s32[3]{0:T(128)S(1)} %copy-done.8, f32[1,1024]{1,0:T(1,128)S(1)} %bitcast.37, bf16[2,160,128]{2,1,0:T(8,128)(2,1)S(1)} %copy-done.7, bf16[2,160,128]{2,1,0:T(8,128)(2,1)S(1)} %collective-permute-done.16.refs_2_, bf16[2,160,128]{2,1,0:T(8,128)(2,1)S(1)} %collective-permute-done.17.refs_3_, ...), custom_call_target="tpu_custom_call" | custom-call | flops 275251200 | bytes 12582912 | tf_op jit(solution)/shard_map/pallas_call | solution.py:234
  133.2 1.7 shard_map.109
  134.9 2.3 %collective-permute-start.21 = (bf16[448,256]{1,0:T(8,128)(2,1)S(1)}, bf16[448,256]{1,0:T(8,128)(2,1)S(1)}, u32[]{:S(2)}, u32[]{:S(2)}) collective-permute-start(bf16[448,256]{1,0:T(8,128)(2,1)S(1)} %get-tuple-element.83), channel_id=1, source_target_pairs={{0,2},{2,4},{4,6},{6,0},{1,3},{3,5},{5,7},{7,1},{8,10},{10,12},{12... | collective-permute-start | bytes 688136 | tf_op jit(solution)/shard_map/ppermute | solution.py:433
  138.1 1.7 shard_map.106
  139.8 2.1 %collective-permute-start.25 = (bf16[448,256]{1,0:T(8,128)(2,1)S(1)}, bf16[448,256]{1,0:T(8,128)(2,1)S(1)}, u32[]{:S(2)}, u32[]{:S(2)}) collective-permute-start(bf16[448,256]{1,0:T(8,128)(2,1)S(1)} %get-tuple-element.87), channel_id=1, source_target_pairs={{0,6},{2,0},{4,2},{6,4},{1,7},{3,1},{5,3},{7,5},{8,14},{10,8},{12,... | collective-permute-start | bytes 688136 | tf_op jit(solution)/shard_map/ppermute | solution.py:433
  141.8 1.7 shard_map.110
  143.6 2.0 %collective-permute-start.24 = (bf16[448,256]{1,0:T(8,128)(2,1)S(1)}, bf16[448,256]{1,0:T(8,128)(2,1)S(1)}, u32[]{:S(2)}, u32[]{:S(2)}) collective-permute-start(bf16[448,256]{1,0:T(8,128)(2,1)S(1)} %get-tuple-element.86), channel_id=1, source_target_pairs={{0,4},{2,6},{4,0},{6,2},{1,5},{3,7},{5,1},{7,3},{8,12},{10,14},{12... | collective-permute-start | bytes 688136 | tf_op jit(solution)/shard_map/ppermute | solution.py:433
  145.6 1.7 shard_map.108
  147.3 1.9 %collective-permute-start.26 = (bf16[448,256]{1,0:T(8,128)(2,1)S(1)}, bf16[448,256]{1,0:T(8,128)(2,1)S(1)}, u32[]{:S(2)}, u32[]{:S(2)}) collective-permute-start(bf16[448,256]{1,0:T(8,128)(2,1)S(1)} %get-tuple-element.88), channel_id=1, source_target_pairs={{0,6},{2,0},{4,2},{6,4},{1,7},{3,1},{5,3},{7,5},{8,14},{10,8},{12,... | collective-permute-start | bytes 688136 | tf_op jit(solution)/shard_map/ppermute | solution.py:433
  149.1 6.0 %collective-permute-done.23.refs_4_ = bf16[448,256]{1,0:T(8,128)(2,1)S(1)} collective-permute-done((bf16[448,256]{1,0:T(8,128)(2,1)S(1)}, bf16[448,256]{1,0:T(8,128)(2,1)S(1)}, u32[]{:S(2)}, u32[]{:S(2)}) %collective-permute-start.23) | collective-permute-done | bytes 229408 | tf_op jit(solution)/shard_map/ppermute | solution.py:433
  155.2 4.9 %collective-permute-done.22.refs_3_ = bf16[448,256]{1,0:T(8,128)(2,1)S(1)} collective-permute-done((bf16[448,256]{1,0:T(8,128)(2,1)S(1)}, bf16[448,256]{1,0:T(8,128)(2,1)S(1)}, u32[]{:S(2)}, u32[]{:S(2)}) %collective-permute-start.22) | collective-permute-done | bytes 229408 | tf_op jit(solution)/shard_map/ppermute | solution.py:433
  160.1 13.9 %collective-permute-done.24.refs_5_ = bf16[448,256]{1,0:T(8,128)(2,1)S(1)} collective-permute-done((bf16[448,256]{1,0:T(8,128)(2,1)S(1)}, bf16[448,256]{1,0:T(8,128)(2,1)S(1)}, u32[]{:S(2)}, u32[]{:S(2)}) %collective-permute-start.24) | collective-permute-done | bytes 229408 | tf_op jit(solution)/shard_map/ppermute | solution.py:433
  174.0 1.8 %shard_map.111 = bf16[3584,256]{1,0:T(8,128)(2,1)} custom-call(s32[3]{0:T(128)S(1)} %copy-done.8, bf16[448,256]{1,0:T(8,128)(2,1)S(1)} %get-tuple-element.81.refs_0_, bf16[448,256]{1,0:T(8,128)(2,1)S(1)} %get-tuple-element.82.refs_1_, bf16[448,256]{1,0:T(8,128)(2,1)S(1)} %collective-permute-done.21.refs_2_, ...), custom_call_target="tpu_custom_call" | custom-call | bytes 12582912 | tf_op jit(solution)/shard_map/pallas_call | solution.py:234
  (86 shorter events, 22.1 us)
Async XLA Ops:
  1.0 12.4 %collective-permute-start.2 = (bf16[512,256]{1,0:T(8,128)(2,1)S(1)}, bf16[512,256]{1,0:T(8,128)(2,1)S(1)}, u32[]{:S(2)}, u32[]{:S(2)}) collective-permute-start(bf16[512,256]{1,0:T(8,128)(2,1)S(1)} %constant_dynamic-slice_fusion), channel_id=1, source_target_pairs={{0,2},{2,4},{4,6},{6,0},{1,3},{3,5},{5,7},{7,1},{8,10},{10,12},{12... | collective-permute-start | bytes 786440 | tf_op jit(solution)/shard_map/ppermute | solution.py:291
  4.0 19.7 %collective-permute-start.1 = (bf16[512,256]{1,0:T(8,128)(2,1)S(1)}, bf16[512,256]{1,0:T(8,128)(2,1)S(1)}, u32[]{:S(2)}, u32[]{:S(2)}) collective-permute-start(bf16[512,256]{1,0:T(8,128)(2,1)S(1)} %constant_dynamic-slice_fusion), channel_id=1, source_target_pairs={{0,4},{2,6},{4,0},{6,2},{1,5},{3,7},{5,1},{7,3},{8,12},{10,14},{12... | collective-permute-start | bytes 786440 | tf_op jit(solution)/shard_map/ppermute | solution.py:291
  6.6 17.1 %collective-permute-start = (bf16[512,256]{1,0:T(8,128)(2,1)S(1)}, bf16[512,256]{1,0:T(8,128)(2,1)S(1)}, u32[]{:S(2)}, u32[]{:S(2)}) collective-permute-start(bf16[512,256]{1,0:T(8,128)(2,1)S(1)} %constant_dynamic-slice_fusion), channel_id=1, source_target_pairs={{0,6},{2,0},{4,2},{6,4},{1,7},{3,1},{5,3},{7,5},{8,14},{10,8},{12,... | collective-permute-start | bytes 786440 | tf_op jit(solution)/shard_map/ppermute | solution.py:291
  23.8 47.6 %copy-start.10 = (bf16[3,512,256]{2,1,0:T(8,128)(2,1)}, bf16[3,512,256]{2,1,0:T(8,128)(2,1)S(1)}, u32[]{:S(2)}) copy-start(bf16[3,512,256]{2,1,0:T(8,128)(2,1)S(1)} %pad_maximum_fusion.refs_13_) | copy-start | bytes 2359300
  23.9 18.7 %collective-permute-start.3 = (bf16[896,256]{1,0:T(8,128)(2,1)S(1)}, bf16[896,256]{1,0:T(8,128)(2,1)S(1)}, u32[]{:S(2)}, u32[]{:S(2)}) collective-permute-start(bf16[896,256]{1,0:T(8,128)(2,1)S(1)} %get-tuple-element.47), channel_id=1, source_target_pairs={{0,2},{2,4},{4,6},{6,0},{1,3},{3,5},{5,7},{7,1},{8,10},{10,12},{12... | collective-permute-start | bytes 1376264 | tf_op jit(solution)/shard_map/ppermute | solution.py:298
  30.0 32.2 %collective-permute-start.8 = (bf16[3,512,256]{2,1,0:T(8,128)(2,1)S(1)}, bf16[3,512,256]{2,1,0:T(8,128)(2,1)S(1)}, u32[]{:S(2)}, u32[]{:S(2)}) collective-permute-start(bf16[3,512,256]{2,1,0:T(8,128)(2,1)S(1)} %pad_maximum_fusion.refs_13_), channel_id=1, source_target_pairs={{0,24},{8,16},{16,8},{24,0},{1,25},{9,17},{17,9},{25,1},{2,26},{10... | collective-permute-start | bytes 2359304 | tf_op jit(solution)/shard_map/ppermute | solution.py:294
  32.4 34.5 %collective-permute-start.7 = (bf16[3,512,256]{2,1,0:T(8,128)(2,1)S(1)}, bf16[3,512,256]{2,1,0:T(8,128)(2,1)S(1)}, u32[]{:S(2)}, u32[]{:S(2)}) collective-permute-start(bf16[3,512,256]{2,1,0:T(8,128)(2,1)S(1)} %pad_maximum_fusion.refs_13_), channel_id=1, source_target_pairs={{0,16},{8,24},{16,0},{24,8},{1,17},{9,25},{17,1},{25,9},{2,18},{10... | collective-permute-start | bytes 2359304 | tf_op jit(solution)/shard_map/ppermute | solution.py:294
  32.9 34.1 %collective-permute-start.6 = (bf16[3,512,256]{2,1,0:T(8,128)(2,1)S(1)}, bf16[3,512,256]{2,1,0:T(8,128)(2,1)S(1)}, u32[]{:S(2)}, u32[]{:S(2)}) collective-permute-start(bf16[3,512,256]{2,1,0:T(8,128)(2,1)S(1)} %pad_maximum_fusion.refs_13_), channel_id=1, source_target_pairs={{0,8},{8,0},{16,24},{24,16},{1,9},{9,1},{17,25},{25,17},{2,10},{10... | collective-permute-start | bytes 2359304 | tf_op jit(solution)/shard_map/ppermute | solution.py:294
  33.5 27.1 %collective-permute-start.4 = (bf16[896,256]{1,0:T(8,128)(2,1)S(1)}, bf16[896,256]{1,0:T(8,128)(2,1)}, u32[]{:S(2)}, u32[]{:S(2)}) collective-permute-start(bf16[896,256]{1,0:T(8,128)(2,1)S(1)} %get-tuple-element.48), channel_id=1, source_target_pairs={{0,4},{2,6},{4,0},{6,2},{1,5},{3,7},{5,1},{7,3},{8,12},{10,14},{12... | collective-permute-start | bytes 1376264 | tf_op jit(solution)/shard_map/ppermute | solution.py:298
  42.6 28.9 %copy-start.18 = (bf16[896,256]{1,0:T(8,128)(2,1)}, bf16[896,256]{1,0:T(8,128)(2,1)S(1)}, u32[]{:S(2)}) copy-start(bf16[896,256]{1,0:T(8,128)(2,1)S(1)} %collective-permute-done.3.refs_1_) | copy-start | bytes 1376260
  42.6 19.6 %collective-permute-start.5 = (bf16[896,256]{1,0:T(8,128)(2,1)S(1)}, bf16[896,256]{1,0:T(8,128)(2,1)}, u32[]{:S(2)}, u32[]{:S(2)}) collective-permute-start(bf16[896,256]{1,0:T(8,128)(2,1)S(1)} %get-tuple-element.49), channel_id=1, source_target_pairs={{0,6},{2,0},{4,2},{6,4},{1,7},{3,1},{5,3},{7,5},{8,14},{10,8},{12,... | collective-permute-start | bytes 1376264 | tf_op jit(solution)/shard_map/ppermute | solution.py:298
  60.6 8.5 %collective-permute-start.9 = (bf16[896,256]{1,0:T(8,128)(2,1)S(1)}, bf16[896,256]{1,0:T(8,128)(2,1)}, u32[]{:S(2)}, u32[]{:S(2)}) collective-permute-start(bf16[896,256]{1,0:T(8,128)(2,1)S(1)} %get-tuple-element.54), channel_id=1, source_target_pairs={{0,1},{1,0},{2,3},{3,2},{4,5},{5,4},{6,7},{7,6},{8,9},{9,8},{10,11... | collective-permute-start | bytes 1376264 | tf_op jit(solution)/shard_map/ppermute | solution.py:301
  62.2 9.3 %copy-start.15 = (bf16[3,512,256]{2,1,0:T(8,128)(2,1)}, bf16[3,512,256]{2,1,0:T(8,128)(2,1)S(1)}, u32[]{:S(2)}) copy-start(bf16[3,512,256]{2,1,0:T(8,128)(2,1)S(1)} %collective-permute-done.8.refs_16_) | copy-start | bytes 2359300
  68.0 2.6 %collective-permute-start.10 = (bf16[896,256]{1,0:T(8,128)(2,1)S(1)}, bf16[896,256]{1,0:T(8,128)(2,1)}, u32[]{:S(2)}, u32[]{:S(2)}) collective-permute-start(bf16[896,256]{1,0:T(8,128)(2,1)S(1)} %collective-permute-done.3.refs_1_), channel_id=1, source_target_pairs={{0,1},{1,0},{2,3},{3,2},{4,5},{5,4},{6,7},{7,6},{8,9},{9,8},{10,11... | collective-permute-start | bytes 1376264 | tf_op jit(solution)/shard_map/ppermute | solution.py:301
  68.0 2.8 %collective-permute-start.11 = (bf16[896,256]{1,0:T(8,128)(2,1)}, bf16[896,256]{1,0:T(8,128)(2,1)}, u32[]{:S(2)}, u32[]{:S(2)}) collective-permute-start(bf16[896,256]{1,0:T(8,128)(2,1)} %collective-permute-done.4.refs_2_), channel_id=1, source_target_pairs={{0,1},{1,0},{2,3},{3,2},{4,5},{5,4},{6,7},{7,6},{8,9},{9,8},{10,11... | collective-permute-start | bytes 1376264 | tf_op jit(solution)/shard_map/ppermute | solution.py:301
  68.5 3.0 %collective-permute-start.12 = (bf16[896,256]{1,0:T(8,128)(2,1)}, bf16[896,256]{1,0:T(8,128)(2,1)}, u32[]{:S(2)}, u32[]{:S(2)}) collective-permute-start(bf16[896,256]{1,0:T(8,128)(2,1)} %collective-permute-done.5.refs_3_), channel_id=1, source_target_pairs={{0,1},{1,0},{2,3},{3,2},{4,5},{5,4},{6,7},{7,6},{8,9},{9,8},{10,11... | collective-permute-start | bytes 1376264 | tf_op jit(solution)/shard_map/ppermute | solution.py:301
  85.6 17.8 %all-to-all-start = ((bf16[4,2,160,128]{3,2,1,0:T(8,128)(2,1)}), bf16[4,2,160,128]{3,2,1,0:T(8,128)(2,1)S(1)}, u32[]{:S(2)}, u32[]{:S(2)}) async-start(bf16[4,2,160,128]{3,2,1,0:T(8,128)(2,1)} %bitcast.40), calls=%async_computation | async-start | bytes 655360 | tf_op jit(solution)/shard_map/all_to_all | solution.py:365
  92.7 14.4 %copy-start.14 = (f32[2048]{0:T(1024)S(1)}, f32[2048]{0:T(1024)}, u32[]{:S(2)}) copy-start(f32[2048]{0:T(1024)} %param.15) | copy-start | bytes 24580
  103.5 9.2 %collective-permute-start.15 = (bf16[2,160,128]{2,1,0:T(8,128)(2,1)S(1)}, bf16[2,160,128]{2,1,0:T(8,128)(2,1)S(1)}, u32[]{:S(2)}, u32[]{:S(2)}) collective-permute-start(bf16[2,160,128]{2,1,0:T(8,128)(2,1)S(1)} %reduce_sum.12), channel_id=1, source_target_pairs={{0,24},{8,16},{16,8},{24,0},{1,25},{9,17},{17,9},{25,1},{2,26},{10... | collective-permute-start | bytes 245768 | tf_op jit(solution)/shard_map/ppermute | solution.py:369
  106.0 6.7 %collective-permute-start.14 = (bf16[2,160,128]{2,1,0:T(8,128)(2,1)S(1)}, bf16[2,160,128]{2,1,0:T(8,128)(2,1)S(1)}, u32[]{:S(2)}, u32[]{:S(2)}) collective-permute-start(bf16[2,160,128]{2,1,0:T(8,128)(2,1)S(1)} %reduce_sum.12), channel_id=1, source_target_pairs={{0,16},{8,24},{16,0},{24,8},{1,17},{9,25},{17,1},{25,9},{2,18},{10... | collective-permute-start | bytes 245768 | tf_op jit(solution)/shard_map/ppermute | solution.py:369
  106.6 6.2 %collective-permute-start.13 = (bf16[2,160,128]{2,1,0:T(8,128)(2,1)S(1)}, bf16[2,160,128]{2,1,0:T(8,128)(2,1)S(1)}, u32[]{:S(2)}, u32[]{:S(2)}) collective-permute-start(bf16[2,160,128]{2,1,0:T(8,128)(2,1)S(1)} %reduce_sum.12), channel_id=1, source_target_pairs={{0,8},{8,0},{16,24},{24,16},{1,9},{9,1},{17,25},{25,17},{2,10},{10... | collective-permute-start | bytes 245768 | tf_op jit(solution)/shard_map/ppermute | solution.py:369
  115.3 8.4 %collective-permute-start.16 = (bf16[2,160,128]{2,1,0:T(8,128)(2,1)}, bf16[2,160,128]{2,1,0:T(8,128)(2,1)S(1)}, u32[]{:S(2)}, u32[]{:S(2)}) collective-permute-start(bf16[2,160,128]{2,1,0:T(8,128)(2,1)} %get-tuple-element.72), channel_id=1, source_target_pairs={{0,6},{2,0},{4,2},{6,4},{1,7},{3,1},{5,3},{7,5},{8,14},{10,8},{12,... | collective-permute-start | bytes 245768 | tf_op jit(solution)/shard_map/ppermute | solution.py:380
  116.8 7.3 %collective-permute-start.17 = (bf16[2,160,128]{2,1,0:T(8,128)(2,1)}, bf16[2,160,128]{2,1,0:T(8,128)(2,1)S(1)}, u32[]{:S(2)}, u32[]{:S(2)}) collective-permute-start(bf16[2,160,128]{2,1,0:T(8,128)(2,1)} %get-tuple-element.73), channel_id=1, source_target_pairs={{0,4},{2,6},{4,0},{6,2},{1,5},{3,7},{5,1},{7,3},{8,12},{10,14},{12... | collective-permute-start | bytes 245768 | tf_op jit(solution)/shard_map/ppermute | solution.py:380
  116.8 7.3 %collective-permute-start.18 = (bf16[2,160,128]{2,1,0:T(8,128)(2,1)}, bf16[2,160,128]{2,1,0:T(8,128)(2,1)S(1)}, u32[]{:S(2)}, u32[]{:S(2)}) collective-permute-start(bf16[2,160,128]{2,1,0:T(8,128)(2,1)} %get-tuple-element.74), channel_id=1, source_target_pairs={{0,2},{2,4},{4,6},{6,0},{1,3},{3,5},{5,7},{7,1},{8,10},{10,12},{12... | collective-permute-start | bytes 245768 | tf_op jit(solution)/shard_map/ppermute | solution.py:380
  130.6 2.5 %collective-permute-start.19 = (bf16[448,1024]{1,0:T(8,128)(2,1)S(1)}, bf16[448,1024]{1,0:T(8,128)(2,1)S(1)}, u32[]{:S(2)}, u32[]{:S(2)}) collective-permute-start(bf16[448,1024]{1,0:T(8,128)(2,1)S(1)} %shard_map.105.mine_ref), channel_id=1, source_target_pairs={{0,1},{1,0},{2,3},{3,2},{4,5},{5,4},{6,7},{7,6},{8,9},{9,8},{10,11... | collective-permute-start | bytes 2752520 | tf_op jit(solution)/shard_map/ppermute | solution.py:426
  132.5 9.3 %collective-permute-start.20 = (bf16[448,1024]{1,0:T(8,128)(2,1)S(1)}, bf16[448,1024]{1,0:T(8,128)(2,1)S(1)}, u32[]{:S(2)}, u32[]{:S(2)}) collective-permute-start(bf16[448,1024]{1,0:T(8,128)(2,1)S(1)} %shard_map.107.mine_ref), channel_id=1, source_target_pairs={{0,1},{1,0},{2,3},{3,2},{4,5},{5,4},{6,7},{7,6},{8,9},{9,8},{10,11... | collective-permute-start | bytes 2752520 | tf_op jit(solution)/shard_map/ppermute | solution.py:426
  134.9 12.4 %collective-permute-start.21 = (bf16[448,256]{1,0:T(8,128)(2,1)S(1)}, bf16[448,256]{1,0:T(8,128)(2,1)S(1)}, u32[]{:S(2)}, u32[]{:S(2)}) collective-permute-start(bf16[448,256]{1,0:T(8,128)(2,1)S(1)} %get-tuple-element.83), channel_id=1, source_target_pairs={{0,2},{2,4},{4,6},{6,0},{1,3},{3,5},{5,7},{7,1},{8,10},{10,12},{12... | collective-permute-start | bytes 688136 | tf_op jit(solution)/shard_map/ppermute | solution.py:433
  137.2 18.0 %collective-permute-start.23 = (bf16[448,256]{1,0:T(8,128)(2,1)S(1)}, bf16[448,256]{1,0:T(8,128)(2,1)S(1)}, u32[]{:S(2)}, u32[]{:S(2)}) collective-permute-start(bf16[448,256]{1,0:T(8,128)(2,1)S(1)} %get-tuple-element.85), channel_id=1, source_target_pairs={{0,4},{2,6},{4,0},{6,2},{1,5},{3,7},{5,1},{7,3},{8,12},{10,14},{12... | collective-permute-start | bytes 688136 | tf_op jit(solution)/shard_map/ppermute | solution.py:433
  139.8 15.4 %collective-permute-start.25 = (bf16[448,256]{1,0:T(8,128)(2,1)S(1)}, bf16[448,256]{1,0:T(8,128)(2,1)S(1)}, u32[]{:S(2)}, u32[]{:S(2)}) collective-permute-start(bf16[448,256]{1,0:T(8,128)(2,1)S(1)} %get-tuple-element.87), channel_id=1, source_target_pairs={{0,6},{2,0},{4,2},{6,4},{1,7},{3,1},{5,3},{7,5},{8,14},{10,8},{12,... | collective-permute-start | bytes 688136 | tf_op jit(solution)/shard_map/ppermute | solution.py:433
  143.5 16.6 %collective-permute-start.22 = (bf16[448,256]{1,0:T(8,128)(2,1)S(1)}, bf16[448,256]{1,0:T(8,128)(2,1)S(1)}, u32[]{:S(2)}, u32[]{:S(2)}) collective-permute-start(bf16[448,256]{1,0:T(8,128)(2,1)S(1)} %get-tuple-element.84), channel_id=1, source_target_pairs={{0,2},{2,4},{4,6},{6,0},{1,3},{3,5},{5,7},{7,1},{8,10},{10,12},{12... | collective-permute-start | bytes 688136 | tf_op jit(solution)/shard_map/ppermute | solution.py:433
  143.6 30.4 %collective-permute-start.24 = (bf16[448,256]{1,0:T(8,128)(2,1)S(1)}, bf16[448,256]{1,0:T(8,128)(2,1)S(1)}, u32[]{:S(2)}, u32[]{:S(2)}) collective-permute-start(bf16[448,256]{1,0:T(8,128)(2,1)S(1)} %get-tuple-element.86), channel_id=1, source_target_pairs={{0,4},{2,6},{4,0},{6,2},{1,5},{3,7},{5,1},{7,3},{8,12},{10,14},{12... | collective-permute-start | bytes 688136 | tf_op jit(solution)/shard_map/ppermute | solution.py:433
  147.3 26.7 %collective-permute-start.26 = (bf16[448,256]{1,0:T(8,128)(2,1)S(1)}, bf16[448,256]{1,0:T(8,128)(2,1)S(1)}, u32[]{:S(2)}, u32[]{:S(2)}) collective-permute-start(bf16[448,256]{1,0:T(8,128)(2,1)S(1)} %get-tuple-element.88), channel_id=1, source_target_pairs={{0,6},{2,0},{4,2},{6,4},{1,7},{3,1},{5,3},{7,5},{8,14},{10,8},{12,... | collective-permute-start | bytes 688136 | tf_op jit(solution)/shard_map/ppermute | solution.py:433
  (17 other events, 55.8 us)

commit v10 on v9

--- a/solution.py
+++ b/solution.py
@@ -53,18 +53,22 @@
     return out
 
 
+def places_of(core, per_group):
+    return [p for p in range(HELD) if (p // per_group) % 2 == core]
+
+
 def stacked(table, per_group):
     every = placed(table).transpose(0, 2, 1)
-    own = [[p for p in range(HELD) if (p // per_group) % 2 == core] for core in range(2)]
-    return np.stack([every[places].reshape(-1, LANES) for places in own])
+    return np.stack([every[places_of(core, per_group)].reshape(-1, LANES) for core in range(2)])
 
 
 def project_kernel(at_ref, per_group, layers, gathered, *refs):
     mine, other = refs[:layers], refs[layers : 2 * layers]
     table_ref, bias_ref, wq_ref, wk_ref, own_ref = refs[2 * layers : 2 * layers + 5]
     rest = refs[2 * layers + 5 :]
-    weights, rest = rest[:-10], rest[-10:]
-    q_ref, k_ref, v_ref, early_ref, total_ref, row_ref, narrow_ref, w_ref, phi_ref, sems = rest
+    weights, rest = rest[:-16], rest[-16:]
+    results, rest = rest[:5], rest[5:]
+    q_ref, k_ref, v_ref, early_ref, total_ref, row_ref, narrow_ref, w_ref, phi_ref, sems, out_sems = rest
     core, layer, slab = at_ref[0], at_ref[1], at_ref[2]
     both, width = other[0].shape
     rows = both // 2
@@ -82,12 +86,30 @@
     fetch(-1, wk_ref, narrow_ref.at[:, pl.ds(narrow, narrow)])
     fetch(0, own_ref, w_ref.at[0, :, pl.ds(0, block)])
     for d in range(1, layers):
-        for m in range(model // part):
-            if gathered:
-                source, start = weights[0].at[m, d - 1], m * part
-            else:
-                source, start = weights[m].at[d - 1], pl.multiple_of((slab ^ m) * part, part)
+        if gathered:
+            sources = [(weights[0].at[m, d - 1], m * part) for m in range(model // part)]
+        else:
+            upper, lower, upper_1, lower_2, upper_2, lower_1 = weights
+            base = [pl.multiple_of((slab ^ m) * 2 * part, part) for m in range(4)]
+            sources = [
+                (upper.at[d - 1], base[0]),
+                (lower.at[d - 1], base[0] + part),
+                (upper_1.at[d - 1], base[1]),
+                (lower_2.at[d - 1], base[2] + part),
+                (upper_2.at[0, d - 1], base[2]),
+                (lower_1.at[0, d - 1], base[1] + part),
+                (upper_2.at[1, d - 1], base[3]),
+                (lower_1.at[1, d - 1], base[3] + part),
+            ]
+        for source, start in sources:
+            start = pl.multiple_of(start, part)
             fetch(d, source, w_ref.at[d // 2, pl.ds(start, part), pl.ds((d % 2) * block, block)])
+
+    kept = []
+
+    def keep(source, to):
+        kept.append(pltpu.make_async_copy(source, to, out_sems.at[len(kept)]))
+        kept[-1].start()
 
     def arrived(slots):
         for slot, copy in copies:
@@ -113,6 +135,8 @@
             right = product[half:] + bias_ref[:, 1:2]
             to = (lanes // LANES) * half
             phi_ref[chunk, to : to + half, :] = (left * right).astype(BF16)
+    keep(q_ref, results[0])
+    keep(k_ref, results[1])
 
     for pair in range(layers // 2):
         arrived((2 * pair, 2 * pair + 1))
@@ -132,12 +156,18 @@
                 late = dot(phi_ref[1, pl.ds(place, PACKED), :], value[rows:, column : column + HEAD_DIM])
                 early_ref[head] = early.astype(BF16)
                 total_ref[head] = (early + late).astype(BF16)
+            own = pl.ds(z * per_group, per_group)
+            keep(total_ref.at[own], results[4].at[own])
+            keep(early_ref.at[own], results[3].at[own])
+            keep(v_ref.at[:, :, pl.ds(lanes, block)], results[2].at[:, :, pl.ds(lanes, block)])
+    for copy in kept:
+        copy.wait()
 
 
 def local_kernel(at_ref, per_group, offset, q_ref, k_ref, v_ref, early_ref, table_ref, bias_ref, num_ref, phi_ref):
     rows = q_ref.shape[1]
     cut = LANES * -(-rows // (2 * LANES))
-    wide = table_ref.shape[2] // 2
+    wide = table_ref.shape[-1] // 2
     local_head = pl.program_id(0) + offset
     head = (2 * (local_head // per_group) + at_ref[0]) * per_group + lax.rem(local_head, per_group)
     lanes = pl.multiple_of((head // HELD) * LANES, LANES)
@@ -146,7 +176,7 @@
     for chunk in range(2):
         query = q_ref[chunk, :, pl.ds(lanes, LANES)]
         key = k_ref[chunk, :, pl.ds(lanes, LANES)]
-        sides = dot(query, table_ref[place]) + bias_ref[...]
+        sides = dot(query, table_ref[0, lax.rem(local_head, HELD // 2)]) + bias_ref[...]
         phi = (sides[:, :PACKED] * sides[:, wide : wide + PACKED]).astype(BF16)
         phi_ref[chunk, 0] = phi
         mine = jnp.where(lane == place, query * jnp.asarray(0.25, BF16), jnp.zeros_like(query))
@@ -163,7 +193,7 @@
                 num = num + dot(weight, v_ref[chunk, :low, :])
             if chunk > 0:
                 num = num + dot(phi[low:high], early_ref[0])
-            num_ref[chunk, low:high, :] = num
+            num_ref[chunk, low:high, :] = num.astype(BF16)
 
 
 def prefix_kernel(at_ref, line_ref, *refs):
@@ -189,7 +219,7 @@
     for num_ref, phi_ref in zip(parts[0::2], parts[1::2]):
         for i in range(phi_ref.shape[1]):
             columns = slice(head * HEAD_DIM, (head + 1) * HEAD_DIM)
-            num = num_ref[0, :, i * HEAD_DIM : (i + 1) * HEAD_DIM]
+            num = num_ref[0, :, i * HEAD_DIM : (i + 1) * HEAD_DIM].astype(F32)
             num = num + dot(phi_ref[0, i], state_ref[head // group, head % group])
             mean_square = jnp.mean(num * num, axis=1, keepdims=True)
             hidden = num * lax.rsqrt(mean_square + 1e-05) * gain_ref[:, columns]
@@ -273,6 +303,7 @@
     query_bias = np.zeros((1, 2 * wide), np.float32)
     query_table[:, :, :PACKED] = placed(first * scale)
     query_table[:, :, wide : wide + PACKED] = placed(second)
+    query_table = np.stack([query_table[places_of(core, per_group)] for core in range(2)])
     query_bias[0, :PACKED] = first_bias * scale
     query_bias[0, wide : wide + PACKED] = second_bias
     query_table, query_bias = jnp.asarray(query_table, BF16), jnp.asarray(query_bias)
@@ -288,16 +319,23 @@
     value_part = lax.dynamic_slice_in_dim(w_value, my_slab * part, part, 0)
     blocks = tokens.reshape(layers, 2 * rows, width)
     sent = [lax.dynamic_index_in_dim(blocks, lax.rem(layer + d, layers), 0, False) for d in range(layers)]
-    stack = jnp.stack([lax.ppermute(value_part, "z", turn(-d)) for d in range(1, layers)])
-    stack, sent = lax.optimization_barrier((stack, sent))
+    quarters = [lax.ppermute(value_part, "z", turn(-d)) for d in range(1, layers)]
+    upper = jnp.stack([quarter[: part // 2] for quarter in quarters])
+    lower = jnp.stack([quarter[part // 2 :] for quarter in quarters])
+    upper, lower, sent = lax.optimization_barrier((upper, lower, sent))
     if slabs == 4:
-        weights = [stack] + [lax.ppermute(stack, "seq", flip(m)) for m in range(1, slabs)]
+        upper_1 = lax.ppermute(upper, "seq", flip(1))
+        lower_2 = lax.ppermute(lower, "seq", flip(2))
+        upper_2 = lax.ppermute(jnp.stack([upper, upper_1]), "seq", flip(2))
+        lower_1 = lax.ppermute(jnp.stack([lower, lower_2]), "seq", flip(1))
+        weights = [upper, lower, upper_1, lower_2, upper_2, lower_1]
     else:
+        stack = jnp.concatenate([upper, lower], axis=1)
         weights = [lax.all_gather(stack, "seq", axis=0, tiled=False)]
     far = layers // 2
     mine = {d: lax.ppermute(sent[d], "z", turn(d)) for d in [far] + [d for d in range(1, layers) if d != far]}
     mine = [sent[0]] + [mine[d] for d in range(1, layers)]
-    mine[1:], weights[1:] = lax.optimization_barrier((mine[1:], weights[1:]))
+    mine[1:], weights[2:] = lax.optimization_barrier((mine[1:], weights[2:]))
     other = [lax.ppermute(piece, "core", swap) for piece in mine]
 
     query, key, value, early, total = call(
@@ -311,13 +349,7 @@
             whole(key_bias.shape),
         ]
         + [anywhere] * (3 + len(weights)),
-        [
-            whole((2, rows, narrow)),
-            whole((2, rows, narrow)),
-            whole((2, rows, layers * value_width)),
-            whole((heads, PACKED, HEAD_DIM)),
-            whole((heads, PACKED, HEAD_DIM)),
-        ],
+        [anywhere] * 5,
         [
             jax.ShapeDtypeStruct((2, rows, narrow), BF16),
             jax.ShapeDtypeStruct((2, rows, narrow), BF16),
@@ -328,11 +360,17 @@
         (blocks, *mine[1:], *other, key_table, key_bias, w_query, w_key, w_value, *weights),
         4 * rows * model * (model // 2 + 2 * narrow),
         [
+            pltpu.VMEM((2, rows, narrow), BF16),
+            pltpu.VMEM((2, rows, narrow), BF16),
+            pltpu.VMEM((2, rows, layers * value_width), BF16),
+            pltpu.VMEM((heads, PACKED, HEAD_DIM), BF16),
+            pltpu.VMEM((heads, PACKED, HEAD_DIM), BF16),
             pltpu.VMEM((2 * rows, model), BF16),
             pltpu.VMEM((model, 2 * narrow), BF16),
             pltpu.VMEM((layers // 2, model, 2 * value_width), BF16),
             pltpu.VMEM((2, heads * PACKED, rows), BF16),
-            pltpu.SemaphoreType.DMA((3 + (layers - 1) * slabs,)),
+            pltpu.SemaphoreType.DMA((3 + (layers - 1) * max(8, slabs),)),
+            pltpu.SemaphoreType.DMA((2 + 3 * layers,)),
         ],
     )
 
@@ -346,7 +384,7 @@
                 whole((2, rows, narrow)),
                 pl.BlockSpec((2, rows, HEAD_DIM), lambda i, _: (0, 0, i + offset)),
                 pl.BlockSpec((1, PACKED, HEAD_DIM), lambda i, _: (i + offset, 0, 0)),
-                whole(query_table.shape),
+                pl.BlockSpec((1,) + query_table.shape[1:], lambda i, at: (at[0], 0, 0, 0)),
                 whole(query_bias.shape),
             ],
             [
@@ -354,7 +392,7 @@
                 pl.BlockSpec((2, 1, rows, PACKED), lambda i, _: (0, i, 0, 0)),
             ],
             [
-                jax.ShapeDtypeStruct((2, rows, count * HEAD_DIM), F32),
+                jax.ShapeDtypeStruct((2, rows, count * HEAD_DIM), BF16),
                 jax.ShapeDtypeStruct((2, count, rows, PACKED), BF16),
             ],
             (query, key, value, early, query_table, query_bias),

time: 179 us -> 198 us (1.11)
  the two profiles are of different devices: /device:TPU:0 before, /device:TPU:9 now
where the time goes in v10:
time: 198 us; the launch traced here: 197 us
  waiting for transfers between devices  71.6 us (36%)
  starting transfers between devices  62.4 us (32%)
  Pallas kernels  49.3 us (25%)
  local copies, waits for them, and re-layouts  12.6 us (6%)
    pallas_call x11, Pallas kernels, call(): pl.pallas_call(kernel, grid_spec=pltpu.PrefetchScalarGridSpec(num_scalar_...  47.4 us
    ppermute x6, waiting for transfers between devices, per_device(): pieces[d, chunk] = lax.ppermute(piece, 'z', turn(d)) if d else piece  30.3 us
    ppermute x4, starting transfers between devices, per_device(): other = [lax.ppermute(piece, 'core', swap) for piece in mine]  27.7 us
    ppermute x3, waiting for transfers between devices, per_device(): lax.ppermute(value_part, 'z', turn(-d))  19.7 us
    ppermute x3, waiting for transfers between devices, per_device(): lax.ppermute(sent[d], 'z', turn(d))  11.8 us
    unnamed x50, local copies, waits for them, and re-layouts  9.38 us
    ppermute x1, waiting for transfers between devices, per_device(): lower_2 = lax.ppermute(lower, 'seq', flip(2))  7.74 us
    ppermute x6, starting transfers between devices, per_device(): pieces[d, chunk] = lax.ppermute(piece, 'z', turn(d)) if d else piece  6.4 us
  transfers between devices with their start and end apart: 29, of which 12 were waited for; matrix products, arithmetic and copies ran while one was open for 1% of the time, Pallas kernels for 14%

profile of v10, /device:TPU:9, one launch (start us, length us, event | category | flops | bytes accessed | tf_op | source)
XLA Modules:
  0.0 197.3 jit_solution(4323727221121107389)
XLA Ops:
  1.0 2.4 %collective-permute-start.1 = (bf16[512,256]{1,0:T(8,128)(2,1)S(1)}, bf16[512,256]{1,0:T(8,128)(2,1)S(1)}, u32[]{:S(2)}, u32[]{:S(2)}) collective-permute-start(bf16[512,256]{1,0:T(8,128)(2,1)S(1)} %constant_dynamic-slice_fusion), channel_id=1, source_target_pairs={{0,4},{2,6},{4,0},{6,2},{1,5},{3,7},{5,1},{7,3},{8,12},{10,14},{12... | collective-permute-start | bytes 786440 | tf_op jit(solution)/shard_map/ppermute | solution.py:322
  4.8 1.6 dynamic-slice_bitcast_fusion
  6.4 9.0 %collective-permute-done.1 = bf16[512,256]{1,0:T(8,128)(2,1)S(1)} collective-permute-done((bf16[512,256]{1,0:T(8,128)(2,1)S(1)}, bf16[512,256]{1,0:T(8,128)(2,1)S(1)}, u32[]{:S(2)}, u32[]{:S(2)}) %collective-permute-start.1) | collective-permute-done | bytes 262176 | tf_op jit(solution)/shard_map/ppermute | solution.py:322
  15.4 10.7 %collective-permute-done.2 = bf16[512,256]{1,0:T(8,128)(2,1)S(1)} collective-permute-done((bf16[512,256]{1,0:T(8,128)(2,1)S(1)}, bf16[512,256]{1,0:T(8,128)(2,1)S(1)}, u32[]{:S(2)}, u32[]{:S(2)}) %collective-permute-start.2) | collective-permute-done | bytes 262176 | tf_op jit(solution)/shard_map/ppermute | solution.py:322
  28.8 7.7 %collective-permute-done.7.refs_16_ = bf16[3,256,256]{2,1,0:T(8,128)(2,1)S(1)} collective-permute-done((bf16[3,256,256]{2,1,0:T(8,128)(2,1)S(1)}, bf16[3,256,256]{2,1,0:T(8,128)(2,1)S(1)}, u32[]{:S(2)}, u32[]{:S(2)}) %collective-permute-start.7) | collective-permute-done | bytes 393248 | tf_op jit(solution)/shard_map/ppermute | solution.py:328
  39.3 2.2 %collective-permute-start.3 = (bf16[896,256]{1,0:T(8,128)(2,1)S(1)}, bf16[896,256]{1,0:T(8,128)(2,1)S(1)}, u32[]{:S(2)}, u32[]{:S(2)}) collective-permute-start(bf16[896,256]{1,0:T(8,128)(2,1)S(1)} %get-tuple-element.49), channel_id=1, source_target_pairs={{0,2},{2,4},{4,6},{6,0},{1,3},{3,5},{5,7},{7,1},{8,10},{10,12},{12... | collective-permute-start | bytes 1376264 | tf_op jit(solution)/shard_map/ppermute | solution.py:336
  42.7 7.2 %collective-permute-done.3.refs_1_ = bf16[896,256]{1,0:T(8,128)(2,1)S(1)} collective-permute-done((bf16[896,256]{1,0:T(8,128)(2,1)S(1)}, bf16[896,256]{1,0:T(8,128)(2,1)S(1)}, u32[]{:S(2)}, u32[]{:S(2)}) %collective-permute-start.3) | collective-permute-done | bytes 458784 | tf_op jit(solution)/shard_map/ppermute | solution.py:336
  49.9 24.4 %collective-permute-start.10 = (bf16[896,256]{1,0:T(8,128)(2,1)S(1)}, bf16[896,256]{1,0:T(8,128)(2,1)}, u32[]{:S(2)}, u32[]{:S(2)}) collective-permute-start(bf16[896,256]{1,0:T(8,128)(2,1)S(1)} %get-tuple-element.57), channel_id=1, source_target_pairs={{0,1},{1,0},{2,3},{3,2},{4,5},{5,4},{6,7},{7,6},{8,9},{9,8},{10,11... | collective-permute-start | bytes 1376264 | tf_op jit(solution)/shard_map/ppermute | solution.py:339
  74.3 4.6 %collective-permute-done.4.refs_2_ = bf16[896,256]{1,0:T(8,128)(2,1)} collective-permute-done((bf16[896,256]{1,0:T(8,128)(2,1)S(1)}, bf16[896,256]{1,0:T(8,128)(2,1)}, u32[]{:S(2)}, u32[]{:S(2)}) %collective-permute-start.4) | collective-permute-done | bytes 458784 | tf_op jit(solution)/shard_map/ppermute | solution.py:336
  79.9 2.8 %collective-permute-start.11 = (bf16[896,256]{1,0:T(8,128)(2,1)S(1)}, bf16[896,256]{1,0:T(8,128)(2,1)}, u32[]{:S(2)}, u32[]{:S(2)}) collective-permute-start(bf16[896,256]{1,0:T(8,128)(2,1)S(1)} %collective-permute-done.3.refs_1_), channel_id=1, source_target_pairs={{0,1},{1,0},{2,3},{3,2},{4,5},{5,4},{6,7},{7,6},{8,9},{9,8},{10,11... | collective-permute-start | bytes 1376264 | tf_op jit(solution)/shard_map/ppermute | solution.py:339
  85.8 14.0 %shard_map.100 = (bf16[2,448,256]{2,1,0:T(8,128)(2,1)}, bf16[2,448,256]{2,1,0:T(8,128)(2,1)}, bf16[2,448,1024]{2,1,0:T(8,128)(2,1)}, bf16[8,160,128]{2,1,0:T(8,128)(2,1)}, bf16[8,160,128]{2,1,0:T(8,128)(2,1)}) custom-call(s32[3]{0:T(128)} %pad_add_fusion.at_ref.core_ref, bf16[4,896,256]{2,1,0:T(8,128)(2,1)} %bitcast.52, bf16[896,256]{1,0:T(8,128)(2,1)} %copy-done.22, ...), custom_call_target="tpu_custom_call" | custom-call | flops 5637144576 | bytes 12582912 | tf_op jit(solution)/shard_map/pallas_call | solution.py:264
  99.9 5.7 %all-to-all-start = ((bf16[4,2,160,128]{3,2,1,0:T(8,128)(2,1)}), bf16[4,2,160,128]{3,2,1,0:T(8,128)(2,1)S(1)}, u32[]{:S(2)}, u32[]{:S(2)}) async-start(bf16[4,2,160,128]{3,2,1,0:T(8,128)(2,1)} %bitcast.57), calls=%async_computation | async-start | bytes 655360 | tf_op jit(solution)/shard_map/all_to_all | solution.py:403
  105.5 7.8 %shard_map.101 = (bf16[2,448,512]{2,1,0:T(8,128)(2,1)}, bf16[2,4,448,160]{3,2,1,0:T(8,128)(2,1)}) custom-call(s32[3]{0:T(128)} %pad_add_fusion.at_ref.core_ref, bf16[2,448,256]{2,1,0:T(8,128)(2,1)} %get-tuple-element.63.refs_0_, bf16[2,448,256]{2,1,0:T(8,128)(2,1)} %get-tuple-element.64.refs_1_, bf16[2,448,1024]{2,1,0:T(8,128)(2,1)} %get-tuple-element.65.refs_2_, ...), custom_call_target="tpu_custom_call" | custom-call | flops 963379200 | bytes 12582912 | tf_op jit(solution)/shard_map/pallas_call | solution.py:264
  114.5 1.6 collective-permute-start.16
  116.1 5.3 %shard_map.102 = (bf16[2,448,256]{2,1,0:T(8,128)(2,1)}, bf16[2,2,448,160]{3,2,1,0:T(8,128)(2,1)}) custom-call(s32[3]{0:T(128)} %pad_add_fusion.at_ref.core_ref, bf16[2,448,256]{2,1,0:T(8,128)(2,1)} %get-tuple-element.63.refs_0_, bf16[2,448,256]{2,1,0:T(8,128)(2,1)} %get-tuple-element.64.refs_1_, bf16[2,448,1024]{2,1,0:T(8,128)(2,1)} %get-tuple-element.65.refs_2_, ...), custom_call_target="tpu_custom_call" | custom-call | flops 481689600 | bytes 12582912 | tf_op jit(solution)/shard_map/pallas_call | solution.py:264
  122.2 1.9 shard_map.103
  126.4 2.1 %collective-permute-start.19 = (bf16[2,160,128]{2,1,0:T(8,128)(2,1)}, bf16[2,160,128]{2,1,0:T(8,128)(2,1)}, u32[]{:S(2)}, u32[]{:S(2)}) collective-permute-start(bf16[2,160,128]{2,1,0:T(8,128)(2,1)} %get-tuple-element.78), channel_id=1, source_target_pairs={{0,2},{2,4},{4,6},{6,0},{1,3},{3,5},{5,7},{7,1},{8,10},{10,12},{12... | collective-permute-start | bytes 245768 | tf_op jit(solution)/shard_map/ppermute | solution.py:418
  129.1 5.9 %shard_map.104 = (bf16[2,448,256]{2,1,0:T(8,128)(2,1)}, bf16[2,2,448,160]{3,2,1,0:T(8,128)(2,1)}) custom-call(s32[3]{0:T(128)} %pad_add_fusion.at_ref.core_ref, bf16[2,448,256]{2,1,0:T(8,128)(2,1)} %get-tuple-element.63.refs_0_, bf16[2,448,256]{2,1,0:T(8,128)(2,1)} %get-tuple-element.64.refs_1_, bf16[2,448,1024]{2,1,0:T(8,128)(2,1)} %get-tuple-element.65.refs_2_, ...), custom_call_target="tpu_custom_call" | custom-call | flops 481689600 | bytes 12582912 | tf_op jit(solution)/shard_map/pallas_call | solution.py:264
  139.4 3.0 %shard_map.107.mine_ref = bf16[448,1024]{1,0:T(8,128)(2,1)S(1)} custom-call(s32[3]{0:T(128)S(1)} %copy-done.8, f32[1,1024]{1,0:T(1,128)S(1)} %bitcast.49, bf16[2,160,128]{2,1,0:T(8,128)(2,1)S(1)} %copy-done.7, bf16[2,160,128]{2,1,0:T(8,128)(2,1)} %collective-permute-done.17.refs_2_, bf16[2,160,128]{2,1,0:T(8,128)(2,1)} %collective-permute-done.18.refs_3_, ...), custom_call_target="tpu_custom_call" | custom-call | flops 275251200 | bytes 12582912 | tf_op jit(solution)/shard_map/pallas_call | solution.py:264
  142.5 3.1 %collective-permute-start.21 = (bf16[448,1024]{1,0:T(8,128)(2,1)S(1)}, bf16[448,1024]{1,0:T(8,128)(2,1)S(1)}, u32[]{:S(2)}, u32[]{:S(2)}) collective-permute-start(bf16[448,1024]{1,0:T(8,128)(2,1)S(1)} %shard_map.107.mine_ref), channel_id=1, source_target_pairs={{0,1},{1,0},{2,3},{3,2},{4,5},{5,4},{6,7},{7,6},{8,9},{9,8},{10,11... | collective-permute-start | bytes 2752520 | tf_op jit(solution)/shard_map/ppermute | solution.py:464
  145.6 2.7 %shard_map.105.mine_ref = bf16[448,1024]{1,0:T(8,128)(2,1)S(1)} custom-call(s32[3]{0:T(128)S(1)} %copy-done.8, f32[1,1024]{1,0:T(1,128)S(1)} %bitcast.50, bf16[2,160,128]{2,1,0:T(8,128)(2,1)S(1)} %copy-done.7, bf16[2,160,128]{2,1,0:T(8,128)(2,1)} %collective-permute-done.17.refs_2_, bf16[2,160,128]{2,1,0:T(8,128)(2,1)} %collective-permute-done.18.refs_3_, ...), custom_call_target="tpu_custom_call" | custom-call | flops 275251200 | bytes 12582912 | tf_op jit(solution)/shard_map/pallas_call | solution.py:264
  148.4 3.4 %copy-done = bf16[2048,2048]{1,0:T(8,128)(2,1)S(1)} copy-done((bf16[2048,2048]{1,0:T(8,128)(2,1)S(1)}, bf16[2048,2048]{1,0:T(8,128)(2,1)}, u32[]{:S(2)}) %copy-start) | copy-done | bytes 8388632
  151.8 1.7 shard_map.110
  154.8 1.7 shard_map.109
  159.5 1.7 shard_map.108
  161.2 1.7 shard_map.106
  162.9 2.1 %collective-permute-start.26 = (bf16[448,256]{1,0:T(8,128)(2,1)S(1)}, bf16[448,256]{1,0:T(8,128)(2,1)S(1)}, u32[]{:S(2)}, u32[]{:S(2)}) collective-permute-start(bf16[448,256]{1,0:T(8,128)(2,1)S(1)} %get-tuple-element.91), channel_id=1, source_target_pairs={{0,6},{2,0},{4,2},{6,4},{1,7},{3,1},{5,3},{7,5},{8,14},{10,8},{12,... | collective-permute-start | bytes 688136 | tf_op jit(solution)/shard_map/ppermute | solution.py:471
  165.0 3.2 %collective-permute-done.25.refs_5_ = bf16[448,256]{1,0:T(8,128)(2,1)S(1)} collective-permute-done((bf16[448,256]{1,0:T(8,128)(2,1)S(1)}, bf16[448,256]{1,0:T(8,128)(2,1)S(1)}, u32[]{:S(2)}, u32[]{:S(2)}) %collective-permute-start.25) | collective-permute-done | bytes 229408 | tf_op jit(solution)/shard_map/ppermute | solution.py:471
  168.2 19.7 %collective-permute-done.22.refs_2_ = bf16[448,256]{1,0:T(8,128)(2,1)S(1)} collective-permute-done((bf16[448,256]{1,0:T(8,128)(2,1)S(1)}, bf16[448,256]{1,0:T(8,128)(2,1)S(1)}, u32[]{:S(2)}, u32[]{:S(2)}) %collective-permute-start.22) | collective-permute-done | bytes 229408 | tf_op jit(solution)/shard_map/ppermute | solution.py:471
  187.8 4.9 %collective-permute-done.24.refs_4_ = bf16[448,256]{1,0:T(8,128)(2,1)S(1)} collective-permute-done((bf16[448,256]{1,0:T(8,128)(2,1)S(1)}, bf16[448,256]{1,0:T(8,128)(2,1)S(1)}, u32[]{:S(2)}, u32[]{:S(2)}) %collective-permute-start.24) | collective-permute-done | bytes 229408 | tf_op jit(solution)/shard_map/ppermute | solution.py:471
  192.8 2.5 %collective-permute-done.26.refs_6_ = bf16[448,256]{1,0:T(8,128)(2,1)S(1)} collective-permute-done((bf16[448,256]{1,0:T(8,128)(2,1)S(1)}, bf16[448,256]{1,0:T(8,128)(2,1)S(1)}, u32[]{:S(2)}, u32[]{:S(2)}) %collective-permute-start.26) | collective-permute-done | bytes 229408 | tf_op jit(solution)/shard_map/ppermute | solution.py:471
  195.3 1.8 shard_map.111
  (101 shorter events, 26.6 us)
Async XLA Ops:
  1.0 14.4 %collective-permute-start.1 = (bf16[512,256]{1,0:T(8,128)(2,1)S(1)}, bf16[512,256]{1,0:T(8,128)(2,1)S(1)}, u32[]{:S(2)}, u32[]{:S(2)}) collective-permute-start(bf16[512,256]{1,0:T(8,128)(2,1)S(1)} %constant_dynamic-slice_fusion), channel_id=1, source_target_pairs={{0,4},{2,6},{4,0},{6,2},{1,5},{3,7},{5,1},{7,3},{8,12},{10,14},{12... | collective-permute-start | bytes 786440 | tf_op jit(solution)/shard_map/ppermute | solution.py:322
  3.3 22.8 %collective-permute-start.2 = (bf16[512,256]{1,0:T(8,128)(2,1)S(1)}, bf16[512,256]{1,0:T(8,128)(2,1)S(1)}, u32[]{:S(2)}, u32[]{:S(2)}) collective-permute-start(bf16[512,256]{1,0:T(8,128)(2,1)S(1)} %constant_dynamic-slice_fusion), channel_id=1, source_target_pairs={{0,2},{2,4},{4,6},{6,0},{1,3},{3,5},{5,7},{7,1},{8,10},{10,12},{12... | collective-permute-start | bytes 786440 | tf_op jit(solution)/shard_map/ppermute | solution.py:322
  3.3 22.8 %collective-permute-start = (bf16[512,256]{1,0:T(8,128)(2,1)S(1)}, bf16[512,256]{1,0:T(8,128)(2,1)S(1)}, u32[]{:S(2)}, u32[]{:S(2)}) collective-permute-start(bf16[512,256]{1,0:T(8,128)(2,1)S(1)} %constant_dynamic-slice_fusion), channel_id=1, source_target_pairs={{0,6},{2,0},{4,2},{6,4},{1,7},{3,1},{5,3},{7,5},{8,14},{10,8},{12,... | collective-permute-start | bytes 786440 | tf_op jit(solution)/shard_map/ppermute | solution.py:322
  26.3 59.5 %copy-start.12 = (bf16[3,256,256]{2,1,0:T(8,128)(2,1)}, bf16[3,256,256]{2,1,0:T(8,128)(2,1)S(1)}, u32[]{:S(2)}) copy-start(bf16[3,256,256]{2,1,0:T(8,128)(2,1)S(1)} %get-tuple-element.52.refs_13_) | copy-start | bytes 1179652
  26.3 59.5 %copy-start.13 = (bf16[3,256,256]{2,1,0:T(8,128)(2,1)}, bf16[3,256,256]{2,1,0:T(8,128)(2,1)S(1)}, u32[]{:S(2)}) copy-start(bf16[3,256,256]{2,1,0:T(8,128)(2,1)S(1)} %get-tuple-element.53.refs_14_) | copy-start | bytes 1179652
  26.3 10.3 %collective-permute-start.7 = (bf16[3,256,256]{2,1,0:T(8,128)(2,1)S(1)}, bf16[3,256,256]{2,1,0:T(8,128)(2,1)S(1)}, u32[]{:S(2)}, u32[]{:S(2)}) collective-permute-start(bf16[3,256,256]{2,1,0:T(8,128)(2,1)S(1)} %get-tuple-element.53.refs_14_), channel_id=1, source_target_pairs={{0,16},{8,24},{16,0},{24,8},{1,17},{9,25},{17,1},{25,9},{2,18},{10... | collective-permute-start | bytes 1179656 | tf_op jit(solution)/shard_map/ppermute | solution.py:328
  27.6 10.3 %collective-permute-start.6 = (bf16[3,256,256]{2,1,0:T(8,128)(2,1)S(1)}, bf16[3,256,256]{2,1,0:T(8,128)(2,1)S(1)}, u32[]{:S(2)}, u32[]{:S(2)}) collective-permute-start(bf16[3,256,256]{2,1,0:T(8,128)(2,1)S(1)} %get-tuple-element.52.refs_13_), channel_id=1, source_target_pairs={{0,8},{8,0},{16,24},{24,16},{1,9},{9,1},{17,25},{25,17},{2,10},{10... | collective-permute-start | bytes 1179656 | tf_op jit(solution)/shard_map/ppermute | solution.py:327
  36.5 49.3 %copy-start.14 = (bf16[3,256,256]{2,1,0:T(8,128)(2,1)}, bf16[3,256,256]{2,1,0:T(8,128)(2,1)S(1)}, u32[]{:S(2)}) copy-start(bf16[3,256,256]{2,1,0:T(8,128)(2,1)S(1)} %collective-permute-done.7.refs_16_) | copy-start | bytes 1179652
  36.6 42.3 %collective-permute-start.9 = (bf16[2,3,256,256]{3,2,1,0:T(8,128)(2,1)S(1)}, bf16[2,3,256,256]{3,2,1,0:T(8,128)(2,1)S(1)}, u32[]{:S(2)}, u32[]{:S(2)}) collective-permute-start(bf16[2,3,256,256]{3,2,1,0:T(8,128)(2,1)S(1)} %pad_maximum_fusion.1), channel_id=1, source_target_pairs={{0,8},{8,0},{16,24},{24,16},{1,9},{9,1},{17,25},{25,17},{2,10},{10... | collective-permute-start | bytes 2359304 | tf_op jit(solution)/shard_map/ppermute | solution.py:330
  38.0 40.9 %collective-permute-start.8 = (bf16[2,3,256,256]{3,2,1,0:T(8,128)(2,1)S(1)}, bf16[2,3,256,256]{3,2,1,0:T(8,128)(2,1)S(1)}, u32[]{:S(2)}, u32[]{:S(2)}) collective-permute-start(bf16[2,3,256,256]{3,2,1,0:T(8,128)(2,1)S(1)} %pad_maximum_fusion), channel_id=1, source_target_pairs={{0,16},{8,24},{16,0},{24,8},{1,17},{9,25},{17,1},{25,9},{2,18},{10... | collective-permute-start | bytes 2359304 | tf_op jit(solution)/shard_map/ppermute | solution.py:329
  39.3 10.6 %collective-permute-start.3 = (bf16[896,256]{1,0:T(8,128)(2,1)S(1)}, bf16[896,256]{1,0:T(8,128)(2,1)S(1)}, u32[]{:S(2)}, u32[]{:S(2)}) collective-permute-start(bf16[896,256]{1,0:T(8,128)(2,1)S(1)} %get-tuple-element.49), channel_id=1, source_target_pairs={{0,2},{2,4},{4,6},{6,0},{1,3},{3,5},{5,7},{7,1},{8,10},{10,12},{12... | collective-permute-start | bytes 1376264 | tf_op jit(solution)/shard_map/ppermute | solution.py:336
  41.5 37.4 %collective-permute-start.4 = (bf16[896,256]{1,0:T(8,128)(2,1)S(1)}, bf16[896,256]{1,0:T(8,128)(2,1)}, u32[]{:S(2)}, u32[]{:S(2)}) collective-permute-start(bf16[896,256]{1,0:T(8,128)(2,1)S(1)} %get-tuple-element.50), channel_id=1, source_target_pairs={{0,4},{2,6},{4,0},{6,2},{1,5},{3,7},{5,1},{7,3},{8,12},{10,14},{12... | collective-permute-start | bytes 1376264 | tf_op jit(solution)/shard_map/ppermute | solution.py:336
  41.5 37.4 %collective-permute-start.5 = (bf16[896,256]{1,0:T(8,128)(2,1)S(1)}, bf16[896,256]{1,0:T(8,128)(2,1)}, u32[]{:S(2)}, u32[]{:S(2)}) collective-permute-start(bf16[896,256]{1,0:T(8,128)(2,1)S(1)} %get-tuple-element.51), channel_id=1, source_target_pairs={{0,6},{2,0},{4,2},{6,4},{1,7},{3,1},{5,3},{7,5},{8,14},{10,8},{12,... | collective-permute-start | bytes 1376264 | tf_op jit(solution)/shard_map/ppermute | solution.py:336
  49.9 33.9 %collective-permute-start.10 = (bf16[896,256]{1,0:T(8,128)(2,1)S(1)}, bf16[896,256]{1,0:T(8,128)(2,1)}, u32[]{:S(2)}, u32[]{:S(2)}) collective-permute-start(bf16[896,256]{1,0:T(8,128)(2,1)S(1)} %get-tuple-element.57), channel_id=1, source_target_pairs={{0,1},{1,0},{2,3},{3,2},{4,5},{5,4},{6,7},{7,6},{8,9},{9,8},{10,11... | collective-permute-start | bytes 1376264 | tf_op jit(solution)/shard_map/ppermute | solution.py:339
  79.9 5.0 %collective-permute-start.11 = (bf16[896,256]{1,0:T(8,128)(2,1)S(1)}, bf16[896,256]{1,0:T(8,128)(2,1)}, u32[]{:S(2)}, u32[]{:S(2)}) collective-permute-start(bf16[896,256]{1,0:T(8,128)(2,1)S(1)} %collective-permute-done.3.refs_1_), channel_id=1, source_target_pairs={{0,1},{1,0},{2,3},{3,2},{4,5},{5,4},{6,7},{7,6},{8,9},{9,8},{10,11... | collective-permute-start | bytes 1376264 | tf_op jit(solution)/shard_map/ppermute | solution.py:339
  82.7 2.4 %collective-permute-start.12 = (bf16[896,256]{1,0:T(8,128)(2,1)}, bf16[896,256]{1,0:T(8,128)(2,1)}, u32[]{:S(2)}, u32[]{:S(2)}) collective-permute-start(bf16[896,256]{1,0:T(8,128)(2,1)} %collective-permute-done.4.refs_2_), channel_id=1, source_target_pairs={{0,1},{1,0},{2,3},{3,2},{4,5},{5,4},{6,7},{7,6},{8,9},{9,8},{10,11... | collective-permute-start | bytes 1376264 | tf_op jit(solution)/shard_map/ppermute | solution.py:339
  82.7 3.1 %collective-permute-start.13 = (bf16[896,256]{1,0:T(8,128)(2,1)}, bf16[896,256]{1,0:T(8,128)(2,1)}, u32[]{:S(2)}, u32[]{:S(2)}) collective-permute-start(bf16[896,256]{1,0:T(8,128)(2,1)} %collective-permute-done.5.refs_3_), channel_id=1, source_target_pairs={{0,1},{1,0},{2,3},{3,2},{4,5},{5,4},{6,7},{7,6},{8,9},{9,8},{10,11... | collective-permute-start | bytes 1376264 | tf_op jit(solution)/shard_map/ppermute | solution.py:339
  99.9 13.5 %all-to-all-start = ((bf16[4,2,160,128]{3,2,1,0:T(8,128)(2,1)}), bf16[4,2,160,128]{3,2,1,0:T(8,128)(2,1)S(1)}, u32[]{:S(2)}, u32[]{:S(2)}) async-start(bf16[4,2,160,128]{3,2,1,0:T(8,128)(2,1)} %bitcast.57), calls=%async_computation | async-start | bytes 655360 | tf_op jit(solution)/shard_map/all_to_all | solution.py:403
  113.4 8.1 %collective-permute-start.14 = (bf16[2,160,128]{2,1,0:T(8,128)(2,1)S(1)}, bf16[2,160,128]{2,1,0:T(8,128)(2,1)S(1)}, u32[]{:S(2)}, u32[]{:S(2)}) collective-permute-start(bf16[2,160,128]{2,1,0:T(8,128)(2,1)S(1)} %reduce_sum.12), channel_id=1, source_target_pairs={{0,8},{8,0},{16,24},{24,16},{1,9},{9,1},{17,25},{25,17},{2,10},{10... | collective-permute-start | bytes 245768 | tf_op jit(solution)/shard_map/ppermute | solution.py:407
  113.7 7.8 %collective-permute-start.15 = (bf16[2,160,128]{2,1,0:T(8,128)(2,1)S(1)}, bf16[2,160,128]{2,1,0:T(8,128)(2,1)S(1)}, u32[]{:S(2)}, u32[]{:S(2)}) collective-permute-start(bf16[2,160,128]{2,1,0:T(8,128)(2,1)S(1)} %reduce_sum.12), channel_id=1, source_target_pairs={{0,16},{8,24},{16,0},{24,8},{1,17},{9,25},{17,1},{25,9},{2,18},{10... | collective-permute-start | bytes 245768 | tf_op jit(solution)/shard_map/ppermute | solution.py:407
  114.5 7.0 %collective-permute-start.16 = (bf16[2,160,128]{2,1,0:T(8,128)(2,1)S(1)}, bf16[2,160,128]{2,1,0:T(8,128)(2,1)S(1)}, u32[]{:S(2)}, u32[]{:S(2)}) collective-permute-start(bf16[2,160,128]{2,1,0:T(8,128)(2,1)S(1)} %reduce_sum.12), channel_id=1, source_target_pairs={{0,24},{8,16},{16,8},{24,0},{1,25},{9,17},{17,9},{25,1},{2,26},{10... | collective-permute-start | bytes 245768 | tf_op jit(solution)/shard_map/ppermute | solution.py:407
  124.1 10.9 %collective-permute-start.17 = (bf16[2,160,128]{2,1,0:T(8,128)(2,1)}, bf16[2,160,128]{2,1,0:T(8,128)(2,1)}, u32[]{:S(2)}, u32[]{:S(2)}) collective-permute-start(bf16[2,160,128]{2,1,0:T(8,128)(2,1)} %get-tuple-element.76), channel_id=1, source_target_pairs={{0,6},{2,0},{4,2},{6,4},{1,7},{3,1},{5,3},{7,5},{8,14},{10,8},{12,... | collective-permute-start | bytes 245768 | tf_op jit(solution)/shard_map/ppermute | solution.py:418
  124.9 10.0 %collective-permute-start.18 = (bf16[2,160,128]{2,1,0:T(8,128)(2,1)}, bf16[2,160,128]{2,1,0:T(8,128)(2,1)}, u32[]{:S(2)}, u32[]{:S(2)}) collective-permute-start(bf16[2,160,128]{2,1,0:T(8,128)(2,1)} %get-tuple-element.77), channel_id=1, source_target_pairs={{0,4},{2,6},{4,0},{6,2},{1,5},{3,7},{5,1},{7,3},{8,12},{10,14},{12... | collective-permute-start | bytes 245768 | tf_op jit(solution)/shard_map/ppermute | solution.py:418
  126.4 8.6 %collective-permute-start.19 = (bf16[2,160,128]{2,1,0:T(8,128)(2,1)}, bf16[2,160,128]{2,1,0:T(8,128)(2,1)}, u32[]{:S(2)}, u32[]{:S(2)}) collective-permute-start(bf16[2,160,128]{2,1,0:T(8,128)(2,1)} %get-tuple-element.78), channel_id=1, source_target_pairs={{0,2},{2,4},{4,6},{6,0},{1,3},{3,5},{5,7},{7,1},{8,10},{10,12},{12... | collective-permute-start | bytes 245768 | tf_op jit(solution)/shard_map/ppermute | solution.py:418
  142.5 5.9 %collective-permute-start.21 = (bf16[448,1024]{1,0:T(8,128)(2,1)S(1)}, bf16[448,1024]{1,0:T(8,128)(2,1)S(1)}, u32[]{:S(2)}, u32[]{:S(2)}) collective-permute-start(bf16[448,1024]{1,0:T(8,128)(2,1)S(1)} %shard_map.107.mine_ref), channel_id=1, source_target_pairs={{0,1},{1,0},{2,3},{3,2},{4,5},{5,4},{6,7},{7,6},{8,9},{9,8},{10,11... | collective-permute-start | bytes 2752520 | tf_op jit(solution)/shard_map/ppermute | solution.py:464
  148.3 6.5 %collective-permute-start.20 = (bf16[448,1024]{1,0:T(8,128)(2,1)S(1)}, bf16[448,1024]{1,0:T(8,128)(2,1)S(1)}, u32[]{:S(2)}, u32[]{:S(2)}) collective-permute-start(bf16[448,1024]{1,0:T(8,128)(2,1)S(1)} %shard_map.105.mine_ref), channel_id=1, source_target_pairs={{0,1},{1,0},{2,3},{3,2},{4,5},{5,4},{6,7},{7,6},{8,9},{9,8},{10,11... | collective-permute-start | bytes 2752520 | tf_op jit(solution)/shard_map/ppermute | solution.py:464
  153.5 9.5 %collective-permute-start.23 = (bf16[448,256]{1,0:T(8,128)(2,1)S(1)}, bf16[448,256]{1,0:T(8,128)(2,1)S(1)}, u32[]{:S(2)}, u32[]{:S(2)}) collective-permute-start(bf16[448,256]{1,0:T(8,128)(2,1)S(1)} %get-tuple-element.88), channel_id=1, source_target_pairs={{0,2},{2,4},{4,6},{6,0},{1,3},{3,5},{5,7},{7,1},{8,10},{10,12},{12... | collective-permute-start | bytes 688136 | tf_op jit(solution)/shard_map/ppermute | solution.py:471
  153.8 14.3 %collective-permute-start.25 = (bf16[448,256]{1,0:T(8,128)(2,1)S(1)}, bf16[448,256]{1,0:T(8,128)(2,1)S(1)}, u32[]{:S(2)}, u32[]{:S(2)}) collective-permute-start(bf16[448,256]{1,0:T(8,128)(2,1)S(1)} %get-tuple-element.90), channel_id=1, source_target_pairs={{0,4},{2,6},{4,0},{6,2},{1,5},{3,7},{5,1},{7,3},{8,12},{10,14},{12... | collective-permute-start | bytes 688136 | tf_op jit(solution)/shard_map/ppermute | solution.py:471
  156.5 31.4 %collective-permute-start.22 = (bf16[448,256]{1,0:T(8,128)(2,1)S(1)}, bf16[448,256]{1,0:T(8,128)(2,1)S(1)}, u32[]{:S(2)}, u32[]{:S(2)}) collective-permute-start(bf16[448,256]{1,0:T(8,128)(2,1)S(1)} %get-tuple-element.87), channel_id=1, source_target_pairs={{0,2},{2,4},{4,6},{6,0},{1,3},{3,5},{5,7},{7,1},{8,10},{10,12},{12... | collective-permute-start | bytes 688136 | tf_op jit(solution)/shard_map/ppermute | solution.py:471
  157.9 34.8 %collective-permute-start.24 = (bf16[448,256]{1,0:T(8,128)(2,1)S(1)}, bf16[448,256]{1,0:T(8,128)(2,1)S(1)}, u32[]{:S(2)}, u32[]{:S(2)}) collective-permute-start(bf16[448,256]{1,0:T(8,128)(2,1)S(1)} %get-tuple-element.89), channel_id=1, source_target_pairs={{0,4},{2,6},{4,0},{6,2},{1,5},{3,7},{5,1},{7,3},{8,12},{10,14},{12... | collective-permute-start | bytes 688136 | tf_op jit(solution)/shard_map/ppermute | solution.py:471
  161.1 31.6 %collective-permute-start.27 = (bf16[448,256]{1,0:T(8,128)(2,1)S(1)}, bf16[448,256]{1,0:T(8,128)(2,1)S(1)}, u32[]{:S(2)}, u32[]{:S(2)}) collective-permute-start(bf16[448,256]{1,0:T(8,128)(2,1)S(1)} %get-tuple-element.92), channel_id=1, source_target_pairs={{0,6},{2,0},{4,2},{6,4},{1,7},{3,1},{5,3},{7,5},{8,14},{10,8},{12,... | collective-permute-start | bytes 688136 | tf_op jit(solution)/shard_map/ppermute | solution.py:471
  162.9 32.4 %collective-permute-start.26 = (bf16[448,256]{1,0:T(8,128)(2,1)S(1)}, bf16[448,256]{1,0:T(8,128)(2,1)S(1)}, u32[]{:S(2)}, u32[]{:S(2)}) collective-permute-start(bf16[448,256]{1,0:T(8,128)(2,1)S(1)} %get-tuple-element.91), channel_id=1, source_target_pairs={{0,6},{2,0},{4,2},{6,4},{1,7},{3,1},{5,3},{7,5},{8,14},{10,8},{12,... | collective-permute-start | bytes 688136 | tf_op jit(solution)/shard_map/ppermute | solution.py:471
  (22 other events, 168.0 us)

commit v11 on v9

--- a/solution.py
+++ b/solution.py
@@ -53,10 +53,13 @@
     return out
 
 
+def places_of(core, per_group):
+    return [p for p in range(HELD) if (p // per_group) % 2 == core]
+
+
 def stacked(table, per_group):
     every = placed(table).transpose(0, 2, 1)
-    own = [[p for p in range(HELD) if (p // per_group) % 2 == core] for core in range(2)]
-    return np.stack([every[places].reshape(-1, LANES) for places in own])
+    return np.stack([every[places_of(core, per_group)].reshape(-1, LANES) for core in range(2)])
 
 
 def project_kernel(at_ref, per_group, layers, gathered, *refs):
@@ -78,8 +81,16 @@
         copies.append((slot, pltpu.make_async_copy(source, to, sems.at[len(copies)])))
         copies[-1][1].start()
 
-    fetch(-1, wq_ref, narrow_ref.at[:, pl.ds(0, narrow)])
-    fetch(-1, wk_ref, narrow_ref.at[:, pl.ds(narrow, narrow)])
+    for chunk in range(2):
+        for d in range(layers):
+            z = lax.rem(layer + layers - d, layers)
+            for piece, place in ((mine[d].at[layer] if d == 0 else mine[d], core), (other[d], 1 - core)):
+                columns = pl.ds(pl.multiple_of((2 * z + place) * width, width), width)
+                at = pl.ds(chunk * rows, rows)
+                fetch(-1 - chunk, piece.at[at], row_ref.at[at, columns])
+        if chunk == 0:
+            fetch(-3, wq_ref, narrow_ref.at[:, pl.ds(0, narrow)])
+            fetch(-3, wk_ref, narrow_ref.at[:, pl.ds(narrow, narrow)])
     fetch(0, own_ref, w_ref.at[0, :, pl.ds(0, block)])
     for d in range(1, layers):
         for m in range(model // part):
@@ -94,21 +105,14 @@
             if slot in slots:
                 copy.wait()
 
-    for d in range(layers):
-        z = lax.rem(layer + layers - d, layers)
-        here = pl.multiple_of((2 * z + core) * width, width)
-        there = pl.multiple_of((2 * z + 1 - core) * width, width)
-        row_ref[:, pl.ds(here, width)] = mine[d][0] if d == 0 else mine[d][...]
-        row_ref[:, pl.ds(there, width)] = other[d][...]
-    arrived((-1,))
     half = table_ref.shape[1] // 2
-    both_narrow = dot(row_ref[...], narrow_ref[...]).astype(BF16)
     for chunk in range(2):
-        at = slice(chunk * rows, (chunk + 1) * rows)
-        q_ref[chunk] = both_narrow[at, :narrow]
-        k_ref[chunk] = both_narrow[at, narrow:]
+        arrived((-1, -3) if chunk == 0 else (-2,))
+        both_narrow = dot(row_ref[chunk * rows : (chunk + 1) * rows, :], narrow_ref[...]).astype(BF16)
+        q_ref[chunk] = both_narrow[:, :narrow]
+        k_ref[chunk] = both_narrow[:, narrow:]
         for lanes in range(0, narrow, LANES):
-            product = dot(table_ref[0], both_narrow[at, narrow + lanes : narrow + lanes + LANES], NT)
+            product = dot(table_ref[0], both_narrow[:, narrow + lanes : narrow + lanes + LANES], NT)
             left = product[:half] + bias_ref[:, 0:1]
             right = product[half:] + bias_ref[:, 1:2]
             to = (lanes // LANES) * half
@@ -137,7 +141,7 @@
 def local_kernel(at_ref, per_group, offset, q_ref, k_ref, v_ref, early_ref, table_ref, bias_ref, num_ref, phi_ref):
     rows = q_ref.shape[1]
     cut = LANES * -(-rows // (2 * LANES))
-    wide = table_ref.shape[2] // 2
+    wide = table_ref.shape[-1] // 2
     local_head = pl.program_id(0) + offset
     head = (2 * (local_head // per_group) + at_ref[0]) * per_group + lax.rem(local_head, per_group)
     lanes = pl.multiple_of((head // HELD) * LANES, LANES)
@@ -146,7 +150,7 @@
     for chunk in range(2):
         query = q_ref[chunk, :, pl.ds(lanes, LANES)]
         key = k_ref[chunk, :, pl.ds(lanes, LANES)]
-        sides = dot(query, table_ref[place]) + bias_ref[...]
+        sides = dot(query, table_ref[0, lax.rem(local_head, HELD // 2)]) + bias_ref[...]
         phi = (sides[:, :PACKED] * sides[:, wide : wide + PACKED]).astype(BF16)
         phi_ref[chunk, 0] = phi
         mine = jnp.where(lane == place, query * jnp.asarray(0.25, BF16), jnp.zeros_like(query))
@@ -273,6 +277,7 @@
     query_bias = np.zeros((1, 2 * wide), np.float32)
     query_table[:, :, :PACKED] = placed(first * scale)
     query_table[:, :, wide : wide + PACKED] = placed(second)
+    query_table = np.stack([query_table[places_of(core, per_group)] for core in range(2)])
     query_bias[0, :PACKED] = first_bias * scale
     query_bias[0, wide : wide + PACKED] = second_bias
     query_table, query_bias = jnp.asarray(query_table, BF16), jnp.asarray(query_bias)
@@ -304,8 +309,7 @@
         lambda at_ref, *refs: project_kernel(at_ref, per_group, layers, slabs != 4, *refs),
         at,
         (1,),
-        [pl.BlockSpec((1, 2 * rows, width), lambda i, at: (at[1], 0, 0))]
-        + [whole((2 * rows, width))] * (2 * layers - 1)
+        [anywhere] * (2 * layers)
         + [
             pl.BlockSpec((1,) + key_table.shape[1:], lambda i, at: (at[0], 0, 0)),
             whole(key_bias.shape),
@@ -332,7 +336,7 @@
             pltpu.VMEM((model, 2 * narrow), BF16),
             pltpu.VMEM((layers // 2, model, 2 * value_width), BF16),
             pltpu.VMEM((2, heads * PACKED, rows), BF16),
-            pltpu.SemaphoreType.DMA((3 + (layers - 1) * slabs,)),
+            pltpu.SemaphoreType.DMA((3 + 4 * layers + (layers - 1) * slabs,)),
         ],
     )
 
@@ -346,7 +350,7 @@
                 whole((2, rows, narrow)),
                 pl.BlockSpec((2, rows, HEAD_DIM), lambda i, _: (0, 0, i + offset)),
                 pl.BlockSpec((1, PACKED, HEAD_DIM), lambda i, _: (i + offset, 0, 0)),
-                whole(query_table.shape),
+                pl.BlockSpec((1,) + query_table.shape[1:], lambda i, at: (at[0], 0, 0, 0)),
                 whole(query_bias.shape),
             ],
             [
@@ -363,12 +367,12 @@
 
     own = total.reshape(layers, per_group, PACKED, HEAD_DIM)
     line = lax.all_to_all(own, "z", split_axis=0, concat_axis=0, tiled=True)
-    locals_ = [local(0, heads // 2)]
+    locals_ = [local(0, 5 * heads // 8)]
     line, locals_ = lax.optimization_barrier((line, locals_))
     slab_total = jnp.sum(line.astype(F32), axis=0).astype(BF16)
     totals = [lax.ppermute(slab_total, "seq", flip(m)) for m in range(1, slabs)]
-    third = local(heads // 2, heads // 4)
-    totals, third = lax.optimization_barrier((totals, third))
+    rest = local(5 * heads // 8, 3 * heads // 8)
+    totals, rest = lax.optimization_barrier((totals, rest))
     piece_shape = (per_group, PACKED, HEAD_DIM)
     prefix = pl.pallas_call(
         prefix_kernel,
@@ -378,7 +382,7 @@
         scratch_shapes=[pltpu.VMEM((layers,) + piece_shape, BF16)],
     )(at, line, *totals)
     prefix = [prefix[0]] + [lax.ppermute(prefix[d], "z", turn(-d)) for d in range(1, layers)]
-    locals_ = locals_ + [third, local(3 * heads // 4, heads // 4)]
+    locals_ = locals_ + [rest]
 
     def hidden(chunk):
         some = rows // 2

time: 179 us -> 181 us (1.011)
  waiting for transfers between devices: 76.5 us -> 81.4 us
  Pallas kernels: 47.9 us -> 44.4 us
    ppermute x3, waiting for transfers between devices: 0.39 us -> 6.19 us  [per_device(): lax.ppermute(prefix[d], 'z', turn(-d))]
    pallas_call x11 -> x10, Pallas kernels: 46 us -> 42.5 us  [call(): pl.pallas_call(kernel, grid_spec=pltpu.PrefetchScalarGridSpec(num_scalar_...]
    unnamed x42 -> x36, local copies, waits for them, and re-layouts: 6.38 us -> 6.87 us
  transfers between devices with their start and end apart: 28 -> 28, of which waited for: 16 -> 17; matrix products, arithmetic and copies ran while one was open for 1% -> 1% of each run, Pallas kernels for 16% -> 14%
where the time goes in v11:
time: 181 us; the launch traced here: 179 us
  waiting for transfers between devices  81.4 us (45%)
  Pallas kernels  44.4 us (25%)
  starting transfers between devices  42.3 us (23%)
  local copies, waits for them, and re-layouts  9.4 us (5%)
    pallas_call x10, Pallas kernels, call(): pl.pallas_call(kernel, grid_spec=pltpu.PrefetchScalarGridSpec(num_scalar_...  42.5 us
    ppermute x3, waiting for transfers between devices, per_device(): lax.ppermute(sent[d], 'z', turn(d))  27.1 us
    ppermute x6, waiting for transfers between devices, per_device(): pieces[d, chunk] = lax.ppermute(piece, 'z', turn(d)) if d else piece  25 us
    ppermute x3, waiting for transfers between devices, per_device(): lax.ppermute(value_part, 'z', turn(-d))  14.2 us
    ppermute x6, starting transfers between devices, per_device(): pieces[d, chunk] = lax.ppermute(piece, 'z', turn(d)) if d else piece  8.96 us
    ppermute x3, starting transfers between devices, per_device(): lax.ppermute(sent[d], 'z', turn(d))  7.73 us
    all_to_all x1, starting transfers between devices, per_device(): line = lax.all_to_all(own, 'z', split_axis=0, concat_axis=0, tiled=True)  7.06 us
    ppermute x3, starting transfers between devices, per_device(): lax.ppermute(value_part, 'z', turn(-d))  7.01 us
  transfers between devices with their start and end apart: 28, of which 17 were waited for; matrix products, arithmetic and copies ran while one was open for 1% of the time, Pallas kernels for 14%

profile of v11, /device:TPU:0, one launch (start us, length us, event | category | flops | bytes accessed | tf_op | source)
XLA Modules:
  0.0 178.7 jit_solution(9338744999754528123)
XLA Ops:
  1.0 3.1 %collective-permute-start.2 = (bf16[512,256]{1,0:T(8,128)(2,1)S(1)}, bf16[512,256]{1,0:T(8,128)(2,1)S(1)}, u32[]{:S(2)}, u32[]{:S(2)}) collective-permute-start(bf16[512,256]{1,0:T(8,128)(2,1)S(1)} %constant_dynamic-slice_fusion), channel_id=1, source_target_pairs={{0,2},{2,4},{4,6},{6,0},{1,3},{3,5},{5,7},{7,1},{8,10},{10,12},{12... | collective-permute-start | bytes 786440 | tf_op jit(solution)/shard_map/ppermute | solution.py:296
  4.0 2.6 %collective-permute-start.1 = (bf16[512,256]{1,0:T(8,128)(2,1)S(1)}, bf16[512,256]{1,0:T(8,128)(2,1)S(1)}, u32[]{:S(2)}, u32[]{:S(2)}) collective-permute-start(bf16[512,256]{1,0:T(8,128)(2,1)S(1)} %constant_dynamic-slice_fusion), channel_id=1, source_target_pairs={{0,4},{2,6},{4,0},{6,2},{1,5},{3,7},{5,1},{7,3},{8,12},{10,14},{12... | collective-permute-start | bytes 786440 | tf_op jit(solution)/shard_map/ppermute | solution.py:296
  9.5 3.8 %collective-permute-done.2 = bf16[512,256]{1,0:T(8,128)(2,1)S(1)} collective-permute-done((bf16[512,256]{1,0:T(8,128)(2,1)S(1)}, bf16[512,256]{1,0:T(8,128)(2,1)S(1)}, u32[]{:S(2)}, u32[]{:S(2)}) %collective-permute-start.2) | collective-permute-done | bytes 262176 | tf_op jit(solution)/shard_map/ppermute | solution.py:296
  13.3 10.4 %collective-permute-done.1 = bf16[512,256]{1,0:T(8,128)(2,1)S(1)} collective-permute-done((bf16[512,256]{1,0:T(8,128)(2,1)S(1)}, bf16[512,256]{1,0:T(8,128)(2,1)S(1)}, u32[]{:S(2)}, u32[]{:S(2)}) %collective-permute-start.1) | collective-permute-done | bytes 262176 | tf_op jit(solution)/shard_map/ppermute | solution.py:296
  23.9 6.1 %collective-permute-start.3 = (bf16[896,256]{1,0:T(8,128)(2,1)S(1)}, bf16[896,256]{1,0:T(8,128)(2,1)S(1)}, u32[]{:S(2)}, u32[]{:S(2)}) collective-permute-start(bf16[896,256]{1,0:T(8,128)(2,1)S(1)} %get-tuple-element.45), channel_id=1, source_target_pairs={{0,2},{2,4},{4,6},{6,0},{1,3},{3,5},{5,7},{7,1},{8,10},{10,12},{12... | collective-permute-start | bytes 1376264 | tf_op jit(solution)/shard_map/ppermute | solution.py:303
  30.0 2.4 %collective-permute-start.8 = (bf16[3,512,256]{2,1,0:T(8,128)(2,1)S(1)}, bf16[3,512,256]{2,1,0:T(8,128)(2,1)S(1)}, u32[]{:S(2)}, u32[]{:S(2)}) collective-permute-start(bf16[3,512,256]{2,1,0:T(8,128)(2,1)S(1)} %pad_maximum_fusion.refs_13_), channel_id=1, source_target_pairs={{0,24},{8,16},{16,8},{24,0},{1,25},{9,17},{17,9},{25,1},{2,26},{10... | collective-permute-start | bytes 2359304 | tf_op jit(solution)/shard_map/ppermute | solution.py:299
  35.1 7.5 %collective-permute-done.3.refs_1_ = bf16[896,256]{1,0:T(8,128)(2,1)S(1)} collective-permute-done((bf16[896,256]{1,0:T(8,128)(2,1)S(1)}, bf16[896,256]{1,0:T(8,128)(2,1)S(1)}, u32[]{:S(2)}, u32[]{:S(2)}) %collective-permute-start.3) | collective-permute-done | bytes 458784 | tf_op jit(solution)/shard_map/ppermute | solution.py:303
  42.6 18.0 %collective-permute-done.4.refs_2_ = bf16[896,256]{1,0:T(8,128)(2,1)} collective-permute-done((bf16[896,256]{1,0:T(8,128)(2,1)S(1)}, bf16[896,256]{1,0:T(8,128)(2,1)}, u32[]{:S(2)}, u32[]{:S(2)}) %collective-permute-start.4) | collective-permute-done | bytes 458784 | tf_op jit(solution)/shard_map/ppermute | solution.py:303
  62.2 4.7 %collective-permute-done.7.refs_15_ = bf16[3,512,256]{2,1,0:T(8,128)(2,1)S(1)} collective-permute-done((bf16[3,512,256]{2,1,0:T(8,128)(2,1)S(1)}, bf16[3,512,256]{2,1,0:T(8,128)(2,1)S(1)}, u32[]{:S(2)}, u32[]{:S(2)}) %collective-permute-start.7) | collective-permute-done | bytes 786464 | tf_op jit(solution)/shard_map/ppermute | solution.py:299
  71.5 14.4 %shard_map.100 = (bf16[2,448,256]{2,1,0:T(8,128)(2,1)}, bf16[2,448,256]{2,1,0:T(8,128)(2,1)}, bf16[2,448,1024]{2,1,0:T(8,128)(2,1)}, bf16[8,160,128]{2,1,0:T(8,128)(2,1)}, bf16[8,160,128]{2,1,0:T(8,128)(2,1)}) custom-call(s32[3]{0:T(128)} %pad_add_fusion.at_ref.core_ref, bf16[4,896,256]{2,1,0:T(8,128)(2,1)} %bitcast.39, bf16[896,256]{1,0:T(8,128)(2,1)} %copy-done.15, ...), custom_call_target="tpu_custom_call" | custom-call | flops 5637144576 | bytes 12582912 | tf_op jit(solution)/shard_map/pallas_call | solution.py:238
  85.9 7.1 %all-to-all-start = ((bf16[4,2,160,128]{3,2,1,0:T(8,128)(2,1)}), bf16[4,2,160,128]{3,2,1,0:T(8,128)(2,1)S(1)}, u32[]{:S(2)}, u32[]{:S(2)}) async-start(bf16[4,2,160,128]{3,2,1,0:T(8,128)(2,1)} %bitcast.40), calls=%async_computation | async-start | bytes 655360 | tf_op jit(solution)/shard_map/all_to_all | solution.py:369
  93.0 9.2 %shard_map.101 = (f32[2,448,640]{2,1,0:T(8,128)}, bf16[2,5,448,160]{3,2,1,0:T(8,128)(2,1)}) custom-call(s32[3]{0:T(128)} %pad_add_fusion.at_ref.core_ref, bf16[2,448,256]{2,1,0:T(8,128)(2,1)} %get-tuple-element.57.refs_0_, bf16[2,448,256]{2,1,0:T(8,128)(2,1)} %get-tuple-element.58.refs_1_, bf16[2,448,1024]{2,1,0:T(8,128)(2,1)} %get-tuple-element.59.refs_2_, ...), custom_call_target="tpu_custom_call" | custom-call | flops 1204224000 | bytes 12582912 | tf_op jit(solution)/shard_map/pallas_call | solution.py:238
  103.8 2.5 %collective-permute-start.15 = (bf16[2,160,128]{2,1,0:T(8,128)(2,1)S(1)}, bf16[2,160,128]{2,1,0:T(8,128)(2,1)S(1)}, u32[]{:S(2)}, u32[]{:S(2)}) collective-permute-start(bf16[2,160,128]{2,1,0:T(8,128)(2,1)S(1)} %reduce_sum.12), channel_id=1, source_target_pairs={{0,24},{8,16},{16,8},{24,0},{1,25},{9,17},{17,9},{25,1},{2,26},{10... | collective-permute-start | bytes 245768 | tf_op jit(solution)/shard_map/ppermute | solution.py:373
  107.4 6.8 %shard_map.102 = (f32[2,448,384]{2,1,0:T(8,128)}, bf16[2,3,448,160]{3,2,1,0:T(8,128)(2,1)}) custom-call(s32[3]{0:T(128)} %pad_add_fusion.at_ref.core_ref, bf16[2,448,256]{2,1,0:T(8,128)(2,1)} %get-tuple-element.57.refs_0_, bf16[2,448,256]{2,1,0:T(8,128)(2,1)} %get-tuple-element.58.refs_1_, bf16[2,448,1024]{2,1,0:T(8,128)(2,1)} %get-tuple-element.59.refs_2_, ...), custom_call_target="tpu_custom_call" | custom-call | flops 722534400 | bytes 12582912 | tf_op jit(solution)/shard_map/pallas_call | solution.py:238
  114.9 1.9 %shard_map.103 = (bf16[2,160,128]{2,1,0:T(8,128)(2,1)}, bf16[2,160,128]{2,1,0:T(8,128)(2,1)}, bf16[2,160,128]{2,1,0:T(8,128)(2,1)}, bf16[2,160,128]{2,1,0:T(8,128)(2,1)}) custom-call(s32[3]{0:T(128)} %pad_add_fusion.at_ref.core_ref, bf16[4,2,160,128]{3,2,1,0:T(8,128)(2,1)} %copy-done.6, bf16[2,160,128]{2,1,0:T(8,128)(2,1)} %copy-done.10, ...), custom_call_target="tpu_custom_call" | custom-call | tf_op jit(solution)/shard_map/pallas_call | solution.py:377
  116.9 2.2 %collective-permute-start.16 = (bf16[2,160,128]{2,1,0:T(8,128)(2,1)}, bf16[2,160,128]{2,1,0:T(8,128)(2,1)S(1)}, u32[]{:S(2)}, u32[]{:S(2)}) collective-permute-start(bf16[2,160,128]{2,1,0:T(8,128)(2,1)} %get-tuple-element.70), channel_id=1, source_target_pairs={{0,6},{2,0},{4,2},{6,4},{1,7},{3,1},{5,3},{7,5},{8,14},{10,8},{12,... | collective-permute-start | bytes 245768 | tf_op jit(solution)/shard_map/ppermute | solution.py:384
  120.2 1.8 %collective-permute-done.16.refs_2_ = bf16[2,160,128]{2,1,0:T(8,128)(2,1)S(1)} collective-permute-done((bf16[2,160,128]{2,1,0:T(8,128)(2,1)}, bf16[2,160,128]{2,1,0:T(8,128)(2,1)S(1)}, u32[]{:S(2)}, u32[]{:S(2)}) %collective-permute-start.16) | collective-permute-done | bytes 81952 | tf_op jit(solution)/shard_map/ppermute | solution.py:384
  122.0 4.4 %collective-permute-done.17.refs_3_ = bf16[2,160,128]{2,1,0:T(8,128)(2,1)S(1)} collective-permute-done((bf16[2,160,128]{2,1,0:T(8,128)(2,1)}, bf16[2,160,128]{2,1,0:T(8,128)(2,1)S(1)}, u32[]{:S(2)}, u32[]{:S(2)}) %collective-permute-start.17) | collective-permute-done | bytes 81952 | tf_op jit(solution)/shard_map/ppermute | solution.py:384
  126.4 1.6 copy-done.1
  131.7 1.8 shard_map.104.mine_ref
  133.5 1.8 shard_map.106.mine_ref
  136.0 1.7 shard_map.108
  137.7 2.2 %collective-permute-start.23 = (bf16[448,256]{1,0:T(8,128)(2,1)S(1)}, bf16[448,256]{1,0:T(8,128)(2,1)S(1)}, u32[]{:S(2)}, u32[]{:S(2)}) collective-permute-start(bf16[448,256]{1,0:T(8,128)(2,1)S(1)} %get-tuple-element.81), channel_id=1, source_target_pairs={{0,4},{2,6},{4,0},{6,2},{1,5},{3,7},{5,1},{7,3},{8,12},{10,14},{12... | collective-permute-start | bytes 688136 | tf_op jit(solution)/shard_map/ppermute | solution.py:437
  140.0 1.7 shard_map.105
  141.6 2.5 %collective-permute-start.25 = (bf16[448,256]{1,0:T(8,128)(2,1)S(1)}, bf16[448,256]{1,0:T(8,128)(2,1)S(1)}, u32[]{:S(2)}, u32[]{:S(2)}) collective-permute-start(bf16[448,256]{1,0:T(8,128)(2,1)S(1)} %get-tuple-element.83), channel_id=1, source_target_pairs={{0,6},{2,0},{4,2},{6,4},{1,7},{3,1},{5,3},{7,5},{8,14},{10,8},{12,... | collective-permute-start | bytes 688136 | tf_op jit(solution)/shard_map/ppermute | solution.py:437
  144.1 1.7 shard_map.109
  147.1 1.7 shard_map.107
  148.8 2.9 %collective-permute-start.26 = (bf16[448,256]{1,0:T(8,128)(2,1)S(1)}, bf16[448,256]{1,0:T(8,128)(2,1)S(1)}, u32[]{:S(2)}, u32[]{:S(2)}) collective-permute-start(bf16[448,256]{1,0:T(8,128)(2,1)S(1)} %get-tuple-element.84), channel_id=1, source_target_pairs={{0,6},{2,0},{4,2},{6,4},{1,7},{3,1},{5,3},{7,5},{8,14},{10,8},{12,... | collective-permute-start | bytes 688136 | tf_op jit(solution)/shard_map/ppermute | solution.py:437
  151.7 6.1 %collective-permute-done.23.refs_4_ = bf16[448,256]{1,0:T(8,128)(2,1)S(1)} collective-permute-done((bf16[448,256]{1,0:T(8,128)(2,1)S(1)}, bf16[448,256]{1,0:T(8,128)(2,1)S(1)}, u32[]{:S(2)}, u32[]{:S(2)}) %collective-permute-start.23) | collective-permute-done | bytes 229408 | tf_op jit(solution)/shard_map/ppermute | solution.py:437
  157.8 5.1 %collective-permute-done.22.refs_3_ = bf16[448,256]{1,0:T(8,128)(2,1)S(1)} collective-permute-done((bf16[448,256]{1,0:T(8,128)(2,1)S(1)}, bf16[448,256]{1,0:T(8,128)(2,1)S(1)}, u32[]{:S(2)}, u32[]{:S(2)}) %collective-permute-start.22) | collective-permute-done | bytes 229408 | tf_op jit(solution)/shard_map/ppermute | solution.py:437
  162.9 13.8 %collective-permute-done.24.refs_5_ = bf16[448,256]{1,0:T(8,128)(2,1)S(1)} collective-permute-done((bf16[448,256]{1,0:T(8,128)(2,1)S(1)}, bf16[448,256]{1,0:T(8,128)(2,1)S(1)}, u32[]{:S(2)}, u32[]{:S(2)}) %collective-permute-start.24) | collective-permute-done | bytes 229408 | tf_op jit(solution)/shard_map/ppermute | solution.py:437
  176.7 1.8 %shard_map.110 = bf16[3584,256]{1,0:T(8,128)(2,1)} custom-call(s32[3]{0:T(128)S(1)} %copy-done.5, bf16[448,256]{1,0:T(8,128)(2,1)S(1)} %get-tuple-element.77.refs_0_, bf16[448,256]{1,0:T(8,128)(2,1)S(1)} %get-tuple-element.78.refs_1_, bf16[448,256]{1,0:T(8,128)(2,1)S(1)} %collective-permute-done.21.refs_2_, ...), custom_call_target="tpu_custom_call" | custom-call | bytes 12582912 | tf_op jit(solution)/shard_map/pallas_call | solution.py:238
  (79 shorter events, 23.0 us)
Async XLA Ops:
  1.0 12.4 %collective-permute-start.2 = (bf16[512,256]{1,0:T(8,128)(2,1)S(1)}, bf16[512,256]{1,0:T(8,128)(2,1)S(1)}, u32[]{:S(2)}, u32[]{:S(2)}) collective-permute-start(bf16[512,256]{1,0:T(8,128)(2,1)S(1)} %constant_dynamic-slice_fusion), channel_id=1, source_target_pairs={{0,2},{2,4},{4,6},{6,0},{1,3},{3,5},{5,7},{7,1},{8,10},{10,12},{12... | collective-permute-start | bytes 786440 | tf_op jit(solution)/shard_map/ppermute | solution.py:296
  4.0 19.7 %collective-permute-start.1 = (bf16[512,256]{1,0:T(8,128)(2,1)S(1)}, bf16[512,256]{1,0:T(8,128)(2,1)S(1)}, u32[]{:S(2)}, u32[]{:S(2)}) collective-permute-start(bf16[512,256]{1,0:T(8,128)(2,1)S(1)} %constant_dynamic-slice_fusion), channel_id=1, source_target_pairs={{0,4},{2,6},{4,0},{6,2},{1,5},{3,7},{5,1},{7,3},{8,12},{10,14},{12... | collective-permute-start | bytes 786440 | tf_op jit(solution)/shard_map/ppermute | solution.py:296
  6.6 17.1 %collective-permute-start = (bf16[512,256]{1,0:T(8,128)(2,1)S(1)}, bf16[512,256]{1,0:T(8,128)(2,1)S(1)}, u32[]{:S(2)}, u32[]{:S(2)}) collective-permute-start(bf16[512,256]{1,0:T(8,128)(2,1)S(1)} %constant_dynamic-slice_fusion), channel_id=1, source_target_pairs={{0,6},{2,0},{4,2},{6,4},{1,7},{3,1},{5,3},{7,5},{8,14},{10,8},{12,... | collective-permute-start | bytes 786440 | tf_op jit(solution)/shard_map/ppermute | solution.py:296
  23.8 47.6 %copy-start.7 = (bf16[3,512,256]{2,1,0:T(8,128)(2,1)}, bf16[3,512,256]{2,1,0:T(8,128)(2,1)S(1)}, u32[]{:S(2)}) copy-start(bf16[3,512,256]{2,1,0:T(8,128)(2,1)S(1)} %pad_maximum_fusion.refs_13_) | copy-start | bytes 2359300
  23.9 18.7 %collective-permute-start.3 = (bf16[896,256]{1,0:T(8,128)(2,1)S(1)}, bf16[896,256]{1,0:T(8,128)(2,1)S(1)}, u32[]{:S(2)}, u32[]{:S(2)}) collective-permute-start(bf16[896,256]{1,0:T(8,128)(2,1)S(1)} %get-tuple-element.45), channel_id=1, source_target_pairs={{0,2},{2,4},{4,6},{6,0},{1,3},{3,5},{5,7},{7,1},{8,10},{10,12},{12... | collective-permute-start | bytes 1376264 | tf_op jit(solution)/shard_map/ppermute | solution.py:303
  30.0 32.2 %collective-permute-start.8 = (bf16[3,512,256]{2,1,0:T(8,128)(2,1)S(1)}, bf16[3,512,256]{2,1,0:T(8,128)(2,1)S(1)}, u32[]{:S(2)}, u32[]{:S(2)}) collective-permute-start(bf16[3,512,256]{2,1,0:T(8,128)(2,1)S(1)} %pad_maximum_fusion.refs_13_), channel_id=1, source_target_pairs={{0,24},{8,16},{16,8},{24,0},{1,25},{9,17},{17,9},{25,1},{2,26},{10... | collective-permute-start | bytes 2359304 | tf_op jit(solution)/shard_map/ppermute | solution.py:299
  32.4 34.5 %collective-permute-start.7 = (bf16[3,512,256]{2,1,0:T(8,128)(2,1)S(1)}, bf16[3,512,256]{2,1,0:T(8,128)(2,1)S(1)}, u32[]{:S(2)}, u32[]{:S(2)}) collective-permute-start(bf16[3,512,256]{2,1,0:T(8,128)(2,1)S(1)} %pad_maximum_fusion.refs_13_), channel_id=1, source_target_pairs={{0,16},{8,24},{16,0},{24,8},{1,17},{9,25},{17,1},{25,9},{2,18},{10... | collective-permute-start | bytes 2359304 | tf_op jit(solution)/shard_map/ppermute | solution.py:299
  32.9 34.1 %collective-permute-start.6 = (bf16[3,512,256]{2,1,0:T(8,128)(2,1)S(1)}, bf16[3,512,256]{2,1,0:T(8,128)(2,1)S(1)}, u32[]{:S(2)}, u32[]{:S(2)}) collective-permute-start(bf16[3,512,256]{2,1,0:T(8,128)(2,1)S(1)} %pad_maximum_fusion.refs_13_), channel_id=1, source_target_pairs={{0,8},{8,0},{16,24},{24,16},{1,9},{9,1},{17,25},{25,17},{2,10},{10... | collective-permute-start | bytes 2359304 | tf_op jit(solution)/shard_map/ppermute | solution.py:299
  33.5 27.1 %collective-permute-start.4 = (bf16[896,256]{1,0:T(8,128)(2,1)S(1)}, bf16[896,256]{1,0:T(8,128)(2,1)}, u32[]{:S(2)}, u32[]{:S(2)}) collective-permute-start(bf16[896,256]{1,0:T(8,128)(2,1)S(1)} %get-tuple-element.46), channel_id=1, source_target_pairs={{0,4},{2,6},{4,0},{6,2},{1,5},{3,7},{5,1},{7,3},{8,12},{10,14},{12... | collective-permute-start | bytes 1376264 | tf_op jit(solution)/shard_map/ppermute | solution.py:303
  42.6 28.9 %copy-start.15 = (bf16[896,256]{1,0:T(8,128)(2,1)}, bf16[896,256]{1,0:T(8,128)(2,1)S(1)}, u32[]{:S(2)}) copy-start(bf16[896,256]{1,0:T(8,128)(2,1)S(1)} %collective-permute-done.3.refs_1_) | copy-start | bytes 1376260
  42.6 19.6 %collective-permute-start.5 = (bf16[896,256]{1,0:T(8,128)(2,1)S(1)}, bf16[896,256]{1,0:T(8,128)(2,1)}, u32[]{:S(2)}, u32[]{:S(2)}) collective-permute-start(bf16[896,256]{1,0:T(8,128)(2,1)S(1)} %get-tuple-element.47), channel_id=1, source_target_pairs={{0,6},{2,0},{4,2},{6,4},{1,7},{3,1},{5,3},{7,5},{8,14},{10,8},{12,... | collective-permute-start | bytes 1376264 | tf_op jit(solution)/shard_map/ppermute | solution.py:303
  60.6 8.5 %collective-permute-start.9 = (bf16[896,256]{1,0:T(8,128)(2,1)S(1)}, bf16[896,256]{1,0:T(8,128)(2,1)}, u32[]{:S(2)}, u32[]{:S(2)}) collective-permute-start(bf16[896,256]{1,0:T(8,128)(2,1)S(1)} %get-tuple-element.52), channel_id=1, source_target_pairs={{0,1},{1,0},{2,3},{3,2},{4,5},{5,4},{6,7},{7,6},{8,9},{9,8},{10,11... | collective-permute-start | bytes 1376264 | tf_op jit(solution)/shard_map/ppermute | solution.py:306
  68.0 2.6 %collective-permute-start.10 = (bf16[896,256]{1,0:T(8,128)(2,1)S(1)}, bf16[896,256]{1,0:T(8,128)(2,1)}, u32[]{:S(2)}, u32[]{:S(2)}) collective-permute-start(bf16[896,256]{1,0:T(8,128)(2,1)S(1)} %collective-permute-done.3.refs_1_), channel_id=1, source_target_pairs={{0,1},{1,0},{2,3},{3,2},{4,5},{5,4},{6,7},{7,6},{8,9},{9,8},{10,11... | collective-permute-start | bytes 1376264 | tf_op jit(solution)/shard_map/ppermute | solution.py:306
  68.0 2.8 %collective-permute-start.11 = (bf16[896,256]{1,0:T(8,128)(2,1)}, bf16[896,256]{1,0:T(8,128)(2,1)}, u32[]{:S(2)}, u32[]{:S(2)}) collective-permute-start(bf16[896,256]{1,0:T(8,128)(2,1)} %collective-permute-done.4.refs_2_), channel_id=1, source_target_pairs={{0,1},{1,0},{2,3},{3,2},{4,5},{5,4},{6,7},{7,6},{8,9},{9,8},{10,11... | collective-permute-start | bytes 1376264 | tf_op jit(solution)/shard_map/ppermute | solution.py:306
  68.5 3.0 %collective-permute-start.12 = (bf16[896,256]{1,0:T(8,128)(2,1)}, bf16[896,256]{1,0:T(8,128)(2,1)}, u32[]{:S(2)}, u32[]{:S(2)}) collective-permute-start(bf16[896,256]{1,0:T(8,128)(2,1)} %collective-permute-done.5.refs_3_), channel_id=1, source_target_pairs={{0,1},{1,0},{2,3},{3,2},{4,5},{5,4},{6,7},{7,6},{8,9},{9,8},{10,11... | collective-permute-start | bytes 1376264 | tf_op jit(solution)/shard_map/ppermute | solution.py:306
  85.9 17.9 %all-to-all-start = ((bf16[4,2,160,128]{3,2,1,0:T(8,128)(2,1)}), bf16[4,2,160,128]{3,2,1,0:T(8,128)(2,1)S(1)}, u32[]{:S(2)}, u32[]{:S(2)}) async-start(bf16[4,2,160,128]{3,2,1,0:T(8,128)(2,1)} %bitcast.40), calls=%async_computation | async-start | bytes 655360 | tf_op jit(solution)/shard_map/all_to_all | solution.py:369
  103.8 10.4 %collective-permute-start.15 = (bf16[2,160,128]{2,1,0:T(8,128)(2,1)S(1)}, bf16[2,160,128]{2,1,0:T(8,128)(2,1)S(1)}, u32[]{:S(2)}, u32[]{:S(2)}) collective-permute-start(bf16[2,160,128]{2,1,0:T(8,128)(2,1)S(1)} %reduce_sum.12), channel_id=1, source_target_pairs={{0,24},{8,16},{16,8},{24,0},{1,25},{9,17},{17,9},{25,1},{2,26},{10... | collective-permute-start | bytes 245768 | tf_op jit(solution)/shard_map/ppermute | solution.py:373
  106.3 7.9 %collective-permute-start.14 = (bf16[2,160,128]{2,1,0:T(8,128)(2,1)S(1)}, bf16[2,160,128]{2,1,0:T(8,128)(2,1)S(1)}, u32[]{:S(2)}, u32[]{:S(2)}) collective-permute-start(bf16[2,160,128]{2,1,0:T(8,128)(2,1)S(1)} %reduce_sum.12), channel_id=1, source_target_pairs={{0,16},{8,24},{16,0},{24,8},{1,17},{9,25},{17,1},{25,9},{2,18},{10... | collective-permute-start | bytes 245768 | tf_op jit(solution)/shard_map/ppermute | solution.py:373
  106.8 7.4 %collective-permute-start.13 = (bf16[2,160,128]{2,1,0:T(8,128)(2,1)S(1)}, bf16[2,160,128]{2,1,0:T(8,128)(2,1)S(1)}, u32[]{:S(2)}, u32[]{:S(2)}) collective-permute-start(bf16[2,160,128]{2,1,0:T(8,128)(2,1)S(1)} %reduce_sum.12), channel_id=1, source_target_pairs={{0,8},{8,0},{16,24},{24,16},{1,9},{9,1},{17,25},{25,17},{2,10},{10... | collective-permute-start | bytes 245768 | tf_op jit(solution)/shard_map/ppermute | solution.py:373
  107.4 19.0 %copy-start = (f32[2,448,640]{2,1,0:T(8,128)S(1)}, f32[2,448,640]{2,1,0:T(8,128)}, u32[]{:S(2)}) copy-start(f32[2,448,640]{2,1,0:T(8,128)} %get-tuple-element.73.refs_5_) | copy-start | bytes 6881284
  107.4 19.0 %copy-start.5 = (s32[3]{0:T(128)S(1)}, s32[3]{0:T(128)}, u32[]{:S(2)}) copy-start(s32[3]{0:T(128)} %pad_add_fusion.at_ref.core_ref) | copy-start | bytes 40
  116.9 5.2 %collective-permute-start.16 = (bf16[2,160,128]{2,1,0:T(8,128)(2,1)}, bf16[2,160,128]{2,1,0:T(8,128)(2,1)S(1)}, u32[]{:S(2)}, u32[]{:S(2)}) collective-permute-start(bf16[2,160,128]{2,1,0:T(8,128)(2,1)} %get-tuple-element.70), channel_id=1, source_target_pairs={{0,6},{2,0},{4,2},{6,4},{1,7},{3,1},{5,3},{7,5},{8,14},{10,8},{12,... | collective-permute-start | bytes 245768 | tf_op jit(solution)/shard_map/ppermute | solution.py:384
  119.1 7.3 %collective-permute-start.17 = (bf16[2,160,128]{2,1,0:T(8,128)(2,1)}, bf16[2,160,128]{2,1,0:T(8,128)(2,1)S(1)}, u32[]{:S(2)}, u32[]{:S(2)}) collective-permute-start(bf16[2,160,128]{2,1,0:T(8,128)(2,1)} %get-tuple-element.71), channel_id=1, source_target_pairs={{0,4},{2,6},{4,0},{6,2},{1,5},{3,7},{5,1},{7,3},{8,12},{10,14},{12... | collective-permute-start | bytes 245768 | tf_op jit(solution)/shard_map/ppermute | solution.py:384
  119.1 7.3 %collective-permute-start.18 = (bf16[2,160,128]{2,1,0:T(8,128)(2,1)}, bf16[2,160,128]{2,1,0:T(8,128)(2,1)S(1)}, u32[]{:S(2)}, u32[]{:S(2)}) collective-permute-start(bf16[2,160,128]{2,1,0:T(8,128)(2,1)} %get-tuple-element.72), channel_id=1, source_target_pairs={{0,2},{2,4},{4,6},{6,0},{1,3},{3,5},{5,7},{7,1},{8,10},{10,12},{12... | collective-permute-start | bytes 245768 | tf_op jit(solution)/shard_map/ppermute | solution.py:384
  133.4 2.5 %collective-permute-start.19 = (bf16[448,1024]{1,0:T(8,128)(2,1)S(1)}, bf16[448,1024]{1,0:T(8,128)(2,1)S(1)}, u32[]{:S(2)}, u32[]{:S(2)}) collective-permute-start(bf16[448,1024]{1,0:T(8,128)(2,1)S(1)} %shard_map.104.mine_ref), channel_id=1, source_target_pairs={{0,1},{1,0},{2,3},{3,2},{4,5},{5,4},{6,7},{7,6},{8,9},{9,8},{10,11... | collective-permute-start | bytes 2752520 | tf_op jit(solution)/shard_map/ppermute | solution.py:430
  135.3 8.8 %collective-permute-start.20 = (bf16[448,1024]{1,0:T(8,128)(2,1)S(1)}, bf16[448,1024]{1,0:T(8,128)(2,1)S(1)}, u32[]{:S(2)}, u32[]{:S(2)}) collective-permute-start(bf16[448,1024]{1,0:T(8,128)(2,1)S(1)} %shard_map.106.mine_ref), channel_id=1, source_target_pairs={{0,1},{1,0},{2,3},{3,2},{4,5},{5,4},{6,7},{7,6},{8,9},{9,8},{10,11... | collective-permute-start | bytes 2752520 | tf_op jit(solution)/shard_map/ppermute | solution.py:430
  137.7 11.1 %collective-permute-start.21 = (bf16[448,256]{1,0:T(8,128)(2,1)S(1)}, bf16[448,256]{1,0:T(8,128)(2,1)S(1)}, u32[]{:S(2)}, u32[]{:S(2)}) collective-permute-start(bf16[448,256]{1,0:T(8,128)(2,1)S(1)} %get-tuple-element.79), channel_id=1, source_target_pairs={{0,2},{2,4},{4,6},{6,0},{1,3},{3,5},{5,7},{7,1},{8,10},{10,12},{12... | collective-permute-start | bytes 688136 | tf_op jit(solution)/shard_map/ppermute | solution.py:437
  137.7 20.1 %collective-permute-start.23 = (bf16[448,256]{1,0:T(8,128)(2,1)S(1)}, bf16[448,256]{1,0:T(8,128)(2,1)S(1)}, u32[]{:S(2)}, u32[]{:S(2)}) collective-permute-start(bf16[448,256]{1,0:T(8,128)(2,1)S(1)} %get-tuple-element.81), channel_id=1, source_target_pairs={{0,4},{2,6},{4,0},{6,2},{1,5},{3,7},{5,1},{7,3},{8,12},{10,14},{12... | collective-permute-start | bytes 688136 | tf_op jit(solution)/shard_map/ppermute | solution.py:437
  141.6 16.2 %collective-permute-start.25 = (bf16[448,256]{1,0:T(8,128)(2,1)S(1)}, bf16[448,256]{1,0:T(8,128)(2,1)S(1)}, u32[]{:S(2)}, u32[]{:S(2)}) collective-permute-start(bf16[448,256]{1,0:T(8,128)(2,1)S(1)} %get-tuple-element.83), channel_id=1, source_target_pairs={{0,6},{2,0},{4,2},{6,4},{1,7},{3,1},{5,3},{7,5},{8,14},{10,8},{12,... | collective-permute-start | bytes 688136 | tf_op jit(solution)/shard_map/ppermute | solution.py:437
  145.8 17.1 %collective-permute-start.22 = (bf16[448,256]{1,0:T(8,128)(2,1)S(1)}, bf16[448,256]{1,0:T(8,128)(2,1)S(1)}, u32[]{:S(2)}, u32[]{:S(2)}) collective-permute-start(bf16[448,256]{1,0:T(8,128)(2,1)S(1)} %get-tuple-element.80), channel_id=1, source_target_pairs={{0,2},{2,4},{4,6},{6,0},{1,3},{3,5},{5,7},{7,1},{8,10},{10,12},{12... | collective-permute-start | bytes 688136 | tf_op jit(solution)/shard_map/ppermute | solution.py:437
  145.9 30.8 %collective-permute-start.24 = (bf16[448,256]{1,0:T(8,128)(2,1)S(1)}, bf16[448,256]{1,0:T(8,128)(2,1)S(1)}, u32[]{:S(2)}, u32[]{:S(2)}) collective-permute-start(bf16[448,256]{1,0:T(8,128)(2,1)S(1)} %get-tuple-element.82), channel_id=1, source_target_pairs={{0,4},{2,6},{4,0},{6,2},{1,5},{3,7},{5,1},{7,3},{8,12},{10,14},{12... | collective-permute-start | bytes 688136 | tf_op jit(solution)/shard_map/ppermute | solution.py:437
  148.8 27.9 %collective-permute-start.26 = (bf16[448,256]{1,0:T(8,128)(2,1)S(1)}, bf16[448,256]{1,0:T(8,128)(2,1)S(1)}, u32[]{:S(2)}, u32[]{:S(2)}) collective-permute-start(bf16[448,256]{1,0:T(8,128)(2,1)S(1)} %get-tuple-element.84), channel_id=1, source_target_pairs={{0,6},{2,0},{4,2},{6,4},{1,7},{3,1},{5,3},{7,5},{8,14},{10,8},{12,... | collective-permute-start | bytes 688136 | tf_op jit(solution)/shard_map/ppermute | solution.py:437
  (14 other events, 53.8 us)

commit v12 on v9

--- a/solution.py
+++ b/solution.py
@@ -289,7 +289,7 @@
     blocks = tokens.reshape(layers, 2 * rows, width)
     sent = [lax.dynamic_index_in_dim(blocks, lax.rem(layer + d, layers), 0, False) for d in range(layers)]
     stack = jnp.stack([lax.ppermute(value_part, "z", turn(-d)) for d in range(1, layers)])
-    stack, sent = lax.optimization_barrier((stack, sent))
+    stack, sent, at = lax.optimization_barrier((stack, sent, at))
     if slabs == 4:
         weights = [stack] + [lax.ppermute(stack, "seq", flip(m)) for m in range(1, slabs)]
     else:
@@ -363,12 +363,10 @@
 
     own = total.reshape(layers, per_group, PACKED, HEAD_DIM)
     line = lax.all_to_all(own, "z", split_axis=0, concat_axis=0, tiled=True)
-    locals_ = [local(0, heads // 2)]
+    locals_ = [local(0, 3 * heads // 4)]
     line, locals_ = lax.optimization_barrier((line, locals_))
     slab_total = jnp.sum(line.astype(F32), axis=0).astype(BF16)
     totals = [lax.ppermute(slab_total, "seq", flip(m)) for m in range(1, slabs)]
-    third = local(heads // 2, heads // 4)
-    totals, third = lax.optimization_barrier((totals, third))
     piece_shape = (per_group, PACKED, HEAD_DIM)
     prefix = pl.pallas_call(
         prefix_kernel,
@@ -378,7 +376,7 @@
         scratch_shapes=[pltpu.VMEM((layers,) + piece_shape, BF16)],
     )(at, line, *totals)
     prefix = [prefix[0]] + [lax.ppermute(prefix[d], "z", turn(-d)) for d in range(1, layers)]
-    locals_ = locals_ + [third, local(3 * heads // 4, heads // 4)]
+    locals_ = locals_ + [local(3 * heads // 4, heads // 4)]
 
     def hidden(chunk):
         some = rows // 2

time: 179 us -> 179 us (level)
  Pallas kernels: 47.9 us -> 44.6 us
  starting transfers between devices: 41.5 us -> 44.2 us
    ppermute x3, waiting for transfers between devices: 0.01 us -> 3.89 us  [per_device(): totals = [lax.ppermute(slab_total, 'seq', flip(m)) for m in range(1, slabs)]]
    pallas_call x11 -> x10, Pallas kernels: 46 us -> 42.7 us  [call(): pl.pallas_call(kernel, grid_spec=pltpu.PrefetchScalarGridSpec(num_scalar_...]
    all_to_all x1, waiting for transfers between devices: 2.61 us -> 0.03 us  [per_device(): line = lax.all_to_all(own, 'z', split_axis=0, concat_axis=0, tiled=True)]
    ppermute x3, starting transfers between devices: 2.35 us -> 4.81 us  [per_device(): lax.ppermute(prefix[d], 'z', turn(-d))]
    unnamed x42 -> x48, local copies, waits for them, and re-layouts: 6.38 us -> 5.94 us
  transfers between devices with their start and end apart: 28 -> 28, of which waited for: 16 -> 17; matrix products, arithmetic and copies ran while one was open for 1% -> 1% of each run, Pallas kernels for 16% -> 14%
where the time goes in v12:
time: 179 us; the launch traced here: 176 us
  waiting for transfers between devices  77.8 us (43%)
  Pallas kernels  44.6 us (25%)
  starting transfers between devices  44.2 us (25%)
  local copies, waits for them, and re-layouts  8.48 us (5%)
    pallas_call x10, Pallas kernels, call(): pl.pallas_call(kernel, grid_spec=pltpu.PrefetchScalarGridSpec(num_scalar_...  42.7 us
    ppermute x3, waiting for transfers between devices, per_device(): lax.ppermute(sent[d], 'z', turn(d))  27 us
    ppermute x6, waiting for transfers between devices, per_device(): pieces[d, chunk] = lax.ppermute(piece, 'z', turn(d)) if d else piece  25.1 us
    ppermute x3, waiting for transfers between devices, per_device(): lax.ppermute(value_part, 'z', turn(-d))  13.6 us
    ppermute x6, starting transfers between devices, per_device(): pieces[d, chunk] = lax.ppermute(piece, 'z', turn(d)) if d else piece  8.97 us
    ppermute x3, starting transfers between devices, per_device(): lax.ppermute(sent[d], 'z', turn(d))  7.73 us
    all_to_all x1, starting transfers between devices, per_device(): line = lax.all_to_all(own, 'z', split_axis=0, concat_axis=0, tiled=True)  7.44 us
    ppermute x3, starting transfers between devices, per_device(): lax.ppermute(value_part, 'z', turn(-d))  7.01 us
  transfers between devices with their start and end apart: 28, of which 17 were waited for; matrix products, arithmetic and copies ran while one was open for 1% of the time, Pallas kernels for 14%

profile of v12, /device:TPU:0, one launch (start us, length us, event | category | flops | bytes accessed | tf_op | source)
XLA Modules:
  0.0 176.2 jit_solution(16348307417245958309)
XLA Ops:
  1.0 3.1 %collective-permute-start.2 = (bf16[512,256]{1,0:T(8,128)(2,1)S(1)}, bf16[512,256]{1,0:T(8,128)(2,1)S(1)}, u32[]{:S(2)}, u32[]{:S(2)}) collective-permute-start(bf16[512,256]{1,0:T(8,128)(2,1)S(1)} %constant_dynamic-slice_fusion.1), channel_id=1, source_target_pairs={{0,2},{2,4},{4,6},{6,0},{1,3},{3,5},{5,7},{7,1},{8,10},{10,12},{12... | collective-permute-start | bytes 786440 | tf_op jit(solution)/shard_map/ppermute | solution.py:291
  4.0 2.6 %collective-permute-start.1 = (bf16[512,256]{1,0:T(8,128)(2,1)S(1)}, bf16[512,256]{1,0:T(8,128)(2,1)S(1)}, u32[]{:S(2)}, u32[]{:S(2)}) collective-permute-start(bf16[512,256]{1,0:T(8,128)(2,1)S(1)} %constant_dynamic-slice_fusion.1), channel_id=1, source_target_pairs={{0,4},{2,6},{4,0},{6,2},{1,5},{3,7},{5,1},{7,3},{8,12},{10,14},{12... | collective-permute-start | bytes 786440 | tf_op jit(solution)/shard_map/ppermute | solution.py:291
  10.2 3.2 %collective-permute-done.2 = bf16[512,256]{1,0:T(8,128)(2,1)S(1)} collective-permute-done((bf16[512,256]{1,0:T(8,128)(2,1)S(1)}, bf16[512,256]{1,0:T(8,128)(2,1)S(1)}, u32[]{:S(2)}, u32[]{:S(2)}) %collective-permute-start.2) | collective-permute-done | bytes 262176 | tf_op jit(solution)/shard_map/ppermute | solution.py:291
  13.3 10.4 %collective-permute-done.1 = bf16[512,256]{1,0:T(8,128)(2,1)S(1)} collective-permute-done((bf16[512,256]{1,0:T(8,128)(2,1)S(1)}, bf16[512,256]{1,0:T(8,128)(2,1)S(1)}, u32[]{:S(2)}, u32[]{:S(2)}) %collective-permute-start.1) | collective-permute-done | bytes 262176 | tf_op jit(solution)/shard_map/ppermute | solution.py:291
  23.9 6.1 %collective-permute-start.3 = (bf16[896,256]{1,0:T(8,128)(2,1)S(1)}, bf16[896,256]{1,0:T(8,128)(2,1)S(1)}, u32[]{:S(2)}, u32[]{:S(2)}) collective-permute-start(bf16[896,256]{1,0:T(8,128)(2,1)S(1)} %get-tuple-element.42), channel_id=1, source_target_pairs={{0,2},{2,4},{4,6},{6,0},{1,3},{3,5},{5,7},{7,1},{8,10},{10,12},{12... | collective-permute-start | bytes 1376264 | tf_op jit(solution)/shard_map/ppermute | solution.py:298
  30.0 2.4 %collective-permute-start.8 = (bf16[3,512,256]{2,1,0:T(8,128)(2,1)S(1)}, bf16[3,512,256]{2,1,0:T(8,128)(2,1)S(1)}, u32[]{:S(2)}, u32[]{:S(2)}) collective-permute-start(bf16[3,512,256]{2,1,0:T(8,128)(2,1)S(1)} %pad_maximum_fusion.refs_13_), channel_id=1, source_target_pairs={{0,24},{8,16},{16,8},{24,0},{1,25},{9,17},{17,9},{25,1},{2,26},{10... | collective-permute-start | bytes 2359304 | tf_op jit(solution)/shard_map/ppermute | solution.py:294
  35.1 7.5 %collective-permute-done.3.refs_1_ = bf16[896,256]{1,0:T(8,128)(2,1)S(1)} collective-permute-done((bf16[896,256]{1,0:T(8,128)(2,1)S(1)}, bf16[896,256]{1,0:T(8,128)(2,1)S(1)}, u32[]{:S(2)}, u32[]{:S(2)}) %collective-permute-start.3) | collective-permute-done | bytes 458784 | tf_op jit(solution)/shard_map/ppermute | solution.py:298
  42.6 17.9 %collective-permute-done.4.refs_2_ = bf16[896,256]{1,0:T(8,128)(2,1)S(1)} collective-permute-done((bf16[896,256]{1,0:T(8,128)(2,1)S(1)}, bf16[896,256]{1,0:T(8,128)(2,1)S(1)}, u32[]{:S(2)}, u32[]{:S(2)}) %collective-permute-start.4) | collective-permute-done | bytes 458784 | tf_op jit(solution)/shard_map/ppermute | solution.py:298
  62.1 4.8 %collective-permute-done.7.refs_15_ = bf16[3,512,256]{2,1,0:T(8,128)(2,1)S(1)} collective-permute-done((bf16[3,512,256]{2,1,0:T(8,128)(2,1)S(1)}, bf16[3,512,256]{2,1,0:T(8,128)(2,1)S(1)}, u32[]{:S(2)}, u32[]{:S(2)}) %collective-permute-start.7) | collective-permute-done | bytes 786464 | tf_op jit(solution)/shard_map/ppermute | solution.py:294
  71.0 14.2 %shard_map.100 = (bf16[2,448,256]{2,1,0:T(8,128)(2,1)}, bf16[2,448,256]{2,1,0:T(8,128)(2,1)}, bf16[2,448,1024]{2,1,0:T(8,128)(2,1)}, bf16[8,160,128]{2,1,0:T(8,128)(2,1)}, bf16[8,160,128]{2,1,0:T(8,128)(2,1)}) custom-call(s32[3]{0:T(128)} %pad_add_fusion.at_ref.core_ref, bf16[4,896,256]{2,1,0:T(8,128)(2,1)} %bitcast.39, bf16[896,256]{1,0:T(8,128)(2,1)} %copy-done.16, ...), custom_call_target="tpu_custom_call" | custom-call | flops 5637144576 | bytes 12582912 | tf_op jit(solution)/shard_map/pallas_call | solution.py:234
  85.2 7.4 %all-to-all-start = ((bf16[4,2,160,128]{3,2,1,0:T(8,128)(2,1)}), bf16[4,2,160,128]{3,2,1,0:T(8,128)(2,1)S(1)}, u32[]{:S(2)}, u32[]{:S(2)}) async-start(bf16[4,2,160,128]{3,2,1,0:T(8,128)(2,1)} %bitcast.40), calls=%async_computation | async-start | bytes 655360 | tf_op jit(solution)/shard_map/all_to_all | solution.py:365
  92.6 10.6 %shard_map.101 = (f32[2,448,768]{2,1,0:T(8,128)}, bf16[2,6,448,160]{3,2,1,0:T(8,128)(2,1)}) custom-call(s32[3]{0:T(128)} %pad_add_fusion.at_ref.core_ref, bf16[2,448,256]{2,1,0:T(8,128)(2,1)} %get-tuple-element.54.refs_0_, bf16[2,448,256]{2,1,0:T(8,128)(2,1)} %get-tuple-element.55.refs_1_, bf16[2,448,1024]{2,1,0:T(8,128)(2,1)} %get-tuple-element.56.refs_2_, ...), custom_call_target="tpu_custom_call" | custom-call | flops 1445068800 | bytes 12582912 | tf_op jit(solution)/shard_map/pallas_call | solution.py:234
  103.3 2.5 %collective-permute-start.15 = (bf16[2,160,128]{2,1,0:T(8,128)(2,1)S(1)}, bf16[2,160,128]{2,1,0:T(8,128)(2,1)S(1)}, u32[]{:S(2)}, u32[]{:S(2)}) collective-permute-start(bf16[2,160,128]{2,1,0:T(8,128)(2,1)S(1)} %reduce_sum.12), channel_id=1, source_target_pairs={{0,24},{8,16},{16,8},{24,0},{1,25},{9,17},{17,9},{25,1},{2,26},{10... | collective-permute-start | bytes 245768 | tf_op jit(solution)/shard_map/ppermute | solution.py:369
  106.9 1.9 %collective-permute-done.15.refs_2_ = bf16[2,160,128]{2,1,0:T(8,128)(2,1)S(1)} collective-permute-done((bf16[2,160,128]{2,1,0:T(8,128)(2,1)S(1)}, bf16[2,160,128]{2,1,0:T(8,128)(2,1)S(1)}, u32[]{:S(2)}, u32[]{:S(2)}) %collective-permute-start.15) | collective-permute-done | bytes 81952 | tf_op jit(solution)/shard_map/ppermute | solution.py:369
  111.7 1.9 %shard_map.102 = (bf16[2,160,128]{2,1,0:T(8,128)(2,1)}, bf16[2,160,128]{2,1,0:T(8,128)(2,1)}, bf16[2,160,128]{2,1,0:T(8,128)(2,1)}, bf16[2,160,128]{2,1,0:T(8,128)(2,1)}) custom-call(s32[3]{0:T(128)} %pad_add_fusion.at_ref.core_ref, bf16[4,2,160,128]{3,2,1,0:T(8,128)(2,1)} %copy-done.7, bf16[2,160,128]{2,1,0:T(8,128)(2,1)} %copy-done.11, ...), custom_call_target="tpu_custom_call" | custom-call | tf_op jit(solution)/shard_map/pallas_call | solution.py:371
  113.6 3.7 %collective-permute-start.16 = (bf16[2,160,128]{2,1,0:T(8,128)(2,1)}, bf16[2,160,128]{2,1,0:T(8,128)(2,1)S(1)}, u32[]{:S(2)}, u32[]{:S(2)}) collective-permute-start(bf16[2,160,128]{2,1,0:T(8,128)(2,1)} %get-tuple-element.62), channel_id=1, source_target_pairs={{0,6},{2,0},{4,2},{6,4},{1,7},{3,1},{5,3},{7,5},{8,14},{10,8},{12,... | collective-permute-start | bytes 245768 | tf_op jit(solution)/shard_map/ppermute | solution.py:378
  118.5 5.8 %shard_map.103 = (f32[2,448,256]{2,1,0:T(8,128)}, bf16[2,2,448,160]{3,2,1,0:T(8,128)(2,1)}) custom-call(s32[3]{0:T(128)} %pad_add_fusion.at_ref.core_ref, bf16[2,448,256]{2,1,0:T(8,128)(2,1)} %get-tuple-element.54.refs_0_, bf16[2,448,256]{2,1,0:T(8,128)(2,1)} %get-tuple-element.55.refs_1_, bf16[2,448,1024]{2,1,0:T(8,128)(2,1)} %get-tuple-element.56.refs_2_, ...), custom_call_target="tpu_custom_call" | custom-call | flops 481689600 | bytes 12582912 | tf_op jit(solution)/shard_map/pallas_call | solution.py:234
  124.9 1.8 %copy-done.1 = bf16[2,6,448,160]{3,2,1,0:T(8,128)(2,1)S(1)} copy-done((bf16[2,6,448,160]{3,2,1,0:T(8,128)(2,1)S(1)}, bf16[2,6,448,160]{3,2,1,0:T(8,128)(2,1)}, u32[]{:S(2)}) %copy-start.1) | copy-done | bytes 1720344
  129.0 1.8 %shard_map.104.mine_ref = bf16[448,1024]{1,0:T(8,128)(2,1)S(1)} custom-call(s32[3]{0:T(128)S(1)} %copy-done.6, f32[1,1024]{1,0:T(1,128)S(1)} %bitcast.36, bf16[2,160,128]{2,1,0:T(8,128)(2,1)S(1)} %copy-done.5, bf16[2,160,128]{2,1,0:T(8,128)(2,1)S(1)} %collective-permute-done.16.refs_2_, bf16[2,160,128]{2,1,0:T(8,128)(2,1)S(1)} %collective-permute-done.17.refs_3_, ...), custom_call_target="tpu_custom_call" | custom-call | flops 275251200 | bytes 12582912 | tf_op jit(solution)/shard_map/pallas_call | solution.py:234
  130.9 1.8 %shard_map.106.mine_ref = bf16[448,1024]{1,0:T(8,128)(2,1)S(1)} custom-call(s32[3]{0:T(128)S(1)} %copy-done.6, f32[1,1024]{1,0:T(1,128)S(1)} %bitcast.37, bf16[2,160,128]{2,1,0:T(8,128)(2,1)S(1)} %copy-done.5, bf16[2,160,128]{2,1,0:T(8,128)(2,1)S(1)} %collective-permute-done.16.refs_2_, bf16[2,160,128]{2,1,0:T(8,128)(2,1)S(1)} %collective-permute-done.17.refs_3_, ...), custom_call_target="tpu_custom_call" | custom-call | flops 275251200 | bytes 12582912 | tf_op jit(solution)/shard_map/pallas_call | solution.py:234
  133.4 1.7 shard_map.108
  135.1 1.8 %collective-permute-start.21 = (bf16[448,256]{1,0:T(8,128)(2,1)S(1)}, bf16[448,256]{1,0:T(8,128)(2,1)S(1)}, u32[]{:S(2)}, u32[]{:S(2)}) collective-permute-start(bf16[448,256]{1,0:T(8,128)(2,1)S(1)} %get-tuple-element.71), channel_id=1, source_target_pairs={{0,2},{2,4},{4,6},{6,0},{1,3},{3,5},{5,7},{7,1},{8,10},{10,12},{12... | collective-permute-start | bytes 688136 | tf_op jit(solution)/shard_map/ppermute | solution.py:431
  137.8 1.7 shard_map.105
  139.5 2.1 %collective-permute-start.25 = (bf16[448,256]{1,0:T(8,128)(2,1)S(1)}, bf16[448,256]{1,0:T(8,128)(2,1)S(1)}, u32[]{:S(2)}, u32[]{:S(2)}) collective-permute-start(bf16[448,256]{1,0:T(8,128)(2,1)S(1)} %get-tuple-element.75), channel_id=1, source_target_pairs={{0,6},{2,0},{4,2},{6,4},{1,7},{3,1},{5,3},{7,5},{8,14},{10,8},{12,... | collective-permute-start | bytes 688136 | tf_op jit(solution)/shard_map/ppermute | solution.py:431
  141.6 1.7 shard_map.109
  143.3 2.0 %collective-permute-start.24 = (bf16[448,256]{1,0:T(8,128)(2,1)S(1)}, bf16[448,256]{1,0:T(8,128)(2,1)S(1)}, u32[]{:S(2)}, u32[]{:S(2)}) collective-permute-start(bf16[448,256]{1,0:T(8,128)(2,1)S(1)} %get-tuple-element.74), channel_id=1, source_target_pairs={{0,4},{2,6},{4,0},{6,2},{1,5},{3,7},{5,1},{7,3},{8,12},{10,14},{12... | collective-permute-start | bytes 688136 | tf_op jit(solution)/shard_map/ppermute | solution.py:431
  145.3 1.7 shard_map.107
  147.0 2.1 %collective-permute-start.26 = (bf16[448,256]{1,0:T(8,128)(2,1)S(1)}, bf16[448,256]{1,0:T(8,128)(2,1)S(1)}, u32[]{:S(2)}, u32[]{:S(2)}) collective-permute-start(bf16[448,256]{1,0:T(8,128)(2,1)S(1)} %get-tuple-element.76), channel_id=1, source_target_pairs={{0,6},{2,0},{4,2},{6,4},{1,7},{3,1},{5,3},{7,5},{8,14},{10,8},{12,... | collective-permute-start | bytes 688136 | tf_op jit(solution)/shard_map/ppermute | solution.py:431
  149.1 6.3 %collective-permute-done.23.refs_4_ = bf16[448,256]{1,0:T(8,128)(2,1)S(1)} collective-permute-done((bf16[448,256]{1,0:T(8,128)(2,1)S(1)}, bf16[448,256]{1,0:T(8,128)(2,1)S(1)}, u32[]{:S(2)}, u32[]{:S(2)}) %collective-permute-start.23) | collective-permute-done | bytes 229408 | tf_op jit(solution)/shard_map/ppermute | solution.py:431
  155.4 4.9 %collective-permute-done.22.refs_3_ = bf16[448,256]{1,0:T(8,128)(2,1)S(1)} collective-permute-done((bf16[448,256]{1,0:T(8,128)(2,1)S(1)}, bf16[448,256]{1,0:T(8,128)(2,1)S(1)}, u32[]{:S(2)}, u32[]{:S(2)}) %collective-permute-start.22) | collective-permute-done | bytes 229408 | tf_op jit(solution)/shard_map/ppermute | solution.py:431
  160.3 13.9 %collective-permute-done.24.refs_5_ = bf16[448,256]{1,0:T(8,128)(2,1)S(1)} collective-permute-done((bf16[448,256]{1,0:T(8,128)(2,1)S(1)}, bf16[448,256]{1,0:T(8,128)(2,1)S(1)}, u32[]{:S(2)}, u32[]{:S(2)}) %collective-permute-start.24) | collective-permute-done | bytes 229408 | tf_op jit(solution)/shard_map/ppermute | solution.py:431
  174.2 1.8 %shard_map.110 = bf16[3584,256]{1,0:T(8,128)(2,1)} custom-call(s32[3]{0:T(128)S(1)} %copy-done.6, bf16[448,256]{1,0:T(8,128)(2,1)S(1)} %get-tuple-element.69.refs_0_, bf16[448,256]{1,0:T(8,128)(2,1)S(1)} %get-tuple-element.70.refs_1_, bf16[448,256]{1,0:T(8,128)(2,1)S(1)} %collective-permute-done.21.refs_2_, ...), custom_call_target="tpu_custom_call" | custom-call | bytes 12582912 | tf_op jit(solution)/shard_map/pallas_call | solution.py:234
  (91 shorter events, 22.8 us)
Async XLA Ops:
  1.0 12.4 %collective-permute-start.2 = (bf16[512,256]{1,0:T(8,128)(2,1)S(1)}, bf16[512,256]{1,0:T(8,128)(2,1)S(1)}, u32[]{:S(2)}, u32[]{:S(2)}) collective-permute-start(bf16[512,256]{1,0:T(8,128)(2,1)S(1)} %constant_dynamic-slice_fusion.1), channel_id=1, source_target_pairs={{0,2},{2,4},{4,6},{6,0},{1,3},{3,5},{5,7},{7,1},{8,10},{10,12},{12... | collective-permute-start | bytes 786440 | tf_op jit(solution)/shard_map/ppermute | solution.py:291
  4.0 19.7 %collective-permute-start.1 = (bf16[512,256]{1,0:T(8,128)(2,1)S(1)}, bf16[512,256]{1,0:T(8,128)(2,1)S(1)}, u32[]{:S(2)}, u32[]{:S(2)}) collective-permute-start(bf16[512,256]{1,0:T(8,128)(2,1)S(1)} %constant_dynamic-slice_fusion.1), channel_id=1, source_target_pairs={{0,4},{2,6},{4,0},{6,2},{1,5},{3,7},{5,1},{7,3},{8,12},{10,14},{12... | collective-permute-start | bytes 786440 | tf_op jit(solution)/shard_map/ppermute | solution.py:291
  6.6 17.1 %collective-permute-start = (bf16[512,256]{1,0:T(8,128)(2,1)S(1)}, bf16[512,256]{1,0:T(8,128)(2,1)S(1)}, u32[]{:S(2)}, u32[]{:S(2)}) collective-permute-start(bf16[512,256]{1,0:T(8,128)(2,1)S(1)} %constant_dynamic-slice_fusion.1), channel_id=1, source_target_pairs={{0,6},{2,0},{4,2},{6,4},{1,7},{3,1},{5,3},{7,5},{8,14},{10,8},{12,... | collective-permute-start | bytes 786440 | tf_op jit(solution)/shard_map/ppermute | solution.py:291
  23.8 47.1 %copy-start.8 = (bf16[3,512,256]{2,1,0:T(8,128)(2,1)}, bf16[3,512,256]{2,1,0:T(8,128)(2,1)S(1)}, u32[]{:S(2)}) copy-start(bf16[3,512,256]{2,1,0:T(8,128)(2,1)S(1)} %pad_maximum_fusion.refs_13_) | copy-start | bytes 2359300
  23.9 18.7 %collective-permute-start.3 = (bf16[896,256]{1,0:T(8,128)(2,1)S(1)}, bf16[896,256]{1,0:T(8,128)(2,1)S(1)}, u32[]{:S(2)}, u32[]{:S(2)}) collective-permute-start(bf16[896,256]{1,0:T(8,128)(2,1)S(1)} %get-tuple-element.42), channel_id=1, source_target_pairs={{0,2},{2,4},{4,6},{6,0},{1,3},{3,5},{5,7},{7,1},{8,10},{10,12},{12... | collective-permute-start | bytes 1376264 | tf_op jit(solution)/shard_map/ppermute | solution.py:298
  30.0 32.1 %collective-permute-start.8 = (bf16[3,512,256]{2,1,0:T(8,128)(2,1)S(1)}, bf16[3,512,256]{2,1,0:T(8,128)(2,1)S(1)}, u32[]{:S(2)}, u32[]{:S(2)}) collective-permute-start(bf16[3,512,256]{2,1,0:T(8,128)(2,1)S(1)} %pad_maximum_fusion.refs_13_), channel_id=1, source_target_pairs={{0,24},{8,16},{16,8},{24,0},{1,25},{9,17},{17,9},{25,1},{2,26},{10... | collective-permute-start | bytes 2359304 | tf_op jit(solution)/shard_map/ppermute | solution.py:294
  32.4 34.5 %collective-permute-start.7 = (bf16[3,512,256]{2,1,0:T(8,128)(2,1)S(1)}, bf16[3,512,256]{2,1,0:T(8,128)(2,1)S(1)}, u32[]{:S(2)}, u32[]{:S(2)}) collective-permute-start(bf16[3,512,256]{2,1,0:T(8,128)(2,1)S(1)} %pad_maximum_fusion.refs_13_), channel_id=1, source_target_pairs={{0,16},{8,24},{16,0},{24,8},{1,17},{9,25},{17,1},{25,9},{2,18},{10... | collective-permute-start | bytes 2359304 | tf_op jit(solution)/shard_map/ppermute | solution.py:294
  32.9 34.1 %collective-permute-start.6 = (bf16[3,512,256]{2,1,0:T(8,128)(2,1)S(1)}, bf16[3,512,256]{2,1,0:T(8,128)(2,1)S(1)}, u32[]{:S(2)}, u32[]{:S(2)}) collective-permute-start(bf16[3,512,256]{2,1,0:T(8,128)(2,1)S(1)} %pad_maximum_fusion.refs_13_), channel_id=1, source_target_pairs={{0,8},{8,0},{16,24},{24,16},{1,9},{9,1},{17,25},{25,17},{2,10},{10... | collective-permute-start | bytes 2359304 | tf_op jit(solution)/shard_map/ppermute | solution.py:294
  33.5 27.0 %collective-permute-start.4 = (bf16[896,256]{1,0:T(8,128)(2,1)S(1)}, bf16[896,256]{1,0:T(8,128)(2,1)S(1)}, u32[]{:S(2)}, u32[]{:S(2)}) collective-permute-start(bf16[896,256]{1,0:T(8,128)(2,1)S(1)} %get-tuple-element.43), channel_id=1, source_target_pairs={{0,4},{2,6},{4,0},{6,2},{1,5},{3,7},{5,1},{7,3},{8,12},{10,14},{12... | collective-permute-start | bytes 1376264 | tf_op jit(solution)/shard_map/ppermute | solution.py:298
  42.6 28.4 %copy-start.16 = (bf16[896,256]{1,0:T(8,128)(2,1)}, bf16[896,256]{1,0:T(8,128)(2,1)S(1)}, u32[]{:S(2)}) copy-start(bf16[896,256]{1,0:T(8,128)(2,1)S(1)} %collective-permute-done.3.refs_1_) | copy-start | bytes 1376260
  42.6 19.5 %collective-permute-start.5 = (bf16[896,256]{1,0:T(8,128)(2,1)S(1)}, bf16[896,256]{1,0:T(8,128)(2,1)S(1)}, u32[]{:S(2)}, u32[]{:S(2)}) collective-permute-start(bf16[896,256]{1,0:T(8,128)(2,1)S(1)} %get-tuple-element.44), channel_id=1, source_target_pairs={{0,6},{2,0},{4,2},{6,4},{1,7},{3,1},{5,3},{7,5},{8,14},{10,8},{12,... | collective-permute-start | bytes 1376264 | tf_op jit(solution)/shard_map/ppermute | solution.py:298
  60.5 10.5 %copy-start.17 = (bf16[896,256]{1,0:T(8,128)(2,1)}, bf16[896,256]{1,0:T(8,128)(2,1)S(1)}, u32[]{:S(2)}) copy-start(bf16[896,256]{1,0:T(8,128)(2,1)S(1)} %collective-permute-done.4.refs_2_) | copy-start | bytes 1376260
  60.5 7.1 %collective-permute-start.9 = (bf16[896,256]{1,0:T(8,128)(2,1)S(1)}, bf16[896,256]{1,0:T(8,128)(2,1)S(1)}, u32[]{:S(2)}, u32[]{:S(2)}) collective-permute-start(bf16[896,256]{1,0:T(8,128)(2,1)S(1)} %get-tuple-element.49), channel_id=1, source_target_pairs={{0,1},{1,0},{2,3},{3,2},{4,5},{5,4},{6,7},{7,6},{8,9},{9,8},{10,11... | collective-permute-start | bytes 1376264 | tf_op jit(solution)/shard_map/ppermute | solution.py:301
  67.0 1.8 %collective-permute-start.10 = (bf16[896,256]{1,0:T(8,128)(2,1)S(1)}, bf16[896,256]{1,0:T(8,128)(2,1)S(1)}, u32[]{:S(2)}, u32[]{:S(2)}) collective-permute-start(bf16[896,256]{1,0:T(8,128)(2,1)S(1)} %collective-permute-done.3.refs_1_), channel_id=1, source_target_pairs={{0,1},{1,0},{2,3},{3,2},{4,5},{5,4},{6,7},{7,6},{8,9},{9,8},{10,11... | collective-permute-start | bytes 1376264 | tf_op jit(solution)/shard_map/ppermute | solution.py:301
  67.0 3.1 %collective-permute-start.11 = (bf16[896,256]{1,0:T(8,128)(2,1)S(1)}, bf16[896,256]{1,0:T(8,128)(2,1)S(1)}, u32[]{:S(2)}, u32[]{:S(2)}) collective-permute-start(bf16[896,256]{1,0:T(8,128)(2,1)S(1)} %collective-permute-done.4.refs_2_), channel_id=1, source_target_pairs={{0,1},{1,0},{2,3},{3,2},{4,5},{5,4},{6,7},{7,6},{8,9},{9,8},{10,11... | collective-permute-start | bytes 1376264 | tf_op jit(solution)/shard_map/ppermute | solution.py:301
  67.5 3.4 %collective-permute-start.12 = (bf16[896,256]{1,0:T(8,128)(2,1)S(1)}, bf16[896,256]{1,0:T(8,128)(2,1)}, u32[]{:S(2)}, u32[]{:S(2)}) collective-permute-start(bf16[896,256]{1,0:T(8,128)(2,1)S(1)} %collective-permute-done.5.refs_3_), channel_id=1, source_target_pairs={{0,1},{1,0},{2,3},{3,2},{4,5},{5,4},{6,7},{7,6},{8,9},{9,8},{10,11... | collective-permute-start | bytes 1376264 | tf_op jit(solution)/shard_map/ppermute | solution.py:301
  85.2 18.1 %all-to-all-start = ((bf16[4,2,160,128]{3,2,1,0:T(8,128)(2,1)}), bf16[4,2,160,128]{3,2,1,0:T(8,128)(2,1)S(1)}, u32[]{:S(2)}, u32[]{:S(2)}) async-start(bf16[4,2,160,128]{3,2,1,0:T(8,128)(2,1)} %bitcast.40), calls=%async_computation | async-start | bytes 655360 | tf_op jit(solution)/shard_map/all_to_all | solution.py:365
  92.6 14.2 %copy-start.12 = (f32[2048]{0:T(1024)S(1)}, f32[2048]{0:T(1024)}, u32[]{:S(2)}) copy-start(f32[2048]{0:T(1024)} %param.15) | copy-start | bytes 24580
  103.3 5.5 %collective-permute-start.15 = (bf16[2,160,128]{2,1,0:T(8,128)(2,1)S(1)}, bf16[2,160,128]{2,1,0:T(8,128)(2,1)S(1)}, u32[]{:S(2)}, u32[]{:S(2)}) collective-permute-start(bf16[2,160,128]{2,1,0:T(8,128)(2,1)S(1)} %reduce_sum.12), channel_id=1, source_target_pairs={{0,24},{8,16},{16,8},{24,0},{1,25},{9,17},{17,9},{25,1},{2,26},{10... | collective-permute-start | bytes 245768 | tf_op jit(solution)/shard_map/ppermute | solution.py:369
  105.8 4.7 %collective-permute-start.14 = (bf16[2,160,128]{2,1,0:T(8,128)(2,1)S(1)}, bf16[2,160,128]{2,1,0:T(8,128)(2,1)S(1)}, u32[]{:S(2)}, u32[]{:S(2)}) collective-permute-start(bf16[2,160,128]{2,1,0:T(8,128)(2,1)S(1)} %reduce_sum.12), channel_id=1, source_target_pairs={{0,16},{8,24},{16,0},{24,8},{1,17},{9,25},{17,1},{25,9},{2,18},{10... | collective-permute-start | bytes 245768 | tf_op jit(solution)/shard_map/ppermute | solution.py:369
  106.3 4.4 %collective-permute-start.13 = (bf16[2,160,128]{2,1,0:T(8,128)(2,1)S(1)}, bf16[2,160,128]{2,1,0:T(8,128)(2,1)S(1)}, u32[]{:S(2)}, u32[]{:S(2)}) collective-permute-start(bf16[2,160,128]{2,1,0:T(8,128)(2,1)S(1)} %reduce_sum.12), channel_id=1, source_target_pairs={{0,8},{8,0},{16,24},{24,16},{1,9},{9,1},{17,25},{25,17},{2,10},{10... | collective-permute-start | bytes 245768 | tf_op jit(solution)/shard_map/ppermute | solution.py:369
  113.6 10.6 %collective-permute-start.16 = (bf16[2,160,128]{2,1,0:T(8,128)(2,1)}, bf16[2,160,128]{2,1,0:T(8,128)(2,1)S(1)}, u32[]{:S(2)}, u32[]{:S(2)}) collective-permute-start(bf16[2,160,128]{2,1,0:T(8,128)(2,1)} %get-tuple-element.62), channel_id=1, source_target_pairs={{0,6},{2,0},{4,2},{6,4},{1,7},{3,1},{5,3},{7,5},{8,14},{10,8},{12,... | collective-permute-start | bytes 245768 | tf_op jit(solution)/shard_map/ppermute | solution.py:378
  117.3 7.6 %collective-permute-start.17 = (bf16[2,160,128]{2,1,0:T(8,128)(2,1)}, bf16[2,160,128]{2,1,0:T(8,128)(2,1)S(1)}, u32[]{:S(2)}, u32[]{:S(2)}) collective-permute-start(bf16[2,160,128]{2,1,0:T(8,128)(2,1)} %get-tuple-element.63), channel_id=1, source_target_pairs={{0,4},{2,6},{4,0},{6,2},{1,5},{3,7},{5,1},{7,3},{8,12},{10,14},{12... | collective-permute-start | bytes 245768 | tf_op jit(solution)/shard_map/ppermute | solution.py:378
  117.3 7.6 %collective-permute-start.18 = (bf16[2,160,128]{2,1,0:T(8,128)(2,1)}, bf16[2,160,128]{2,1,0:T(8,128)(2,1)S(1)}, u32[]{:S(2)}, u32[]{:S(2)}) collective-permute-start(bf16[2,160,128]{2,1,0:T(8,128)(2,1)} %get-tuple-element.64), channel_id=1, source_target_pairs={{0,2},{2,4},{4,6},{6,0},{1,3},{3,5},{5,7},{7,1},{8,10},{10,12},{12... | collective-permute-start | bytes 245768 | tf_op jit(solution)/shard_map/ppermute | solution.py:378
  130.8 2.5 %collective-permute-start.19 = (bf16[448,1024]{1,0:T(8,128)(2,1)S(1)}, bf16[448,1024]{1,0:T(8,128)(2,1)S(1)}, u32[]{:S(2)}, u32[]{:S(2)}) collective-permute-start(bf16[448,1024]{1,0:T(8,128)(2,1)S(1)} %shard_map.104.mine_ref), channel_id=1, source_target_pairs={{0,1},{1,0},{2,3},{3,2},{4,5},{5,4},{6,7},{7,6},{8,9},{9,8},{10,11... | collective-permute-start | bytes 2752520 | tf_op jit(solution)/shard_map/ppermute | solution.py:424
  132.7 8.8 %collective-permute-start.20 = (bf16[448,1024]{1,0:T(8,128)(2,1)S(1)}, bf16[448,1024]{1,0:T(8,128)(2,1)S(1)}, u32[]{:S(2)}, u32[]{:S(2)}) collective-permute-start(bf16[448,1024]{1,0:T(8,128)(2,1)S(1)} %shard_map.106.mine_ref), channel_id=1, source_target_pairs={{0,1},{1,0},{2,3},{3,2},{4,5},{5,4},{6,7},{7,6},{8,9},{9,8},{10,11... | collective-permute-start | bytes 2752520 | tf_op jit(solution)/shard_map/ppermute | solution.py:424
  135.1 12.0 %collective-permute-start.21 = (bf16[448,256]{1,0:T(8,128)(2,1)S(1)}, bf16[448,256]{1,0:T(8,128)(2,1)S(1)}, u32[]{:S(2)}, u32[]{:S(2)}) collective-permute-start(bf16[448,256]{1,0:T(8,128)(2,1)S(1)} %get-tuple-element.71), channel_id=1, source_target_pairs={{0,2},{2,4},{4,6},{6,0},{1,3},{3,5},{5,7},{7,1},{8,10},{10,12},{12... | collective-permute-start | bytes 688136 | tf_op jit(solution)/shard_map/ppermute | solution.py:431
  136.9 18.5 %collective-permute-start.23 = (bf16[448,256]{1,0:T(8,128)(2,1)S(1)}, bf16[448,256]{1,0:T(8,128)(2,1)S(1)}, u32[]{:S(2)}, u32[]{:S(2)}) collective-permute-start(bf16[448,256]{1,0:T(8,128)(2,1)S(1)} %get-tuple-element.73), channel_id=1, source_target_pairs={{0,4},{2,6},{4,0},{6,2},{1,5},{3,7},{5,1},{7,3},{8,12},{10,14},{12... | collective-permute-start | bytes 688136 | tf_op jit(solution)/shard_map/ppermute | solution.py:431
  139.5 15.9 %collective-permute-start.25 = (bf16[448,256]{1,0:T(8,128)(2,1)S(1)}, bf16[448,256]{1,0:T(8,128)(2,1)S(1)}, u32[]{:S(2)}, u32[]{:S(2)}) collective-permute-start(bf16[448,256]{1,0:T(8,128)(2,1)S(1)} %get-tuple-element.75), channel_id=1, source_target_pairs={{0,6},{2,0},{4,2},{6,4},{1,7},{3,1},{5,3},{7,5},{8,14},{10,8},{12,... | collective-permute-start | bytes 688136 | tf_op jit(solution)/shard_map/ppermute | solution.py:431
  143.3 17.0 %collective-permute-start.22 = (bf16[448,256]{1,0:T(8,128)(2,1)S(1)}, bf16[448,256]{1,0:T(8,128)(2,1)S(1)}, u32[]{:S(2)}, u32[]{:S(2)}) collective-permute-start(bf16[448,256]{1,0:T(8,128)(2,1)S(1)} %get-tuple-element.72), channel_id=1, source_target_pairs={{0,2},{2,4},{4,6},{6,0},{1,3},{3,5},{5,7},{7,1},{8,10},{10,12},{12... | collective-permute-start | bytes 688136 | tf_op jit(solution)/shard_map/ppermute | solution.py:431
  143.3 30.9 %collective-permute-start.24 = (bf16[448,256]{1,0:T(8,128)(2,1)S(1)}, bf16[448,256]{1,0:T(8,128)(2,1)S(1)}, u32[]{:S(2)}, u32[]{:S(2)}) collective-permute-start(bf16[448,256]{1,0:T(8,128)(2,1)S(1)} %get-tuple-element.74), channel_id=1, source_target_pairs={{0,4},{2,6},{4,0},{6,2},{1,5},{3,7},{5,1},{7,3},{8,12},{10,14},{12... | collective-permute-start | bytes 688136 | tf_op jit(solution)/shard_map/ppermute | solution.py:431
  147.0 27.2 %collective-permute-start.26 = (bf16[448,256]{1,0:T(8,128)(2,1)S(1)}, bf16[448,256]{1,0:T(8,128)(2,1)S(1)}, u32[]{:S(2)}, u32[]{:S(2)}) collective-permute-start(bf16[448,256]{1,0:T(8,128)(2,1)S(1)} %get-tuple-element.76), channel_id=1, source_target_pairs={{0,6},{2,0},{4,2},{6,4},{1,7},{3,1},{5,3},{7,5},{8,14},{10,8},{12,... | collective-permute-start | bytes 688136 | tf_op jit(solution)/shard_map/ppermute | solution.py:431
  (20 other events, 72.7 us)

commit v13 on v12

--- a/solution.py
+++ b/solution.py
@@ -359,6 +359,7 @@
             ],
             (query, key, value, early, query_table, query_bias),
             count * rows * rows * 1200,
+            mib=44,
         )
 
     own = total.reshape(layers, per_group, PACKED, HEAD_DIM)

time: 179 us -> 182 us (1.017)
  local copies, waits for them, and re-layouts: 8.48 us -> 16.8 us
  Pallas kernels: 44.6 us -> 39.3 us
  waiting for transfers between devices: 77.8 us -> 75.8 us
    unnamed x48 -> x56, local copies, waits for them, and re-layouts: 5.94 us -> 12.2 us
    pallas_call x10, Pallas kernels: 42.7 us -> 37.4 us  [call(): pl.pallas_call(kernel, grid_spec=pltpu.PrefetchScalarGridSpec(num_scalar_...]
  transfers between devices with their start and end apart: 28 -> 28, of which waited for: 17 -> 16; matrix products, arithmetic and copies ran while one was open for 1% -> 2% of each run, Pallas kernels for 14% -> 11%
where the time goes in v13:
time: 182 us; the launch traced here: 179 us
  waiting for transfers between devices  75.8 us (42%)
  starting transfers between devices  44.3 us (24%)
  Pallas kernels  39.3 us (22%)
  local copies, waits for them, and re-layouts  16.8 us (9%)
  other arithmetic  2.34 us (1%)
    pallas_call x10, Pallas kernels, call(): pl.pallas_call(kernel, grid_spec=pltpu.PrefetchScalarGridSpec(num_scalar_...  37.4 us
    ppermute x3, waiting for transfers between devices, per_device(): lax.ppermute(sent[d], 'z', turn(d))  27 us
    ppermute x6, waiting for transfers between devices, per_device(): pieces[d, chunk] = lax.ppermute(piece, 'z', turn(d)) if d else piece  25.1 us
    ppermute x3, waiting for transfers between devices, per_device(): lax.ppermute(value_part, 'z', turn(-d))  13.6 us
    unnamed x56, local copies, waits for them, and re-layouts  12.2 us
    ppermute x6, starting transfers between devices, per_device(): pieces[d, chunk] = lax.ppermute(piece, 'z', turn(d)) if d else piece  8.97 us
    ppermute x3, starting transfers between devices, per_device(): lax.ppermute(sent[d], 'z', turn(d))  7.73 us
    all_to_all x1, starting transfers between devices, per_device(): line = lax.all_to_all(own, 'z', split_axis=0, concat_axis=0, tiled=True)  7.45 us
  transfers between devices with their start and end apart: 28, of which 16 were waited for; matrix products, arithmetic and copies ran while one was open for 2% of the time, Pallas kernels for 11%

profile of v13, /device:TPU:0, one launch (start us, length us, event | category | flops | bytes accessed | tf_op | source)
XLA Modules:
  0.0 178.9 jit_solution(9477026924780666641)
XLA Ops:
  1.0 3.1 %collective-permute-start.2 = (bf16[512,256]{1,0:T(8,128)(2,1)S(1)}, bf16[512,256]{1,0:T(8,128)(2,1)S(1)}, u32[]{:S(2)}, u32[]{:S(2)}) collective-permute-start(bf16[512,256]{1,0:T(8,128)(2,1)S(1)} %constant_dynamic-slice_fusion.1), channel_id=1, source_target_pairs={{0,2},{2,4},{4,6},{6,0},{1,3},{3,5},{5,7},{7,1},{8,10},{10,12},{12... | collective-permute-start | bytes 786440 | tf_op jit(solution)/shard_map/ppermute | solution.py:291
  4.0 2.6 %collective-permute-start.1 = (bf16[512,256]{1,0:T(8,128)(2,1)S(1)}, bf16[512,256]{1,0:T(8,128)(2,1)S(1)}, u32[]{:S(2)}, u32[]{:S(2)}) collective-permute-start(bf16[512,256]{1,0:T(8,128)(2,1)S(1)} %constant_dynamic-slice_fusion.1), channel_id=1, source_target_pairs={{0,4},{2,6},{4,0},{6,2},{1,5},{3,7},{5,1},{7,3},{8,12},{10,14},{12... | collective-permute-start | bytes 786440 | tf_op jit(solution)/shard_map/ppermute | solution.py:291
  10.1 3.2 %collective-permute-done.2 = bf16[512,256]{1,0:T(8,128)(2,1)S(1)} collective-permute-done((bf16[512,256]{1,0:T(8,128)(2,1)S(1)}, bf16[512,256]{1,0:T(8,128)(2,1)S(1)}, u32[]{:S(2)}, u32[]{:S(2)}) %collective-permute-start.2) | collective-permute-done | bytes 262176 | tf_op jit(solution)/shard_map/ppermute | solution.py:291
  13.3 10.4 %collective-permute-done.1 = bf16[512,256]{1,0:T(8,128)(2,1)S(1)} collective-permute-done((bf16[512,256]{1,0:T(8,128)(2,1)S(1)}, bf16[512,256]{1,0:T(8,128)(2,1)S(1)}, u32[]{:S(2)}, u32[]{:S(2)}) %collective-permute-start.1) | collective-permute-done | bytes 262176 | tf_op jit(solution)/shard_map/ppermute | solution.py:291
  23.9 6.1 %collective-permute-start.3 = (bf16[896,256]{1,0:T(8,128)(2,1)S(1)}, bf16[896,256]{1,0:T(8,128)(2,1)S(1)}, u32[]{:S(2)}, u32[]{:S(2)}) collective-permute-start(bf16[896,256]{1,0:T(8,128)(2,1)S(1)} %get-tuple-element.42), channel_id=1, source_target_pairs={{0,2},{2,4},{4,6},{6,0},{1,3},{3,5},{5,7},{7,1},{8,10},{10,12},{12... | collective-permute-start | bytes 1376264 | tf_op jit(solution)/shard_map/ppermute | solution.py:298
  30.0 2.4 %collective-permute-start.8 = (bf16[3,512,256]{2,1,0:T(8,128)(2,1)S(1)}, bf16[3,512,256]{2,1,0:T(8,128)(2,1)S(1)}, u32[]{:S(2)}, u32[]{:S(2)}) collective-permute-start(bf16[3,512,256]{2,1,0:T(8,128)(2,1)S(1)} %pad_maximum_fusion.refs_13_), channel_id=1, source_target_pairs={{0,24},{8,16},{16,8},{24,0},{1,25},{9,17},{17,9},{25,1},{2,26},{10... | collective-permute-start | bytes 2359304 | tf_op jit(solution)/shard_map/ppermute | solution.py:294
  35.1 7.5 %collective-permute-done.3.refs_1_ = bf16[896,256]{1,0:T(8,128)(2,1)S(1)} collective-permute-done((bf16[896,256]{1,0:T(8,128)(2,1)S(1)}, bf16[896,256]{1,0:T(8,128)(2,1)S(1)}, u32[]{:S(2)}, u32[]{:S(2)}) %collective-permute-start.3) | collective-permute-done | bytes 458784 | tf_op jit(solution)/shard_map/ppermute | solution.py:298
  42.6 17.9 %collective-permute-done.4.refs_2_ = bf16[896,256]{1,0:T(8,128)(2,1)S(1)} collective-permute-done((bf16[896,256]{1,0:T(8,128)(2,1)S(1)}, bf16[896,256]{1,0:T(8,128)(2,1)S(1)}, u32[]{:S(2)}, u32[]{:S(2)}) %collective-permute-start.4) | collective-permute-done | bytes 458784 | tf_op jit(solution)/shard_map/ppermute | solution.py:298
  60.5 1.6 collective-permute-done.5.refs_3_
  62.1 4.8 %collective-permute-done.7.refs_15_ = bf16[3,512,256]{2,1,0:T(8,128)(2,1)S(1)} collective-permute-done((bf16[3,512,256]{2,1,0:T(8,128)(2,1)S(1)}, bf16[3,512,256]{2,1,0:T(8,128)(2,1)S(1)}, u32[]{:S(2)}, u32[]{:S(2)}) %collective-permute-start.7) | collective-permute-done | bytes 786464 | tf_op jit(solution)/shard_map/ppermute | solution.py:294
  71.0 14.1 %shard_map.100 = (bf16[2,448,256]{2,1,0:T(8,128)(2,1)}, bf16[2,448,256]{2,1,0:T(8,128)(2,1)}, bf16[2,448,1024]{2,1,0:T(8,128)(2,1)}, bf16[8,160,128]{2,1,0:T(8,128)(2,1)}, bf16[8,160,128]{2,1,0:T(8,128)(2,1)}) custom-call(s32[3]{0:T(128)} %pad_add_fusion.at_ref.core_ref, bf16[4,896,256]{2,1,0:T(8,128)(2,1)} %bitcast.39, bf16[896,256]{1,0:T(8,128)(2,1)} %copy-done.20, ...), custom_call_target="tpu_custom_call" | custom-call | flops 5637144576 | bytes 12582912 | tf_op jit(solution)/shard_map/pallas_call | solution.py:234
  85.1 7.5 %all-to-all-start = ((bf16[4,2,160,128]{3,2,1,0:T(8,128)(2,1)}), bf16[4,2,160,128]{3,2,1,0:T(8,128)(2,1)}, u32[]{:S(2)}, u32[]{:S(2)}) async-start(bf16[4,2,160,128]{3,2,1,0:T(8,128)(2,1)} %bitcast.40), calls=%async_computation | async-start | bytes 655360 | tf_op jit(solution)/shard_map/all_to_all | solution.py:366
  98.3 8.0 %shard_map.101 = (f32[2,448,768]{2,1,0:T(8,128)S(1)}, bf16[2,6,448,160]{3,2,1,0:T(8,128)(2,1)S(1)}) custom-call(s32[3]{0:T(128)S(1)} %copy-done.13, bf16[2,448,256]{2,1,0:T(8,128)(2,1)S(1)} %copy-done.6, bf16[2,448,256]{2,1,0:T(8,128)(2,1)S(1)} %copy-done.8, bf16[2,448,1024]{2,1,0:T(8,128)(2,1)S(1)} %copy-done.2, bf16[8,160,128]{2,1,0:T(8,128)(2,1)S(1)} %copy-done.11, ...), custom_call_target="tpu_custom_call" | custom-call | flops 1445068800 | bytes 12582912 | tf_op jit(solution)/shard_map/pallas_call | solution.py:234
  107.9 1.7 reduce_sum.12
  109.6 2.5 %collective-permute-start.15 = (bf16[2,160,128]{2,1,0:T(8,128)(2,1)}, bf16[2,160,128]{2,1,0:T(8,128)(2,1)}, u32[]{:S(2)}, u32[]{:S(2)}) collective-permute-start(bf16[2,160,128]{2,1,0:T(8,128)(2,1)} %reduce_sum.12), channel_id=1, source_target_pairs={{0,24},{8,16},{16,8},{24,0},{1,25},{9,17},{17,9},{25,1},{2,26},{10... | collective-permute-start | bytes 245768 | tf_op jit(solution)/shard_map/ppermute | solution.py:370
  115.3 1.7 collective-permute-done.14.refs_1_
  117.3 1.9 %shard_map.102 = (bf16[2,160,128]{2,1,0:T(8,128)(2,1)}, bf16[2,160,128]{2,1,0:T(8,128)(2,1)}, bf16[2,160,128]{2,1,0:T(8,128)(2,1)}, bf16[2,160,128]{2,1,0:T(8,128)(2,1)}) custom-call(s32[3]{0:T(128)} %pad_add_fusion.at_ref.core_ref, bf16[4,2,160,128]{3,2,1,0:T(8,128)(2,1)} %all-to-all-done.line_ref, bf16[2,160,128]{2,1,0:T(8,128)(2,1)} %collective-permute-done.13.refs_0_, ...), custom_call_target="tpu_custom_call" | custom-call | tf_op jit(solution)/shard_map/pallas_call | solution.py:372
  119.2 3.8 %collective-permute-start.16 = (bf16[2,160,128]{2,1,0:T(8,128)(2,1)}, bf16[2,160,128]{2,1,0:T(8,128)(2,1)S(1)}, u32[]{:S(2)}, u32[]{:S(2)}) collective-permute-start(bf16[2,160,128]{2,1,0:T(8,128)(2,1)} %get-tuple-element.62), channel_id=1, source_target_pairs={{0,6},{2,0},{4,2},{6,4},{1,7},{3,1},{5,3},{7,5},{8,14},{10,8},{12,... | collective-permute-start | bytes 245768 | tf_op jit(solution)/shard_map/ppermute | solution.py:379
  128.6 3.1 %shard_map.103 = (f32[2,448,256]{2,1,0:T(8,128)S(1)}, bf16[2,2,448,160]{3,2,1,0:T(8,128)(2,1)S(1)}) custom-call(s32[3]{0:T(128)S(1)} %copy-done.14, bf16[2,448,256]{2,1,0:T(8,128)(2,1)S(1)} %copy-done.7, bf16[2,448,256]{2,1,0:T(8,128)(2,1)S(1)} %copy-done.9, bf16[2,448,1024]{2,1,0:T(8,128)(2,1)S(1)} %copy-done.3, bf16[8,160,128]{2,1,0:T(8,128)(2,1)S(1)} %copy-done.12, ...), custom_call_target="tpu_custom_call" | custom-call | flops 481689600 | bytes 12582912 | tf_op jit(solution)/shard_map/pallas_call | solution.py:234
  131.8 1.8 shard_map.104.mine_ref
  133.6 1.8 shard_map.106.mine_ref
  136.1 1.7 shard_map.108
  137.8 2.4 %collective-permute-start.21 = (bf16[448,256]{1,0:T(8,128)(2,1)S(1)}, bf16[448,256]{1,0:T(8,128)(2,1)S(1)}, u32[]{:S(2)}, u32[]{:S(2)}) collective-permute-start(bf16[448,256]{1,0:T(8,128)(2,1)S(1)} %get-tuple-element.71), channel_id=1, source_target_pairs={{0,2},{2,4},{4,6},{6,0},{1,3},{3,5},{5,7},{7,1},{8,10},{10,12},{12... | collective-permute-start | bytes 688136 | tf_op jit(solution)/shard_map/ppermute | solution.py:432
  141.1 1.7 shard_map.105
  142.8 1.6 collective-permute-start.25
  144.4 1.7 shard_map.109
  146.6 2.0 %collective-permute-start.24 = (bf16[448,256]{1,0:T(8,128)(2,1)S(1)}, bf16[448,256]{1,0:T(8,128)(2,1)S(1)}, u32[]{:S(2)}, u32[]{:S(2)}) collective-permute-start(bf16[448,256]{1,0:T(8,128)(2,1)S(1)} %get-tuple-element.74), channel_id=1, source_target_pairs={{0,4},{2,6},{4,0},{6,2},{1,5},{3,7},{5,1},{7,3},{8,12},{10,14},{12... | collective-permute-start | bytes 688136 | tf_op jit(solution)/shard_map/ppermute | solution.py:432
  148.6 1.7 shard_map.107
  151.8 6.2 %collective-permute-done.23.refs_4_ = bf16[448,256]{1,0:T(8,128)(2,1)S(1)} collective-permute-done((bf16[448,256]{1,0:T(8,128)(2,1)S(1)}, bf16[448,256]{1,0:T(8,128)(2,1)S(1)}, u32[]{:S(2)}, u32[]{:S(2)}) %collective-permute-start.23) | collective-permute-done | bytes 229408 | tf_op jit(solution)/shard_map/ppermute | solution.py:432
  158.1 4.9 %collective-permute-done.22.refs_3_ = bf16[448,256]{1,0:T(8,128)(2,1)S(1)} collective-permute-done((bf16[448,256]{1,0:T(8,128)(2,1)S(1)}, bf16[448,256]{1,0:T(8,128)(2,1)S(1)}, u32[]{:S(2)}, u32[]{:S(2)}) %collective-permute-start.22) | collective-permute-done | bytes 229408 | tf_op jit(solution)/shard_map/ppermute | solution.py:432
  163.0 13.9 %collective-permute-done.24.refs_5_ = bf16[448,256]{1,0:T(8,128)(2,1)S(1)} collective-permute-done((bf16[448,256]{1,0:T(8,128)(2,1)S(1)}, bf16[448,256]{1,0:T(8,128)(2,1)S(1)}, u32[]{:S(2)}, u32[]{:S(2)}) %collective-permute-start.24) | collective-permute-done | bytes 229408 | tf_op jit(solution)/shard_map/ppermute | solution.py:432
  176.9 1.8 %shard_map.110 = bf16[3584,256]{1,0:T(8,128)(2,1)} custom-call(s32[3]{0:T(128)S(1)} %copy-done.14, bf16[448,256]{1,0:T(8,128)(2,1)S(1)} %get-tuple-element.69.refs_0_, bf16[448,256]{1,0:T(8,128)(2,1)S(1)} %get-tuple-element.70.refs_1_, bf16[448,256]{1,0:T(8,128)(2,1)S(1)} %collective-permute-done.21.refs_2_, ...), custom_call_target="tpu_custom_call" | custom-call | bytes 12582912 | tf_op jit(solution)/shard_map/pallas_call | solution.py:234
  (99 shorter events, 31.3 us)
Async XLA Ops:
  1.0 12.4 %collective-permute-start.2 = (bf16[512,256]{1,0:T(8,128)(2,1)S(1)}, bf16[512,256]{1,0:T(8,128)(2,1)S(1)}, u32[]{:S(2)}, u32[]{:S(2)}) collective-permute-start(bf16[512,256]{1,0:T(8,128)(2,1)S(1)} %constant_dynamic-slice_fusion.1), channel_id=1, source_target_pairs={{0,2},{2,4},{4,6},{6,0},{1,3},{3,5},{5,7},{7,1},{8,10},{10,12},{12... | collective-permute-start | bytes 786440 | tf_op jit(solution)/shard_map/ppermute | solution.py:291
  4.0 19.7 %collective-permute-start.1 = (bf16[512,256]{1,0:T(8,128)(2,1)S(1)}, bf16[512,256]{1,0:T(8,128)(2,1)S(1)}, u32[]{:S(2)}, u32[]{:S(2)}) collective-permute-start(bf16[512,256]{1,0:T(8,128)(2,1)S(1)} %constant_dynamic-slice_fusion.1), channel_id=1, source_target_pairs={{0,4},{2,6},{4,0},{6,2},{1,5},{3,7},{5,1},{7,3},{8,12},{10,14},{12... | collective-permute-start | bytes 786440 | tf_op jit(solution)/shard_map/ppermute | solution.py:291
  6.6 17.1 %collective-permute-start = (bf16[512,256]{1,0:T(8,128)(2,1)S(1)}, bf16[512,256]{1,0:T(8,128)(2,1)S(1)}, u32[]{:S(2)}, u32[]{:S(2)}) collective-permute-start(bf16[512,256]{1,0:T(8,128)(2,1)S(1)} %constant_dynamic-slice_fusion.1), channel_id=1, source_target_pairs={{0,6},{2,0},{4,2},{6,4},{1,7},{3,1},{5,3},{7,5},{8,14},{10,8},{12,... | collective-permute-start | bytes 786440 | tf_op jit(solution)/shard_map/ppermute | solution.py:291
  23.8 47.1 %copy-start.16 = (bf16[3,512,256]{2,1,0:T(8,128)(2,1)}, bf16[3,512,256]{2,1,0:T(8,128)(2,1)S(1)}, u32[]{:S(2)}) copy-start(bf16[3,512,256]{2,1,0:T(8,128)(2,1)S(1)} %pad_maximum_fusion.refs_13_) | copy-start | bytes 2359300
  23.9 68.7 %copy-start.13 = (s32[3]{0:T(128)S(1)}, s32[3]{0:T(128)}, u32[]{:S(2)}) copy-start(s32[3]{0:T(128)} %pad_add_fusion.at_ref.core_ref) | copy-start | bytes 40
  23.9 68.7 %copy-start.15 = (f32[1,512]{1,0:T(1,128)S(1)}, f32[1,512]{1,0:T(1,128)}, u32[]{:S(2)}) copy-start(f32[1,512]{1,0:T(1,128)} %constant.61.clone.refs_5_) | copy-start | bytes 6148
  23.9 18.7 %collective-permute-start.3 = (bf16[896,256]{1,0:T(8,128)(2,1)S(1)}, bf16[896,256]{1,0:T(8,128)(2,1)S(1)}, u32[]{:S(2)}, u32[]{:S(2)}) collective-permute-start(bf16[896,256]{1,0:T(8,128)(2,1)S(1)} %get-tuple-element.42), channel_id=1, source_target_pairs={{0,2},{2,4},{4,6},{6,0},{1,3},{3,5},{5,7},{7,1},{8,10},{10,12},{12... | collective-permute-start | bytes 1376264 | tf_op jit(solution)/shard_map/ppermute | solution.py:298
  30.0 32.1 %collective-permute-start.8 = (bf16[3,512,256]{2,1,0:T(8,128)(2,1)S(1)}, bf16[3,512,256]{2,1,0:T(8,128)(2,1)S(1)}, u32[]{:S(2)}, u32[]{:S(2)}) collective-permute-start(bf16[3,512,256]{2,1,0:T(8,128)(2,1)S(1)} %pad_maximum_fusion.refs_13_), channel_id=1, source_target_pairs={{0,24},{8,16},{16,8},{24,0},{1,25},{9,17},{17,9},{25,1},{2,26},{10... | collective-permute-start | bytes 2359304 | tf_op jit(solution)/shard_map/ppermute | solution.py:294
  32.5 34.5 %collective-permute-start.7 = (bf16[3,512,256]{2,1,0:T(8,128)(2,1)S(1)}, bf16[3,512,256]{2,1,0:T(8,128)(2,1)S(1)}, u32[]{:S(2)}, u32[]{:S(2)}) collective-permute-start(bf16[3,512,256]{2,1,0:T(8,128)(2,1)S(1)} %pad_maximum_fusion.refs_13_), channel_id=1, source_target_pairs={{0,16},{8,24},{16,0},{24,8},{1,17},{9,25},{17,1},{25,9},{2,18},{10... | collective-permute-start | bytes 2359304 | tf_op jit(solution)/shard_map/ppermute | solution.py:294
  33.0 34.1 %collective-permute-start.6 = (bf16[3,512,256]{2,1,0:T(8,128)(2,1)S(1)}, bf16[3,512,256]{2,1,0:T(8,128)(2,1)S(1)}, u32[]{:S(2)}, u32[]{:S(2)}) collective-permute-start(bf16[3,512,256]{2,1,0:T(8,128)(2,1)S(1)} %pad_maximum_fusion.refs_13_), channel_id=1, source_target_pairs={{0,8},{8,0},{16,24},{24,16},{1,9},{9,1},{17,25},{25,17},{2,10},{10... | collective-permute-start | bytes 2359304 | tf_op jit(solution)/shard_map/ppermute | solution.py:294
  33.5 27.0 %collective-permute-start.4 = (bf16[896,256]{1,0:T(8,128)(2,1)S(1)}, bf16[896,256]{1,0:T(8,128)(2,1)S(1)}, u32[]{:S(2)}, u32[]{:S(2)}) collective-permute-start(bf16[896,256]{1,0:T(8,128)(2,1)S(1)} %get-tuple-element.43), channel_id=1, source_target_pairs={{0,4},{2,6},{4,0},{6,2},{1,5},{3,7},{5,1},{7,3},{8,12},{10,14},{12... | collective-permute-start | bytes 1376264 | tf_op jit(solution)/shard_map/ppermute | solution.py:298
  42.6 28.4 %copy-start.20 = (bf16[896,256]{1,0:T(8,128)(2,1)}, bf16[896,256]{1,0:T(8,128)(2,1)S(1)}, u32[]{:S(2)}) copy-start(bf16[896,256]{1,0:T(8,128)(2,1)S(1)} %collective-permute-done.3.refs_1_) | copy-start | bytes 1376260
  42.6 19.5 %collective-permute-start.5 = (bf16[896,256]{1,0:T(8,128)(2,1)S(1)}, bf16[896,256]{1,0:T(8,128)(2,1)S(1)}, u32[]{:S(2)}, u32[]{:S(2)}) collective-permute-start(bf16[896,256]{1,0:T(8,128)(2,1)S(1)} %get-tuple-element.44), channel_id=1, source_target_pairs={{0,6},{2,0},{4,2},{6,4},{1,7},{3,1},{5,3},{7,5},{8,14},{10,8},{12,... | collective-permute-start | bytes 1376264 | tf_op jit(solution)/shard_map/ppermute | solution.py:298
  60.5 7.1 %collective-permute-start.9 = (bf16[896,256]{1,0:T(8,128)(2,1)S(1)}, bf16[896,256]{1,0:T(8,128)(2,1)S(1)}, u32[]{:S(2)}, u32[]{:S(2)}) collective-permute-start(bf16[896,256]{1,0:T(8,128)(2,1)S(1)} %get-tuple-element.49), channel_id=1, source_target_pairs={{0,1},{1,0},{2,3},{3,2},{4,5},{5,4},{6,7},{7,6},{8,9},{9,8},{10,11... | collective-permute-start | bytes 1376264 | tf_op jit(solution)/shard_map/ppermute | solution.py:301
  67.1 1.8 %collective-permute-start.10 = (bf16[896,256]{1,0:T(8,128)(2,1)S(1)}, bf16[896,256]{1,0:T(8,128)(2,1)S(1)}, u32[]{:S(2)}, u32[]{:S(2)}) collective-permute-start(bf16[896,256]{1,0:T(8,128)(2,1)S(1)} %collective-permute-done.3.refs_1_), channel_id=1, source_target_pairs={{0,1},{1,0},{2,3},{3,2},{4,5},{5,4},{6,7},{7,6},{8,9},{9,8},{10,11... | collective-permute-start | bytes 1376264 | tf_op jit(solution)/shard_map/ppermute | solution.py:301
  67.1 3.1 %collective-permute-start.11 = (bf16[896,256]{1,0:T(8,128)(2,1)S(1)}, bf16[896,256]{1,0:T(8,128)(2,1)S(1)}, u32[]{:S(2)}, u32[]{:S(2)}) collective-permute-start(bf16[896,256]{1,0:T(8,128)(2,1)S(1)} %collective-permute-done.4.refs_2_), channel_id=1, source_target_pairs={{0,1},{1,0},{2,3},{3,2},{4,5},{5,4},{6,7},{7,6},{8,9},{9,8},{10,11... | collective-permute-start | bytes 1376264 | tf_op jit(solution)/shard_map/ppermute | solution.py:301
  67.6 3.4 %collective-permute-start.12 = (bf16[896,256]{1,0:T(8,128)(2,1)S(1)}, bf16[896,256]{1,0:T(8,128)(2,1)}, u32[]{:S(2)}, u32[]{:S(2)}) collective-permute-start(bf16[896,256]{1,0:T(8,128)(2,1)S(1)} %collective-permute-done.5.refs_3_), channel_id=1, source_target_pairs={{0,1},{1,0},{2,3},{3,2},{4,5},{5,4},{6,7},{7,6},{8,9},{9,8},{10,11... | collective-permute-start | bytes 1376264 | tf_op jit(solution)/shard_map/ppermute | solution.py:301
  85.1 22.7 %all-to-all-start = ((bf16[4,2,160,128]{3,2,1,0:T(8,128)(2,1)}), bf16[4,2,160,128]{3,2,1,0:T(8,128)(2,1)}, u32[]{:S(2)}, u32[]{:S(2)}) async-start(bf16[4,2,160,128]{3,2,1,0:T(8,128)(2,1)} %bitcast.40), calls=%async_computation | async-start | bytes 655360 | tf_op jit(solution)/shard_map/all_to_all | solution.py:366
  109.6 5.7 %collective-permute-start.15 = (bf16[2,160,128]{2,1,0:T(8,128)(2,1)}, bf16[2,160,128]{2,1,0:T(8,128)(2,1)}, u32[]{:S(2)}, u32[]{:S(2)}) collective-permute-start(bf16[2,160,128]{2,1,0:T(8,128)(2,1)} %reduce_sum.12), channel_id=1, source_target_pairs={{0,24},{8,16},{16,8},{24,0},{1,25},{9,17},{17,9},{25,1},{2,26},{10... | collective-permute-start | bytes 245768 | tf_op jit(solution)/shard_map/ppermute | solution.py:370
  112.0 5.0 %collective-permute-start.14 = (bf16[2,160,128]{2,1,0:T(8,128)(2,1)}, bf16[2,160,128]{2,1,0:T(8,128)(2,1)}, u32[]{:S(2)}, u32[]{:S(2)}) collective-permute-start(bf16[2,160,128]{2,1,0:T(8,128)(2,1)} %reduce_sum.12), channel_id=1, source_target_pairs={{0,16},{8,24},{16,0},{24,8},{1,17},{9,25},{17,1},{25,9},{2,18},{10... | collective-permute-start | bytes 245768 | tf_op jit(solution)/shard_map/ppermute | solution.py:370
  112.5 4.8 %collective-permute-start.13 = (bf16[2,160,128]{2,1,0:T(8,128)(2,1)}, bf16[2,160,128]{2,1,0:T(8,128)(2,1)}, u32[]{:S(2)}, u32[]{:S(2)}) collective-permute-start(bf16[2,160,128]{2,1,0:T(8,128)(2,1)} %reduce_sum.12), channel_id=1, source_target_pairs={{0,8},{8,0},{16,24},{24,16},{1,9},{9,1},{17,25},{25,17},{2,10},{10... | collective-permute-start | bytes 245768 | tf_op jit(solution)/shard_map/ppermute | solution.py:370
  119.2 12.5 %collective-permute-start.16 = (bf16[2,160,128]{2,1,0:T(8,128)(2,1)}, bf16[2,160,128]{2,1,0:T(8,128)(2,1)S(1)}, u32[]{:S(2)}, u32[]{:S(2)}) collective-permute-start(bf16[2,160,128]{2,1,0:T(8,128)(2,1)} %get-tuple-element.62), channel_id=1, source_target_pairs={{0,6},{2,0},{4,2},{6,4},{1,7},{3,1},{5,3},{7,5},{8,14},{10,8},{12,... | collective-permute-start | bytes 245768 | tf_op jit(solution)/shard_map/ppermute | solution.py:379
  123.0 8.7 %collective-permute-start.17 = (bf16[2,160,128]{2,1,0:T(8,128)(2,1)}, bf16[2,160,128]{2,1,0:T(8,128)(2,1)S(1)}, u32[]{:S(2)}, u32[]{:S(2)}) collective-permute-start(bf16[2,160,128]{2,1,0:T(8,128)(2,1)} %get-tuple-element.63), channel_id=1, source_target_pairs={{0,4},{2,6},{4,0},{6,2},{1,5},{3,7},{5,1},{7,3},{8,12},{10,14},{12... | collective-permute-start | bytes 245768 | tf_op jit(solution)/shard_map/ppermute | solution.py:379
  123.0 8.7 %collective-permute-start.18 = (bf16[2,160,128]{2,1,0:T(8,128)(2,1)}, bf16[2,160,128]{2,1,0:T(8,128)(2,1)S(1)}, u32[]{:S(2)}, u32[]{:S(2)}) collective-permute-start(bf16[2,160,128]{2,1,0:T(8,128)(2,1)} %get-tuple-element.64), channel_id=1, source_target_pairs={{0,2},{2,4},{4,6},{6,0},{1,3},{3,5},{5,7},{7,1},{8,10},{10,12},{12... | collective-permute-start | bytes 245768 | tf_op jit(solution)/shard_map/ppermute | solution.py:379
  133.6 2.5 %collective-permute-start.19 = (bf16[448,1024]{1,0:T(8,128)(2,1)S(1)}, bf16[448,1024]{1,0:T(8,128)(2,1)S(1)}, u32[]{:S(2)}, u32[]{:S(2)}) collective-permute-start(bf16[448,1024]{1,0:T(8,128)(2,1)S(1)} %shard_map.104.mine_ref), channel_id=1, source_target_pairs={{0,1},{1,0},{2,3},{3,2},{4,5},{5,4},{6,7},{7,6},{8,9},{9,8},{10,11... | collective-permute-start | bytes 2752520 | tf_op jit(solution)/shard_map/ppermute | solution.py:425
  135.4 9.0 %collective-permute-start.20 = (bf16[448,1024]{1,0:T(8,128)(2,1)S(1)}, bf16[448,1024]{1,0:T(8,128)(2,1)S(1)}, u32[]{:S(2)}, u32[]{:S(2)}) collective-permute-start(bf16[448,1024]{1,0:T(8,128)(2,1)S(1)} %shard_map.106.mine_ref), channel_id=1, source_target_pairs={{0,1},{1,0},{2,3},{3,2},{4,5},{5,4},{6,7},{7,6},{8,9},{9,8},{10,11... | collective-permute-start | bytes 2752520 | tf_op jit(solution)/shard_map/ppermute | solution.py:425
  137.8 12.5 %collective-permute-start.21 = (bf16[448,256]{1,0:T(8,128)(2,1)S(1)}, bf16[448,256]{1,0:T(8,128)(2,1)S(1)}, u32[]{:S(2)}, u32[]{:S(2)}) collective-permute-start(bf16[448,256]{1,0:T(8,128)(2,1)S(1)} %get-tuple-element.71), channel_id=1, source_target_pairs={{0,2},{2,4},{4,6},{6,0},{1,3},{3,5},{5,7},{7,1},{8,10},{10,12},{12... | collective-permute-start | bytes 688136 | tf_op jit(solution)/shard_map/ppermute | solution.py:432
  140.2 17.9 %collective-permute-start.23 = (bf16[448,256]{1,0:T(8,128)(2,1)S(1)}, bf16[448,256]{1,0:T(8,128)(2,1)S(1)}, u32[]{:S(2)}, u32[]{:S(2)}) collective-permute-start(bf16[448,256]{1,0:T(8,128)(2,1)S(1)} %get-tuple-element.73), channel_id=1, source_target_pairs={{0,4},{2,6},{4,0},{6,2},{1,5},{3,7},{5,1},{7,3},{8,12},{10,14},{12... | collective-permute-start | bytes 688136 | tf_op jit(solution)/shard_map/ppermute | solution.py:432
  142.8 15.3 %collective-permute-start.25 = (bf16[448,256]{1,0:T(8,128)(2,1)S(1)}, bf16[448,256]{1,0:T(8,128)(2,1)S(1)}, u32[]{:S(2)}, u32[]{:S(2)}) collective-permute-start(bf16[448,256]{1,0:T(8,128)(2,1)S(1)} %get-tuple-element.75), channel_id=1, source_target_pairs={{0,6},{2,0},{4,2},{6,4},{1,7},{3,1},{5,3},{7,5},{8,14},{10,8},{12,... | collective-permute-start | bytes 688136 | tf_op jit(solution)/shard_map/ppermute | solution.py:432
  146.1 16.9 %collective-permute-start.22 = (bf16[448,256]{1,0:T(8,128)(2,1)S(1)}, bf16[448,256]{1,0:T(8,128)(2,1)S(1)}, u32[]{:S(2)}, u32[]{:S(2)}) collective-permute-start(bf16[448,256]{1,0:T(8,128)(2,1)S(1)} %get-tuple-element.72), channel_id=1, source_target_pairs={{0,2},{2,4},{4,6},{6,0},{1,3},{3,5},{5,7},{7,1},{8,10},{10,12},{12... | collective-permute-start | bytes 688136 | tf_op jit(solution)/shard_map/ppermute | solution.py:432
  146.6 30.3 %collective-permute-start.24 = (bf16[448,256]{1,0:T(8,128)(2,1)S(1)}, bf16[448,256]{1,0:T(8,128)(2,1)S(1)}, u32[]{:S(2)}, u32[]{:S(2)}) collective-permute-start(bf16[448,256]{1,0:T(8,128)(2,1)S(1)} %get-tuple-element.74), channel_id=1, source_target_pairs={{0,4},{2,6},{4,0},{6,2},{1,5},{3,7},{5,1},{7,3},{8,12},{10,14},{12... | collective-permute-start | bytes 688136 | tf_op jit(solution)/shard_map/ppermute | solution.py:432
  150.3 26.6 %collective-permute-start.26 = (bf16[448,256]{1,0:T(8,128)(2,1)S(1)}, bf16[448,256]{1,0:T(8,128)(2,1)S(1)}, u32[]{:S(2)}, u32[]{:S(2)}) collective-permute-start(bf16[448,256]{1,0:T(8,128)(2,1)S(1)} %get-tuple-element.76), channel_id=1, source_target_pairs={{0,6},{2,0},{4,2},{6,4},{1,7},{3,1},{5,3},{7,5},{8,14},{10,8},{12,... | collective-permute-start | bytes 688136 | tf_op jit(solution)/shard_map/ppermute | solution.py:432
  (24 other events, 139.0 us)
